TPU v7x, 512 devices: a whole 4x4x16 slice. The times are simulated.
512 devices in a mesh: ctx: 8 (over x, core), clu: 16 (over z), tp: 4 (over y).
Axes of the slice: x: 4, y: 4, z: 16, core: 2. Of those that a mesh axis runs over, the one named last changes fastest.
Arguments:
- tokens: bfloat16 [8, 4096, 4096], P('ctx', 'clu'), may hold values from -32 to 32
- proj_weight: bfloat16 [4096, 2, 2048], P(('ctx', 'clu'), None, 'tp'), may hold values from -0.09375 to 0.09375
- clusters: int32 [8, 4096, 16], P('ctx', 'clu', 'tp'), may hold values from 0 to 63, as said below
Outputs:
- attended: bfloat16 [8, 4096, 2048], P('ctx', 'clu', 'tp')
Inputs may be any that keep to these rules, and one draw needn't show every extreme that they name: `clusters`: owner k of head h holds ids k * 4 to (k + 1) * 4 - 1. In each aligned block of 256 positions of a sequence, for every head, at most 32 positions have ids of one owner; for each sequence and head one owner has exactly 32 positions in every block.
All inputs are finite; a program needn't handle non-finite values.
Results may differ from a plain program's by a relative error of at most 0.0068.
Values may be sent and summed in bfloat16 or wider, within the bound.
No kernel may reach another device: no remote copies, remote signals or barrier semaphores. Data moves between devices by JAX's collectives and lax.ppermute only.
A program may use at most 64 MiB of HBM per device.

v0:
```python
import jax
import jax.numpy as jnp
from jax import lax
from jax.sharding import PartitionSpec as P

CLUSTERS = 64


def body(tokens, proj_weight, clusters):
    local_rows = tokens[0]
    row_count = local_rows.shape[0]
    owners = lax.axis_size("clu")
    heads_here = clusters.shape[2]
    proj_width = proj_weight.shape[2]
    head_dim = proj_width // heads_here
    capacity = 2 * row_count // owners
    per_owner = CLUSTERS // owners
    length = row_count * owners
    total_slots = owners * capacity
    score_scale = head_dim ** (-0.5)
    weight_piece = lax.all_gather(proj_weight, ("ctx", "clu"), axis=0, tiled=True)
    flat_piece = weight_piece.reshape(weight_piece.shape[0], 2 * proj_width)
    summed = jnp.dot(local_rows, flat_piece, preferred_element_type=jnp.float32)
    projected = summed.astype(jnp.bfloat16)
    queries = projected[:, :proj_width].reshape(row_count, heads_here, head_dim)
    values = projected[:, proj_width:].reshape(row_count, heads_here, head_dim)
    features = jnp.concatenate([queries, values], axis=2).transpose(1, 0, 2)
    cluster_ids = clusters[0]
    owner_of = cluster_ids // per_owner
    onehot = (owner_of[:, :, None] == jnp.arange(owners, dtype=jnp.int32)[None, None, :]).astype(
        jnp.int32
    )
    rank_in = jnp.sum((jnp.cumsum(onehot, axis=0) - onehot) * onehot, axis=2)
    slot_of = (owner_of * capacity + rank_in).T
    head_rows = jnp.arange(heads_here, dtype=jnp.int32)[:, None]
    token_index = jnp.broadcast_to(
        jnp.arange(row_count, dtype=jnp.int32)[None, :], (heads_here, row_count)
    )
    source = jnp.zeros((heads_here, total_slots), jnp.int32).at[head_rows, slot_of].set(token_index)
    positions = lax.axis_index("clu") * row_count + jnp.arange(row_count, dtype=jnp.int32)
    labels = cluster_ids.T * length + positions[None, :]
    slot_tags = (
        jnp.full((heads_here, total_slots), -1, jnp.int32).at[head_rows, slot_of].set(labels)
    )
    outgoing = jnp.take_along_axis(features, source[:, :, None], axis=1)
    outgoing = jnp.where((slot_tags >= 0)[:, :, None], outgoing, jnp.zeros_like(outgoing))
    outgoing = outgoing.reshape(heads_here, owners, capacity, 2 * head_dim)
    slot_tags = slot_tags.reshape(heads_here, owners, capacity)

    def attend_head(head_item):
        slot_block, key_tags = head_item
        flattened = slot_block.reshape(-1, 2 * head_dim)
        key_rows = flattened[:, :head_dim]
        value_rows = flattened[:, head_dim:]
        key_tags = key_tags.reshape(-1)
        scores = (
            jnp.einsum("qd,kd->qk", key_rows, key_rows, preferred_element_type=jnp.float32)
            * score_scale
        )
        tag_group = key_tags // length
        tag_pos = key_tags % length
        admitted = (
            (key_tags[None, :] >= 0)
            & (tag_group[None, :] == tag_group[:, None])
            & (tag_pos[None, :] <= tag_pos[:, None])
        )
        scores = jnp.where(key_tags[None, :] == key_tags[:, None], -100000.0, scores)
        scores = jnp.where(admitted, scores, -1e30)
        row_max = jnp.max(scores, axis=1, keepdims=True)
        exp_scores = jnp.exp(scores - row_max)
        row_total = jnp.sum(exp_scores, axis=1, keepdims=True)
        probabilities = (exp_scores / row_total).astype(jnp.bfloat16)
        result = jnp.dot(probabilities, value_rows, preferred_element_type=jnp.float32).astype(
            jnp.bfloat16
        )
        return result.reshape(slot_block.shape[0], slot_block.shape[1], head_dim)

    replies = lax.map(
        attend_head,
        (
            lax.all_to_all(outgoing, "clu", split_axis=1, concat_axis=1, tiled=True),
            lax.all_to_all(slot_tags, "clu", split_axis=1, concat_axis=1, tiled=True),
        ),
    )
    returned = lax.all_to_all(replies, "clu", split_axis=1, concat_axis=1, tiled=True)
    returned = returned.reshape(heads_here, total_slots, head_dim)
    gathered = jnp.take_along_axis(returned, slot_of[:, :, None], axis=1)
    return gathered.transpose(1, 0, 2).reshape(1, row_count, heads_here * head_dim)


def solution(mesh):
    return jax.shard_map(
        body,
        mesh=mesh,
        in_specs=(P("ctx", "clu", None), P(("ctx", "clu"), None, "tp"), P("ctx", "clu", "tp")),
        out_specs=P("ctx", "clu", "tp"),
        check_vma=False,
    )
```

profile of v0, /device:TPU:24, one launch (start us, length us, event | category | flops | bytes accessed | tf_op | source)
XLA Modules:
  0.0 317.0 jit_solution(4863949393739321248)
XLA Ops:
  6.5 0.7 all-gather.2.cloned.1.call-update
  7.3 0.7 fusion.21
  8.0 2.3 reduce-window.6
  10.7 0.7 multiply_reduce_fusion
  11.5 0.7 and_reduce_fusion
  12.2 4.3 %scatter_custom_fusion = s32[2048]{0:T(1024)S(1)} fusion(s32[1024]{0:T(1024)S(1)} %bitcast.129, s32[1024]{0:T(1024)S(1)} %bitcast.128, s32[]{:T(128)} %constant.140.clone.1), kind=kCustom, calls=%fused_computation.70 | custom fusion | bytes 8196
  16.6 0.7 reshape.271
  17.3 15.2 %all-to-all-start = ((s32[16,1,128]{2,1,0:T(1,128)}), s32[16,1,128]{2,1,0:T(1,128)S(1)}, u32[]{:S(2)}, u32[]{:S(2)}) async-start(s32[16,1,128]{2,1,0:T(1,128)} %reshape.271), calls=%async_computation | async-start | bytes 16384 | tf_op jit(solution)/shard_map/all_to_all | solution.py:82
  32.6 4.3 %scatter_custom_fusion.1 = s32[2048]{0:T(1024)S(1)} fusion(s32[1024]{0:T(1024)S(1)} %bitcast.130, s32[1024]{0:T(1024)S(1)} %bitcast.131, s32[]{:T(128)} %copy.66), kind=kCustom, calls=%fused_computation.67 | custom fusion | bytes 8196
  37.2 125.1 %all-gather.2.cloned.1.call-done = bf16[4096,2,512]{2,1,0:T(2,128)(2,1)} async-done(((bf16[32,2,512]{2,1,0:T(2,128)(2,1)}), bf16[4096,2,512]{2,1,0:T(2,128)(2,1)}) %all-gather.2.cloned.1.call-update) | async-done | bytes 8388624 | tf_op jit(solution)/shard_map/all_gather | solution.py:21
  162.3 9.3 %copy.47 = bf16[512,8,2,512]{3,1,2,0:T(8,128)(2,1)} copy(bf16[512,8,2,512]{3,2,1,0:T(2,128)(2,1)} %bitcast.117) | data formatting | bytes 16777216
  171.6 5.7 %fusion.8 = bf16[256,1024]{1,0:T(8,128)(2,1)S(1)} fusion(bf16[4096,1024]{1,0:T(8,128)(2,1)} %bitcast.118, bf16[1,256,4096]{2,1,0:T(8,128)(2,1)S(1)} %copy-done), kind=kOutput, calls=%fused_computation.27 | convolution fusion | flops 2147745792 | bytes 11010048 | tf_op jit(solution)/shard_map/dot_general | solution.py:23
  177.5 20.6 %gather_fusion = bf16[2048,256]{1,0:T(8,128)(2,1)} fusion(bf16[4,256,256]{2,1,0:T(8,128)(2,1)S(1)} %maximum_bitcast_fusion, s32[2048]{0:T(1024)S(1)} %bitcast.114), kind=kCustom, calls=%fused_computation | custom fusion | bytes 2113536 | tf_op jit(solution)/shard_map/jit(take_along_axis)/gather | solution.py:45
  198.1 2.6 fusion.11
  200.7 6.9 %all-to-all-start.1 = ((bf16[4,16,32,256]{3,2,0,1:T(8,128)(2,1)}), bf16[4,16,32,256]{3,2,0,1:T(8,128)(2,1)S(1)}, u32[]{:S(2)}, u32[]{:S(2)}) async-start(bf16[4,16,32,256]{3,2,0,1:T(8,128)(2,1)} %fusion.11), calls=%async_computation.1 | async-start | bytes 2097152 | tf_op jit(solution)/shard_map/all_to_all | solution.py:81
  208.9 49.1 %all-to-all-done.1 = bf16[4,16,32,256]{3,2,0,1:T(8,128)(2,1)S(1)} async-done(((bf16[4,16,32,256]{3,2,0,1:T(8,128)(2,1)}), bf16[4,16,32,256]{3,2,0,1:T(8,128)(2,1)S(1)}, u32[]{:S(2)}, u32[]{:S(2)}) %all-to-all-start.1) | async-done | bytes 1048608 | tf_op jit(solution)/shard_map/all_to_all | solution.py:81
  258.0 7.9 %while.12 = (s32[]{:T(128)}, bf16[4,16,32,128]{3,2,0,1:T(8,128)(2,1)}, s32[4,16,32]{2,0,1:T(4,128)S(1)}, bf16[4,16,32,256]{3,2,0,1:T(8,128)(2,1)S(1)}, s32[]{:T(128)}) while((s32[]{:T(128)}, bf16[4,16,32,128]{3,2,0,1:T(8,128)(2,1)}, s32[4,16,32]{2,0,1:T(4,128)S(1)}, bf16[4,16,32,256]{3,2,0,1:T(8,128)(2,1)S(1)}, s32[]{:T(128)}) %tuple.43), condition=%wide.region_8.9_spmd, body=%wide.region_5.8_spmd.sunk | while | flops 137962496 | bytes 4365393 | solution.py:78
  259.3 0.8 constant_dynamic-update-slice_fusion.2
  261.3 0.7 constant_dynamic-update-slice_fusion.2
  265.2 0.7 constant_dynamic-update-slice_fusion.2
  265.9 8.0 %all-to-all-start.2 = ((bf16[4,16,32,128]{3,2,0,1:T(8,128)(2,1)}), bf16[4,16,32,128]{3,2,0,1:T(8,128)(2,1)S(1)}, u32[]{:S(2)}, u32[]{:S(2)}) async-start(bf16[4,16,32,128]{3,2,0,1:T(8,128)(2,1)} %get-tuple-element.61), calls=%async_computation.2 | async-start | bytes 1048576 | tf_op jit(solution)/shard_map/all_to_all | solution.py:85
  273.9 29.1 %all-to-all-done.2 = bf16[4,16,32,128]{3,2,0,1:T(8,128)(2,1)S(1)} async-done(((bf16[4,16,32,128]{3,2,0,1:T(8,128)(2,1)}), bf16[4,16,32,128]{3,2,0,1:T(8,128)(2,1)S(1)}, u32[]{:S(2)}, u32[]{:S(2)}) %all-to-all-start.2) | async-done | bytes 524320 | tf_op jit(solution)/shard_map/all_to_all | solution.py:85
  303.1 5.8 %gather_fusion.1 = bf16[1024,128]{1,0:T(8,128)(2,1)S(1)} fusion(bf16[4,512,128]{2,1,0:T(8,128)(2,1)S(1)} %bitcast.116, s32[1024]{0:T(1024)S(1)} %bitcast.115), kind=kCustom, calls=%fused_computation.1 | custom fusion | bytes 532480 | tf_op jit(solution)/shard_map/jit(take_along_axis)/gather | solution.py:87
  309.4 0.8 reshape.223
  (73 shorter events, 8.4 us)
Async XLA Ops:
  6.5 165.1 %copy-start = (bf16[1,256,4096]{2,1,0:T(8,128)(2,1)S(1)}, bf16[1,256,4096]{2,1,0:T(8,128)(2,1)}, u32[]{:S(2)}) copy-start(bf16[1,256,4096]{2,1,0:T(8,128)(2,1)} %param.5) | copy-start | bytes 6291460
  6.5 155.8 %all-gather.2.cloned.1.call-start = ((), (), s32[]{:S(2)}) async-start(), calls=%async_computation.3 | async-start | bytes 8454144 | tf_op jit(solution)/shard_map/all_gather | solution.py:21
  17.3 183.4 %all-to-all-start = ((s32[16,1,128]{2,1,0:T(1,128)}), s32[16,1,128]{2,1,0:T(1,128)S(1)}, u32[]{:S(2)}, u32[]{:S(2)}) async-start(s32[16,1,128]{2,1,0:T(1,128)} %reshape.271), calls=%async_computation | async-start | bytes 16384 | tf_op jit(solution)/shard_map/all_to_all | solution.py:82
  200.7 57.3 %all-to-all-start.1 = ((bf16[4,16,32,256]{3,2,0,1:T(8,128)(2,1)}), bf16[4,16,32,256]{3,2,0,1:T(8,128)(2,1)S(1)}, u32[]{:S(2)}, u32[]{:S(2)}) async-start(bf16[4,16,32,256]{3,2,0,1:T(8,128)(2,1)} %fusion.11), calls=%async_computation.1 | async-start | bytes 2097152 | tf_op jit(solution)/shard_map/all_to_all | solution.py:81
  265.9 37.2 %all-to-all-start.2 = ((bf16[4,16,32,128]{3,2,0,1:T(8,128)(2,1)}), bf16[4,16,32,128]{3,2,0,1:T(8,128)(2,1)S(1)}, u32[]{:S(2)}, u32[]{:S(2)}) async-start(bf16[4,16,32,128]{3,2,0,1:T(8,128)(2,1)} %get-tuple-element.61), calls=%async_computation.2 | async-start | bytes 1048576 | tf_op jit(solution)/shard_map/all_to_all | solution.py:85
Sparse Core Ops, SparseCore 0:
  10.5 151.7 all-gather.1
where the time goes:
time: 318 us; the launch traced here: 317 us
  waiting for transfers between devices  204 us (64%)
  local copies, waits for them, and re-layouts  50.8 us (16%)
  starting transfers between devices  30.1 us (9%)
  between operations  13.6 us (4%)
  matrix products  9.37 us (3%)
  other arithmetic  8.99 us (3%)
    all_gather x1, waiting for transfers between devices, body(): lax.all_gather(proj_weight, ('ctx', 'clu'), axis=0, tiled=True)  125 us
    all_to_all x1, waiting for transfers between devices, body(): lax.all_to_all(outgoing, 'clu', split_axis=1, concat_axis=1, tiled=True)  49.1 us
    all_to_all x1, waiting for transfers between devices, body(): lax.all_to_all(replies, 'clu', split_axis=1, concat_axis=1, tiled=True)  29.1 us
    gather x1, local copies, waits for them, and re-layouts, body(): outgoing = jnp.take_along_axis(features, source[:, :, None], axis=1)  20.6 us
    unnamed x14, local copies, waits for them, and re-layouts  18.8 us
    all_to_all x1, starting transfers between devices, body(): lax.all_to_all(slot_tags, 'clu', split_axis=1, concat_axis=1, tiled=True)  15.2 us
    all_to_all x1, starting transfers between devices, body(): lax.all_to_all(replies, 'clu', split_axis=1, concat_axis=1, tiled=True)  7.98 us
    all_to_all x1, starting transfers between devices, body(): lax.all_to_all(outgoing, 'clu', split_axis=1, concat_axis=1, tiled=True)  6.94 us
  transfers between devices with their start and end apart: 4, of which 3 were waited for; matrix products, arithmetic and copies ran while one was open for 17% of the time, Pallas kernels for 0%

commit v1 on v0

v1 whole, which is shorter than its diff:
```python
import jax
import jax.numpy as jnp
from jax import lax
from jax.experimental import pallas as pl
from jax.experimental.pallas import tpu as pltpu
from jax.sharding import PartitionSpec as P

CLUSTERS = 64
BF16 = jnp.bfloat16
F32 = jnp.float32
VMEM_LIMIT = 48 * 1024 * 1024


def vmem_call(kernel, out_shape, count, flops=0, bytes_accessed=0):
    vmem = pl.BlockSpec(memory_space=pltpu.VMEM)
    return pl.pallas_call(
        kernel,
        out_shape=out_shape,
        in_specs=[vmem] * count,
        out_specs=jax.tree.map(lambda _: vmem, out_shape),
        compiler_params=pltpu.CompilerParams(vmem_limit_bytes=VMEM_LIMIT),
        cost_estimate=pl.CostEstimate(
            flops=flops, bytes_accessed=bytes_accessed, transcendentals=0
        ),
    )


def routing(ids, owners, capacity):
    rows, heads = ids.shape
    per_owner = CLUSTERS // owners
    slots = owners * capacity

    def kernel(ids_ref, ids_t_ref, slot_row_ref, slot_col_ref, tag_ref):
        above = lax.broadcasted_iota(jnp.int32, (rows, rows), 0)
        across = lax.broadcasted_iota(jnp.int32, (rows, rows), 1)
        before_col = (across < above).astype(BF16)
        before_row = (above < across).astype(BF16)
        for h in range(heads):
            id_col = ids_ref[:, h : h + 1]
            owner_col = id_col // per_owner
            hot = owner_col == lax.broadcasted_iota(jnp.int32, (rows, owners), 1)
            count = jnp.dot(before_col, hot.astype(BF16), preferred_element_type=F32)
            rank = jnp.sum(jnp.where(hot, count, 0.0), axis=1, keepdims=True)
            slot_col = owner_col * capacity + rank.astype(jnp.int32)
            slot_col_ref[:, h : h + 1] = slot_col
            id_row = ids_t_ref[h : h + 1, :]
            owner_row = id_row // per_owner
            hot = owner_row == lax.broadcasted_iota(jnp.int32, (owners, rows), 0)
            count = jnp.dot(hot.astype(BF16), before_row, preferred_element_type=F32)
            rank = jnp.sum(jnp.where(hot, count, 0.0), axis=0, keepdims=True)
            slot_row_ref[h : h + 1, :] = owner_row * capacity + rank.astype(jnp.int32)
            tag = (id_row - owner_row * per_owner + 1).astype(BF16)
            place = slot_col == lax.broadcasted_iota(jnp.int32, (rows, slots), 1)
            tags = jnp.dot(
                jnp.broadcast_to(tag, (16, rows)), place.astype(BF16), preferred_element_type=F32
            )
            tag_ref[h : h + 1, :] = tags[:1].astype(jnp.int32)

    return vmem_call(
        kernel,
        (
            jax.ShapeDtypeStruct((heads, rows), jnp.int32),
            jax.ShapeDtypeStruct((rows, heads), jnp.int32),
            jax.ShapeDtypeStruct((heads, slots), jnp.int32),
        ),
        2,
    )(ids, ids.T)


def pack(partial, slot_row, owners, capacity, head_dim):
    parts, rows, width = partial.shape
    heads = slot_row.shape[0]
    half = width // 2
    slots = owners * capacity

    def kernel(partial_ref, slot_ref, out_ref):
        def columns(first):
            cols = slice(first, first + head_dim)
            total = partial_ref[0, :, cols].astype(F32)
            for p in range(1, parts):
                total += partial_ref[p, :, cols].astype(F32)
            return total.astype(BF16)

        for h in range(heads):
            place = lax.broadcasted_iota(jnp.int32, (slots, rows), 0) == slot_ref[h : h + 1, :]
            place = place.astype(BF16)
            for m in range(2):
                packed = jnp.dot(
                    place, columns(m * half + h * head_dim), preferred_element_type=F32
                ).astype(BF16)
                out_ref[
                    :, h * capacity : (h + 1) * capacity, m * head_dim : (m + 1) * head_dim
                ] = packed.reshape(owners, capacity, head_dim)

    return vmem_call(
        kernel, jax.ShapeDtypeStruct((owners, heads * capacity, 2 * head_dim), BF16), 2
    )(partial, slot_row)


def attend(blocks, tags, capacity, per_owner):
    sources, rows, width = blocks.shape
    head_dim = width // 2
    heads = rows // capacity
    slots = sources * capacity
    scale = head_dim ** (-0.5)

    def kernel(block_ref, tag_ref, out_ref):
        query = lax.broadcasted_iota(jnp.int32, (slots, slots), 0)
        key = lax.broadcasted_iota(jnp.int32, (slots, slots), 1)
        for h in range(heads):
            here = slice(h * capacity, (h + 1) * capacity)
            keys = block_ref[:, here, :head_dim].reshape(slots, head_dim)
            values = block_ref[:, here, head_dim:].reshape(slots, head_dim)
            kinds = lax.broadcasted_iota(jnp.int32, (16, slots), 0) + 1
            member = (tag_ref[h : h + 1, :] == kinds).astype(BF16)
            same = lax.dot_general(
                member, member, (((0,), (0,)), ((), ())), preferred_element_type=F32
            )
            scores = lax.dot_general(
                keys, keys, (((1,), (1,)), ((), ())), preferred_element_type=F32
            )
            scores = scores * scale
            scores = jnp.where(query == key, -100000.0, scores)
            scores = jnp.where((same > 0.5) & (key <= query), scores, -1e30)
            row_max = jnp.max(scores, axis=1, keepdims=True)
            weights = jnp.exp(scores - row_max)
            total = jnp.sum(weights, axis=1, keepdims=True)
            probabilities = (weights / total).astype(BF16)
            result = jnp.dot(probabilities, values, preferred_element_type=F32).astype(BF16)
            out_ref[:, here, :] = result.reshape(sources, capacity, head_dim)

    return vmem_call(kernel, jax.ShapeDtypeStruct((sources, rows, head_dim), BF16), 2)(
        blocks, tags
    )


def unpack(returned, slot_col, capacity):
    owners, height, head_dim = returned.shape
    rows, heads = slot_col.shape
    slots = owners * capacity

    def kernel(block_ref, slot_ref, out_ref):
        for h in range(heads):
            block = block_ref[:, h * capacity : (h + 1) * capacity, :].reshape(slots, head_dim)
            place = slot_ref[:, h : h + 1] == lax.broadcasted_iota(jnp.int32, (rows, slots), 1)
            out_ref[:, h * head_dim : (h + 1) * head_dim] = jnp.dot(
                place.astype(BF16), block, preferred_element_type=F32
            ).astype(BF16)

    return vmem_call(kernel, jax.ShapeDtypeStruct((rows, heads * head_dim), BF16), 2)(
        returned, slot_col
    )


def shifted(block, step, size):
    return lax.ppermute(block, "clu", [(i, (i + step) % size) for i in range(size)])


def gather_z(own):
    size = lax.axis_size("clu")
    me = lax.axis_index("clu")
    from_minus4 = shifted(own, 4, size)
    from_plus4 = shifted(own, -4, size)
    from_8 = shifted(own, 8, size)
    four = jnp.stack([own, from_plus4, from_8, from_minus4])
    from_minus1 = shifted(four, 1, size)
    from_plus1 = shifted(four, -1, size)
    minus2 = shifted(jnp.stack([own, from_minus4]), 2, size)
    plus2 = shifted(jnp.stack([own, from_plus4]), -2, size)
    order = jnp.stack(
        [
            four,
            from_plus1,
            jnp.stack([plus2[0], plus2[1], minus2[1], minus2[0]]),
            jnp.concatenate([from_minus1[1:], from_minus1[:1]]),
        ],
        axis=1,
    )
    return order.reshape((size,) + own.shape), me


def body(tokens, proj_weight, clusters):
    rows, depth = tokens.shape[1:]
    owners = lax.axis_size("clu")
    heads = clusters.shape[2]
    shard = proj_weight.shape[0]
    width = 2 * proj_weight.shape[2]
    head_dim = proj_weight.shape[2] // heads
    capacity = 2 * rows // owners
    per_owner = CLUSTERS // owners
    cores = lax.axis_size("core")
    chips = lax.axis_size("x")
    core = lax.axis_index("core")

    pieces = tokens[0].reshape(rows, chips, depth // chips).transpose(1, 0, 2)
    pieces = lax.all_to_all(pieces, "x", split_axis=0, concat_axis=0, tiled=True)
    pieces = pieces.reshape(chips * rows, depth // chips)

    slot_row, slot_col, slot_tags = routing(clusters[0], owners, capacity)
    slot_tags = slot_tags.reshape(heads, owners, capacity).transpose(1, 0, 2)
    key_tags = lax.all_to_all(slot_tags, "clu", split_axis=0, concat_axis=0, tiled=True)
    key_tags = key_tags.transpose(1, 0, 2).reshape(heads, owners * capacity)

    own = proj_weight.reshape(shard, width)
    ring, me = gather_z(own)
    ring = jnp.roll(ring, me, axis=0).reshape(owners * shard, width)
    other = lax.ppermute(ring, "core", [(0, 1), (1, 0)])
    deep = owners * shard
    mine = lax.dynamic_slice_in_dim(pieces, core * deep, deep, 1)
    theirs = lax.dynamic_slice_in_dim(pieces, (1 - core) * deep, deep, 1)
    partial = jnp.dot(mine, ring, preferred_element_type=F32)
    partial = partial + jnp.dot(theirs, other, preferred_element_type=F32)
    partial = partial.astype(BF16).reshape(chips, rows, width)
    partial = lax.all_to_all(partial, "x", split_axis=0, concat_axis=0, tiled=True)

    outgoing = pack(partial, slot_row, owners, capacity, head_dim)
    incoming = lax.all_to_all(outgoing, "clu", split_axis=0, concat_axis=0, tiled=True)
    replies = attend(incoming, key_tags, capacity, per_owner)
    returned = lax.all_to_all(replies, "clu", split_axis=0, concat_axis=0, tiled=True)
    return unpack(returned, slot_col, capacity)[None]


def solution(mesh):
    names = mesh.axis_names
    ctx, clu, tp = (mesh.shape[name] for name in names)
    fine = jax.sharding.Mesh(
        mesh.devices.reshape(ctx // 2, 2, clu, tp), ("x", "core") + names[1:]
    )
    ctx_axes = ("x", "core")
    return jax.shard_map(
        body,
        mesh=fine,
        in_specs=(
            P(ctx_axes, "clu", None),
            P(ctx_axes + ("clu",), None, "tp"),
            P(ctx_axes, "clu", "tp"),
        ),
        out_specs=P(ctx_axes, "clu", "tp"),
        check_vma=False,
    )
```

time: 318 us -> 211 us (0.66)
  waiting for transfers between devices: 204 us -> 89.1 us
  local copies, waits for them, and re-layouts: 50.8 us -> 9.13 us
  blocking collectives: 0 us -> 37.3 us
  starting transfers between devices: 30.1 us -> 59.1 us
  between operations: 13.6 us -> 0.28 us
  Pallas kernels: 0 us -> 7.67 us
  other arithmetic: 8.99 us -> 2.31 us
  matrix products: 9.37 us -> 5.56 us
    all_gather x1 -> x0, waiting for transfers between devices: 125 us -> none  [body(): lax.all_gather(proj_weight, ('ctx', 'clu'), axis=0, tiled=True)]
    ppermute x0 -> x8, starting transfers between devices: none -> 41.2 us  [the longest x7 39.3 us: shifted(): lax.ppermute(block, 'clu', [(i, (i + step) % size) for i in range(size)])]
    all_to_all x0 -> x1, blocking collectives: none -> 37.3 us  [body(): lax.all_to_all(replies, 'clu', split_axis=0, concat_axis=0, tiled=True)]
    gather x2 -> x0, local copies, waits for them, and re-layouts: 26.4 us -> none  [the longest x1 20.6 us: body(): outgoing = jnp.take_along_axis(features, source[:, :, None], axis=1)]
    unnamed x14 -> x10, local copies, waits for them, and re-layouts: 18.8 us -> 5.73 us
    all_to_all x3 -> x4, starting transfers between devices: 30.1 us -> 17.9 us  [the longest x1 5.99 us: body(): lax.all_to_all(slot_tags, 'clu', split_axis=0, concat_axis=0, tiled=True)]
    pallas_call x0 -> x4, Pallas kernels: none -> 7.67 us  [the longest x1 3.07 us: attend(): vmem_call(kernel, jax.ShapeDtypeStruct((sources, rows, head_dim), BF16), 2)]
    ppermute x0 -> x8, waiting for transfers between devices: none -> 6.83 us  [the longest x7 6.82 us: shifted(): lax.ppermute(block, 'clu', [(i, (i + step) % size) for i in range(size)])]
  transfers between devices with their start and end apart: 4 -> 12, of which waited for: 3 -> 5; matrix products, arithmetic and copies ran while one was open for 17% -> 6% of each run, Pallas kernels for 0% -> 2%
where the time goes in v1:
time: 211 us
  waiting for transfers between devices  89.1 us (42%)
  starting transfers between devices  59.1 us (28%)
  blocking collectives  37.3 us (18%)
  local copies, waits for them, and re-layouts  9.13 us (4%)
  Pallas kernels  7.67 us (4%)
  matrix products  5.56 us (3%)
  other arithmetic  2.31 us (1%)
    all_to_all x1, waiting for transfers between devices, body(): lax.all_to_all(outgoing, 'clu', split_axis=0, concat_axis=0, tiled=True)  46.2 us
    ppermute x7, starting transfers between devices, shifted(): lax.ppermute(block, 'clu', [(i, (i + step) % size) for i in range(size)])  39.3 us
    all_to_all x1, blocking collectives, body(): lax.all_to_all(replies, 'clu', split_axis=0, concat_axis=0, tiled=True)  37.3 us
    all_to_all x1, waiting for transfers between devices, body(): lax.all_to_all(partial, 'x', split_axis=0, concat_axis=0, tiled=True)  24.4 us
    all_to_all x1, waiting for transfers between devices, body(): lax.all_to_all(slot_tags, 'clu', split_axis=0, concat_axis=0, tiled=True)  10.6 us
    ppermute x7, waiting for transfers between devices, shifted(): lax.ppermute(block, 'clu', [(i, (i + step) % size) for i in range(size)])  6.82 us
    all_to_all x1, starting transfers between devices, body(): lax.all_to_all(slot_tags, 'clu', split_axis=0, concat_axis=0, tiled=True)  5.99 us
    unnamed x10, local copies, waits for them, and re-layouts  5.73 us
  transfers between devices with their start and end apart: 12, of which 5 were waited for; matrix products, arithmetic and copies ran while one was open for 6% of the time, Pallas kernels for 2%

profile of v1, /device:TPU:24, one launch (start us, length us, event | category | flops | bytes accessed | tf_op | source)
XLA Modules:
  0.0 210.5 jit_solution(12876972189600488262)
XLA Ops:
  0.9 12.7 %collective-permute-start = (bf16[32,1024]{1,0:T(8,128)(2,1)S(1)}, bf16[32,1024]{1,0:T(8,128)(2,1)S(1)}, u32[]{:S(2)}, u32[]{:S(2)}) collective-permute-start(bf16[32,1024]{1,0:T(8,128)(2,1)S(1)} %bitcast.51), channel_id=1, source_target_pairs={{0,48},{4,52},{8,56},{12,60},{16,0},{20,4},{24,8},{28,12},{32,16},... | collective-permute-start | bytes 196616 | tf_op jit(solution)/shard_map/ppermute | solution.py:156
  13.6 1.9 collective-permute-start.2
  15.5 10.8 %collective-permute-start.1 = (bf16[32,1024]{1,0:T(8,128)(2,1)S(1)}, bf16[32,1024]{1,0:T(8,128)(2,1)S(1)}, u32[]{:S(2)}, u32[]{:S(2)}) collective-permute-start(bf16[32,1024]{1,0:T(8,128)(2,1)S(1)} %bitcast.53), channel_id=1, source_target_pairs={{0,32},{4,36},{8,40},{12,44},{16,48},{20,52},{24,56},{28,60},{32,0... | collective-permute-start | bytes 196616 | tf_op jit(solution)/shard_map/ppermute | solution.py:156
  26.3 4.1 %copy.15 = bf16[1,256,4096]{1,2,0:T(8,128)(2,1)} copy(bf16[1,256,4096]{2,1,0:T(8,128)(2,1)} %param.3) | data formatting | bytes 4194304 | tf_op args[0]
  30.5 4.4 %all-to-all-start = ((bf16[4,256,1024]{1,2,0:T(8,128)(2,1)}), bf16[4,256,1024]{1,2,0:T(8,128)(2,1)S(1)}, u32[]{:S(2)}, u32[]{:S(2)}) async-start(bf16[4,256,1024]{1,2,0:T(8,128)(2,1)} %bitcast.37), calls=%async_computation | async-start | bytes 4194304 | tf_op jit(solution)/shard_map/all_to_all | solution.py:196
  35.0 3.4 %collective-permute-start.5 = (bf16[2,32,1024]{2,1,0:T(8,128)(2,1)S(1)}, bf16[2,32,1024]{2,1,0:T(8,128)(2,1)S(1)}, u32[]{:S(2)}, u32[]{:S(2)}) collective-permute-start(bf16[2,32,1024]{2,1,0:T(8,128)(2,1)S(1)} %get-tuple-element.16), channel_id=1, source_target_pairs={{0,8},{4,12},{8,16},{12,20},{16,24},{20,28},{24,32},{28,36},{32,40... | collective-permute-start | bytes 393224 | tf_op jit(solution)/shard_map/ppermute | solution.py:156
  38.4 2.9 %collective-permute-start.6 = (bf16[4,32,1024]{2,1,0:T(8,128)(2,1)S(1)}, bf16[4,32,1024]{2,1,0:T(8,128)(2,1)S(1)}, u32[]{:S(2)}, u32[]{:S(2)}) collective-permute-start(bf16[4,32,1024]{2,1,0:T(8,128)(2,1)S(1)} %get-tuple-element.12), channel_id=1, source_target_pairs={{0,4},{4,8},{8,12},{12,16},{16,20},{20,24},{24,28},{28,32},{32,36}... | collective-permute-start | bytes 786440 | tf_op jit(solution)/shard_map/ppermute | solution.py:156
  41.4 4.1 %collective-permute-start.3 = (bf16[4,32,1024]{2,1,0:T(8,128)(2,1)S(1)}, bf16[4,32,1024]{2,1,0:T(8,128)(2,1)S(1)}, u32[]{:S(2)}, u32[]{:S(2)}) collective-permute-start(bf16[4,32,1024]{2,1,0:T(8,128)(2,1)S(1)} %get-tuple-element.12), channel_id=1, source_target_pairs={{0,60},{4,0},{8,4},{12,8},{16,12},{20,16},{24,20},{28,24},{32,28},... | collective-permute-start | bytes 786440 | tf_op jit(solution)/shard_map/ppermute | solution.py:156
  45.5 3.4 %collective-permute-start.4 = (bf16[2,32,1024]{2,1,0:T(8,128)(2,1)S(1)}, bf16[2,32,1024]{2,1,0:T(8,128)(2,1)S(1)}, u32[]{:S(2)}, u32[]{:S(2)}) collective-permute-start(bf16[2,32,1024]{2,1,0:T(8,128)(2,1)S(1)} %get-tuple-element.15), channel_id=1, source_target_pairs={{0,56},{4,60},{8,0},{12,4},{16,8},{20,12},{24,16},{28,20},{32,24},... | collective-permute-start | bytes 393224 | tf_op jit(solution)/shard_map/ppermute | solution.py:156
  48.9 6.8 %collective-permute-done.4 = bf16[2,32,1024]{2,1,0:T(8,128)(2,1)S(1)} collective-permute-done((bf16[2,32,1024]{2,1,0:T(8,128)(2,1)S(1)}, bf16[2,32,1024]{2,1,0:T(8,128)(2,1)S(1)}, u32[]{:S(2)}, u32[]{:S(2)}) %collective-permute-start.4) | collective-permute-done | bytes 131104 | tf_op jit(solution)/shard_map/ppermute | solution.py:156
  57.4 1.9 collective-permute-start.7
  60.4 2.5 %copy.16 = bf16[4,256,1024]{2,1,0:T(8,128)(2,1)} copy(bf16[4,256,1024]{1,2,0:T(8,128)(2,1)S(1)} %all-to-all-done) | data formatting | bytes 4194304 | tf_op jit(solution)/shard_map/all_to_all | solution.py:196
  62.9 2.9 %fusion.2 = f32[1024,1024]{1,0:T(8,128)S(1)} fusion(bf16[512,1024]{1,0:T(8,128)(2,1)} %bitcast.14, bf16[1024,1024]{1,0:T(8,128)(2,1)} %bitcast.39, s32[]{:T(128)S(6)} %select_n.19), kind=kOutput, calls=%fused_computation.6 | convolution fusion | flops 1073741824 | bytes 6291460 | tf_op jit(solution)/shard_map/dot_general | solution.py:211
  65.8 2.6 %add_convert_fusion = bf16[1024,1024]{1,0:T(8,128)(2,1)} fusion(f32[1024,1024]{1,0:T(8,128)S(1)} %fusion.2, bf16[512,1024]{1,0:T(8,128)(2,1)S(1)} %collective-permute-done.7, bf16[1024,1024]{1,0:T(8,128)(2,1)S(1)} %bitcast.40, s32[]{:T(128)S(6)} %select_n.22), kind=kOutput, calls=%fused_computation | convolution fusion | flops 1075838976 | bytes 8388612 | tf_op jit(solution)/shard_map/dot_general | solution.py:212
  68.5 3.9 %all-to-all-start.1 = ((bf16[4,256,1024]{2,1,0:T(8,128)(2,1)}), bf16[4,256,1024]{2,1,0:T(8,128)(2,1)S(1)}, u32[]{:S(2)}, u32[]{:S(2)}) async-start(bf16[4,256,1024]{2,1,0:T(8,128)(2,1)} %bitcast.38), calls=%async_computation.1 | async-start | bytes 4194304 | tf_op jit(solution)/shard_map/all_to_all | solution.py:214
  72.5 1.7 shard_map.37
  74.9 24.4 %all-to-all-done.1.partial_ref = bf16[4,256,1024]{2,1,0:T(8,128)(2,1)S(1)} async-done(((bf16[4,256,1024]{2,1,0:T(8,128)(2,1)}), bf16[4,256,1024]{2,1,0:T(8,128)(2,1)S(1)}, u32[]{:S(2)}, u32[]{:S(2)}) %all-to-all-start.1) | async-done | bytes 2097184 | tf_op jit(solution)/shard_map/all_to_all | solution.py:214
  99.3 6.0 %all-to-all-start.3 = ((s32[16,1,128]{2,1,0:T(1,128)}), s32[16,1,128]{2,1,0:T(1,128)S(1)}, u32[]{:S(2)}, u32[]{:S(2)}) async-start(s32[16,1,128]{2,1,0:T(1,128)} %reshape.28), calls=%async_computation.3 | async-start | bytes 16384 | tf_op jit(solution)/shard_map/all_to_all | solution.py:201
  105.3 1.8 shard_map.38
  107.1 10.6 %all-to-all-done.3 = s32[16,1,128]{2,1,0:T(1,128)S(1)} async-done(((s32[16,1,128]{2,1,0:T(1,128)}), s32[16,1,128]{2,1,0:T(1,128)S(1)}, u32[]{:S(2)}, u32[]{:S(2)}) %all-to-all-start.3) | async-done | bytes 8224 | tf_op jit(solution)/shard_map/all_to_all | solution.py:201
  117.7 3.7 %all-to-all-start.2 = ((bf16[16,128,256]{2,1,0:T(8,128)(2,1)}), bf16[16,128,256]{2,1,0:T(8,128)(2,1)S(1)}, u32[]{:S(2)}, u32[]{:S(2)}) async-start(bf16[16,128,256]{2,1,0:T(8,128)(2,1)} %shard_map.38), calls=%async_computation.2 | async-start | bytes 2097152 | tf_op jit(solution)/shard_map/all_to_all | solution.py:217
  122.7 46.2 %all-to-all-done.2.block_ref = bf16[16,128,256]{2,1,0:T(8,128)(2,1)S(1)} async-done(((bf16[16,128,256]{2,1,0:T(8,128)(2,1)}), bf16[16,128,256]{2,1,0:T(8,128)(2,1)S(1)}, u32[]{:S(2)}, u32[]{:S(2)}) %all-to-all-start.2) | async-done | bytes 1048608 | tf_op jit(solution)/shard_map/all_to_all | solution.py:217
  169.0 3.1 %shard_map.39 = bf16[16,128,128]{2,1,0:T(8,128)(2,1)S(1)} custom-call(bf16[16,128,256]{2,1,0:T(8,128)(2,1)S(1)} %all-to-all-done.2.block_ref, s32[4,512]{1,0:T(4,128)S(1)} %reshape.27.tag_ref), custom_call_target="tpu_custom_call" | custom-call | tf_op jit(solution)/shard_map/pallas_call | solution.py:132
  172.0 37.3 %all_to_all.25.block_ref = bf16[16,128,128]{2,1,0:T(8,128)(2,1)S(1)} all-to-all(bf16[16,128,128]{2,1,0:T(8,128)(2,1)S(1)} %shard_map.39), channel_id=1, replica_groups=mesh['x'=4,'core'=2,'clu'=16,'tp'=4] {'clu'}, dimensions={0} | all-to-all | bytes 1048576 | tf_op jit(solution)/shard_map/all_to_all | solution.py:219
  (35 shorter events, 7.1 us)
Async XLA Ops:
  0.9 34.1 %collective-permute-start = (bf16[32,1024]{1,0:T(8,128)(2,1)S(1)}, bf16[32,1024]{1,0:T(8,128)(2,1)S(1)}, u32[]{:S(2)}, u32[]{:S(2)}) collective-permute-start(bf16[32,1024]{1,0:T(8,128)(2,1)S(1)} %bitcast.51), channel_id=1, source_target_pairs={{0,48},{4,52},{8,56},{12,60},{16,0},{20,4},{24,8},{28,12},{32,16},... | collective-permute-start | bytes 196616 | tf_op jit(solution)/shard_map/ppermute | solution.py:156
  13.6 21.3 %collective-permute-start.2 = (bf16[32,1024]{1,0:T(8,128)(2,1)S(1)}, bf16[32,1024]{1,0:T(8,128)(2,1)S(1)}, u32[]{:S(2)}, u32[]{:S(2)}) collective-permute-start(bf16[32,1024]{1,0:T(8,128)(2,1)S(1)} %bitcast.52), channel_id=1, source_target_pairs={{0,16},{4,20},{8,24},{12,28},{16,32},{20,36},{24,40},{28,44},{32,4... | collective-permute-start | bytes 196616 | tf_op jit(solution)/shard_map/ppermute | solution.py:156
  15.5 22.9 %collective-permute-start.1 = (bf16[32,1024]{1,0:T(8,128)(2,1)S(1)}, bf16[32,1024]{1,0:T(8,128)(2,1)S(1)}, u32[]{:S(2)}, u32[]{:S(2)}) collective-permute-start(bf16[32,1024]{1,0:T(8,128)(2,1)S(1)} %bitcast.53), channel_id=1, source_target_pairs={{0,32},{4,36},{8,40},{12,44},{16,48},{20,52},{24,56},{28,60},{32,0... | collective-permute-start | bytes 196616 | tf_op jit(solution)/shard_map/ppermute | solution.py:156
  30.4 4.4 %copy-start.2 = (bf16[32,2,512]{2,1,0:T(2,128)(2,1)S(1)}, bf16[32,2,512]{2,1,0:T(2,128)(2,1)}, u32[]{:S(2)}) copy-start(bf16[32,2,512]{2,1,0:T(2,128)(2,1)} %param.4) | copy-start | bytes 196612
  30.5 29.9 %all-to-all-start = ((bf16[4,256,1024]{1,2,0:T(8,128)(2,1)}), bf16[4,256,1024]{1,2,0:T(8,128)(2,1)S(1)}, u32[]{:S(2)}, u32[]{:S(2)}) async-start(bf16[4,256,1024]{1,2,0:T(8,128)(2,1)} %bitcast.37), calls=%async_computation | async-start | bytes 4194304 | tf_op jit(solution)/shard_map/all_to_all | solution.py:196
  35.0 13.9 %collective-permute-start.5 = (bf16[2,32,1024]{2,1,0:T(8,128)(2,1)S(1)}, bf16[2,32,1024]{2,1,0:T(8,128)(2,1)S(1)}, u32[]{:S(2)}, u32[]{:S(2)}) collective-permute-start(bf16[2,32,1024]{2,1,0:T(8,128)(2,1)S(1)} %get-tuple-element.16), channel_id=1, source_target_pairs={{0,8},{4,12},{8,16},{12,20},{16,24},{20,28},{24,32},{28,36},{32,40... | collective-permute-start | bytes 393224 | tf_op jit(solution)/shard_map/ppermute | solution.py:156
  38.4 17.3 %collective-permute-start.6 = (bf16[4,32,1024]{2,1,0:T(8,128)(2,1)S(1)}, bf16[4,32,1024]{2,1,0:T(8,128)(2,1)S(1)}, u32[]{:S(2)}, u32[]{:S(2)}) collective-permute-start(bf16[4,32,1024]{2,1,0:T(8,128)(2,1)S(1)} %get-tuple-element.12), channel_id=1, source_target_pairs={{0,4},{4,8},{8,12},{12,16},{16,20},{20,24},{24,28},{28,32},{32,36}... | collective-permute-start | bytes 786440 | tf_op jit(solution)/shard_map/ppermute | solution.py:156
  41.4 14.5 %collective-permute-start.3 = (bf16[4,32,1024]{2,1,0:T(8,128)(2,1)S(1)}, bf16[4,32,1024]{2,1,0:T(8,128)(2,1)S(1)}, u32[]{:S(2)}, u32[]{:S(2)}) collective-permute-start(bf16[4,32,1024]{2,1,0:T(8,128)(2,1)S(1)} %get-tuple-element.12), channel_id=1, source_target_pairs={{0,60},{4,0},{8,4},{12,8},{16,12},{20,16},{24,20},{28,24},{32,28},... | collective-permute-start | bytes 786440 | tf_op jit(solution)/shard_map/ppermute | solution.py:156
  45.5 10.2 %collective-permute-start.4 = (bf16[2,32,1024]{2,1,0:T(8,128)(2,1)S(1)}, bf16[2,32,1024]{2,1,0:T(8,128)(2,1)S(1)}, u32[]{:S(2)}, u32[]{:S(2)}) collective-permute-start(bf16[2,32,1024]{2,1,0:T(8,128)(2,1)S(1)} %get-tuple-element.15), channel_id=1, source_target_pairs={{0,56},{4,60},{8,0},{12,4},{16,8},{20,12},{24,16},{28,20},{32,24},... | collective-permute-start | bytes 393224 | tf_op jit(solution)/shard_map/ppermute | solution.py:156
  57.4 8.4 %collective-permute-start.7 = (bf16[512,1024]{1,0:T(8,128)(2,1)}, bf16[512,1024]{1,0:T(8,128)(2,1)S(1)}, u32[]{:S(2)}, u32[]{:S(2)}) collective-permute-start(bf16[512,1024]{1,0:T(8,128)(2,1)} %bitcast.14), channel_id=1, source_target_pairs={{0,64},{64,0},{1,65},{65,1},{2,66},{66,2},{3,67},{67,3},{4,68},{68... | collective-permute-start | bytes 3145736 | tf_op jit(solution)/shard_map/ppermute | solution.py:207
  62.9 3.0 %copy-start.1 = (bf16[4,256,1024]{2,1,0:T(8,128)(2,1)S(1)}, bf16[4,256,1024]{2,1,0:T(8,128)(2,1)}, u32[]{:S(2)}) copy-start(bf16[4,256,1024]{2,1,0:T(8,128)(2,1)} %copy.16) | copy-start | bytes 6291460
  68.5 3.9 %copy-start = (s32[1,256,4]{1,2,0:T(4,128)S(1)}, s32[1,256,4]{1,2,0:T(4,128)}, u32[]{:S(2)}) copy-start(s32[1,256,4]{1,2,0:T(4,128)} %param.5) | copy-start | bytes 12292
  68.5 30.9 %all-to-all-start.1 = ((bf16[4,256,1024]{2,1,0:T(8,128)(2,1)}), bf16[4,256,1024]{2,1,0:T(8,128)(2,1)S(1)}, u32[]{:S(2)}, u32[]{:S(2)}) async-start(bf16[4,256,1024]{2,1,0:T(8,128)(2,1)} %bitcast.38), calls=%async_computation.1 | async-start | bytes 4194304 | tf_op jit(solution)/shard_map/all_to_all | solution.py:214
  99.3 18.4 %all-to-all-start.3 = ((s32[16,1,128]{2,1,0:T(1,128)}), s32[16,1,128]{2,1,0:T(1,128)S(1)}, u32[]{:S(2)}, u32[]{:S(2)}) async-start(s32[16,1,128]{2,1,0:T(1,128)} %reshape.28), calls=%async_computation.3 | async-start | bytes 16384 | tf_op jit(solution)/shard_map/all_to_all | solution.py:201
  117.7 51.2 %all-to-all-start.2 = ((bf16[16,128,256]{2,1,0:T(8,128)(2,1)}), bf16[16,128,256]{2,1,0:T(8,128)(2,1)S(1)}, u32[]{:S(2)}, u32[]{:S(2)}) async-start(bf16[16,128,256]{2,1,0:T(8,128)(2,1)} %shard_map.38), calls=%async_computation.2 | async-start | bytes 2097152 | tf_op jit(solution)/shard_map/all_to_all | solution.py:217

commit v2 on v1

--- a/solution.py
+++ b/solution.py
@@ -6,6 +6,7 @@
 from jax.sharding import PartitionSpec as P
 
 CLUSTERS = 64
+GROUPS = 2
 BF16 = jnp.bfloat16
 F32 = jnp.float32
 VMEM_LIMIT = 48 * 1024 * 1024
@@ -28,48 +29,64 @@
 def routing(ids, owners, capacity):
     rows, heads = ids.shape
     per_owner = CLUSTERS // owners
-    slots = owners * capacity
-
-    def kernel(ids_ref, ids_t_ref, slot_row_ref, slot_col_ref, tag_ref):
+
+    def kernel(ids_ref, ids_t_ref, slot_row_ref, slot_col_ref):
         above = lax.broadcasted_iota(jnp.int32, (rows, rows), 0)
         across = lax.broadcasted_iota(jnp.int32, (rows, rows), 1)
         before_col = (across < above).astype(BF16)
         before_row = (above < across).astype(BF16)
         for h in range(heads):
-            id_col = ids_ref[:, h : h + 1]
-            owner_col = id_col // per_owner
+            owner_col = ids_ref[:, h : h + 1] // per_owner
             hot = owner_col == lax.broadcasted_iota(jnp.int32, (rows, owners), 1)
             count = jnp.dot(before_col, hot.astype(BF16), preferred_element_type=F32)
             rank = jnp.sum(jnp.where(hot, count, 0.0), axis=1, keepdims=True)
-            slot_col = owner_col * capacity + rank.astype(jnp.int32)
-            slot_col_ref[:, h : h + 1] = slot_col
-            id_row = ids_t_ref[h : h + 1, :]
-            owner_row = id_row // per_owner
+            slot_col_ref[:, h : h + 1] = owner_col * capacity + rank.astype(jnp.int32)
+            owner_row = ids_t_ref[h : h + 1, :] // per_owner
             hot = owner_row == lax.broadcasted_iota(jnp.int32, (owners, rows), 0)
             count = jnp.dot(hot.astype(BF16), before_row, preferred_element_type=F32)
             rank = jnp.sum(jnp.where(hot, count, 0.0), axis=0, keepdims=True)
             slot_row_ref[h : h + 1, :] = owner_row * capacity + rank.astype(jnp.int32)
-            tag = (id_row - owner_row * per_owner + 1).astype(BF16)
-            place = slot_col == lax.broadcasted_iota(jnp.int32, (rows, slots), 1)
-            tags = jnp.dot(
-                jnp.broadcast_to(tag, (16, rows)), place.astype(BF16), preferred_element_type=F32
-            )
-            tag_ref[h : h + 1, :] = tags[:1].astype(jnp.int32)
 
     return vmem_call(
         kernel,
         (
             jax.ShapeDtypeStruct((heads, rows), jnp.int32),
             jax.ShapeDtypeStruct((rows, heads), jnp.int32),
-            jax.ShapeDtypeStruct((heads, slots), jnp.int32),
         ),
         2,
     )(ids, ids.T)
 
 
-def pack(partial, slot_row, owners, capacity, head_dim):
+def owned_tags(all_ids, me, capacity):
+    sources, heads, rows = all_ids.shape
+    per_owner = CLUSTERS // sources
+    slots = sources * capacity
+
+    def kernel(ids_ref, me_ref, tag_ref):
+        above = lax.broadcasted_iota(jnp.int32, (rows, rows), 0)
+        across = lax.broadcasted_iota(jnp.int32, (rows, rows), 1)
+        before = (above < across).astype(BF16)
+        lane = lax.broadcasted_iota(jnp.int32, (sources, capacity, rows), 1)
+        for h in range(heads):
+            ids = ids_ref[:, h, :]
+            owner = ids // per_owner
+            mine = owner == me_ref[...]
+            rank = jnp.dot(mine.astype(BF16), before, preferred_element_type=F32)
+            rank = jnp.where(mine, rank.astype(jnp.int32), -1)
+            tag = ids - owner * per_owner + 1
+            placed = jnp.where(rank[:, None, :] == lane, tag[:, None, :], 0)
+            tag_ref[:, h : h + 1] = jnp.sum(
+                placed.reshape(slots, rows), axis=1, keepdims=True
+            )
+
+    return vmem_call(kernel, jax.ShapeDtypeStruct((slots, heads), jnp.int32), 2)(
+        all_ids, jnp.broadcast_to(me, (1, 1)).astype(jnp.int32)
+    )
+
+
+def pack(partial, slot_row, first_head, owners, capacity, head_dim):
     parts, rows, width = partial.shape
-    heads = slot_row.shape[0]
+    heads = width // (2 * head_dim)
     half = width // 2
     slots = owners * capacity
 
@@ -82,7 +99,8 @@
             return total.astype(BF16)
 
         for h in range(heads):
-            place = lax.broadcasted_iota(jnp.int32, (slots, rows), 0) == slot_ref[h : h + 1, :]
+            row = first_head + h
+            place = lax.broadcasted_iota(jnp.int32, (slots, rows), 0) == slot_ref[row : row + 1, :]
             place = place.astype(BF16)
             for m in range(2):
                 packed = jnp.dot(
@@ -97,7 +115,7 @@
     )(partial, slot_row)
 
 
-def attend(blocks, tags, capacity, per_owner):
+def attend(blocks, tags, first_head, capacity):
     sources, rows, width = blocks.shape
     head_dim = width // 2
     heads = rows // capacity
@@ -111,10 +129,11 @@
             here = slice(h * capacity, (h + 1) * capacity)
             keys = block_ref[:, here, :head_dim].reshape(slots, head_dim)
             values = block_ref[:, here, head_dim:].reshape(slots, head_dim)
-            kinds = lax.broadcasted_iota(jnp.int32, (16, slots), 0) + 1
-            member = (tag_ref[h : h + 1, :] == kinds).astype(BF16)
+            col = first_head + h
+            kinds = lax.broadcasted_iota(jnp.int32, (slots, 128), 1) + 1
+            member = (tag_ref[:, col : col + 1] == kinds).astype(BF16)
             same = lax.dot_general(
-                member, member, (((0,), (0,)), ((), ())), preferred_element_type=F32
+                member, member, (((1,), (1,)), ((), ())), preferred_element_type=F32
             )
             scores = lax.dot_general(
                 keys, keys, (((1,), (1,)), ((), ())), preferred_element_type=F32
@@ -135,21 +154,24 @@
 
 
 def unpack(returned, slot_col, capacity):
-    owners, height, head_dim = returned.shape
+    owners, height, head_dim = returned[0].shape
+    in_group = height // capacity
     rows, heads = slot_col.shape
     slots = owners * capacity
 
-    def kernel(block_ref, slot_ref, out_ref):
-        for h in range(heads):
-            block = block_ref[:, h * capacity : (h + 1) * capacity, :].reshape(slots, head_dim)
+    def kernel(*refs):
+        slot_ref, out_ref = refs[-2:]
+        for h in range(heads):
+            first = h % in_group * capacity
+            block = refs[h // in_group][:, first : first + capacity, :].reshape(slots, head_dim)
             place = slot_ref[:, h : h + 1] == lax.broadcasted_iota(jnp.int32, (rows, slots), 1)
             out_ref[:, h * head_dim : (h + 1) * head_dim] = jnp.dot(
                 place.astype(BF16), block, preferred_element_type=F32
             ).astype(BF16)
 
-    return vmem_call(kernel, jax.ShapeDtypeStruct((rows, heads * head_dim), BF16), 2)(
-        returned, slot_col
-    )
+    return vmem_call(
+        kernel, jax.ShapeDtypeStruct((rows, heads * head_dim), BF16), len(returned) + 1
+    )(*returned, slot_col)
 
 
 def shifted(block, step, size):
@@ -158,7 +180,6 @@
 
 def gather_z(own):
     size = lax.axis_size("clu")
-    me = lax.axis_index("clu")
     from_minus4 = shifted(own, 4, size)
     from_plus4 = shifted(own, -4, size)
     from_8 = shifted(own, 8, size)
@@ -176,7 +197,7 @@
         ],
         axis=1,
     )
-    return order.reshape((size,) + own.shape), me
+    return order.reshape((size,) + own.shape)
 
 
 def body(tokens, proj_weight, clusters):
@@ -187,8 +208,6 @@
     width = 2 * proj_weight.shape[2]
     head_dim = proj_weight.shape[2] // heads
     capacity = 2 * rows // owners
-    per_owner = CLUSTERS // owners
-    cores = lax.axis_size("core")
     chips = lax.axis_size("x")
     core = lax.axis_index("core")
 
@@ -196,27 +215,32 @@
     pieces = lax.all_to_all(pieces, "x", split_axis=0, concat_axis=0, tiled=True)
     pieces = pieces.reshape(chips * rows, depth // chips)
 
-    slot_row, slot_col, slot_tags = routing(clusters[0], owners, capacity)
-    slot_tags = slot_tags.reshape(heads, owners, capacity).transpose(1, 0, 2)
-    key_tags = lax.all_to_all(slot_tags, "clu", split_axis=0, concat_axis=0, tiled=True)
-    key_tags = key_tags.transpose(1, 0, 2).reshape(heads, owners * capacity)
-
-    own = proj_weight.reshape(shard, width)
-    ring, me = gather_z(own)
+    me = lax.axis_index("clu")
+    slot_row, slot_col = routing(clusters[0], owners, capacity)
+    all_ids = lax.all_gather(clusters[0].T, "clu", axis=0, tiled=False)
+    tags = owned_tags(all_ids, me, capacity)
+
+    group_width = width // GROUPS
+    own = proj_weight.reshape(shard, 2, GROUPS, group_width // 2).transpose(0, 2, 1, 3)
+    ring = gather_z(own.reshape(shard, width))
     ring = jnp.roll(ring, me, axis=0).reshape(owners * shard, width)
     other = lax.ppermute(ring, "core", [(0, 1), (1, 0)])
     deep = owners * shard
     mine = lax.dynamic_slice_in_dim(pieces, core * deep, deep, 1)
     theirs = lax.dynamic_slice_in_dim(pieces, (1 - core) * deep, deep, 1)
-    partial = jnp.dot(mine, ring, preferred_element_type=F32)
-    partial = partial + jnp.dot(theirs, other, preferred_element_type=F32)
-    partial = partial.astype(BF16).reshape(chips, rows, width)
-    partial = lax.all_to_all(partial, "x", split_axis=0, concat_axis=0, tiled=True)
-
-    outgoing = pack(partial, slot_row, owners, capacity, head_dim)
-    incoming = lax.all_to_all(outgoing, "clu", split_axis=0, concat_axis=0, tiled=True)
-    replies = attend(incoming, key_tags, capacity, per_owner)
-    returned = lax.all_to_all(replies, "clu", split_axis=0, concat_axis=0, tiled=True)
+
+    returned = []
+    for g in range(GROUPS):
+        cols = slice(g * group_width, (g + 1) * group_width)
+        first_head = g * heads // GROUPS
+        partial = jnp.dot(mine, ring[:, cols], preferred_element_type=F32)
+        partial = partial + jnp.dot(theirs, other[:, cols], preferred_element_type=F32)
+        partial = partial.astype(BF16).reshape(chips, rows, group_width)
+        partial = lax.all_to_all(partial, "x", split_axis=0, concat_axis=0, tiled=True)
+        outgoing = pack(partial, slot_row, first_head, owners, capacity, head_dim)
+        incoming = lax.all_to_all(outgoing, "clu", split_axis=0, concat_axis=0, tiled=True)
+        replies = attend(incoming, tags, first_head, capacity)
+        returned.append(lax.all_to_all(replies, "clu", split_axis=0, concat_axis=0, tiled=True))
     return unpack(returned, slot_col, capacity)[None]
 
 

time: 211 us -> 241 us (1.14)
  blocking collectives: 37.3 us -> 66.9 us
  waiting for transfers between devices: 89.1 us -> 67.5 us
  starting transfers between devices: 59.1 us -> 76.2 us
  matrix products: 5.56 us -> 7.97 us
    all_gather x0 -> x1, blocking collectives: none -> 47.2 us  [body(): all_ids = lax.all_gather(clusters[0].T, 'clu', axis=0, tiled=False)]
    all_to_all x1 -> x2, waiting for transfers between devices: 46.2 us -> 24.4 us  [body(): lax.all_to_all(outgoing, 'clu', split_axis=0, concat_axis=0, tiled=True)]
    all_to_all x1, blocking collectives: 37.3 us -> 19.7 us  [body(): lax.all_to_all(replies, 'clu', split_axis=0, concat_axis=0, tiled=True)]
    all_to_all x1 -> x2, starting transfers between devices: 3.65 us -> 13.1 us  [body(): lax.all_to_all(outgoing, 'clu', split_axis=0, concat_axis=0, tiled=True)]
    all_to_all x1 -> x2, waiting for transfers between devices: 24.4 us -> 18.8 us  [body(): lax.all_to_all(partial, 'x', split_axis=0, concat_axis=0, tiled=True)]
    all_to_all x1, starting transfers between devices: 5.99 us -> 10.4 us  [body(): lax.all_to_all(replies, 'clu', split_axis=0, concat_axis=0, tiled=True)]
    all_to_all x1, waiting for transfers between devices: 1.08 us -> 5.2 us  [body(): lax.all_to_all(pieces, 'x', split_axis=0, concat_axis=0, tiled=True)]
    all_to_all x1 -> x2, starting transfers between devices: 3.87 us -> 7.03 us  [body(): lax.all_to_all(partial, 'x', split_axis=0, concat_axis=0, tiled=True)]
  transfers between devices with their start and end apart: 12 -> 14, of which waited for: 5 -> 6; matrix products, arithmetic and copies ran while one was open for 6% -> 6% of each run, Pallas kernels for 2% -> 4%
where the time goes in v2:
time: 241 us; the launch traced here: 239 us
  starting transfers between devices  76.2 us (32%)
  waiting for transfers between devices  67.5 us (28%)
  blocking collectives  66.9 us (28%)
  Pallas kernels  10 us (4%)
  local copies, waits for them, and re-layouts  9.05 us (4%)
  matrix products  7.97 us (3%)
    all_gather x1, blocking collectives, body(): all_ids = lax.all_gather(clusters[0].T, 'clu', axis=0, tiled=False)  47.2 us
    ppermute x7, starting transfers between devices, shifted(): lax.ppermute(block, 'clu', [(i, (i + step) % size) for i in range(size)])  39.3 us
    all_to_all x2, waiting for transfers between devices, body(): lax.all_to_all(outgoing, 'clu', split_axis=0, concat_axis=0, tiled=True)  24.4 us
    all_to_all x1, blocking collectives, body(): lax.all_to_all(replies, 'clu', split_axis=0, concat_axis=0, tiled=True)  19.7 us
    all_to_all x2, waiting for transfers between devices, body(): lax.all_to_all(partial, 'x', split_axis=0, concat_axis=0, tiled=True)  18.8 us
    all_to_all x2, starting transfers between devices, body(): lax.all_to_all(outgoing, 'clu', split_axis=0, concat_axis=0, tiled=True)  13.1 us
    all_to_all x1, waiting for transfers between devices, body(): lax.all_to_all(replies, 'clu', split_axis=0, concat_axis=0, tiled=True)  12 us
    all_to_all x1, starting transfers between devices, body(): lax.all_to_all(replies, 'clu', split_axis=0, concat_axis=0, tiled=True)  10.4 us
  transfers between devices with their start and end apart: 14, of which 6 were waited for; matrix products, arithmetic and copies ran while one was open for 6% of the time, Pallas kernels for 4%

profile of v2, /device:TPU:24, one launch (start us, length us, event | category | flops | bytes accessed | tf_op | source)
XLA Modules:
  0.0 238.6 jit_solution(10464808706638192671)
XLA Ops:
  0.9 12.7 %collective-permute-start = (bf16[32,1024]{1,0:T(8,128)(2,1)S(1)}, bf16[32,1024]{1,0:T(8,128)(2,1)S(1)}, u32[]{:S(2)}, u32[]{:S(2)}) collective-permute-start(bf16[32,1024]{1,0:T(8,128)(2,1)S(1)} %reshape.23), channel_id=1, source_target_pairs={{0,48},{4,52},{8,56},{12,60},{16,0},{20,4},{24,8},{28,12},{32,16},... | collective-permute-start | bytes 196616 | tf_op jit(solution)/shard_map/ppermute | solution.py:178
  15.5 10.8 %collective-permute-start.1 = (bf16[32,1024]{1,0:T(8,128)(2,1)S(1)}, bf16[32,1024]{1,0:T(8,128)(2,1)S(1)}, u32[]{:S(2)}, u32[]{:S(2)}) collective-permute-start(bf16[32,1024]{1,0:T(8,128)(2,1)S(1)} %reshape.23), channel_id=1, source_target_pairs={{0,32},{4,36},{8,40},{12,44},{16,48},{20,52},{24,56},{28,60},{32,0... | collective-permute-start | bytes 196616 | tf_op jit(solution)/shard_map/ppermute | solution.py:178
  27.3 3.4 %collective-permute-start.5 = (bf16[2,32,1024]{2,1,0:T(8,128)(2,1)S(1)}, bf16[2,32,1024]{2,1,0:T(8,128)(2,1)S(1)}, u32[]{:S(2)}, u32[]{:S(2)}) collective-permute-start(bf16[2,32,1024]{2,1,0:T(8,128)(2,1)S(1)} %get-tuple-element.14), channel_id=1, source_target_pairs={{0,8},{4,12},{8,16},{12,20},{16,24},{20,28},{24,32},{28,36},{32,40... | collective-permute-start | bytes 393224 | tf_op jit(solution)/shard_map/ppermute | solution.py:178
  30.7 4.1 %copy.13 = bf16[1,256,4096]{1,2,0:T(8,128)(2,1)} copy(bf16[1,256,4096]{2,1,0:T(8,128)(2,1)} %param.3) | data formatting | bytes 4194304 | tf_op args[0]
  34.8 4.5 %all-to-all-start = ((bf16[4,256,1024]{1,2,0:T(8,128)(2,1)}), bf16[4,256,1024]{1,2,0:T(8,128)(2,1)}, u32[]{:S(2)}, u32[]{:S(2)}) async-start(bf16[4,256,1024]{1,2,0:T(8,128)(2,1)} %bitcast.1), calls=%async_computation | async-start | bytes 4194304 | tf_op jit(solution)/shard_map/all_to_all | solution.py:215
  39.3 2.9 %collective-permute-start.6 = (bf16[4,32,1024]{2,1,0:T(8,128)(2,1)S(1)}, bf16[4,32,1024]{2,1,0:T(8,128)(2,1)S(1)}, u32[]{:S(2)}, u32[]{:S(2)}) collective-permute-start(bf16[4,32,1024]{2,1,0:T(8,128)(2,1)S(1)} %get-tuple-element.10), channel_id=1, source_target_pairs={{0,4},{4,8},{8,12},{12,16},{16,20},{20,24},{24,28},{28,32},{32,36}... | collective-permute-start | bytes 786440 | tf_op jit(solution)/shard_map/ppermute | solution.py:178
  42.2 4.1 %collective-permute-start.3 = (bf16[4,32,1024]{2,1,0:T(8,128)(2,1)S(1)}, bf16[4,32,1024]{2,1,0:T(8,128)(2,1)S(1)}, u32[]{:S(2)}, u32[]{:S(2)}) collective-permute-start(bf16[4,32,1024]{2,1,0:T(8,128)(2,1)S(1)} %get-tuple-element.10), channel_id=1, source_target_pairs={{0,60},{4,0},{8,4},{12,8},{16,12},{20,16},{24,20},{28,24},{32,28},... | collective-permute-start | bytes 786440 | tf_op jit(solution)/shard_map/ppermute | solution.py:178
  46.4 3.4 %collective-permute-start.4 = (bf16[2,32,1024]{2,1,0:T(8,128)(2,1)S(1)}, bf16[2,32,1024]{2,1,0:T(8,128)(2,1)S(1)}, u32[]{:S(2)}, u32[]{:S(2)}) collective-permute-start(bf16[2,32,1024]{2,1,0:T(8,128)(2,1)S(1)} %get-tuple-element.13), channel_id=1, source_target_pairs={{0,56},{4,60},{8,0},{12,4},{16,8},{20,12},{24,16},{28,20},{32,24},... | collective-permute-start | bytes 393224 | tf_op jit(solution)/shard_map/ppermute | solution.py:178
  49.8 7.1 %collective-permute-done.4 = bf16[2,32,1024]{2,1,0:T(8,128)(2,1)S(1)} collective-permute-done((bf16[2,32,1024]{2,1,0:T(8,128)(2,1)S(1)}, bf16[2,32,1024]{2,1,0:T(8,128)(2,1)S(1)}, u32[]{:S(2)}, u32[]{:S(2)}) %collective-permute-start.4) | collective-permute-done | bytes 131104 | tf_op jit(solution)/shard_map/ppermute | solution.py:178
  59.6 5.2 %all-to-all-done = bf16[4,256,1024]{1,2,0:T(8,128)(2,1)} async-done(((bf16[4,256,1024]{1,2,0:T(8,128)(2,1)}), bf16[4,256,1024]{1,2,0:T(8,128)(2,1)}, u32[]{:S(2)}, u32[]{:S(2)}) %all-to-all-start) | async-done | bytes 2097184 | tf_op jit(solution)/shard_map/all_to_all | solution.py:215
  64.8 3.0 %copy.14 = bf16[4,256,1024]{2,1,0:T(8,128)(2,1)S(1)} copy(bf16[4,256,1024]{1,2,0:T(8,128)(2,1)} %all-to-all-done) | data formatting | bytes 4194304 | tf_op jit(solution)/shard_map/all_to_all | solution.py:215
  68.5 2.7 %add_convert_fusion = bf16[1024,512]{1,0:T(8,128)(2,1)} fusion(f32[1024,512]{1,0:T(8,128)S(1)} %fusion.3, bf16[1024,1024]{1,0:T(8,128)(2,1)S(1)} %bitcast.32, s32[]{:T(128)S(6)} %select_n.22, bf16[512,1024]{1,0:T(8,128)(2,1)} %collective-permute-done.7), kind=kOutput, calls=%fused_computation.2 | convolution fusion | flops 537919488 | bytes 4718596 | tf_op jit(solution)/shard_map/dot_general | solution.py:237
  71.2 3.5 %all-to-all-start.4 = ((bf16[4,256,512]{2,1,0:T(8,128)(2,1)}), bf16[4,256,512]{2,1,0:T(8,128)(2,1)S(1)}, u32[]{:S(2)}, u32[]{:S(2)}) async-start(bf16[4,256,512]{2,1,0:T(8,128)(2,1)} %bitcast.36), calls=%async_computation.4 | async-start | bytes 2097152 | tf_op jit(solution)/shard_map/all_to_all | solution.py:239
  76.5 2.8 %add_convert_fusion.1 = bf16[1024,512]{1,0:T(8,128)(2,1)} fusion(f32[1024,512]{1,0:T(8,128)S(1)} %fusion.5, bf16[1024,1024]{1,0:T(8,128)(2,1)S(1)} %bitcast.34, s32[]{:T(128)S(6)} %select_n.22, bf16[512,1024]{1,0:T(8,128)(2,1)} %collective-permute-done.7), kind=kOutput, calls=%fused_computation.3 | convolution fusion | flops 537919488 | bytes 4718596 | tf_op jit(solution)/shard_map/dot_general | solution.py:237
  79.3 8.8 %all-to-all-done.4.partial_ref = bf16[4,256,512]{2,1,0:T(8,128)(2,1)S(1)} async-done(((bf16[4,256,512]{2,1,0:T(8,128)(2,1)}), bf16[4,256,512]{2,1,0:T(8,128)(2,1)S(1)}, u32[]{:S(2)}, u32[]{:S(2)}) %all-to-all-start.4) | async-done | bytes 1048608 | tf_op jit(solution)/shard_map/all_to_all | solution.py:239
  88.1 3.5 %all-to-all-start.1 = ((bf16[4,256,512]{2,1,0:T(8,128)(2,1)}), bf16[4,256,512]{2,1,0:T(8,128)(2,1)S(1)}, u32[]{:S(2)}, u32[]{:S(2)}) async-start(bf16[4,256,512]{2,1,0:T(8,128)(2,1)} %bitcast.35), calls=%async_computation.1 | async-start | bytes 2097152 | tf_op jit(solution)/shard_map/all_to_all | solution.py:239
  93.7 10.0 %all-to-all-done.1.partial_ref = bf16[4,256,512]{2,1,0:T(8,128)(2,1)S(1)} async-done(((bf16[4,256,512]{2,1,0:T(8,128)(2,1)}), bf16[4,256,512]{2,1,0:T(8,128)(2,1)S(1)}, u32[]{:S(2)}, u32[]{:S(2)}) %all-to-all-start.1) | async-done | bytes 1048608 | tf_op jit(solution)/shard_map/all_to_all | solution.py:239
  103.7 6.8 %all-to-all-start.5 = ((bf16[16,64,256]{2,1,0:T(8,128)(2,1)}), bf16[16,64,256]{2,1,0:T(8,128)(2,1)S(1)}, u32[]{:S(2)}, u32[]{:S(2)}) async-start(bf16[16,64,256]{2,1,0:T(8,128)(2,1)} %shard_map.41), calls=%async_computation.5 | async-start | bytes 1048576 | tf_op jit(solution)/shard_map/all_to_all | solution.py:241
  111.7 24.4 %all-to-all-done.5.block_ref = bf16[16,64,256]{2,1,0:T(8,128)(2,1)S(1)} async-done(((bf16[16,64,256]{2,1,0:T(8,128)(2,1)}), bf16[16,64,256]{2,1,0:T(8,128)(2,1)S(1)}, u32[]{:S(2)}, u32[]{:S(2)}) %all-to-all-start.5) | async-done | bytes 524320 | tf_op jit(solution)/shard_map/all_to_all | solution.py:241
  136.1 6.3 %all-to-all-start.2 = ((bf16[16,64,256]{2,1,0:T(8,128)(2,1)}), bf16[16,64,256]{2,1,0:T(8,128)(2,1)S(1)}, u32[]{:S(2)}, u32[]{:S(2)}) async-start(bf16[16,64,256]{2,1,0:T(8,128)(2,1)} %shard_map.38), calls=%async_computation.2 | async-start | bytes 1048576 | tf_op jit(solution)/shard_map/all_to_all | solution.py:241
  142.5 47.2 %all-gather.1.ids_ref = s32[16,4,256]{2,1,0:T(4,128)S(1)} all-gather(s32[1,4,256]{2,1,0:T(4,128)S(1)} %bitcast.30), channel_id=2, replica_groups=mesh['x'=4,'core'=2,'clu'=16,'tp'=4] {'clu'}, dimensions={0}, use_global_device_ids=true | all-gather | bytes 69632 | tf_op jit(solution)/shard_map/all_gather | solution.py:220
  193.5 10.4 %all-to-all-start.6 = ((bf16[16,64,128]{2,1,0:T(8,128)(2,1)}), bf16[16,64,128]{2,1,0:T(8,128)(2,1)S(1)}, u32[]{:S(2)}, u32[]{:S(2)}) async-start(bf16[16,64,128]{2,1,0:T(8,128)(2,1)} %shard_map.42), calls=%async_computation.6 | async-start | bytes 524288 | tf_op jit(solution)/shard_map/all_to_all | solution.py:243
  205.7 12.0 %all-to-all-done.6.refs_1_ = bf16[16,64,128]{2,1,0:T(8,128)(2,1)S(1)} async-done(((bf16[16,64,128]{2,1,0:T(8,128)(2,1)}), bf16[16,64,128]{2,1,0:T(8,128)(2,1)S(1)}, u32[]{:S(2)}, u32[]{:S(2)}) %all-to-all-start.6) | async-done | bytes 262176 | tf_op jit(solution)/shard_map/all_to_all | solution.py:243
  217.7 19.7 %all_to_all.35.refs_0_ = bf16[16,64,128]{2,1,0:T(8,128)(2,1)S(1)} all-to-all(bf16[16,64,128]{2,1,0:T(8,128)(2,1)S(1)} %shard_map.40), channel_id=1, replica_groups=mesh['x'=4,'core'=2,'clu'=16,'tp'=4] {'clu'}, dimensions={0} | all-to-all | bytes 524288 | tf_op jit(solution)/shard_map/all_to_all | solution.py:243
  (36 shorter events, 19.0 us)
Async XLA Ops:
  0.9 26.4 %collective-permute-start = (bf16[32,1024]{1,0:T(8,128)(2,1)S(1)}, bf16[32,1024]{1,0:T(8,128)(2,1)S(1)}, u32[]{:S(2)}, u32[]{:S(2)}) collective-permute-start(bf16[32,1024]{1,0:T(8,128)(2,1)S(1)} %reshape.23), channel_id=1, source_target_pairs={{0,48},{4,52},{8,56},{12,60},{16,0},{20,4},{24,8},{28,12},{32,16},... | collective-permute-start | bytes 196616 | tf_op jit(solution)/shard_map/ppermute | solution.py:178
  13.6 13.6 %collective-permute-start.2 = (bf16[32,1024]{1,0:T(8,128)(2,1)S(1)}, bf16[32,1024]{1,0:T(8,128)(2,1)S(1)}, u32[]{:S(2)}, u32[]{:S(2)}) collective-permute-start(bf16[32,1024]{1,0:T(8,128)(2,1)S(1)} %reshape.23), channel_id=1, source_target_pairs={{0,16},{4,20},{8,24},{12,28},{16,32},{20,36},{24,40},{28,44},{32,4... | collective-permute-start | bytes 196616 | tf_op jit(solution)/shard_map/ppermute | solution.py:178
  15.5 23.7 %collective-permute-start.1 = (bf16[32,1024]{1,0:T(8,128)(2,1)S(1)}, bf16[32,1024]{1,0:T(8,128)(2,1)S(1)}, u32[]{:S(2)}, u32[]{:S(2)}) collective-permute-start(bf16[32,1024]{1,0:T(8,128)(2,1)S(1)} %reshape.23), channel_id=1, source_target_pairs={{0,32},{4,36},{8,40},{12,44},{16,48},{20,52},{24,56},{28,60},{32,0... | collective-permute-start | bytes 196616 | tf_op jit(solution)/shard_map/ppermute | solution.py:178
  27.3 22.4 %collective-permute-start.5 = (bf16[2,32,1024]{2,1,0:T(8,128)(2,1)S(1)}, bf16[2,32,1024]{2,1,0:T(8,128)(2,1)S(1)}, u32[]{:S(2)}, u32[]{:S(2)}) collective-permute-start(bf16[2,32,1024]{2,1,0:T(8,128)(2,1)S(1)} %get-tuple-element.14), channel_id=1, source_target_pairs={{0,8},{4,12},{8,16},{12,20},{16,24},{20,28},{24,32},{28,36},{32,40... | collective-permute-start | bytes 393224 | tf_op jit(solution)/shard_map/ppermute | solution.py:178
  34.8 30.0 %all-to-all-start = ((bf16[4,256,1024]{1,2,0:T(8,128)(2,1)}), bf16[4,256,1024]{1,2,0:T(8,128)(2,1)}, u32[]{:S(2)}, u32[]{:S(2)}) async-start(bf16[4,256,1024]{1,2,0:T(8,128)(2,1)} %bitcast.1), calls=%async_computation | async-start | bytes 4194304 | tf_op jit(solution)/shard_map/all_to_all | solution.py:215
  39.3 17.6 %collective-permute-start.6 = (bf16[4,32,1024]{2,1,0:T(8,128)(2,1)S(1)}, bf16[4,32,1024]{2,1,0:T(8,128)(2,1)S(1)}, u32[]{:S(2)}, u32[]{:S(2)}) collective-permute-start(bf16[4,32,1024]{2,1,0:T(8,128)(2,1)S(1)} %get-tuple-element.10), channel_id=1, source_target_pairs={{0,4},{4,8},{8,12},{12,16},{16,20},{20,24},{24,28},{28,32},{32,36}... | collective-permute-start | bytes 786440 | tf_op jit(solution)/shard_map/ppermute | solution.py:178
  42.2 14.7 %collective-permute-start.3 = (bf16[4,32,1024]{2,1,0:T(8,128)(2,1)S(1)}, bf16[4,32,1024]{2,1,0:T(8,128)(2,1)S(1)}, u32[]{:S(2)}, u32[]{:S(2)}) collective-permute-start(bf16[4,32,1024]{2,1,0:T(8,128)(2,1)S(1)} %get-tuple-element.10), channel_id=1, source_target_pairs={{0,60},{4,0},{8,4},{12,8},{16,12},{20,16},{24,20},{28,24},{32,28},... | collective-permute-start | bytes 786440 | tf_op jit(solution)/shard_map/ppermute | solution.py:178
  46.4 10.5 %collective-permute-start.4 = (bf16[2,32,1024]{2,1,0:T(8,128)(2,1)S(1)}, bf16[2,32,1024]{2,1,0:T(8,128)(2,1)S(1)}, u32[]{:S(2)}, u32[]{:S(2)}) collective-permute-start(bf16[2,32,1024]{2,1,0:T(8,128)(2,1)S(1)} %get-tuple-element.13), channel_id=1, source_target_pairs={{0,56},{4,60},{8,0},{12,4},{16,8},{20,12},{24,16},{28,20},{32,24},... | collective-permute-start | bytes 393224 | tf_op jit(solution)/shard_map/ppermute | solution.py:178
  57.6 10.1 %copy-start.1 = (bf16[16,32,1024]{2,1,0:T(8,128)(2,1)}, bf16[16,32,1024]{2,1,0:T(8,128)(2,1)S(1)}, u32[]{:S(2)}) copy-start(bf16[16,32,1024]{2,1,0:T(8,128)(2,1)S(1)} %fusion) | copy-start | bytes 3145732
  57.6 10.9 %collective-permute-start.7 = (bf16[512,1024]{1,0:T(8,128)(2,1)S(1)}, bf16[512,1024]{1,0:T(8,128)(2,1)}, u32[]{:S(2)}, u32[]{:S(2)}) collective-permute-start(bf16[512,1024]{1,0:T(8,128)(2,1)S(1)} %bitcast.38), channel_id=1, source_target_pairs={{0,64},{64,0},{1,65},{65,1},{2,66},{66,2},{3,67},{67,3},{4,68},{68... | collective-permute-start | bytes 3145736 | tf_op jit(solution)/shard_map/ppermute | solution.py:227
  71.2 16.8 %all-to-all-start.4 = ((bf16[4,256,512]{2,1,0:T(8,128)(2,1)}), bf16[4,256,512]{2,1,0:T(8,128)(2,1)S(1)}, u32[]{:S(2)}, u32[]{:S(2)}) async-start(bf16[4,256,512]{2,1,0:T(8,128)(2,1)} %bitcast.36), calls=%async_computation.4 | async-start | bytes 2097152 | tf_op jit(solution)/shard_map/all_to_all | solution.py:239
  79.3 12.3 %copy-start = (s32[1,256,4]{1,2,0:T(4,128)S(1)}, s32[1,256,4]{1,2,0:T(4,128)}, u32[]{:S(2)}) copy-start(s32[1,256,4]{1,2,0:T(4,128)} %param.5) | copy-start | bytes 12292
  88.1 15.6 %all-to-all-start.1 = ((bf16[4,256,512]{2,1,0:T(8,128)(2,1)}), bf16[4,256,512]{2,1,0:T(8,128)(2,1)S(1)}, u32[]{:S(2)}, u32[]{:S(2)}) async-start(bf16[4,256,512]{2,1,0:T(8,128)(2,1)} %bitcast.35), calls=%async_computation.1 | async-start | bytes 2097152 | tf_op jit(solution)/shard_map/all_to_all | solution.py:239
  103.7 32.4 %all-to-all-start.5 = ((bf16[16,64,256]{2,1,0:T(8,128)(2,1)}), bf16[16,64,256]{2,1,0:T(8,128)(2,1)S(1)}, u32[]{:S(2)}, u32[]{:S(2)}) async-start(bf16[16,64,256]{2,1,0:T(8,128)(2,1)} %shard_map.41), calls=%async_computation.5 | async-start | bytes 1048576 | tf_op jit(solution)/shard_map/all_to_all | solution.py:241
  136.1 57.4 %all-to-all-start.2 = ((bf16[16,64,256]{2,1,0:T(8,128)(2,1)}), bf16[16,64,256]{2,1,0:T(8,128)(2,1)S(1)}, u32[]{:S(2)}, u32[]{:S(2)}) async-start(bf16[16,64,256]{2,1,0:T(8,128)(2,1)} %shard_map.38), calls=%async_computation.2 | async-start | bytes 1048576 | tf_op jit(solution)/shard_map/all_to_all | solution.py:241
  193.5 24.2 %all-to-all-start.6 = ((bf16[16,64,128]{2,1,0:T(8,128)(2,1)}), bf16[16,64,128]{2,1,0:T(8,128)(2,1)S(1)}, u32[]{:S(2)}, u32[]{:S(2)}) async-start(bf16[16,64,128]{2,1,0:T(8,128)(2,1)} %shard_map.42), calls=%async_computation.6 | async-start | bytes 524288 | tf_op jit(solution)/shard_map/all_to_all | solution.py:243

commit v3 on v1

v3 whole, which is shorter than its diff:
```python
import jax
import jax.numpy as jnp
from jax import lax
from jax.experimental import pallas as pl
from jax.experimental.pallas import tpu as pltpu
from jax.sharding import PartitionSpec as P

CLUSTERS = 64
GROUPS = 2
BF16 = jnp.bfloat16
F32 = jnp.float32
VMEM_LIMIT = 48 * 1024 * 1024


def vmem_call(kernel, out_shape, in_smem, **kwargs):
    vmem = pl.BlockSpec(memory_space=pltpu.VMEM)
    smem = pl.BlockSpec(memory_space=pltpu.SMEM)
    return pl.pallas_call(
        kernel,
        out_shape=out_shape,
        in_specs=[smem if flag else vmem for flag in in_smem],
        out_specs=jax.tree.map(lambda _: vmem, out_shape),
        compiler_params=pltpu.CompilerParams(vmem_limit_bytes=VMEM_LIMIT),
        **kwargs,
    )


def scalar(value):
    return jnp.reshape(value, (1,)).astype(jnp.int32)


def iota(shape, dim):
    return lax.broadcasted_iota(jnp.int32, shape, dim)


def routing(ids, owners, capacity):
    rows, heads = ids.shape
    per_owner = CLUSTERS // owners

    def kernel(ids_ref, ids_t_ref, slot_row_ref, slot_col_ref, tag_ref):
        before_col = (iota((rows, rows), 1) < iota((rows, rows), 0)).astype(BF16)
        before_row = (iota((rows, rows), 0) < iota((rows, rows), 1)).astype(BF16)
        for h in range(heads):
            owner_col = ids_ref[:, h : h + 1] // per_owner
            hot = owner_col == iota((rows, owners), 1)
            count = jnp.dot(before_col, hot.astype(BF16), preferred_element_type=F32)
            rank_col = jnp.sum(jnp.where(hot, count, 0.0), axis=1, keepdims=True)
            rank_col = rank_col.astype(jnp.int32)
            slot_col_ref[:, h : h + 1] = owner_col * capacity + rank_col
            id_row = ids_t_ref[h : h + 1, :]
            owner_row = id_row // per_owner
            hot = owner_row == iota((owners, rows), 0)
            count = jnp.dot(hot.astype(BF16), before_row, preferred_element_type=F32)
            rank = jnp.sum(jnp.where(hot, count, 0.0), axis=0, keepdims=True)
            slot_row_ref[h : h + 1, :] = owner_row * capacity + rank.astype(jnp.int32)
            tag = jnp.where(hot, id_row - owner_row * per_owner + 1, 0)
            place = rank_col == iota((rows, capacity), 1)
            tags = jnp.dot(tag.astype(BF16), place.astype(BF16), preferred_element_type=F32)
            tag_ref[:, h * capacity : (h + 1) * capacity] = tags.astype(jnp.int32)

    return vmem_call(
        kernel,
        (
            jax.ShapeDtypeStruct((heads, rows), jnp.int32),
            jax.ShapeDtypeStruct((rows, heads), jnp.int32),
            jax.ShapeDtypeStruct((owners, heads * capacity), jnp.int32),
        ),
        (False, False),
    )(ids, ids.T)


def cut_tokens(local_rows, core, chips):
    rows, depth = local_rows.shape
    half = depth // chips // 2

    def kernel(core_ref, in_ref, out_ref):
        out_ref[0] = in_ref[...]

    return pl.pallas_call(
        kernel,
        grid_spec=pltpu.PrefetchScalarGridSpec(
            num_scalar_prefetch=1,
            grid=(chips, 2),
            in_specs=[
                pl.BlockSpec((rows, half), lambda p, j, core: (0, 2 * p + (core[0] + j) % 2))
            ],
            out_specs=pl.BlockSpec((1, rows, half), lambda p, j, core: (p, 0, j)),
        ),
        out_shape=jax.ShapeDtypeStruct((chips, rows, 2 * half), BF16),
    )(scalar(core), local_rows)


def assemble(blocks, distances, me, size):
    height, width = blocks[0].shape[-2:]

    def kernel(me_ref, *refs):
        out_ref = refs[-1]
        for ref, block_distances in zip(refs, distances):
            for j, distance in enumerate(block_distances):
                at = lax.rem(me_ref[0] + distance + size, size) * height
                block = ref[...] if len(ref.shape) == 2 else ref[j]
                out_ref[pl.ds(pl.multiple_of(at, height), height), :] = block

    return vmem_call(
        kernel,
        jax.ShapeDtypeStruct((size * height, width), BF16),
        (True,) + (False,) * len(blocks),
    )(scalar(me), *blocks)


def first_dot(pieces, ring, cost):
    chips, rows, depth = pieces.shape
    half, width = ring.shape

    def kernel(pieces_ref, ring_ref, out_ref):
        for p in range(chips):
            out_ref[p] = jnp.dot(
                pieces_ref[p, :, :half], ring_ref[...], preferred_element_type=F32
            )

    return vmem_call(
        kernel,
        jax.ShapeDtypeStruct((chips, rows, width), F32),
        (False,) * 2,
        cost_estimate=cost,
    )(pieces, ring)


def second_dot(first, pieces, ring, steps, me, groups):
    chips, rows, depth = pieces.shape
    half, width = ring.shape
    part = width // groups

    def kernel(me_ref, first_ref, pieces_ref, ring_ref, *out_refs):
        for i, step in enumerate(steps):
            p = lax.rem(me_ref[0] + step + chips, chips)
            total = first_ref[p] + jnp.dot(
                pieces_ref[p, :, half:], ring_ref[...], preferred_element_type=F32
            )
            for g in range(groups):
                out_refs[i * groups + g][...] = total[:, g * part : (g + 1) * part].astype(BF16)

    return vmem_call(
        kernel,
        (jax.ShapeDtypeStruct((rows, part), BF16),) * (len(steps) * groups),
        (True, False, False, False),
    )(scalar(me), first, pieces, ring)


def pack(partials, slot_row, owners, capacity, head_dim):
    parts = len(partials[0])
    groups = len(partials)
    rows, width = partials[0][0].shape
    in_group = width // (2 * head_dim)
    heads = in_group * groups
    slots = owners * capacity

    def kernel(*refs):
        slot_ref, out_ref = refs[-2:]

        def columns(g, first):
            cols = slice(first, first + head_dim)
            total = refs[g * parts][:, cols].astype(F32)
            for p in range(1, parts):
                total += refs[g * parts + p][:, cols].astype(F32)
            return total.astype(BF16)

        for h in range(heads):
            place = iota((slots, rows), 0) == slot_ref[h : h + 1, :]
            place = place.astype(BF16)
            for m in range(2):
                first = (m * in_group + h % in_group) * head_dim
                packed = jnp.dot(
                    place, columns(h // in_group, first), preferred_element_type=F32
                ).astype(BF16)
                out_ref[
                    :, h * capacity : (h + 1) * capacity, m * head_dim : (m + 1) * head_dim
                ] = packed.reshape(owners, capacity, head_dim)

    return vmem_call(
        kernel,
        jax.ShapeDtypeStruct((owners, heads * capacity, 2 * head_dim), BF16),
        (False,) * (parts * groups + 1),
    )(*[part for group in partials for part in group], slot_row)


def attend(blocks, tags, capacity):
    sources, rows, width = blocks.shape
    head_dim = width // 2
    heads = rows // capacity
    slots = sources * capacity
    scale = head_dim ** (-0.5)
    step = slots // 4

    def kernel(block_ref, tag_ref, out_ref):
        spread = iota((slots, sources), 0) // capacity == iota((slots, sources), 1)
        all_tags = jnp.dot(
            spread.astype(BF16), tag_ref[...].astype(F32).astype(BF16), preferred_element_type=F32
        )
        offset = iota((slots, rows), 1) - iota((slots, rows), 0) % capacity
        kinds = (iota((slots, 128), 1) + 1).astype(F32)
        for h in range(heads):
            here = slice(h * capacity, (h + 1) * capacity)
            keys = block_ref[:, here, :head_dim].reshape(slots, head_dim)
            values = block_ref[:, here, head_dim:].reshape(slots, head_dim)
            tag = jnp.sum(
                jnp.where(offset == h * capacity, all_tags, 0.0), axis=1, keepdims=True
            )
            member = (tag == kinds).astype(BF16)
            for first in range(0, slots, step):
                last = first + step
                same = lax.dot_general(
                    member[first:last],
                    member[:last],
                    (((1,), (1,)), ((), ())),
                    preferred_element_type=F32,
                )
                scores = lax.dot_general(
                    keys[first:last],
                    keys[:last],
                    (((1,), (1,)), ((), ())),
                    preferred_element_type=F32,
                )
                query = iota((step, last), 0) + first
                key = iota((step, last), 1)
                scores = scores * scale
                scores = jnp.where(query == key, -100000.0, scores)
                scores = jnp.where((same > 0.5) & (key <= query), scores, -1e30)
                row_max = jnp.max(scores, axis=1, keepdims=True)
                weights = jnp.exp(scores - row_max)
                total = jnp.sum(weights, axis=1, keepdims=True)
                probabilities = (weights / total).astype(BF16)
                result = jnp.dot(probabilities, values[:last], preferred_element_type=F32)
                out_ref[first // capacity : last // capacity, here, :] = result.astype(
                    BF16
                ).reshape(step // capacity, capacity, head_dim)

    return vmem_call(
        kernel, jax.ShapeDtypeStruct((sources, rows, head_dim), BF16), (False, False)
    )(blocks, tags)


def unpack(returned, slot_col, capacity):
    owners, height, head_dim = returned.shape
    rows, heads = slot_col.shape
    slots = owners * capacity

    def kernel(block_ref, slot_ref, out_ref):
        for h in range(heads):
            block = block_ref[:, h * capacity : (h + 1) * capacity, :].reshape(slots, head_dim)
            place = slot_ref[:, h : h + 1] == iota((rows, slots), 1)
            out_ref[:, h * head_dim : (h + 1) * head_dim] = jnp.dot(
                place.astype(BF16), block, preferred_element_type=F32
            ).astype(BF16)

    return vmem_call(
        kernel, jax.ShapeDtypeStruct((rows, heads * head_dim), BF16), (False, False)
    )(returned, slot_col)


def shifted(block, step, axis, size):
    return lax.ppermute(block, axis, [(i, (i + step) % size) for i in range(size)])


def gather_z(own):
    size = lax.axis_size("clu")
    from_minus4 = shifted(own, 4, "clu", size)
    from_plus4 = shifted(own, -4, "clu", size)
    from_8 = shifted(own, 8, "clu", size)
    four = jnp.stack([own, from_plus4, from_8, from_minus4])
    from_minus1 = shifted(four, 1, "clu", size)
    from_plus1 = shifted(four, -1, "clu", size)
    minus2 = shifted(jnp.stack([own, from_minus4]), 2, "clu", size)
    plus2 = shifted(jnp.stack([own, from_plus4]), -2, "clu", size)
    return assemble(
        [four, from_minus1, from_plus1, minus2, plus2],
        [(0, 4, 8, -4), (-1, 3, 7, -5), (1, 5, -7, -3), (-2, -6), (2, 6)],
        lax.axis_index("clu"),
        size,
    )


def body(tokens, proj_weight, clusters):
    rows, depth = tokens.shape[1:]
    owners = lax.axis_size("clu")
    heads = clusters.shape[2]
    shard = proj_weight.shape[0]
    width = 2 * proj_weight.shape[2]
    head_dim = proj_weight.shape[2] // heads
    capacity = 2 * rows // owners
    chips = lax.axis_size("x")

    own = proj_weight.reshape(shard, 2, GROUPS, width // GROUPS // 2).transpose(0, 2, 1, 3)
    ring = gather_z(own.reshape(shard, width))
    other = lax.ppermute(ring, "core", [(0, 1), (1, 0)])

    pieces = cut_tokens(tokens[0], lax.axis_index("core"), chips)
    pieces = lax.all_to_all(pieces, "x", split_axis=0, concat_axis=0, tiled=True)
    cost = pl.CostEstimate(
        flops=2 * chips * rows * depth // chips // 2 * width,
        bytes_accessed=8 * 1024 * 1024,
        transcendentals=0,
    )
    first = first_dot(pieces, ring, cost)
    steps = (2, 1, -1, 0)
    sent = second_dot(first, pieces, other, steps, lax.axis_index("x"), GROUPS)

    slot_row, slot_col, slot_tags = routing(clusters[0], owners, capacity)
    slot_tags, sent = lax.optimization_barrier((slot_tags, sent))
    partials = [[] for _ in range(GROUPS)]
    for g in range(GROUPS):
        for i, step in enumerate(steps):
            part = sent[i * GROUPS + g]
            partials[g].append(part if step == 0 else shifted(part, step, "x", chips))
    tags = lax.all_to_all(slot_tags, "clu", split_axis=0, concat_axis=0, tiled=True)

    outgoing = pack(partials, slot_row, owners, capacity, head_dim)
    outgoing, tags = lax.optimization_barrier((outgoing, tags))
    incoming = lax.all_to_all(outgoing, "clu", split_axis=0, concat_axis=0, tiled=True)
    replies = attend(incoming, tags, capacity)
    returned = lax.all_to_all(replies, "clu", split_axis=0, concat_axis=0, tiled=True)
    return unpack(returned, slot_col, capacity)[None]


def solution(mesh):
    names = mesh.axis_names
    ctx, clu, tp = (mesh.shape[name] for name in names)
    fine = jax.sharding.Mesh(
        mesh.devices.reshape(ctx // 2, 2, clu, tp), ("x", "core") + names[1:]
    )
    ctx_axes = ("x", "core")
    return jax.shard_map(
        body,
        mesh=fine,
        in_specs=(
            P(ctx_axes, "clu", None),
            P(ctx_axes + ("clu",), None, "tp"),
            P(ctx_axes, "clu", "tp"),
        ),
        out_specs=P(ctx_axes, "clu", "tp"),
        check_vma=False,
    )
```

time: 211 us -> 217 us (1.028)
  waiting for transfers between devices: 89.1 us -> 19.4 us
  blocking collectives: 37.3 us -> 88.2 us
  starting transfers between devices: 59.1 us -> 79.3 us
  Pallas kernels: 7.67 us -> 23.7 us
  matrix products: 5.56 us -> 0 us
  local copies, waits for them, and re-layouts: 9.13 us -> 5.06 us
  other arithmetic: 2.31 us -> 0.06 us
    all_to_all x2 -> x0, waiting for transfers between devices: 70.6 us -> none  [the longest x1 46.2 us: body(): lax.all_to_all(outgoing, 'clu', split_axis=0, concat_axis=0, tiled=True)]
    all_to_all x0 -> x1, blocking collectives: none -> 53.5 us  [body(): lax.all_to_all(outgoing, 'clu', split_axis=0, concat_axis=0, tiled=True)]
    ppermute x7 -> x13, starting transfers between devices: 39.3 us -> 64.2 us  [shifted(): lax.ppermute(block, axis, [(i, (i + step) % size) for i in range(size)])]
    pallas_call x2 -> x6, Pallas kernels: 4.26 us -> 20.9 us  [the longest x1 6.05 us: attend(): vmem_call(kernel, jax.ShapeDtypeStruct((sources, rows, head_dim), BF16),...]
    all_to_all x2 -> x0, starting transfers between devices: 7.53 us -> none  [the longest x1 3.87 us: body(): lax.all_to_all(partial, 'x', split_axis=0, concat_axis=0, tiled=True)]
    ppermute x7 -> x13, waiting for transfers between devices: 6.82 us -> 12.9 us  [shifted(): lax.ppermute(block, axis, [(i, (i + step) % size) for i in range(size)])]
    dot_general x2 -> x0, matrix products: 5.56 us -> none  [the longest x1 2.94 us: body(): partial = jnp.dot(mine, ring, preferred_element_type=F32)]
    all_to_all x1, waiting for transfers between devices: 10.6 us -> 6.49 us  [body(): lax.all_to_all(slot_tags, 'clu', split_axis=0, concat_axis=0, tiled=True)]
  transfers between devices with their start and end apart: 12 -> 16, of which waited for: 5 -> 6; matrix products, arithmetic and copies ran while one was open for 6% -> 0% of each run, Pallas kernels for 2% -> 3%
where the time goes in v3:
time: 217 us; the launch traced here: 216 us
  blocking collectives  88.2 us (41%)
  starting transfers between devices  79.3 us (37%)
  Pallas kernels  23.7 us (11%)
  waiting for transfers between devices  19.4 us (9%)
  local copies, waits for them, and re-layouts  5.06 us (2%)
    ppermute x13, starting transfers between devices, shifted(): lax.ppermute(block, axis, [(i, (i + step) % size) for i in range(size)])  64.2 us
    all_to_all x1, blocking collectives, body(): lax.all_to_all(outgoing, 'clu', split_axis=0, concat_axis=0, tiled=True)  53.5 us
    all_to_all x1, blocking collectives, body(): lax.all_to_all(replies, 'clu', split_axis=0, concat_axis=0, tiled=True)  34.8 us
    ppermute x13, waiting for transfers between devices, shifted(): lax.ppermute(block, axis, [(i, (i + step) % size) for i in range(size)])  12.9 us
    all_to_all x1, starting transfers between devices, body(): lax.all_to_all(slot_tags, 'clu', split_axis=0, concat_axis=0, tiled=True)  8.74 us
    all_to_all x1, waiting for transfers between devices, body(): lax.all_to_all(slot_tags, 'clu', split_axis=0, concat_axis=0, tiled=True)  6.49 us
    pallas_call x1, Pallas kernels, attend(): vmem_call(kernel, jax.ShapeDtypeStruct((sources, rows, head_dim), BF16),...  6.05 us
    pallas_call x1, Pallas kernels, cut_tokens(): pl.pallas_call(kernel, grid_spec=pltpu.PrefetchScalarGridSpec(num_scalar_...  5.75 us
  transfers between devices with their start and end apart: 16, of which 6 were waited for; matrix products, arithmetic and copies ran while one was open for 0% of the time, Pallas kernels for 3%

profile of v3, /device:TPU:24, one launch (start us, length us, event | category | flops | bytes accessed | tf_op | source)
XLA Modules:
  0.0 216.0 jit_solution(2472689932304612419)
XLA Ops:
  0.0 5.7 %shard_map.38 = bf16[4,256,1024]{2,1,0:T(8,128)(2,1)} custom-call(s32[1]{0:T(128)} %bitcast.3.core_ref, bf16[256,4096]{1,0:T(8,128)(2,1)} %bitcast.21), custom_call_target="tpu_custom_call" | custom-call | tf_op jit(solution)/shard_map/pallas_call | solution.py:79
  5.7 4.4 %all-to-all-start = ((bf16[4,256,1024]{2,1,0:T(8,128)(2,1)}), bf16[4,256,1024]{2,1,0:T(8,128)(2,1)S(1)}, u32[]{:S(2)}, u32[]{:S(2)}) async-start(bf16[4,256,1024]{2,1,0:T(8,128)(2,1)} %shard_map.38), calls=%async_computation | async-start | bytes 4194304 | tf_op jit(solution)/shard_map/all_to_all | solution.py:298
  10.2 9.1 %collective-permute-start.2 = (bf16[32,1024]{1,0:T(8,128)(2,1)S(1)}, bf16[32,1024]{1,0:T(8,128)(2,1)S(1)}, u32[]{:S(2)}, u32[]{:S(2)}) collective-permute-start(bf16[32,1024]{1,0:T(8,128)(2,1)S(1)} %reshape.21), channel_id=1, source_target_pairs={{0,16},{4,20},{8,24},{12,28},{16,32},{20,36},{24,40},{28,44},{32,4... | collective-permute-start | bytes 196616 | tf_op jit(solution)/shard_map/ppermute | solution.py:262
  19.3 5.6 %collective-permute-start = (bf16[32,1024]{1,0:T(8,128)(2,1)S(1)}, bf16[32,1024]{1,0:T(8,128)(2,1)S(1)}, u32[]{:S(2)}, u32[]{:S(2)}) collective-permute-start(bf16[32,1024]{1,0:T(8,128)(2,1)S(1)} %reshape.21), channel_id=1, source_target_pairs={{0,48},{4,52},{8,56},{12,60},{16,0},{20,4},{24,8},{28,12},{32,16},... | collective-permute-start | bytes 196616 | tf_op jit(solution)/shard_map/ppermute | solution.py:262
  24.9 10.8 %collective-permute-start.1 = (bf16[32,1024]{1,0:T(8,128)(2,1)S(1)}, bf16[32,1024]{1,0:T(8,128)(2,1)S(1)}, u32[]{:S(2)}, u32[]{:S(2)}) collective-permute-start(bf16[32,1024]{1,0:T(8,128)(2,1)S(1)} %reshape.21), channel_id=1, source_target_pairs={{0,32},{4,36},{8,40},{12,44},{16,48},{20,52},{24,56},{28,60},{32,0... | collective-permute-start | bytes 196616 | tf_op jit(solution)/shard_map/ppermute | solution.py:262
  35.8 4.0 %collective-permute-done.1 = bf16[32,1024]{1,0:T(8,128)(2,1)S(1)} collective-permute-done((bf16[32,1024]{1,0:T(8,128)(2,1)S(1)}, bf16[32,1024]{1,0:T(8,128)(2,1)S(1)}, u32[]{:S(2)}, u32[]{:S(2)}) %collective-permute-start.1) | collective-permute-done | bytes 65568 | tf_op jit(solution)/shard_map/ppermute | solution.py:262
  39.8 7.3 %collective-permute-start.3 = (bf16[4,32,1024]{2,1,0:T(8,128)(2,1)S(1)}, bf16[4,32,1024]{2,1,0:T(8,128)(2,1)S(1)}, u32[]{:S(2)}, u32[]{:S(2)}) collective-permute-start(bf16[4,32,1024]{2,1,0:T(8,128)(2,1)S(1)} %pad_maximum_fusion.refs_0_), channel_id=1, source_target_pairs={{0,4},{4,8},{8,12},{12,16},{16,20},{20,24},{24,28},{28,32},{32,36}... | collective-permute-start | bytes 786440 | tf_op jit(solution)/shard_map/ppermute | solution.py:262
  47.1 3.2 %collective-permute-start.4 = (bf16[4,32,1024]{2,1,0:T(8,128)(2,1)S(1)}, bf16[4,32,1024]{2,1,0:T(8,128)(2,1)S(1)}, u32[]{:S(2)}, u32[]{:S(2)}) collective-permute-start(bf16[4,32,1024]{2,1,0:T(8,128)(2,1)S(1)} %pad_maximum_fusion.refs_0_), channel_id=1, source_target_pairs={{0,60},{4,0},{8,4},{12,8},{16,12},{20,16},{24,20},{28,24},{32,28},... | collective-permute-start | bytes 786440 | tf_op jit(solution)/shard_map/ppermute | solution.py:262
  50.4 2.1 collective-permute-start.5
  52.5 5.9 %collective-permute-start.6 = (bf16[2,32,1024]{2,1,0:T(8,128)(2,1)S(1)}, bf16[2,32,1024]{2,1,0:T(8,128)(2,1)S(1)}, u32[]{:S(2)}, u32[]{:S(2)}) collective-permute-start(bf16[2,32,1024]{2,1,0:T(8,128)(2,1)S(1)} %get-tuple-element.49), channel_id=1, source_target_pairs={{0,56},{4,60},{8,0},{12,4},{16,8},{20,12},{24,16},{28,20},{32,24},... | collective-permute-start | bytes 393224 | tf_op jit(solution)/shard_map/ppermute | solution.py:262
  58.4 3.0 %collective-permute-done.5.refs_3_ = bf16[2,32,1024]{2,1,0:T(8,128)(2,1)S(1)} collective-permute-done((bf16[2,32,1024]{2,1,0:T(8,128)(2,1)S(1)}, bf16[2,32,1024]{2,1,0:T(8,128)(2,1)S(1)}, u32[]{:S(2)}, u32[]{:S(2)}) %collective-permute-start.5) | collective-permute-done | bytes 131104 | tf_op jit(solution)/shard_map/ppermute | solution.py:262
  71.4 3.2 %shard_map.40.first_ref = f32[4,256,1024]{2,1,0:T(8,128)} custom-call(bf16[4,256,1024]{2,1,0:T(8,128)(2,1)S(1)} %all-to-all-done.pieces_ref, bf16[512,1024]{1,0:T(8,128)(2,1)S(1)} %shard_map.39.ring_ref), custom_call_target="tpu_custom_call" | custom-call | flops 1073741824 | bytes 8388608 | tf_op jit(solution)/shard_map/pallas_call | solution.py:121
  74.6 4.6 %shard_map.41 = (bf16[256,512]{1,0:T(8,128)(2,1)}, bf16[256,512]{1,0:T(8,128)(2,1)}, bf16[256,512]{1,0:T(8,128)(2,1)}, bf16[256,512]{1,0:T(8,128)(2,1)}, bf16[25...) custom-call(s32[1]{0:T(128)} %bitcast.2.me_ref, ...), custom_call_target="tpu_custom_call" | custom-call | tf_op jit(solution)/shard_map/pallas_call | solution.py:143
  79.2 5.2 %collective-permute-start.10 = (bf16[256,512]{1,0:T(8,128)(2,1)S(1)}, bf16[256,512]{1,0:T(8,128)(2,1)S(1)}, u32[]{:S(2)}, u32[]{:S(2)}) collective-permute-start(bf16[256,512]{1,0:T(8,128)(2,1)S(1)} %get-tuple-element.38), channel_id=1, source_target_pairs={{0,384},{128,0},{256,128},{384,256},{1,385},{129,1},{257,129},{385... | collective-permute-start | bytes 786440 | tf_op jit(solution)/shard_map/ppermute | solution.py:262
  84.3 2.8 %collective-permute-start.11 = (bf16[256,512]{1,0:T(8,128)(2,1)}, bf16[256,512]{1,0:T(8,128)(2,1)S(1)}, u32[]{:S(2)}, u32[]{:S(2)}) collective-permute-start(bf16[256,512]{1,0:T(8,128)(2,1)} %get-tuple-element.40), channel_id=1, source_target_pairs={{0,256},{128,384},{256,0},{384,128},{1,257},{129,385},{257,1},{385... | collective-permute-start | bytes 786440 | tf_op jit(solution)/shard_map/ppermute | solution.py:262
  87.1 2.8 %collective-permute-start.12 = (bf16[256,512]{1,0:T(8,128)(2,1)}, bf16[256,512]{1,0:T(8,128)(2,1)S(1)}, u32[]{:S(2)}, u32[]{:S(2)}) collective-permute-start(bf16[256,512]{1,0:T(8,128)(2,1)} %get-tuple-element.41), channel_id=1, source_target_pairs={{0,128},{128,256},{256,384},{384,0},{1,129},{129,257},{257,385},{3... | collective-permute-start | bytes 786440 | tf_op jit(solution)/shard_map/ppermute | solution.py:262
  89.9 4.3 %collective-permute-start.13 = (bf16[256,512]{1,0:T(8,128)(2,1)}, bf16[256,512]{1,0:T(8,128)(2,1)S(1)}, u32[]{:S(2)}, u32[]{:S(2)}) collective-permute-start(bf16[256,512]{1,0:T(8,128)(2,1)} %get-tuple-element.42), channel_id=1, source_target_pairs={{0,384},{128,0},{256,128},{384,256},{1,385},{129,1},{257,129},{385... | collective-permute-start | bytes 786440 | tf_op jit(solution)/shard_map/ppermute | solution.py:262
  94.2 3.4 %collective-permute-start.8 = (bf16[256,512]{1,0:T(8,128)(2,1)}, bf16[256,512]{1,0:T(8,128)(2,1)S(1)}, u32[]{:S(2)}, u32[]{:S(2)}) collective-permute-start(bf16[256,512]{1,0:T(8,128)(2,1)} %get-tuple-element.36), channel_id=1, source_target_pairs={{0,256},{128,384},{256,0},{384,128},{1,257},{129,385},{257,1},{385... | collective-permute-start | bytes 786440 | tf_op jit(solution)/shard_map/ppermute | solution.py:262
  99.5 8.7 %all-to-all-start.1 = ((s32[16,1,128]{2,1,0:T(1,128)}), s32[16,1,128]{2,1,0:T(1,128)S(1)}, u32[]{:S(2)}, u32[]{:S(2)}) async-start(s32[16,1,128]{2,1,0:T(1,128)} %bitcast.13), calls=%async_computation.1 | async-start | bytes 16384 | tf_op jit(solution)/shard_map/all_to_all | solution.py:315
  108.4 4.8 %collective-permute-done.9.refs_1_ = bf16[256,512]{1,0:T(8,128)(2,1)S(1)} collective-permute-done((bf16[256,512]{1,0:T(8,128)(2,1)}, bf16[256,512]{1,0:T(8,128)(2,1)S(1)}, u32[]{:S(2)}, u32[]{:S(2)}) %collective-permute-start.9) | collective-permute-done | bytes 262176 | tf_op jit(solution)/shard_map/ppermute | solution.py:262
  114.0 6.5 %all-to-all-done.1 = s32[16,1,128]{2,1,0:T(1,128)S(1)} async-done(((s32[16,1,128]{2,1,0:T(1,128)}), s32[16,1,128]{2,1,0:T(1,128)S(1)}, u32[]{:S(2)}, u32[]{:S(2)}) %all-to-all-start.1) | async-done | bytes 8224 | tf_op jit(solution)/shard_map/all_to_all | solution.py:315
  120.5 53.5 %all_to_all.27.block_ref = bf16[16,128,256]{2,1,0:T(8,128)(2,1)S(1)} all-to-all(bf16[16,128,256]{2,1,0:T(8,128)(2,1)S(1)} %shard_map.42), channel_id=1, replica_groups=mesh['x'=4,'core'=2,'clu'=16,'tp'=4] {'clu'}, dimensions={0} | all-to-all | bytes 2097152 | tf_op jit(solution)/shard_map/all_to_all | solution.py:319
  173.9 6.0 %shard_map.43 = bf16[16,128,128]{2,1,0:T(8,128)(2,1)S(1)} custom-call(bf16[16,128,256]{2,1,0:T(8,128)(2,1)S(1)} %all_to_all.27.block_ref, s32[16,128]{1,0:T(8,128)S(1)} %bitcast.18), custom_call_target="tpu_custom_call" | custom-call | tf_op jit(solution)/shard_map/pallas_call | solution.py:238
  180.0 34.8 %all_to_all.28.block_ref = bf16[16,128,128]{2,1,0:T(8,128)(2,1)S(1)} all-to-all(bf16[16,128,128]{2,1,0:T(8,128)(2,1)S(1)} %shard_map.43), channel_id=1, replica_groups=mesh['x'=4,'core'=2,'clu'=16,'tp'=4] {'clu'}, dimensions={0} | all-to-all | bytes 1048576 | tf_op jit(solution)/shard_map/all_to_all | solution.py:321
  (39 shorter events, 14.1 us)
Async XLA Ops:
  5.7 4.4 %copy-start.7 = (bf16[32,2,512]{2,1,0:T(2,128)(2,1)S(1)}, bf16[32,2,512]{2,1,0:T(2,128)(2,1)}, u32[]{:S(2)}) copy-start(bf16[32,2,512]{2,1,0:T(2,128)(2,1)} %param.4) | copy-start | bytes 196612
  5.7 65.6 %all-to-all-start = ((bf16[4,256,1024]{2,1,0:T(8,128)(2,1)}), bf16[4,256,1024]{2,1,0:T(8,128)(2,1)S(1)}, u32[]{:S(2)}, u32[]{:S(2)}) async-start(bf16[4,256,1024]{2,1,0:T(8,128)(2,1)} %shard_map.38), calls=%async_computation | async-start | bytes 4194304 | tf_op jit(solution)/shard_map/all_to_all | solution.py:298
  10.2 59.0 %copy-start.6 = (s32[1,256,4]{1,2,0:T(4,128)S(1)}, s32[1,256,4]{1,2,0:T(4,128)}, u32[]{:S(2)}) copy-start(s32[1,256,4]{1,2,0:T(4,128)} %param.5) | copy-start | bytes 12292
  10.2 25.5 %collective-permute-start.2 = (bf16[32,1024]{1,0:T(8,128)(2,1)S(1)}, bf16[32,1024]{1,0:T(8,128)(2,1)S(1)}, u32[]{:S(2)}, u32[]{:S(2)}) collective-permute-start(bf16[32,1024]{1,0:T(8,128)(2,1)S(1)} %reshape.21), channel_id=1, source_target_pairs={{0,16},{4,20},{8,24},{12,28},{16,32},{20,36},{24,40},{28,44},{32,4... | collective-permute-start | bytes 196616 | tf_op jit(solution)/shard_map/ppermute | solution.py:262
  19.3 16.4 %collective-permute-start = (bf16[32,1024]{1,0:T(8,128)(2,1)S(1)}, bf16[32,1024]{1,0:T(8,128)(2,1)S(1)}, u32[]{:S(2)}, u32[]{:S(2)}) collective-permute-start(bf16[32,1024]{1,0:T(8,128)(2,1)S(1)} %reshape.21), channel_id=1, source_target_pairs={{0,48},{4,52},{8,56},{12,60},{16,0},{20,4},{24,8},{28,12},{32,16},... | collective-permute-start | bytes 196616 | tf_op jit(solution)/shard_map/ppermute | solution.py:262
  24.9 14.9 %collective-permute-start.1 = (bf16[32,1024]{1,0:T(8,128)(2,1)S(1)}, bf16[32,1024]{1,0:T(8,128)(2,1)S(1)}, u32[]{:S(2)}, u32[]{:S(2)}) collective-permute-start(bf16[32,1024]{1,0:T(8,128)(2,1)S(1)} %reshape.21), channel_id=1, source_target_pairs={{0,32},{4,36},{8,40},{12,44},{16,48},{20,52},{24,56},{28,60},{32,0... | collective-permute-start | bytes 196616 | tf_op jit(solution)/shard_map/ppermute | solution.py:262
  39.8 23.1 %collective-permute-start.3 = (bf16[4,32,1024]{2,1,0:T(8,128)(2,1)S(1)}, bf16[4,32,1024]{2,1,0:T(8,128)(2,1)S(1)}, u32[]{:S(2)}, u32[]{:S(2)}) collective-permute-start(bf16[4,32,1024]{2,1,0:T(8,128)(2,1)S(1)} %pad_maximum_fusion.refs_0_), channel_id=1, source_target_pairs={{0,4},{4,8},{8,12},{12,16},{16,20},{20,24},{24,28},{28,32},{32,36}... | collective-permute-start | bytes 786440 | tf_op jit(solution)/shard_map/ppermute | solution.py:262
  47.1 16.5 %collective-permute-start.4 = (bf16[4,32,1024]{2,1,0:T(8,128)(2,1)S(1)}, bf16[4,32,1024]{2,1,0:T(8,128)(2,1)S(1)}, u32[]{:S(2)}, u32[]{:S(2)}) collective-permute-start(bf16[4,32,1024]{2,1,0:T(8,128)(2,1)S(1)} %pad_maximum_fusion.refs_0_), channel_id=1, source_target_pairs={{0,60},{4,0},{8,4},{12,8},{16,12},{20,16},{24,20},{28,24},{32,28},... | collective-permute-start | bytes 786440 | tf_op jit(solution)/shard_map/ppermute | solution.py:262
  50.4 11.0 %collective-permute-start.5 = (bf16[2,32,1024]{2,1,0:T(8,128)(2,1)S(1)}, bf16[2,32,1024]{2,1,0:T(8,128)(2,1)S(1)}, u32[]{:S(2)}, u32[]{:S(2)}) collective-permute-start(bf16[2,32,1024]{2,1,0:T(8,128)(2,1)S(1)} %get-tuple-element.50), channel_id=1, source_target_pairs={{0,8},{4,12},{8,16},{12,20},{16,24},{20,28},{24,32},{28,36},{32,40... | collective-permute-start | bytes 393224 | tf_op jit(solution)/shard_map/ppermute | solution.py:262
  52.5 9.8 %collective-permute-start.6 = (bf16[2,32,1024]{2,1,0:T(8,128)(2,1)S(1)}, bf16[2,32,1024]{2,1,0:T(8,128)(2,1)S(1)}, u32[]{:S(2)}, u32[]{:S(2)}) collective-permute-start(bf16[2,32,1024]{2,1,0:T(8,128)(2,1)S(1)} %get-tuple-element.49), channel_id=1, source_target_pairs={{0,56},{4,60},{8,0},{12,4},{16,8},{20,12},{24,16},{28,20},{32,24},... | collective-permute-start | bytes 393224 | tf_op jit(solution)/shard_map/ppermute | solution.py:262
  62.2 0.6 copy-start.4
  62.9 0.7 copy-start
  63.6 0.7 copy-start.2
  64.3 0.9 copy-start.1
  65.3 0.9 copy-start.3
  66.2 0.9 copy-start.5
  67.2 7.4 %collective-permute-start.7 = (bf16[512,1024]{1,0:T(8,128)(2,1)S(1)}, bf16[512,1024]{1,0:T(8,128)(2,1)}, u32[]{:S(2)}, u32[]{:S(2)}) collective-permute-start(bf16[512,1024]{1,0:T(8,128)(2,1)S(1)} %shard_map.39.ring_ref), channel_id=1, source_target_pairs={{0,64},{64,0},{1,65},{65,1},{2,66},{66,2},{3,67},{67,3},{4,68},{68... | collective-permute-start | bytes 3145736 | tf_op jit(solution)/shard_map/ppermute | solution.py:295
  79.2 18.4 %collective-permute-start.10 = (bf16[256,512]{1,0:T(8,128)(2,1)S(1)}, bf16[256,512]{1,0:T(8,128)(2,1)S(1)}, u32[]{:S(2)}, u32[]{:S(2)}) collective-permute-start(bf16[256,512]{1,0:T(8,128)(2,1)S(1)} %get-tuple-element.38), channel_id=1, source_target_pairs={{0,384},{128,0},{256,128},{384,256},{1,385},{129,1},{257,129},{385... | collective-permute-start | bytes 786440 | tf_op jit(solution)/shard_map/ppermute | solution.py:262
  84.3 23.9 %collective-permute-start.11 = (bf16[256,512]{1,0:T(8,128)(2,1)}, bf16[256,512]{1,0:T(8,128)(2,1)S(1)}, u32[]{:S(2)}, u32[]{:S(2)}) collective-permute-start(bf16[256,512]{1,0:T(8,128)(2,1)} %get-tuple-element.40), channel_id=1, source_target_pairs={{0,256},{128,384},{256,0},{384,128},{1,257},{129,385},{257,1},{385... | collective-permute-start | bytes 786440 | tf_op jit(solution)/shard_map/ppermute | solution.py:262
  87.1 21.1 %collective-permute-start.12 = (bf16[256,512]{1,0:T(8,128)(2,1)}, bf16[256,512]{1,0:T(8,128)(2,1)S(1)}, u32[]{:S(2)}, u32[]{:S(2)}) collective-permute-start(bf16[256,512]{1,0:T(8,128)(2,1)} %get-tuple-element.41), channel_id=1, source_target_pairs={{0,128},{128,256},{256,384},{384,0},{1,129},{129,257},{257,385},{3... | collective-permute-start | bytes 786440 | tf_op jit(solution)/shard_map/ppermute | solution.py:262
  89.9 18.4 %collective-permute-start.13 = (bf16[256,512]{1,0:T(8,128)(2,1)}, bf16[256,512]{1,0:T(8,128)(2,1)S(1)}, u32[]{:S(2)}, u32[]{:S(2)}) collective-permute-start(bf16[256,512]{1,0:T(8,128)(2,1)} %get-tuple-element.42), channel_id=1, source_target_pairs={{0,384},{128,0},{256,128},{384,256},{1,385},{129,1},{257,129},{385... | collective-permute-start | bytes 786440 | tf_op jit(solution)/shard_map/ppermute | solution.py:262
  94.2 14.2 %collective-permute-start.8 = (bf16[256,512]{1,0:T(8,128)(2,1)}, bf16[256,512]{1,0:T(8,128)(2,1)S(1)}, u32[]{:S(2)}, u32[]{:S(2)}) collective-permute-start(bf16[256,512]{1,0:T(8,128)(2,1)} %get-tuple-element.36), channel_id=1, source_target_pairs={{0,256},{128,384},{256,0},{384,128},{1,257},{129,385},{257,1},{385... | collective-permute-start | bytes 786440 | tf_op jit(solution)/shard_map/ppermute | solution.py:262
  97.6 15.7 %collective-permute-start.9 = (bf16[256,512]{1,0:T(8,128)(2,1)}, bf16[256,512]{1,0:T(8,128)(2,1)S(1)}, u32[]{:S(2)}, u32[]{:S(2)}) collective-permute-start(bf16[256,512]{1,0:T(8,128)(2,1)} %get-tuple-element.37), channel_id=1, source_target_pairs={{0,128},{128,256},{256,384},{384,0},{1,129},{129,257},{257,385},{3... | collective-permute-start | bytes 786440 | tf_op jit(solution)/shard_map/ppermute | solution.py:262
  99.5 21.0 %all-to-all-start.1 = ((s32[16,1,128]{2,1,0:T(1,128)}), s32[16,1,128]{2,1,0:T(1,128)S(1)}, u32[]{:S(2)}, u32[]{:S(2)}) async-start(s32[16,1,128]{2,1,0:T(1,128)} %bitcast.13), calls=%async_computation.1 | async-start | bytes 16384 | tf_op jit(solution)/shard_map/all_to_all | solution.py:315

commit v4 on v2

v4 whole, which is shorter than its diff:
```python
import jax
import jax.numpy as jnp
from jax import lax
from jax.experimental import pallas as pl
from jax.experimental.pallas import tpu as pltpu
from jax.sharding import PartitionSpec as P

CLUSTERS = 64
GROUPS = 2
BF16 = jnp.bfloat16
F32 = jnp.float32
VMEM_LIMIT = 48 * 1024 * 1024


def vmem_call(kernel, out_shape, in_smem, **kwargs):
    vmem = pl.BlockSpec(memory_space=pltpu.VMEM)
    smem = pl.BlockSpec(memory_space=pltpu.SMEM)
    return pl.pallas_call(
        kernel,
        out_shape=out_shape,
        in_specs=[smem if flag else vmem for flag in in_smem],
        out_specs=jax.tree.map(lambda _: vmem, out_shape),
        compiler_params=pltpu.CompilerParams(vmem_limit_bytes=VMEM_LIMIT),
        **kwargs,
    )


def scalar(value):
    return jnp.reshape(value, (1,)).astype(jnp.int32)


def iota(shape, dim):
    return lax.broadcasted_iota(jnp.int32, shape, dim)


def routing(ids, owners, capacity):
    rows, heads = ids.shape
    per_owner = CLUSTERS // owners

    def kernel(ids_ref, ids_t_ref, slot_row_ref, slot_col_ref):
        before_col = (iota((rows, rows), 1) < iota((rows, rows), 0)).astype(BF16)
        before_row = (iota((rows, rows), 0) < iota((rows, rows), 1)).astype(BF16)
        for h in range(heads):
            owner_col = ids_ref[:, h : h + 1] // per_owner
            hot = owner_col == iota((rows, owners), 1)
            count = jnp.dot(before_col, hot.astype(BF16), preferred_element_type=F32)
            rank = jnp.sum(jnp.where(hot, count, 0.0), axis=1, keepdims=True)
            slot_col_ref[:, h : h + 1] = owner_col * capacity + rank.astype(jnp.int32)
            owner_row = ids_t_ref[h : h + 1, :] // per_owner
            hot = owner_row == iota((owners, rows), 0)
            count = jnp.dot(hot.astype(BF16), before_row, preferred_element_type=F32)
            rank = jnp.sum(jnp.where(hot, count, 0.0), axis=0, keepdims=True)
            slot_row_ref[h : h + 1, :] = owner_row * capacity + rank.astype(jnp.int32)

    return vmem_call(
        kernel,
        (
            jax.ShapeDtypeStruct((heads, rows), jnp.int32),
            jax.ShapeDtypeStruct((rows, heads), jnp.int32),
        ),
        (False, False),
    )(ids, ids.T)


def owned_mask(all_ids, me, heads, capacity):
    sources, id_rows, lanes = all_ids.shape
    per_head = 2 * sources * capacity // 4 // lanes
    rows = per_head * lanes
    per_owner = CLUSTERS // sources
    slots = sources * capacity

    def kernel(me_ref, ids_ref, out_ref):
        before = (iota((rows, rows), 0) < iota((rows, rows), 1)).astype(BF16)
        place = iota((sources, capacity, rows), 1)
        kinds = iota((slots, 128), 1) + 1
        query = iota((slots, slots), 0)
        key = iota((slots, slots), 1)
        outside = jnp.where(query == key, -100000.0, 0.0)
        for h in range(heads):
            ids = jnp.concatenate(
                [ids_ref[:, h * per_head + j, :] for j in range(per_head)], axis=1
            )
            ids = ids.astype(F32).astype(jnp.int32)
            owner = ids // per_owner
            mine = owner == me_ref[0]
            rank = jnp.dot(mine.astype(BF16), before, preferred_element_type=F32)
            rank = jnp.where(mine, rank.astype(jnp.int32), -1)
            tag = ids - owner * per_owner + 1
            placed = jnp.where(rank[:, None, :] == place, tag[:, None, :], 0)
            tag = jnp.sum(placed.reshape(slots, rows), axis=1, keepdims=True)
            member = (tag == kinds).astype(BF16)
            same = lax.dot_general(
                member, member, (((1,), (1,)), ((), ())), preferred_element_type=F32
            )
            out_ref[h] = jnp.where((same > 0.5) & (key <= query), outside, -1e30)

    return vmem_call(kernel, jax.ShapeDtypeStruct((heads, slots, slots), F32), (True, False))(
        scalar(me), all_ids
    )


def cut_tokens(local_rows, x, core, steps, chips):
    rows, depth = local_rows.shape
    half = depth // chips // 2

    def kernel(x_ref, core_ref, in_ref, *refs):
        out_refs, sems = refs[:-1], refs[-1]
        copies = []
        for i, step in enumerate(steps):
            chip = lax.rem(x_ref[0] + step + chips, chips)
            for j in range(2):
                first = (2 * chip + lax.rem(core_ref[0] + j, 2)) * half
                copies.append(
                    pltpu.make_async_copy(
                        in_ref.at[:, pl.ds(pl.multiple_of(first, half), half)],
                        out_refs[i].at[:, j * half : (j + 1) * half],
                        sems.at[2 * i + j],
                    )
                )
        for copy in copies:
            copy.start()
        for copy in copies:
            copy.wait()

    smem = pl.BlockSpec(memory_space=pltpu.SMEM)
    whole = pl.BlockSpec(memory_space=pl.ANY)
    return pl.pallas_call(
        kernel,
        out_shape=(jax.ShapeDtypeStruct((rows, 2 * half), BF16),) * len(steps),
        in_specs=[smem, smem, whole],
        out_specs=(whole,) * len(steps),
        scratch_shapes=[pltpu.SemaphoreType.DMA((2 * len(steps),))],
    )(scalar(x), scalar(core), local_rows)


def assemble(parts, starts, me, size, width):
    height, wide = parts[0].shape[1:]
    classes = 4
    id_rows = 16

    def kernel(me_ref, *refs):
        part_refs = refs[: len(parts)]
        weight_ref, id_ref, sems = refs[len(parts) :]
        copies = []
        for ref, (step, first) in zip(part_refs, starts):
            kind = lax.rem(me_ref[0] + step + size, classes)
            for j in range(ref.shape[0]):
                device = kind + classes * (first + j)
                at = pl.multiple_of(device * height, height)
                copies.append((ref.at[j, :, :width], weight_ref.at[pl.ds(at, height), :]))
                copies.append((ref.at[j, :id_rows, width:], id_ref.at[device]))
        copies = [
            pltpu.make_async_copy(source, target, sems.at[i])
            for i, (source, target) in enumerate(copies)
        ]
        for copy in copies:
            copy.start()
        for copy in copies:
            copy.wait()

    whole = pl.BlockSpec(memory_space=pl.ANY)
    return pl.pallas_call(
        kernel,
        out_shape=(
            jax.ShapeDtypeStruct((size * height, width), BF16),
            jax.ShapeDtypeStruct((size, id_rows, wide - width), BF16),
        ),
        in_specs=[pl.BlockSpec(memory_space=pltpu.SMEM)] + [whole] * len(parts),
        out_specs=(whole, whole),
        scratch_shapes=[pltpu.SemaphoreType.DMA((2 * size,))],
    )(scalar(me), *parts)


def project(pieces, ring, other, groups):
    rows, depth = pieces[0].shape
    half, width = ring.shape
    part = width // groups

    def kernel(*refs):
        piece_refs = refs[: len(pieces)]
        ring_ref, other_ref = refs[len(pieces) : len(pieces) + 2]
        out_refs = refs[len(pieces) + 2 :]
        for i, piece_ref in enumerate(piece_refs):
            for g in range(groups):
                cols = slice(g * part, (g + 1) * part)
                total = jnp.dot(
                    piece_ref[:, :half], ring_ref[:, cols], preferred_element_type=F32
                ) + jnp.dot(piece_ref[:, half:], other_ref[:, cols], preferred_element_type=F32)
                out_refs[i * groups + g][...] = total.astype(BF16)

    return vmem_call(
        kernel,
        (jax.ShapeDtypeStruct((rows, part), BF16),) * (len(pieces) * groups),
        (False,) * (len(pieces) + 2),
    )(*pieces, ring, other)


def pack(partials, slot_row, owners, capacity, head_dim):
    parts = len(partials[0])
    groups = len(partials)
    rows, width = partials[0][0].shape
    in_group = width // (2 * head_dim)
    heads = in_group * groups
    slots = owners * capacity

    def kernel(*refs):
        slot_ref, out_ref = refs[-2:]

        def columns(g, first):
            cols = slice(first, first + head_dim)
            total = refs[g * parts][:, cols].astype(F32)
            for p in range(1, parts):
                total += refs[g * parts + p][:, cols].astype(F32)
            return total.astype(BF16)

        for h in range(heads):
            place = iota((slots, rows), 0) == slot_ref[h : h + 1, :]
            place = place.astype(BF16)
            for m in range(2):
                first = (m * in_group + h % in_group) * head_dim
                packed = jnp.dot(
                    place, columns(h // in_group, first), preferred_element_type=F32
                ).astype(BF16)
                out_ref[
                    :, h * capacity : (h + 1) * capacity, m * head_dim : (m + 1) * head_dim
                ] = packed.reshape(owners, capacity, head_dim)

    return vmem_call(
        kernel,
        jax.ShapeDtypeStruct((owners, heads * capacity, 2 * head_dim), BF16),
        (False,) * (parts * groups + 1),
    )(*[part for group in partials for part in group], slot_row)


def attend(blocks, mask, capacity):
    sources, rows, width = blocks.shape
    head_dim = width // 2
    heads = rows // capacity
    slots = sources * capacity
    scale = head_dim ** (-0.5)

    def kernel(block_ref, mask_ref, out_ref):
        for h in range(heads):
            here = slice(h * capacity, (h + 1) * capacity)
            keys = block_ref[:, here, :head_dim].reshape(slots, head_dim)
            values = block_ref[:, here, head_dim:].reshape(slots, head_dim)
            scores = lax.dot_general(
                keys, keys, (((1,), (1,)), ((), ())), preferred_element_type=F32
            )
            mask = mask_ref[h]
            scores = jnp.where(mask == 0.0, scores * scale, mask)
            row_max = jnp.max(scores, axis=1, keepdims=True)
            weights = jnp.exp(scores - row_max)
            total = jnp.sum(weights, axis=1, keepdims=True)
            probabilities = (weights / total).astype(BF16)
            result = jnp.dot(probabilities, values, preferred_element_type=F32).astype(BF16)
            out_ref[:, here, :] = result.reshape(sources, capacity, head_dim)

    return vmem_call(
        kernel, jax.ShapeDtypeStruct((sources, rows, head_dim), BF16), (False, False)
    )(blocks, mask)


def unpack(returned, slot_col, capacity):
    owners, height, head_dim = returned.shape
    rows, heads = slot_col.shape
    slots = owners * capacity

    def kernel(block_ref, slot_ref, out_ref):
        for h in range(heads):
            block = block_ref[:, h * capacity : (h + 1) * capacity, :].reshape(slots, head_dim)
            place = slot_ref[:, h : h + 1] == iota((rows, slots), 1)
            out_ref[:, h * head_dim : (h + 1) * head_dim] = jnp.dot(
                place.astype(BF16), block, preferred_element_type=F32
            ).astype(BF16)

    return vmem_call(
        kernel, jax.ShapeDtypeStruct((rows, heads * head_dim), BF16), (False, False)
    )(returned, slot_col)


CLU = ("zq", "zr")


def shifted(block, step, axis):
    size = lax.axis_size(axis)
    return lax.ppermute(block, axis, [(i, (i + step) % size) for i in range(size)])


def body(tokens, proj_weight, clusters):
    rows, depth = tokens.shape[1:]
    owners = lax.axis_size(CLU)
    me = lax.axis_index(CLU)
    heads = clusters.shape[2]
    shard = proj_weight.shape[0]
    width = 2 * proj_weight.shape[2]
    head_dim = proj_weight.shape[2] // heads
    capacity = 2 * rows // owners
    chips = lax.axis_size("x")

    own = proj_weight.reshape(shard, 2, GROUPS, width // GROUPS // 2).transpose(0, 2, 1, 3)
    ids = clusters[0].T.astype(BF16).reshape(-1, 128)
    ids = jnp.pad(ids, ((0, shard - ids.shape[0]), (0, 0)))
    own = jnp.concatenate([own.reshape(shard, width), ids], axis=1)
    four = lax.all_to_all(
        jnp.broadcast_to(own, (4,) + own.shape), "zq", split_axis=0, concat_axis=0, tiled=True
    )
    steps = (2, 1, -1, 0)
    pieces = cut_tokens(tokens[0], lax.axis_index("x"), lax.axis_index("core"), steps, chips)
    pieces = [p if s == 0 else shifted(p, s, "x") for p, s in zip(pieces, steps)]

    parts = [
        four,
        shifted(four, 1, CLU),
        shifted(four, -1, CLU),
        shifted(four[:2], 2, CLU),
        shifted(four[2:], -2, CLU),
    ]
    starts = [(0, 0), (-1, 0), (1, 0), (-2, 0), (2, 2)]
    ring, all_ids = assemble(parts, starts, me, owners, width)
    other = lax.ppermute(ring, "core", [(0, 1), (1, 0)])
    sent = project(pieces, ring, other, GROUPS)

    slot_row, slot_col = routing(clusters[0], owners, capacity)
    partials = [[] for _ in range(GROUPS)]
    for g in range(GROUPS):
        for i, step in enumerate(steps):
            part = sent[i * GROUPS + g]
            partials[g].append(part if step == 0 else shifted(part, -step, "x"))
    mask = owned_mask(all_ids, me, heads, capacity)
    outgoing = pack(partials, slot_row, owners, capacity, head_dim)
    incoming = lax.all_to_all(outgoing, CLU, split_axis=0, concat_axis=0, tiled=True)
    replies = attend(incoming, mask, capacity)
    returned = lax.all_to_all(replies, CLU, split_axis=0, concat_axis=0, tiled=True)
    return unpack(returned, slot_col, capacity)[None]


def solution(mesh):
    ctx, clu, tp = (mesh.shape[name] for name in mesh.axis_names)
    fine = jax.sharding.Mesh(
        mesh.devices.reshape(ctx // 2, 2, clu // 4, 4, tp), ("x", "core") + CLU + ("tp",)
    )
    ctx_axes = ("x", "core")
    return jax.shard_map(
        body,
        mesh=fine,
        in_specs=(
            P(ctx_axes, CLU, None),
            P(ctx_axes + CLU, None, "tp"),
            P(ctx_axes, CLU, "tp"),
        ),
        out_specs=P(ctx_axes, CLU, "tp"),
        check_vma=False,
    )
```

time: 241 us -> 329 us (1.37)
  Pallas kernels: 10 us -> 111 us
  starting transfers between devices: 76.2 us -> 55.5 us
  waiting for transfers between devices: 67.5 us -> 78.4 us
  matrix products: 7.97 us -> 0 us
  blocking collectives: 66.9 us -> 71 us
    pallas_call x4 -> x6, Pallas kernels: 6.81 us -> 109 us  [the longest x1 64.7 us: cut_tokens(): pl.pallas_call(kernel, out_shape=(jax.ShapeDtypeStruct((rows, 2 * half),...]
    all_to_all x1 -> x2, blocking collectives: 19.7 us -> 71 us  [the longest x1 36.8 us: body(): lax.all_to_all(replies, CLU, split_axis=0, concat_axis=0, tiled=True)]
    all_gather x1 -> x0, blocking collectives: 47.2 us -> none  [body(): all_ids = lax.all_gather(clusters[0].T, 'clu', axis=0, tiled=False)]
    all_to_all x6 -> x1, starting transfers between devices: 35 us -> 4.67 us  [body(): lax.all_to_all(outgoing, CLU, split_axis=0, concat_axis=0, tiled=True)]
    ppermute x7 -> x13, waiting for transfers between devices: 7.1 us -> 33.2 us  [shifted(): lax.ppermute(block, axis, [(i, (i + step) % size) for i in range(size)])]
    all_to_all x6 -> x1, waiting for transfers between devices: 60.4 us -> 45.1 us  [body(): lax.all_to_all(outgoing, CLU, split_axis=0, concat_axis=0, tiled=True)]
    ppermute x7 -> x13, starting transfers between devices: 39.3 us -> 48.9 us  [shifted(): lax.ppermute(block, axis, [(i, (i + step) % size) for i in range(size)])]
    dot_general x4 -> x0, matrix products: 7.97 us -> none  [the longest x2 5.5 us: body(): jnp.dot(theirs, other[:, cols], preferred_element_type=F32)]
  transfers between devices with their start and end apart: 14 -> 15, of which waited for: 6 -> 9; matrix products, arithmetic and copies ran while one was open for 6% -> 0% of each run, Pallas kernels for 4% -> 21%
where the time goes in v4:
time: 329 us; the launch traced here: 327 us
  Pallas kernels  111 us (34%)
  waiting for transfers between devices  78.4 us (24%)
  blocking collectives  71 us (22%)
  starting transfers between devices  55.5 us (17%)
  local copies, waits for them, and re-layouts  9.4 us (3%)
    pallas_call x1, Pallas kernels, cut_tokens(): pl.pallas_call(kernel, out_shape=(jax.ShapeDtypeStruct((rows, 2 * half),...  64.7 us
    ppermute x13, starting transfers between devices, shifted(): lax.ppermute(block, axis, [(i, (i + step) % size) for i in range(size)])  48.9 us
    all_to_all x1, waiting for transfers between devices, body(): lax.all_to_all(outgoing, CLU, split_axis=0, concat_axis=0, tiled=True)  45.1 us
    all_to_all x1, blocking collectives, body(): lax.all_to_all(replies, CLU, split_axis=0, concat_axis=0, tiled=True)  36.8 us
    pallas_call x1, Pallas kernels, assemble(): pl.pallas_call(kernel, out_shape=(jax.ShapeDtypeStruct((size * height, wi...  35.1 us
    all_to_all x1, blocking collectives, body(): lax.all_to_all(jnp.broadcast_to(own, (4,) + own.shape), 'zq', split_axis=...  34.2 us
    ppermute x13, waiting for transfers between devices, shifted(): lax.ppermute(block, axis, [(i, (i + step) % size) for i in range(size)])  33.2 us
    unnamed x24, local copies, waits for them, and re-layouts  8.24 us
  transfers between devices with their start and end apart: 15, of which 9 were waited for; matrix products, arithmetic and copies ran while one was open for 0% of the time, Pallas kernels for 21%

profile of v4, /device:TPU:24, one launch (start us, length us, event | category | flops | bytes accessed | tf_op | source)
XLA Modules:
  0.0 326.6 jit_solution(11435784946395042679)
XLA Ops:
  1.7 34.2 %all_to_all.15.refs_0_ = bf16[4,32,1152]{2,1,0:T(8,128)(2,1)S(1)} all-to-all(bf16[4,32,1152]{2,1,0:T(8,128)(2,1)S(1)} %broadcast_in_dim.6), channel_id=1, replica_groups=mesh['x'=4,'core'=2,'zq'=4,'zr'=4,'tp'=4] {'zq'}, dimensions={0} | all-to-all | bytes 589824 | tf_op jit(solution)/shard_map/all_to_all | solution.py:305
  36.0 6.8 %collective-permute-start.3 = (bf16[4,32,1152]{2,1,0:T(8,128)(2,1)S(1)}, bf16[4,32,1152]{2,1,0:T(8,128)(2,1)S(1)}, u32[]{:S(2)}, u32[]{:S(2)}) collective-permute-start(bf16[4,32,1152]{2,1,0:T(8,128)(2,1)S(1)} %all_to_all.15.refs_0_), channel_id=1, source_target_pairs={{0,4},{4,8},{8,12},{12,16},{16,20},{20,24},{24,28},{28,32},{32,36}... | collective-permute-start | bytes 884744 | tf_op jit(solution)/shard_map/ppermute | solution.py:287
  44.7 4.4 %collective-permute-start.5 = (bf16[2,32,1152]{2,1,0:T(8,128)(2,1)S(1)}, bf16[2,32,1152]{2,1,0:T(8,128)(2,1)S(1)}, u32[]{:S(2)}, u32[]{:S(2)}) collective-permute-start(bf16[2,32,1152]{2,1,0:T(8,128)(2,1)S(1)} %get-tuple-element.38), channel_id=1, source_target_pairs={{0,8},{4,12},{8,16},{12,20},{16,24},{20,28},{24,32},{28,36},{32,40... | collective-permute-start | bytes 442376 | tf_op jit(solution)/shard_map/ppermute | solution.py:287
  49.1 3.5 %collective-permute-start.6 = (bf16[2,32,1152]{2,1,0:T(8,128)(2,1)S(1)}, bf16[2,32,1152]{2,1,0:T(8,128)(2,1)S(1)}, u32[]{:S(2)}, u32[]{:S(2)}) collective-permute-start(bf16[2,32,1152]{2,1,0:T(8,128)(2,1)S(1)} %get-tuple-element.37), channel_id=1, source_target_pairs={{0,56},{4,60},{8,0},{12,4},{16,8},{20,12},{24,16},{28,20},{32,24},... | collective-permute-start | bytes 442376 | tf_op jit(solution)/shard_map/ppermute | solution.py:287
  52.7 2.9 collective-permute-done.5.refs_3_
  55.6 3.4 %collective-permute-done.6.refs_4_ = bf16[2,32,1152]{2,1,0:T(8,128)(2,1)S(1)} collective-permute-done((bf16[2,32,1152]{2,1,0:T(8,128)(2,1)S(1)}, bf16[2,32,1152]{2,1,0:T(8,128)(2,1)S(1)}, u32[]{:S(2)}, u32[]{:S(2)}) %collective-permute-start.6) | collective-permute-done | bytes 147488 | tf_op jit(solution)/shard_map/ppermute | solution.py:287
  59.8 35.1 %shard_map.38 = (bf16[512,1024]{1,0:T(8,128)(2,1)}, bf16[16,16,128]{2,1,0:T(8,128)(2,1)}) custom-call(s32[1]{0:T(128)} %bitcast.3.me_ref, bf16[4,32,1152]{2,1,0:T(8,128)(2,1)} %copy-done.6, bf16[4,32,1152]{2,1,0:T(8,128)(2,1)} %copy-done.8, bf16[4,32,1152]{2,1,0:T(8,128)(2,1)} %copy-done.9, bf16[2,32,1152]{2,1,0:T(8,128)(2,1)} %copy-done.10, ...), custom_call_target="tpu_custom_call" | custom-call | tf_op jit(solution)/shard_map/pallas_call | solution.py:162
  96.9 64.7 %shard_map.37 = (bf16[256,1024]{1,0:T(8,128)(2,1)}, bf16[256,1024]{1,0:T(8,128)(2,1)}, bf16[256,1024]{1,0:T(8,128)(2,1)}, bf16[256,1024]{1,0:T(8,128)(2,1)}) custom-call(s32[1]{0:T(128)} %bitcast.x_ref, s32[1]{0:T(128)} %bitcast.1.core_ref, bf16[256,4096]{1,0:T(8,128)(2,1)} %bitcast.12), custom_call_target="tpu_custom_call" | custom-call | tf_op jit(solution)/shard_map/pallas_call | solution.py:127
  161.6 4.9 %collective-permute-start = (bf16[256,1024]{1,0:T(8,128)(2,1)}, bf16[256,1024]{1,0:T(8,128)(2,1)S(1)}, u32[]{:S(2)}, u32[]{:S(2)}) collective-permute-start(bf16[256,1024]{1,0:T(8,128)(2,1)} %get-tuple-element.21), channel_id=1, source_target_pairs={{0,256},{128,384},{256,0},{384,128},{1,257},{129,385},{257,1},{385... | collective-permute-start | bytes 1572872 | tf_op jit(solution)/shard_map/ppermute | solution.py:287
  166.6 2.5 collective-permute-start.1
  169.1 4.6 %collective-permute-start.2 = (bf16[256,1024]{1,0:T(8,128)(2,1)}, bf16[256,1024]{1,0:T(8,128)(2,1)S(1)}, u32[]{:S(2)}, u32[]{:S(2)}) collective-permute-start(bf16[256,1024]{1,0:T(8,128)(2,1)} %get-tuple-element.23), channel_id=1, source_target_pairs={{0,384},{128,0},{256,128},{384,256},{1,385},{129,1},{257,129},{385... | collective-permute-start | bytes 1572872 | tf_op jit(solution)/shard_map/ppermute | solution.py:287
  173.6 6.4 %collective-permute-done.refs_0_ = bf16[256,1024]{1,0:T(8,128)(2,1)S(1)} collective-permute-done((bf16[256,1024]{1,0:T(8,128)(2,1)}, bf16[256,1024]{1,0:T(8,128)(2,1)S(1)}, u32[]{:S(2)}, u32[]{:S(2)}) %collective-permute-start) | collective-permute-done | bytes 524320 | tf_op jit(solution)/shard_map/ppermute | solution.py:287
  180.0 10.8 %collective-permute-done.1.refs_1_ = bf16[256,1024]{1,0:T(8,128)(2,1)S(1)} collective-permute-done((bf16[256,1024]{1,0:T(8,128)(2,1)}, bf16[256,1024]{1,0:T(8,128)(2,1)S(1)}, u32[]{:S(2)}, u32[]{:S(2)}) %collective-permute-start.1) | collective-permute-done | bytes 524320 | tf_op jit(solution)/shard_map/ppermute | solution.py:287
  194.2 3.8 %shard_map.39 = (bf16[256,512]{1,0:T(8,128)(2,1)S(1)}, bf16[256,512]{1,0:T(8,128)(2,1)}, bf16[256,512]{1,0:T(8,128)(2,1)S(1)}, bf16[256,512]{1,0:T(8,128)(2,1)S(...) custom-call(bf16[256,1024]{1,0:T(8,128)(2,1)S(1)} %collective-permut, ...), custom_call_target="tpu_custom_call" | custom-call | tf_op jit(solution)/shard_map/pallas_call | solution.py:191
  197.9 3.3 %collective-permute-start.10 = (bf16[256,512]{1,0:T(8,128)(2,1)S(1)}, bf16[256,512]{1,0:T(8,128)(2,1)S(1)}, u32[]{:S(2)}, u32[]{:S(2)}) collective-permute-start(bf16[256,512]{1,0:T(8,128)(2,1)S(1)} %get-tuple-element.28), channel_id=1, source_target_pairs={{0,128},{128,256},{256,384},{384,0},{1,129},{129,257},{257,385},{3... | collective-permute-start | bytes 786440 | tf_op jit(solution)/shard_map/ppermute | solution.py:287
  201.3 4.6 %collective-permute-start.11 = (bf16[256,512]{1,0:T(8,128)(2,1)}, bf16[256,512]{1,0:T(8,128)(2,1)S(1)}, u32[]{:S(2)}, u32[]{:S(2)}) collective-permute-start(bf16[256,512]{1,0:T(8,128)(2,1)} %get-tuple-element.30), channel_id=1, source_target_pairs={{0,256},{128,384},{256,0},{384,128},{1,257},{129,385},{257,1},{385... | collective-permute-start | bytes 786440 | tf_op jit(solution)/shard_map/ppermute | solution.py:287
  205.8 3.3 %collective-permute-start.12 = (bf16[256,512]{1,0:T(8,128)(2,1)S(1)}, bf16[256,512]{1,0:T(8,128)(2,1)S(1)}, u32[]{:S(2)}, u32[]{:S(2)}) collective-permute-start(bf16[256,512]{1,0:T(8,128)(2,1)S(1)} %get-tuple-element.31), channel_id=1, source_target_pairs={{0,384},{128,0},{256,128},{384,256},{1,385},{129,1},{257,129},{385... | collective-permute-start | bytes 786440 | tf_op jit(solution)/shard_map/ppermute | solution.py:287
  211.7 2.8 collective-permute-start.8
  214.5 3.7 %collective-permute-start.9 = (bf16[256,512]{1,0:T(8,128)(2,1)S(1)}, bf16[256,512]{1,0:T(8,128)(2,1)S(1)}, u32[]{:S(2)}, u32[]{:S(2)}) collective-permute-start(bf16[256,512]{1,0:T(8,128)(2,1)S(1)} %get-tuple-element.27), channel_id=1, source_target_pairs={{0,384},{128,0},{256,128},{384,256},{1,385},{129,1},{257,129},{385... | collective-permute-start | bytes 786440 | tf_op jit(solution)/shard_map/ppermute | solution.py:287
  219.1 3.2 collective-permute-done.13.refs_6_
  222.3 4.7 %collective-permute-done.8.refs_0_ = bf16[256,512]{1,0:T(8,128)(2,1)S(1)} collective-permute-done((bf16[256,512]{1,0:T(8,128)(2,1)S(1)}, bf16[256,512]{1,0:T(8,128)(2,1)S(1)}, u32[]{:S(2)}, u32[]{:S(2)}) %collective-permute-start.8) | collective-permute-done | bytes 262176 | tf_op jit(solution)/shard_map/ppermute | solution.py:287
  230.5 4.7 %all-to-all-start.1 = ((bf16[16,128,256]{2,1,0:T(8,128)(2,1)}), bf16[16,128,256]{2,1,0:T(8,128)(2,1)S(1)}, u32[]{:S(2)}, u32[]{:S(2)}) async-start(bf16[16,128,256]{2,1,0:T(8,128)(2,1)} %shard_map.41), calls=%async_computation.1 | async-start | bytes 2097152 | tf_op jit(solution)/shard_map/all_to_all | solution.py:332
  239.2 45.1 %all-to-all-done.1.block_ref = bf16[16,128,256]{2,1,0:T(8,128)(2,1)S(1)} async-done(((bf16[16,128,256]{2,1,0:T(8,128)(2,1)}), bf16[16,128,256]{2,1,0:T(8,128)(2,1)S(1)}, u32[]{:S(2)}, u32[]{:S(2)}) %all-to-all-start.1) | async-done | bytes 1048608 | tf_op jit(solution)/shard_map/all_to_all | solution.py:332
  288.6 36.8 %all_to_all.16.block_ref = bf16[16,128,128]{2,1,0:T(8,128)(2,1)S(1)} all-to-all(bf16[16,128,128]{2,1,0:T(8,128)(2,1)S(1)} %shard_map.43), channel_id=1, replica_groups=mesh['x'=4,'core'=2,'zq'=4,'zr'=4,'tp'=4] {'zq','zr'}, dimensions={0} | all-to-all | bytes 1048576 | tf_op jit(solution)/shard_map/all_to_all | solution.py:334
  (49 shorter events, 26.1 us)
Async XLA Ops:
  36.0 23.0 %copy-start.6 = (bf16[4,32,1152]{2,1,0:T(8,128)(2,1)}, bf16[4,32,1152]{2,1,0:T(8,128)(2,1)S(1)}, u32[]{:S(2)}) copy-start(bf16[4,32,1152]{2,1,0:T(8,128)(2,1)S(1)} %all_to_all.15.refs_0_) | copy-start | bytes 884740
  36.0 182.3 %copy-start.5 = (s32[1,256,4]{1,2,0:T(4,128)S(1)}, s32[1,256,4]{1,2,0:T(4,128)}, u32[]{:S(2)}) copy-start(s32[1,256,4]{1,2,0:T(4,128)} %param.5) | copy-start | bytes 12292
  36.0 23.0 %collective-permute-start.3 = (bf16[4,32,1152]{2,1,0:T(8,128)(2,1)S(1)}, bf16[4,32,1152]{2,1,0:T(8,128)(2,1)S(1)}, u32[]{:S(2)}, u32[]{:S(2)}) collective-permute-start(bf16[4,32,1152]{2,1,0:T(8,128)(2,1)S(1)} %all_to_all.15.refs_0_), channel_id=1, source_target_pairs={{0,4},{4,8},{8,12},{12,16},{16,20},{20,24},{24,28},{28,32},{32,36}... | collective-permute-start | bytes 884744 | tf_op jit(solution)/shard_map/ppermute | solution.py:287
  42.8 16.2 %collective-permute-start.4 = (bf16[4,32,1152]{2,1,0:T(8,128)(2,1)S(1)}, bf16[4,32,1152]{2,1,0:T(8,128)(2,1)S(1)}, u32[]{:S(2)}, u32[]{:S(2)}) collective-permute-start(bf16[4,32,1152]{2,1,0:T(8,128)(2,1)S(1)} %all_to_all.15.refs_0_), channel_id=1, source_target_pairs={{0,60},{4,0},{8,4},{12,8},{16,12},{20,16},{24,20},{28,24},{32,28},... | collective-permute-start | bytes 884744 | tf_op jit(solution)/shard_map/ppermute | solution.py:287
  44.7 10.8 %collective-permute-start.5 = (bf16[2,32,1152]{2,1,0:T(8,128)(2,1)S(1)}, bf16[2,32,1152]{2,1,0:T(8,128)(2,1)S(1)}, u32[]{:S(2)}, u32[]{:S(2)}) collective-permute-start(bf16[2,32,1152]{2,1,0:T(8,128)(2,1)S(1)} %get-tuple-element.38), channel_id=1, source_target_pairs={{0,8},{4,12},{8,16},{12,20},{16,24},{20,28},{24,32},{28,36},{32,40... | collective-permute-start | bytes 442376 | tf_op jit(solution)/shard_map/ppermute | solution.py:287
  49.1 9.8 %collective-permute-start.6 = (bf16[2,32,1152]{2,1,0:T(8,128)(2,1)S(1)}, bf16[2,32,1152]{2,1,0:T(8,128)(2,1)S(1)}, u32[]{:S(2)}, u32[]{:S(2)}) collective-permute-start(bf16[2,32,1152]{2,1,0:T(8,128)(2,1)S(1)} %get-tuple-element.37), channel_id=1, source_target_pairs={{0,56},{4,60},{8,0},{12,4},{16,8},{20,12},{24,16},{28,20},{32,24},... | collective-permute-start | bytes 442376 | tf_op jit(solution)/shard_map/ppermute | solution.py:287
  55.6 3.4 %copy-start.10 = (bf16[2,32,1152]{2,1,0:T(8,128)(2,1)}, bf16[2,32,1152]{2,1,0:T(8,128)(2,1)S(1)}, u32[]{:S(2)}) copy-start(bf16[2,32,1152]{2,1,0:T(8,128)(2,1)S(1)} %collective-permute-done.5.refs_3_) | copy-start | bytes 442372
  95.0 96.0 %collective-permute-start.7 = (bf16[512,1024]{1,0:T(8,128)(2,1)}, bf16[512,1024]{1,0:T(8,128)(2,1)S(1)}, u32[]{:S(2)}, u32[]{:S(2)}) collective-permute-start(bf16[512,1024]{1,0:T(8,128)(2,1)} %get-tuple-element.25.refs_4_), channel_id=1, source_target_pairs={{0,64},{64,0},{1,65},{65,1},{2,66},{66,2},{3,67},{67,3},{4,68},{68... | collective-permute-start | bytes 3145736 | tf_op jit(solution)/shard_map/ppermute | solution.py:321
  161.6 18.4 %collective-permute-start = (bf16[256,1024]{1,0:T(8,128)(2,1)}, bf16[256,1024]{1,0:T(8,128)(2,1)S(1)}, u32[]{:S(2)}, u32[]{:S(2)}) collective-permute-start(bf16[256,1024]{1,0:T(8,128)(2,1)} %get-tuple-element.21), channel_id=1, source_target_pairs={{0,256},{128,384},{256,0},{384,128},{1,257},{129,385},{257,1},{385... | collective-permute-start | bytes 1572872 | tf_op jit(solution)/shard_map/ppermute | solution.py:287
  166.6 24.2 %collective-permute-start.1 = (bf16[256,1024]{1,0:T(8,128)(2,1)}, bf16[256,1024]{1,0:T(8,128)(2,1)S(1)}, u32[]{:S(2)}, u32[]{:S(2)}) collective-permute-start(bf16[256,1024]{1,0:T(8,128)(2,1)} %get-tuple-element.22), channel_id=1, source_target_pairs={{0,128},{128,256},{256,384},{384,0},{1,129},{129,257},{257,385},{3... | collective-permute-start | bytes 1572872 | tf_op jit(solution)/shard_map/ppermute | solution.py:287
  169.1 21.9 %collective-permute-start.2 = (bf16[256,1024]{1,0:T(8,128)(2,1)}, bf16[256,1024]{1,0:T(8,128)(2,1)S(1)}, u32[]{:S(2)}, u32[]{:S(2)}) collective-permute-start(bf16[256,1024]{1,0:T(8,128)(2,1)} %get-tuple-element.23), channel_id=1, source_target_pairs={{0,384},{128,0},{256,128},{384,256},{1,385},{129,1},{257,129},{385... | collective-permute-start | bytes 1572872 | tf_op jit(solution)/shard_map/ppermute | solution.py:287
  190.9 1.0 copy-start.7
  191.9 1.2 copy-start.2
  193.1 1.0 copy-start.3
  194.2 41.0 %copy-start.4 = (bf16[16,16,128]{2,1,0:T(8,128)(2,1)S(1)}, bf16[16,16,128]{2,1,0:T(8,128)(2,1)}, u32[]{:S(2)}) copy-start(bf16[16,16,128]{2,1,0:T(8,128)(2,1)} %get-tuple-element.35.ids_ref) | copy-start | bytes 196612
  197.9 16.6 %collective-permute-start.10 = (bf16[256,512]{1,0:T(8,128)(2,1)S(1)}, bf16[256,512]{1,0:T(8,128)(2,1)S(1)}, u32[]{:S(2)}, u32[]{:S(2)}) collective-permute-start(bf16[256,512]{1,0:T(8,128)(2,1)S(1)} %get-tuple-element.28), channel_id=1, source_target_pairs={{0,128},{128,256},{256,384},{384,0},{1,129},{129,257},{257,385},{3... | collective-permute-start | bytes 786440 | tf_op jit(solution)/shard_map/ppermute | solution.py:287
  201.3 17.8 %collective-permute-start.11 = (bf16[256,512]{1,0:T(8,128)(2,1)}, bf16[256,512]{1,0:T(8,128)(2,1)S(1)}, u32[]{:S(2)}, u32[]{:S(2)}) collective-permute-start(bf16[256,512]{1,0:T(8,128)(2,1)} %get-tuple-element.30), channel_id=1, source_target_pairs={{0,256},{128,384},{256,0},{384,128},{1,257},{129,385},{257,1},{385... | collective-permute-start | bytes 786440 | tf_op jit(solution)/shard_map/ppermute | solution.py:287
  205.8 13.2 %collective-permute-start.12 = (bf16[256,512]{1,0:T(8,128)(2,1)S(1)}, bf16[256,512]{1,0:T(8,128)(2,1)S(1)}, u32[]{:S(2)}, u32[]{:S(2)}) collective-permute-start(bf16[256,512]{1,0:T(8,128)(2,1)S(1)} %get-tuple-element.31), channel_id=1, source_target_pairs={{0,384},{128,0},{256,128},{384,256},{1,385},{129,1},{257,129},{385... | collective-permute-start | bytes 786440 | tf_op jit(solution)/shard_map/ppermute | solution.py:287
  209.2 13.1 %collective-permute-start.13 = (bf16[256,512]{1,0:T(8,128)(2,1)S(1)}, bf16[256,512]{1,0:T(8,128)(2,1)S(1)}, u32[]{:S(2)}, u32[]{:S(2)}) collective-permute-start(bf16[256,512]{1,0:T(8,128)(2,1)S(1)} %get-tuple-element.32), channel_id=1, source_target_pairs={{0,128},{128,256},{256,384},{384,0},{1,129},{129,257},{257,385},{3... | collective-permute-start | bytes 786440 | tf_op jit(solution)/shard_map/ppermute | solution.py:287
  211.7 15.3 %collective-permute-start.8 = (bf16[256,512]{1,0:T(8,128)(2,1)S(1)}, bf16[256,512]{1,0:T(8,128)(2,1)S(1)}, u32[]{:S(2)}, u32[]{:S(2)}) collective-permute-start(bf16[256,512]{1,0:T(8,128)(2,1)S(1)} %get-tuple-element.26), channel_id=1, source_target_pairs={{0,256},{128,384},{256,0},{384,128},{1,257},{129,385},{257,1},{385... | collective-permute-start | bytes 786440 | tf_op jit(solution)/shard_map/ppermute | solution.py:287
  214.5 14.2 %collective-permute-start.9 = (bf16[256,512]{1,0:T(8,128)(2,1)S(1)}, bf16[256,512]{1,0:T(8,128)(2,1)S(1)}, u32[]{:S(2)}, u32[]{:S(2)}) collective-permute-start(bf16[256,512]{1,0:T(8,128)(2,1)S(1)} %get-tuple-element.27), channel_id=1, source_target_pairs={{0,384},{128,0},{256,128},{384,256},{1,385},{129,1},{257,129},{385... | collective-permute-start | bytes 786440 | tf_op jit(solution)/shard_map/ppermute | solution.py:287
  230.5 53.8 %all-to-all-start.1 = ((bf16[16,128,256]{2,1,0:T(8,128)(2,1)}), bf16[16,128,256]{2,1,0:T(8,128)(2,1)S(1)}, u32[]{:S(2)}, u32[]{:S(2)}) async-start(bf16[16,128,256]{2,1,0:T(8,128)(2,1)} %shard_map.41), calls=%async_computation.1 | async-start | bytes 2097152 | tf_op jit(solution)/shard_map/all_to_all | solution.py:332
  237.2 2.0 copy-start
  284.3 2.2 copy-start.1
  (3 other events, 2.3 us)

commit v5 on v4

v5 whole, which is shorter than its diff:
```python
import jax
import jax.numpy as jnp
from jax import lax
from jax.experimental import pallas as pl
from jax.experimental.pallas import tpu as pltpu
from jax.sharding import PartitionSpec as P

CLUSTERS = 64
BF16 = jnp.bfloat16
F32 = jnp.float32
VMEM_LIMIT = 48 * 1024 * 1024


def vmem_call(kernel, out_shape, in_smem, **kwargs):
    vmem = pl.BlockSpec(memory_space=pltpu.VMEM)
    smem = pl.BlockSpec(memory_space=pltpu.SMEM)
    return pl.pallas_call(
        kernel,
        out_shape=out_shape,
        in_specs=[smem if flag else vmem for flag in in_smem],
        out_specs=jax.tree.map(lambda _: vmem, out_shape),
        compiler_params=pltpu.CompilerParams(vmem_limit_bytes=VMEM_LIMIT),
        **kwargs,
    )


def scalar(value):
    return jnp.reshape(value, (1,)).astype(jnp.int32)


def iota(shape, dim):
    return lax.broadcasted_iota(jnp.int32, shape, dim)


def routing(ids, owners, capacity):
    rows, heads = ids.shape
    per_owner = CLUSTERS // owners

    def kernel(ids_ref, ids_t_ref, slot_row_ref, slot_col_ref):
        before_col = (iota((rows, rows), 1) < iota((rows, rows), 0)).astype(BF16)
        before_row = (iota((rows, rows), 0) < iota((rows, rows), 1)).astype(BF16)
        for h in range(heads):
            owner_col = ids_ref[:, h : h + 1] // per_owner
            hot = owner_col == iota((rows, owners), 1)
            count = jnp.dot(before_col, hot.astype(BF16), preferred_element_type=F32)
            rank = jnp.sum(jnp.where(hot, count, 0.0), axis=1, keepdims=True)
            slot_col_ref[:, h : h + 1] = owner_col * capacity + rank.astype(jnp.int32)
            owner_row = ids_t_ref[h : h + 1, :] // per_owner
            hot = owner_row == iota((owners, rows), 0)
            count = jnp.dot(hot.astype(BF16), before_row, preferred_element_type=F32)
            rank = jnp.sum(jnp.where(hot, count, 0.0), axis=0, keepdims=True)
            slot_row_ref[h : h + 1, :] = owner_row * capacity + rank.astype(jnp.int32)

    return vmem_call(
        kernel,
        (
            jax.ShapeDtypeStruct((heads, rows), jnp.int32),
            jax.ShapeDtypeStruct((rows, heads), jnp.int32),
        ),
        (False, False),
    )(ids, ids.T)


def owned_mask(all_ids, me, heads, capacity):
    sources, id_rows, lanes = all_ids.shape
    per_head = 2 * sources * capacity // 4 // lanes
    rows = per_head * lanes
    per_owner = CLUSTERS // sources
    slots = sources * capacity

    def kernel(me_ref, ids_ref, out_ref):
        before = (iota((rows, rows), 0) < iota((rows, rows), 1)).astype(BF16)
        place = iota((sources, capacity, rows), 1)
        kinds = iota((slots, 128), 1) + 1
        query = iota((slots, slots), 0)
        key = iota((slots, slots), 1)
        outside = jnp.where(query == key, -100000.0, 0.0)
        for h in range(heads):
            ids = jnp.concatenate(
                [ids_ref[:, h * per_head + j, :] for j in range(per_head)], axis=1
            )
            ids = ids.astype(F32).astype(jnp.int32)
            owner = ids // per_owner
            mine = owner == me_ref[0]
            rank = jnp.dot(mine.astype(BF16), before, preferred_element_type=F32)
            rank = jnp.where(mine, rank.astype(jnp.int32), -1)
            tag = ids - owner * per_owner + 1
            placed = jnp.where(rank[:, None, :] == place, tag[:, None, :], 0)
            tag = jnp.sum(placed.reshape(slots, rows), axis=1, keepdims=True)
            member = (tag == kinds).astype(BF16)
            same = lax.dot_general(
                member, member, (((1,), (1,)), ((), ())), preferred_element_type=F32
            )
            out_ref[h] = jnp.where((same > 0.5) & (key <= query), outside, -1e30)

    return vmem_call(kernel, jax.ShapeDtypeStruct((heads, slots, slots), F32), (True, False))(
        scalar(me), all_ids
    )


def cut_tokens(local_rows, core, parity, chips, owners):
    rows, depth = local_rows.shape
    half = depth // chips // 2
    shard = half // owners

    def kernel(core_ref, parity_ref, in_ref, own_ref, other_ref, order_ref):
        @pl.when(pl.program_id(0) == 0)
        def _():
            at = iota((half, half), 0)
            kind = at // shard % 2
            target = at // (2 * shard) * shard + at % shard
            target = target + jnp.where(kind == parity_ref[0], 0, half // 2)
            order_ref[...] = (target == iota((half, half), 1)).astype(BF16)

        def ordered(block):
            return jnp.dot(block, order_ref[...], preferred_element_type=F32).astype(BF16)

        first = ordered(in_ref[:, :half])
        second = ordered(in_ref[:, half:])
        mine_first = core_ref[0] == 0
        own_ref[0] = jnp.where(mine_first, first, second)
        other_ref[0] = jnp.where(mine_first, second, first)

    out_spec = pl.BlockSpec((1, rows, half), lambda p, core, parity: (p, 0, 0))
    return pl.pallas_call(
        kernel,
        grid_spec=pltpu.PrefetchScalarGridSpec(
            num_scalar_prefetch=2,
            grid=(chips,),
            in_specs=[pl.BlockSpec((rows, 2 * half), lambda p, core, parity: (0, p))],
            out_specs=(out_spec, out_spec),
            scratch_shapes=[pltpu.VMEM((half, half), BF16)],
        ),
        out_shape=(jax.ShapeDtypeStruct((chips, rows, half), BF16),) * 2,
    )(scalar(core), scalar(parity), local_rows)


def add_products(total, tokens, weights, places, x):
    chips, rows, half = tokens[0].shape
    width = weights[0].shape[1]
    given = [] if total is None else [total]

    def kernel(x_ref, *refs):
        out_ref = refs[-1]
        token_refs = refs[len(given) : len(given) + 2]
        weight_refs = refs[len(given) + 2 : -1]
        for i, token_ref in enumerate(token_refs):
            result = refs[0][i] if given else 0.0
            for weight_ref, (step, first) in zip(weight_refs, places):
                chip = lax.rem(x_ref[0] + step + chips, chips)
                depth = weight_ref.shape[0]
                result = result + jnp.dot(
                    token_ref[chip, :, first : first + depth],
                    weight_ref[...],
                    preferred_element_type=F32,
                )
            out_ref[i] = result

    operands = given + list(tokens) + list(weights)
    return vmem_call(
        kernel,
        jax.ShapeDtypeStruct((2, rows, width), F32),
        (True,) + (False,) * len(operands),
    )(scalar(x), *operands)


def last_products(total, tokens, weights, places, x):
    chips, rows, half = tokens[0].shape
    width = weights[0].shape[1]

    def kernel(x_ref, total_ref, own_ref, other_ref, *refs):
        weight_refs = refs[:-2]
        for i, (token_ref, out_ref) in enumerate(zip((own_ref, other_ref), refs[-2:])):
            result = total_ref[i]
            for weight_ref, (step, first) in zip(weight_refs, places):
                chip = lax.rem(x_ref[0] + step + chips, chips)
                depth = weight_ref.shape[0]
                result = result + jnp.dot(
                    token_ref[chip, :, first : first + depth],
                    weight_ref[...],
                    preferred_element_type=F32,
                )
            out_ref[...] = result.astype(out_ref.dtype)

    return vmem_call(
        kernel,
        (jax.ShapeDtypeStruct((rows, width), F32), jax.ShapeDtypeStruct((rows, width), BF16)),
        (True,) + (False,) * (3 + len(weights)),
    )(scalar(x), total, *tokens, *weights)


def pack(own, received, slot_row, owners, capacity, head_dim):
    rows, width = own.shape
    heads = slot_row.shape[0]
    slots = owners * capacity

    def kernel(own_ref, received_ref, slot_ref, out_ref):
        for h in range(heads):
            place = iota((slots, rows), 0) == slot_ref[h : h + 1, :]
            place = place.astype(BF16)
            for m in range(2):
                cols = slice((m * heads + h) * head_dim, (m * heads + h + 1) * head_dim)
                total = own_ref[:, cols] + received_ref[:, cols].astype(F32)
                packed = jnp.dot(
                    place, total.astype(BF16), preferred_element_type=F32
                ).astype(BF16)
                out_ref[
                    :, h * capacity : (h + 1) * capacity, m * head_dim : (m + 1) * head_dim
                ] = packed.reshape(owners, capacity, head_dim)

    return vmem_call(
        kernel,
        jax.ShapeDtypeStruct((owners, heads * capacity, 2 * head_dim), BF16),
        (False,) * 3,
    )(own, received, slot_row)


def attend(blocks, mask, capacity):
    sources, rows, width = blocks.shape
    head_dim = width // 2
    heads = rows // capacity
    slots = sources * capacity
    scale = head_dim ** (-0.5)

    def kernel(block_ref, mask_ref, out_ref):
        for h in range(heads):
            here = slice(h * capacity, (h + 1) * capacity)
            keys = block_ref[:, here, :head_dim].reshape(slots, head_dim)
            values = block_ref[:, here, head_dim:].reshape(slots, head_dim)
            scores = lax.dot_general(
                keys, keys, (((1,), (1,)), ((), ())), preferred_element_type=F32
            )
            mask = mask_ref[h]
            scores = jnp.where(mask == 0.0, scores * scale, mask)
            row_max = jnp.max(scores, axis=1, keepdims=True)
            weights = jnp.exp(scores - row_max)
            total = jnp.sum(weights, axis=1, keepdims=True)
            probabilities = (weights / total).astype(BF16)
            result = jnp.dot(probabilities, values, preferred_element_type=F32).astype(BF16)
            out_ref[:, here, :] = result.reshape(sources, capacity, head_dim)

    return vmem_call(
        kernel, jax.ShapeDtypeStruct((sources, rows, head_dim), BF16), (False, False)
    )(blocks, mask)


def unpack(returned, slot_col, capacity):
    owners, height, head_dim = returned.shape
    rows, heads = slot_col.shape
    slots = owners * capacity

    def kernel(block_ref, slot_ref, out_ref):
        for h in range(heads):
            block = block_ref[:, h * capacity : (h + 1) * capacity, :].reshape(slots, head_dim)
            place = slot_ref[:, h : h + 1] == iota((rows, slots), 1)
            out_ref[:, h * head_dim : (h + 1) * head_dim] = jnp.dot(
                place.astype(BF16), block, preferred_element_type=F32
            ).astype(BF16)

    return vmem_call(
        kernel, jax.ShapeDtypeStruct((rows, heads * head_dim), BF16), (False, False)
    )(returned, slot_col)


CLU = ("zh", "zl")


def shifted(block, step, axis):
    size = lax.axis_size(axis)
    return lax.ppermute(block, axis, [(i, (i + step) % size) for i in range(size)])


def round_x(block):
    half = block.shape[0] // 2
    below = shifted(block, 1, "x")
    above = shifted(block, -1, "x")
    return [below, above, shifted(below[:half], 1, "x"), shifted(above[half:], -1, "x")]


def body(tokens, proj_weight, clusters):
    rows, depth = tokens.shape[1:]
    owners = lax.axis_size(CLU)
    me = lax.axis_index(CLU)
    parity = lax.axis_index("zl")
    x = lax.axis_index("x")
    heads = clusters.shape[2]
    shard = proj_weight.shape[0]
    width = 2 * proj_weight.shape[2]
    head_dim = proj_weight.shape[2] // heads
    capacity = 2 * rows // owners
    chips = lax.axis_size("x")

    ids = clusters[0].T.astype(BF16).reshape(-1, 128)
    ids = jnp.pad(ids, ((0, shard - ids.shape[0]), (0, 0)))
    own = jnp.concatenate([proj_weight.reshape(shard, width), ids], axis=1)
    same = lax.all_gather(own, "zh", axis=0)
    low, high = shifted(same[:4], 1, CLU), shifted(same[4:], -1, CLU)
    rest = jnp.concatenate([low, high], axis=0)

    mine, send = cut_tokens(tokens[0], lax.axis_index("core"), parity, chips, owners)
    theirs = lax.ppermute(send, "core", [(0, 1), (1, 0)])

    first = same[:, :, :width].reshape(-1, width)
    second = rest[:, :, :width].reshape(-1, width)
    first_x, second_x = round_x(first), round_x(second)
    half = first.shape[0]
    both = (mine, theirs)
    total = add_products(
        None, both, [first] + first_x[:2], [(0, 0), (-1, 0), (1, 0)], x
    )
    total = add_products(
        total, both, [second] + second_x[:2], [(0, half), (-1, half), (1, half)], x
    )
    kept, given = last_products(
        total,
        both,
        first_x[2:] + second_x[2:],
        [(2, 0), (2, half // 2), (2, half), (2, half + half // 2)],
        x,
    )
    received = lax.ppermute(given, "core", [(0, 1), (1, 0)])

    slot_row, slot_col = routing(clusters[0], owners, capacity)
    outgoing = pack(kept, received, slot_row, owners, capacity, head_dim)
    incoming = lax.all_to_all(outgoing, CLU, split_axis=0, concat_axis=0, tiled=True)

    same_ids, rest_ids = same[:, :16, width:], rest[:, :16, width:]
    even = jnp.where(parity == 0, same_ids, rest_ids)
    odd = jnp.where(parity == 0, rest_ids, same_ids)
    all_ids = jnp.stack([even, odd], axis=1).reshape((owners,) + even.shape[1:])
    mask = owned_mask(all_ids, me, heads, capacity)
    replies = attend(incoming, mask, capacity)
    returned = lax.all_to_all(replies, CLU, split_axis=0, concat_axis=0, tiled=True)
    return unpack(returned, slot_col, capacity)[None]


def solution(mesh):
    ctx, clu, tp = (mesh.shape[name] for name in mesh.axis_names)
    fine = jax.sharding.Mesh(
        mesh.devices.reshape(ctx // 2, 2, clu // 2, 2, tp), ("x", "core") + CLU + ("tp",)
    )
    ctx_axes = ("x", "core")
    return jax.shard_map(
        body,
        mesh=fine,
        in_specs=(
            P(ctx_axes, CLU, None),
            P(ctx_axes + CLU, None, "tp"),
            P(ctx_axes, CLU, "tp"),
        ),
        out_specs=P(ctx_axes, CLU, "tp"),
        check_vma=False,
    )
```

time: 329 us -> 206 us (0.63)
  Pallas kernels: 111 us -> 21.1 us
  waiting for transfers between devices: 78.4 us -> 47.8 us
  starting transfers between devices: 55.5 us -> 46.2 us
  local copies, waits for them, and re-layouts: 9.4 us -> 13.8 us
  blocking collectives: 71 us -> 74.6 us
    pallas_call x3 -> x4, Pallas kernels: 104 us -> 13.4 us  [the longest x2 4.83 us: add_products(): vmem_call(kernel, jax.ShapeDtypeStruct((2, rows, width), F32), (True,) +...]
    all_gather x0 -> x1, blocking collectives: none -> 37.6 us  [body(): same = lax.all_gather(own, 'zh', axis=0)]
    all_to_all x1 -> x0, blocking collectives: 34.2 us -> none  [body(): lax.all_to_all(jnp.broadcast_to(own, (4,) + own.shape), 'zq', split_axis=...]
    ppermute x13 -> x10, waiting for transfers between devices: 33.2 us -> 1.14 us  [shifted(): lax.ppermute(block, axis, [(i, (i + step) % size) for i in range(size)])]
    ppermute x13 -> x10, starting transfers between devices: 48.9 us -> 35.1 us  [shifted(): lax.ppermute(block, axis, [(i, (i + step) % size) for i in range(size)])]
    slice x1 -> x7, local copies, waits for them, and re-layouts: 0.02 us -> 5.8 us  [the longest x2 2.46 us: round_x(): below[:half]]
    unnamed x24 -> x26, local copies, waits for them, and re-layouts: 8.24 us -> 7.84 us
  transfers between devices with their start and end apart: 15 -> 13, of which waited for: 9 -> 3; matrix products, arithmetic and copies ran while one was open for 0% -> 3% of each run, Pallas kernels for 21% -> 6%
where the time goes in v5:
time: 206 us; the launch traced here: 205 us
  blocking collectives  74.6 us (36%)
  waiting for transfers between devices  47.8 us (23%)
  starting transfers between devices  46.2 us (22%)
  Pallas kernels  21.1 us (10%)
  local copies, waits for them, and re-layouts  13.8 us (7%)
    all_to_all x1, waiting for transfers between devices, body(): lax.all_to_all(outgoing, CLU, split_axis=0, concat_axis=0, tiled=True)  45.4 us
    all_gather x1, blocking collectives, body(): same = lax.all_gather(own, 'zh', axis=0)  37.6 us
    all_to_all x1, blocking collectives, body(): lax.all_to_all(replies, CLU, split_axis=0, concat_axis=0, tiled=True)  36.9 us
    ppermute x10, starting transfers between devices, shifted(): lax.ppermute(block, axis, [(i, (i + step) % size) for i in range(size)])  35.1 us
    unnamed x26, local copies, waits for them, and re-layouts  7.84 us
    all_to_all x1, starting transfers between devices, body(): lax.all_to_all(outgoing, CLU, split_axis=0, concat_axis=0, tiled=True)  7.2 us
    pallas_call x2, Pallas kernels, add_products(): vmem_call(kernel, jax.ShapeDtypeStruct((2, rows, width), F32), (True,) +...  4.83 us
    pallas_call x1, Pallas kernels, cut_tokens(): pl.pallas_call(kernel, grid_spec=pltpu.PrefetchScalarGridSpec(num_scalar_...  4.82 us
  transfers between devices with their start and end apart: 13, of which 3 were waited for; matrix products, arithmetic and copies ran while one was open for 3% of the time, Pallas kernels for 6%

profile of v5, /device:TPU:24, one launch (start us, length us, event | category | flops | bytes accessed | tf_op | source)
XLA Modules:
  0.0 205.5 jit_solution(11280335446152853629)
XLA Ops:
  1.6 37.6 %all-gather = bf16[256,1152]{1,0:T(8,128)(2,1)S(1)} all-gather(bf16[32,1152]{1,0:T(8,128)(2,1)S(1)} %fusion.1), channel_id=2, replica_groups=mesh['x'=4,'core'=2,'zh'=8,'zl'=2,'tp'=4] {'zh'}, dimensions={0}, use_global_device_ids=true | all-gather | bytes 663552 | tf_op jit(solution)/shard_map/all_gather | solution.py:296
  40.0 3.3 %collective-permute-start.3 = (bf16[4,32,1152]{2,1,0:T(8,128)(2,1)}, bf16[4,32,1152]{2,1,0:T(8,128)(2,1)S(1)}, u32[]{:S(2)}, u32[]{:S(2)}) collective-permute-start(bf16[4,32,1152]{2,1,0:T(8,128)(2,1)} %bitcast.8), channel_id=1, source_target_pairs={{0,4},{4,8},{8,12},{12,16},{16,20},{20,24},{24,28},{28,32},{32,36}... | collective-permute-start | bytes 884744 | tf_op jit(solution)/shard_map/ppermute | solution.py:270
  43.4 3.7 %collective-permute-start.4 = (bf16[4,32,1152]{2,1,0:T(8,128)(2,1)S(1)}, bf16[4,32,1152]{2,1,0:T(8,128)(2,1)S(1)}, u32[]{:S(2)}, u32[]{:S(2)}) collective-permute-start(bf16[4,32,1152]{2,1,0:T(8,128)(2,1)S(1)} %bitcast.36), channel_id=1, source_target_pairs={{0,60},{4,0},{8,4},{12,8},{16,12},{20,16},{24,20},{28,24},{32,28},... | collective-permute-start | bytes 884744 | tf_op jit(solution)/shard_map/ppermute | solution.py:270
  47.1 4.7 %collective-permute-start.2 = (bf16[256,1024]{1,0:T(8,128)(2,1)S(1)}, bf16[256,1024]{1,0:T(8,128)(2,1)}, u32[]{:S(2)}, u32[]{:S(2)}) collective-permute-start(bf16[256,1024]{1,0:T(8,128)(2,1)S(1)} %bitcast.24), channel_id=1, source_target_pairs={{0,384},{128,0},{256,128},{384,256},{1,385},{129,1},{257,129},{385... | collective-permute-start | bytes 1572872 | tf_op jit(solution)/shard_map/ppermute | solution.py:270
  51.8 1.9 collective-permute-start.1
  53.8 4.8 %shard_map.37 = (bf16[4,256,512]{2,1,0:T(8,128)(2,1)}, bf16[4,256,512]{2,1,0:T(8,128)(2,1)}) custom-call(s32[1]{0:T(128)} %bitcast.1.core_ref, s32[1]{0:T(128)} %bitcast.2.parity_ref, bf16[256,4096]{1,0:T(8,128)(2,1)} %bitcast.35), custom_call_target="tpu_custom_call" | custom-call | tf_op jit(solution)/shard_map/pallas_call | solution.py:125
  58.6 2.0 collective-permute-start
  60.8 5.1 %collective-permute-start.6 = (bf16[256,1024]{1,0:T(8,128)(2,1)S(1)}, bf16[256,1024]{1,0:T(8,128)(2,1)S(1)}, u32[]{:S(2)}, u32[]{:S(2)}) collective-permute-start(bf16[256,1024]{1,0:T(8,128)(2,1)S(1)} %bitcast.27), channel_id=1, source_target_pairs={{0,384},{128,0},{256,128},{384,256},{1,385},{129,1},{257,129},{385... | collective-permute-start | bytes 1572872 | tf_op jit(solution)/shard_map/ppermute | solution.py:270
  65.9 1.9 collective-permute-start.5
  69.5 5.1 %collective-permute-start.8 = (bf16[128,1024]{1,0:T(8,128)(2,1)}, bf16[128,1024]{1,0:T(8,128)(2,1)S(1)}, u32[]{:S(2)}, u32[]{:S(2)}) collective-permute-start(bf16[128,1024]{1,0:T(8,128)(2,1)} %slice.47), channel_id=1, source_target_pairs={{0,384},{128,0},{256,128},{384,256},{1,385},{129,1},{257,129},{385... | collective-permute-start | bytes 786440 | tf_op jit(solution)/shard_map/ppermute | solution.py:270
  76.3 1.9 collective-permute-start.7
  79.0 5.5 %collective-permute-start.10 = (bf16[128,1024]{1,0:T(8,128)(2,1)}, bf16[128,1024]{1,0:T(8,128)(2,1)}, u32[]{:S(2)}, u32[]{:S(2)}) collective-permute-start(bf16[128,1024]{1,0:T(8,128)(2,1)} %slice.49), channel_id=1, source_target_pairs={{0,384},{128,0},{256,128},{384,256},{1,385},{129,1},{257,129},{385... | collective-permute-start | bytes 786440 | tf_op jit(solution)/shard_map/ppermute | solution.py:270
  85.5 1.9 collective-permute-start.9
  87.4 2.3 %shard_map.38.refs_0_ = f32[2,256,1024]{2,1,0:T(8,128)S(1)} custom-call(s32[1]{0:T(128)} %bitcast.x_ref, bf16[4,256,512]{2,1,0:T(8,128)(2,1)S(1)} %copy-done.2, bf16[4,256,512]{2,1,0:T(8,128)(2,1)S(1)} %collective-permute-done.refs_1_.refs_2_.other_ref, bf16[256,1024]{1,0:T(8,128)(2,1)S(1)} %bitcast.26, bf16[256,1024]{1,0:T(8,128)(2,1)} %collective-permute-done.1.refs_3_, ...), custom_call_target="tpu_custom_call" | custom-call | tf_op jit(solution)/shard_map/pallas_call | solution.py:160
  91.0 2.6 %shard_map.39.total_ref = f32[2,256,1024]{2,1,0:T(8,128)S(1)} custom-call(s32[1]{0:T(128)} %bitcast.x_ref, f32[2,256,1024]{2,1,0:T(8,128)} %copy-done.3, bf16[4,256,512]{2,1,0:T(8,128)(2,1)S(1)} %copy-done.2, bf16[4,256,512]{2,1,0:T(8,128)(2,1)S(1)} %collective-permute-done.refs_1_.refs_2_.other_ref, bf16[256,1024]{1,0:T(8,128)(2,1)S(1)} %bitcast.29, ...), custom_call_target="tpu_custom_call" | custom-call | tf_op jit(solution)/shard_map/pallas_call | solution.py:160
  96.1 3.8 %shard_map.40 = (f32[256,1024]{1,0:T(8,128)S(1)}, bf16[256,1024]{1,0:T(8,128)(2,1)}) custom-call(s32[1]{0:T(128)} %bitcast.x_ref, f32[2,256,1024]{2,1,0:T(8,128)} %copy-done.4, bf16[4,256,512]{2,1,0:T(8,128)(2,1)S(1)} %copy-done.2, bf16[4,256,512]{2,1,0:T(8,128)(2,1)S(1)} %collective-permute-done.refs_1_.refs_2_.other_ref, ...), custom_call_target="tpu_custom_call" | custom-call | tf_op jit(solution)/shard_map/pallas_call | solution.py:185
  99.9 1.9 collective-permute-start.11
  105.6 7.2 %all-to-all-start = ((bf16[16,128,256]{2,1,0:T(8,128)(2,1)}), bf16[16,128,256]{2,1,0:T(8,128)(2,1)S(1)}, u32[]{:S(2)}, u32[]{:S(2)}) async-start(bf16[16,128,256]{2,1,0:T(8,128)(2,1)} %shard_map.42), calls=%async_computation | async-start | bytes 2097152 | tf_op jit(solution)/shard_map/all_to_all | solution.py:325
  113.6 2.0 shard_map.43.mask_ref
  115.7 1.9 copy-done
  117.6 45.4 %all-to-all-done.block_ref = bf16[16,128,256]{2,1,0:T(8,128)(2,1)S(1)} async-done(((bf16[16,128,256]{2,1,0:T(8,128)(2,1)}), bf16[16,128,256]{2,1,0:T(8,128)(2,1)S(1)}, u32[]{:S(2)}, u32[]{:S(2)}) %all-to-all-start) | async-done | bytes 1048608 | tf_op jit(solution)/shard_map/all_to_all | solution.py:325
  163.0 2.2 %copy-done.1 = f32[4,512,512]{2,1,0:T(8,128)S(1)} copy-done((f32[4,512,512]{2,1,0:T(8,128)S(1)}, f32[4,512,512]{2,1,0:T(8,128)}, u32[]{:S(2)}) %copy-start.1) | copy-done | bytes 4194328
  165.2 2.1 %shard_map.44 = bf16[16,128,128]{2,1,0:T(8,128)(2,1)S(1)} custom-call(bf16[16,128,256]{2,1,0:T(8,128)(2,1)S(1)} %all-to-all-done.block_ref, f32[4,512,512]{2,1,0:T(8,128)S(1)} %copy-done.1), custom_call_target="tpu_custom_call" | custom-call | tf_op jit(solution)/shard_map/pallas_call | solution.py:242
  167.3 36.9 %all_to_all.10.block_ref = bf16[16,128,128]{2,1,0:T(8,128)(2,1)S(1)} all-to-all(bf16[16,128,128]{2,1,0:T(8,128)(2,1)S(1)} %shard_map.44), channel_id=1, replica_groups=mesh['x'=4,'core'=2,'zh'=8,'zl'=2,'tp'=4] {'zh','zl'}, dimensions={0} | all-to-all | bytes 1048576 | tf_op jit(solution)/shard_map/all_to_all | solution.py:333
  (53 shorter events, 17.2 us)
Async XLA Ops:
  39.2 7.9 %copy-start.10 = (bf16[256,1152]{1,0:T(8,128)(2,1)}, bf16[256,1152]{1,0:T(8,128)(2,1)S(1)}, u32[]{:S(2)}) copy-start(bf16[256,1152]{1,0:T(8,128)(2,1)S(1)} %all-gather) | copy-start | bytes 1769476
  40.0 20.6 %collective-permute-start.3 = (bf16[4,32,1152]{2,1,0:T(8,128)(2,1)}, bf16[4,32,1152]{2,1,0:T(8,128)(2,1)S(1)}, u32[]{:S(2)}, u32[]{:S(2)}) collective-permute-start(bf16[4,32,1152]{2,1,0:T(8,128)(2,1)} %bitcast.8), channel_id=1, source_target_pairs={{0,4},{4,8},{8,12},{12,16},{16,20},{20,24},{24,28},{28,32},{32,36}... | collective-permute-start | bytes 884744 | tf_op jit(solution)/shard_map/ppermute | solution.py:270
  43.4 17.3 %collective-permute-start.4 = (bf16[4,32,1152]{2,1,0:T(8,128)(2,1)S(1)}, bf16[4,32,1152]{2,1,0:T(8,128)(2,1)S(1)}, u32[]{:S(2)}, u32[]{:S(2)}) collective-permute-start(bf16[4,32,1152]{2,1,0:T(8,128)(2,1)S(1)} %bitcast.36), channel_id=1, source_target_pairs={{0,60},{4,0},{8,4},{12,8},{16,12},{20,16},{24,20},{28,24},{32,28},... | collective-permute-start | bytes 884744 | tf_op jit(solution)/shard_map/ppermute | solution.py:270
  47.1 20.7 %collective-permute-start.2 = (bf16[256,1024]{1,0:T(8,128)(2,1)S(1)}, bf16[256,1024]{1,0:T(8,128)(2,1)}, u32[]{:S(2)}, u32[]{:S(2)}) collective-permute-start(bf16[256,1024]{1,0:T(8,128)(2,1)S(1)} %bitcast.24), channel_id=1, source_target_pairs={{0,384},{128,0},{256,128},{384,256},{1,385},{129,1},{257,129},{385... | collective-permute-start | bytes 1572872 | tf_op jit(solution)/shard_map/ppermute | solution.py:270
  51.8 22.8 %collective-permute-start.1 = (bf16[256,1024]{1,0:T(8,128)(2,1)S(1)}, bf16[256,1024]{1,0:T(8,128)(2,1)}, u32[]{:S(2)}, u32[]{:S(2)}) collective-permute-start(bf16[256,1024]{1,0:T(8,128)(2,1)S(1)} %bitcast.25), channel_id=1, source_target_pairs={{0,128},{128,256},{256,384},{384,0},{1,129},{129,257},{257,385},{3... | collective-permute-start | bytes 1572872 | tf_op jit(solution)/shard_map/ppermute | solution.py:270
  58.6 28.8 %copy-start.2 = (bf16[4,256,512]{2,1,0:T(8,128)(2,1)S(1)}, bf16[4,256,512]{2,1,0:T(8,128)(2,1)}, u32[]{:S(2)}) copy-start(bf16[4,256,512]{2,1,0:T(8,128)(2,1)} %get-tuple-element.11.refs_0_.refs_1_.own_ref) | copy-start | bytes 3145732
  58.6 28.8 %collective-permute-start = (bf16[4,256,512]{2,1,0:T(8,128)(2,1)}, bf16[4,256,512]{2,1,0:T(8,128)(2,1)S(1)}, u32[]{:S(2)}, u32[]{:S(2)}) collective-permute-start(bf16[4,256,512]{2,1,0:T(8,128)(2,1)} %get-tuple-element.12), channel_id=1, source_target_pairs={{0,64},{64,0},{1,65},{65,1},{2,66},{66,2},{3,67},{67,3},{4,68},{68... | collective-permute-start | bytes 3145736 | tf_op jit(solution)/shard_map/ppermute | solution.py:301
  60.7 24.6 %copy-start.11 = (bf16[8,32,1152]{2,1,0:T(8,128)(2,1)}, bf16[8,32,1152]{2,1,0:T(8,128)(2,1)S(1)}, u32[]{:S(2)}) copy-start(bf16[8,32,1152]{2,1,0:T(8,128)(2,1)S(1)} %constant_dynamic-update-slice_fusion) | copy-start | bytes 1769476
  60.8 17.5 %collective-permute-start.6 = (bf16[256,1024]{1,0:T(8,128)(2,1)S(1)}, bf16[256,1024]{1,0:T(8,128)(2,1)S(1)}, u32[]{:S(2)}, u32[]{:S(2)}) collective-permute-start(bf16[256,1024]{1,0:T(8,128)(2,1)S(1)} %bitcast.27), channel_id=1, source_target_pairs={{0,384},{128,0},{256,128},{384,256},{1,385},{129,1},{257,129},{385... | collective-permute-start | bytes 1572872 | tf_op jit(solution)/shard_map/ppermute | solution.py:270
  65.9 18.6 %collective-permute-start.5 = (bf16[256,1024]{1,0:T(8,128)(2,1)S(1)}, bf16[256,1024]{1,0:T(8,128)(2,1)S(1)}, u32[]{:S(2)}, u32[]{:S(2)}) collective-permute-start(bf16[256,1024]{1,0:T(8,128)(2,1)S(1)} %bitcast.28), channel_id=1, source_target_pairs={{0,128},{128,256},{256,384},{384,0},{1,129},{129,257},{257,385},{3... | collective-permute-start | bytes 1572872 | tf_op jit(solution)/shard_map/ppermute | solution.py:270
  69.5 25.4 %collective-permute-start.8 = (bf16[128,1024]{1,0:T(8,128)(2,1)}, bf16[128,1024]{1,0:T(8,128)(2,1)S(1)}, u32[]{:S(2)}, u32[]{:S(2)}) collective-permute-start(bf16[128,1024]{1,0:T(8,128)(2,1)} %slice.47), channel_id=1, source_target_pairs={{0,384},{128,0},{256,128},{384,256},{1,385},{129,1},{257,129},{385... | collective-permute-start | bytes 786440 | tf_op jit(solution)/shard_map/ppermute | solution.py:270
  76.3 18.6 %collective-permute-start.7 = (bf16[128,1024]{1,0:T(8,128)(2,1)}, bf16[128,1024]{1,0:T(8,128)(2,1)}, u32[]{:S(2)}, u32[]{:S(2)}) collective-permute-start(bf16[128,1024]{1,0:T(8,128)(2,1)} %slice.46), channel_id=1, source_target_pairs={{0,128},{128,256},{256,384},{384,0},{1,129},{129,257},{257,385},{3... | collective-permute-start | bytes 786440 | tf_op jit(solution)/shard_map/ppermute | solution.py:270
  78.3 6.3 %copy-start.5 = (bf16[256,1024]{1,0:T(8,128)(2,1)}, bf16[256,1024]{1,0:T(8,128)(2,1)S(1)}, u32[]{:S(2)}) copy-start(bf16[256,1024]{1,0:T(8,128)(2,1)S(1)} %collective-permute-done.6.refs_5_) | copy-start | bytes 1572868
  79.0 15.9 %collective-permute-start.10 = (bf16[128,1024]{1,0:T(8,128)(2,1)}, bf16[128,1024]{1,0:T(8,128)(2,1)}, u32[]{:S(2)}, u32[]{:S(2)}) collective-permute-start(bf16[128,1024]{1,0:T(8,128)(2,1)} %slice.49), channel_id=1, source_target_pairs={{0,384},{128,0},{256,128},{384,256},{1,385},{129,1},{257,129},{385... | collective-permute-start | bytes 786440 | tf_op jit(solution)/shard_map/ppermute | solution.py:270
  85.5 10.7 %collective-permute-start.9 = (bf16[128,1024]{1,0:T(8,128)(2,1)}, bf16[128,1024]{1,0:T(8,128)(2,1)}, u32[]{:S(2)}, u32[]{:S(2)}) collective-permute-start(bf16[128,1024]{1,0:T(8,128)(2,1)} %slice.48), channel_id=1, source_target_pairs={{0,128},{128,256},{256,384},{384,0},{1,129},{129,257},{257,385},{3... | collective-permute-start | bytes 786440 | tf_op jit(solution)/shard_map/ppermute | solution.py:270
  87.4 3.6 %copy-start.6 = (bf16[256,1024]{1,0:T(8,128)(2,1)S(1)}, bf16[256,1024]{1,0:T(8,128)(2,1)}, u32[]{:S(2)}) copy-start(bf16[256,1024]{1,0:T(8,128)(2,1)} %copy-done.5) | copy-start | bytes 1572868
  87.4 3.6 %copy-start.8 = (bf16[256,1024]{1,0:T(8,128)(2,1)S(1)}, bf16[256,1024]{1,0:T(8,128)(2,1)}, u32[]{:S(2)}) copy-start(bf16[256,1024]{1,0:T(8,128)(2,1)} %copy-done.7) | copy-start | bytes 1572868
  89.7 1.4 copy-start.3
  93.6 1.4 copy-start.4
  95.0 6.8 %copy-start.9 = (s32[1,256,4]{1,2,0:T(4,128)S(1)}, s32[1,256,4]{1,2,0:T(4,128)}, u32[]{:S(2)}) copy-start(s32[1,256,4]{1,2,0:T(4,128)} %param.5) | copy-start | bytes 12292
  99.9 4.0 %collective-permute-start.11 = (bf16[256,1024]{1,0:T(8,128)(2,1)}, bf16[256,1024]{1,0:T(8,128)(2,1)S(1)}, u32[]{:S(2)}, u32[]{:S(2)}) collective-permute-start(bf16[256,1024]{1,0:T(8,128)(2,1)} %get-tuple-element.14), channel_id=1, source_target_pairs={{0,64},{64,0},{1,65},{65,1},{2,66},{66,2},{3,67},{67,3},{4,68},{68... | collective-permute-start | bytes 1572872 | tf_op jit(solution)/shard_map/ppermute | solution.py:321
  105.6 57.4 %all-to-all-start = ((bf16[16,128,256]{2,1,0:T(8,128)(2,1)}), bf16[16,128,256]{2,1,0:T(8,128)(2,1)S(1)}, u32[]{:S(2)}, u32[]{:S(2)}) async-start(bf16[16,128,256]{2,1,0:T(8,128)(2,1)} %shard_map.42), calls=%async_computation | async-start | bytes 2097152 | tf_op jit(solution)/shard_map/all_to_all | solution.py:325
  115.7 2.0 copy-start
  163.0 2.2 %copy-start.1 = (f32[4,512,512]{2,1,0:T(8,128)S(1)}, f32[4,512,512]{2,1,0:T(8,128)}, u32[]{:S(2)}) copy-start(f32[4,512,512]{2,1,0:T(8,128)} %copy-done) | copy-start | bytes 12582916
  (1 other events, 0.9 us)

commit v6 on v4

v6 whole, which is shorter than its diff:
```python
import jax
import jax.numpy as jnp
from jax import lax
from jax.experimental import pallas as pl
from jax.experimental.pallas import tpu as pltpu
from jax.sharding import PartitionSpec as P

CLUSTERS = 64
BF16 = jnp.bfloat16
F32 = jnp.float32
VMEM_LIMIT = 48 * 1024 * 1024


def vmem_call(kernel, out_shape, in_smem, **kwargs):
    vmem = pl.BlockSpec(memory_space=pltpu.VMEM)
    smem = pl.BlockSpec(memory_space=pltpu.SMEM)
    return pl.pallas_call(
        kernel,
        out_shape=out_shape,
        in_specs=[smem if flag else vmem for flag in in_smem],
        out_specs=jax.tree.map(lambda _: vmem, out_shape),
        compiler_params=pltpu.CompilerParams(vmem_limit_bytes=VMEM_LIMIT),
        **kwargs,
    )


def scalar(value):
    return jnp.reshape(value, (1,)).astype(jnp.int32)


def iota(shape, dim):
    return lax.broadcasted_iota(jnp.int32, shape, dim)


def routing(ids, owners, capacity):
    rows, heads = ids.shape
    per_owner = CLUSTERS // owners

    def kernel(ids_ref, ids_t_ref, slot_row_ref, slot_col_ref):
        before_col = (iota((rows, rows), 1) < iota((rows, rows), 0)).astype(BF16)
        before_row = (iota((rows, rows), 0) < iota((rows, rows), 1)).astype(BF16)
        for h in range(heads):
            owner_col = ids_ref[:, h : h + 1] // per_owner
            hot = owner_col == iota((rows, owners), 1)
            count = jnp.dot(before_col, hot.astype(BF16), preferred_element_type=F32)
            rank = jnp.sum(jnp.where(hot, count, 0.0), axis=1, keepdims=True)
            slot_col_ref[:, h : h + 1] = owner_col * capacity + rank.astype(jnp.int32)
            owner_row = ids_t_ref[h : h + 1, :] // per_owner
            hot = owner_row == iota((owners, rows), 0)
            count = jnp.dot(hot.astype(BF16), before_row, preferred_element_type=F32)
            rank = jnp.sum(jnp.where(hot, count, 0.0), axis=0, keepdims=True)
            slot_row_ref[h : h + 1, :] = owner_row * capacity + rank.astype(jnp.int32)

    return vmem_call(
        kernel,
        (
            jax.ShapeDtypeStruct((heads, rows), jnp.int32),
            jax.ShapeDtypeStruct((rows, heads), jnp.int32),
        ),
        (False, False),
    )(ids, ids.T)


def owned_mask(all_ids, me, chosen, capacity):
    sources, id_rows, lanes = all_ids.shape
    per_head = 2 * sources * capacity // 4 // lanes
    rows = per_head * lanes
    per_owner = CLUSTERS // sources
    slots = sources * capacity

    def kernel(me_ref, ids_ref, out_ref):
        before = (iota((rows, rows), 0) < iota((rows, rows), 1)).astype(BF16)
        place = iota((sources, capacity, rows), 1)
        kinds = iota((slots, 128), 1) + 1
        query = iota((slots, slots), 0)
        key = iota((slots, slots), 1)
        outside = jnp.where(query == key, -100000.0, 0.0)
        for i, h in enumerate(chosen):
            ids = jnp.concatenate(
                [ids_ref[:, h * per_head + j, :] for j in range(per_head)], axis=1
            )
            ids = ids.astype(F32).astype(jnp.int32)
            owner = ids // per_owner
            mine = owner == me_ref[0]
            rank = jnp.dot(mine.astype(BF16), before, preferred_element_type=F32)
            rank = jnp.where(mine, rank.astype(jnp.int32), -1)
            tag = ids - owner * per_owner + 1
            placed = jnp.where(rank[:, None, :] == place, tag[:, None, :], 0)
            tag = jnp.sum(placed.reshape(slots, rows), axis=1, keepdims=True)
            member = (tag == kinds).astype(BF16)
            same = lax.dot_general(
                member, member, (((1,), (1,)), ((), ())), preferred_element_type=F32
            )
            out_ref[i] = jnp.where((same > 0.5) & (key <= query), outside, -1e30)

    return vmem_call(kernel, jax.ShapeDtypeStruct((len(chosen), slots, slots), F32), (True, False))(
        scalar(me), all_ids
    )


def cut_tokens(local_rows, core, chips):
    rows, depth = local_rows.shape
    half = depth // chips // 2

    def kernel(core_ref, in_ref, out_ref, sems):
        copies = []
        for p in range(chips):
            for j in range(2):
                first = (2 * p + lax.rem(core_ref[0] + j, 2)) * half
                copies.append(
                    pltpu.make_async_copy(
                        in_ref.at[:, pl.ds(pl.multiple_of(first, half), half)],
                        out_ref.at[p, :, j * half : (j + 1) * half],
                        sems.at[2 * p + j],
                    )
                )
        for copy in copies:
            copy.start()
        for copy in copies:
            copy.wait()

    return pl.pallas_call(
        kernel,
        out_shape=jax.ShapeDtypeStruct((chips, rows, 2 * half), BF16),
        in_specs=[
            pl.BlockSpec(memory_space=pltpu.SMEM),
            pl.BlockSpec(memory_space=pl.ANY),
        ],
        out_specs=pl.BlockSpec(memory_space=pltpu.VMEM),
        scratch_shapes=[pltpu.SemaphoreType.DMA((2 * chips,))],
        compiler_params=pltpu.CompilerParams(vmem_limit_bytes=VMEM_LIMIT),
    )(scalar(core), local_rows)


def project(pieces, ring, other, x, steps, first, width):
    chips, rows, depth = pieces.shape
    half = ring.shape[0]
    cols = slice(first, first + width)

    def kernel(x_ref, pieces_ref, ring_ref, other_ref, *out_refs):
        for step, out_ref in zip(steps, out_refs):
            p = lax.rem(x_ref[0] + step + chips, chips)
            total = jnp.dot(
                pieces_ref[p, :, :half], ring_ref[:, cols], preferred_element_type=F32
            ) + jnp.dot(pieces_ref[p, :, half:], other_ref[:, cols], preferred_element_type=F32)
            out_ref[...] = total.astype(BF16)

    return vmem_call(
        kernel,
        (jax.ShapeDtypeStruct((rows, width), BF16),) * len(steps),
        (True, False, False, False),
    )(scalar(x), pieces, ring, other)


def add(partials):
    def kernel(*refs):
        total = refs[0][...].astype(F32)
        for ref in refs[1:-1]:
            total += ref[...].astype(F32)
        refs[-1][...] = total.astype(BF16)

    return vmem_call(
        kernel, jax.ShapeDtypeStruct(partials[0].shape, BF16), (False,) * len(partials)
    )(*partials)


def pack(partials, slot_row, chosen, owners, capacity, head_dim):
    rows, width = partials[0].shape
    heads = len(chosen)
    slots = owners * capacity

    def kernel(*refs):
        slot_ref, out_ref = refs[-2:]
        for i, h in enumerate(chosen):
            place = iota((slots, rows), 0) == slot_ref[h : h + 1, :]
            place = place.astype(BF16)
            for m in range(2):
                cols = slice((m * heads + i) * head_dim, (m * heads + i + 1) * head_dim)
                total = refs[0][:, cols].astype(F32)
                for ref in refs[1:-2]:
                    total += ref[:, cols].astype(F32)
                packed = jnp.dot(
                    place, total.astype(BF16), preferred_element_type=F32
                ).astype(BF16)
                out_ref[
                    :, i * capacity : (i + 1) * capacity, m * head_dim : (m + 1) * head_dim
                ] = packed.reshape(owners, capacity, head_dim)

    return vmem_call(
        kernel,
        jax.ShapeDtypeStruct((owners, heads * capacity, 2 * head_dim), BF16),
        (False,) * (len(partials) + 1),
    )(*partials, slot_row)


def attend(blocks, mask, capacity):
    sources, rows, width = blocks.shape
    head_dim = width // 2
    heads = rows // capacity
    slots = sources * capacity
    scale = head_dim ** (-0.5)

    def kernel(block_ref, mask_ref, out_ref):
        for h in range(heads):
            here = slice(h * capacity, (h + 1) * capacity)
            keys = block_ref[:, here, :head_dim].reshape(slots, head_dim)
            values = block_ref[:, here, head_dim:].reshape(slots, head_dim)
            scores = lax.dot_general(
                keys, keys, (((1,), (1,)), ((), ())), preferred_element_type=F32
            )
            mask = mask_ref[h]
            scores = jnp.where(mask == 0.0, scores * scale, mask)
            row_max = jnp.max(scores, axis=1, keepdims=True)
            weights = jnp.exp(scores - row_max)
            total = jnp.sum(weights, axis=1, keepdims=True)
            probabilities = (weights / total).astype(BF16)
            result = jnp.dot(probabilities, values, preferred_element_type=F32).astype(BF16)
            out_ref[:, here, :] = result.reshape(sources, capacity, head_dim)

    return vmem_call(
        kernel, jax.ShapeDtypeStruct((sources, rows, head_dim), BF16), (False, False)
    )(blocks, mask)


def attend_all(gathered, own, all_ids, ids, me, chosen):
    devices, rows, width = gathered.shape
    heads = len(chosen)
    head_dim = width // 2 // heads
    lanes = all_ids.shape[2]
    per_head = rows // lanes
    scale = head_dim ** (-0.5)

    def kernel(me_ref, gathered_ref, own_ref, all_ids_ref, ids_ref, out_ref, score_ref):
        ahead = iota((rows, rows), 1) - iota((rows, rows), 0)
        for i, h in enumerate(chosen):
            cols = slice(i * head_dim, (i + 1) * head_dim)
            values = slice((heads + i) * head_dim, (heads + i + 1) * head_dim)
            queries = own_ref[:, cols]
            query_ids = ids_ref[:, h : h + 1].astype(F32)
            row_max = jnp.full((rows, 1), -jnp.inf, F32)
            for z in range(devices):
                key_ids = jnp.concatenate(
                    [all_ids_ref[z, h * per_head + j : h * per_head + j + 1, :] for j in range(per_head)],
                    axis=1,
                ).astype(F32)
                scores = lax.dot_general(
                    queries,
                    gathered_ref[z, :, cols],
                    (((1,), (1,)), ((), ())),
                    preferred_element_type=F32,
                )
                offset = (me_ref[0] - z) * rows
                scores = jnp.where(ahead == offset, -100000.0, scores * scale)
                scores = jnp.where((query_ids == key_ids) & (ahead <= offset), scores, -1e30)
                score_ref[:, z * rows : (z + 1) * rows] = scores
                row_max = jnp.maximum(row_max, jnp.max(scores, axis=1, keepdims=True))
            total = jnp.zeros((rows, 1), F32)
            for z in range(devices):
                part = jnp.exp(score_ref[:, z * rows : (z + 1) * rows] - row_max)
                score_ref[:, z * rows : (z + 1) * rows] = part
                total += jnp.sum(part, axis=1, keepdims=True)
            inverse = 1.0 / total
            result = jnp.zeros((rows, head_dim), F32)
            for z in range(devices):
                part = (score_ref[:, z * rows : (z + 1) * rows] * inverse).astype(BF16)
                result += jnp.dot(
                    part, gathered_ref[z, :, values], preferred_element_type=F32
                )
            out_ref[:, cols] = result.astype(BF16)

    return vmem_call(
        kernel,
        jax.ShapeDtypeStruct((rows, heads * head_dim), BF16),
        (True,) + (False,) * 4,
        scratch_shapes=[pltpu.VMEM((rows, devices * rows), F32)],
    )(scalar(me), gathered, own, all_ids, ids)


def unpack(dense, returned, slot_col, chosen, capacity):
    owners, height, head_dim = returned.shape
    rows, width = dense.shape
    slots = owners * capacity

    def kernel(dense_ref, block_ref, slot_ref, out_ref):
        out_ref[:, :width] = dense_ref[...]
        for i, h in enumerate(chosen):
            block = block_ref[:, i * capacity : (i + 1) * capacity, :].reshape(slots, head_dim)
            place = slot_ref[:, h : h + 1] == iota((rows, slots), 1)
            out_ref[:, h * head_dim : (h + 1) * head_dim] = jnp.dot(
                place.astype(BF16), block, preferred_element_type=F32
            ).astype(BF16)

    return vmem_call(
        kernel,
        jax.ShapeDtypeStruct((rows, width + len(chosen) * head_dim), BF16),
        (False,) * 3,
    )(dense, returned, slot_col)


def shifted(block, step, axis):
    size = lax.axis_size(axis)
    return lax.ppermute(block, axis, [(i, (i + step) % size) for i in range(size)])


def gather_z(own):
    from_minus4 = shifted(own, 4, "clu")
    from_plus4 = shifted(own, -4, "clu")
    from_8 = shifted(own, 8, "clu")
    four = jnp.stack([own, from_plus4, from_8, from_minus4])
    minus2 = shifted(jnp.stack([own, from_minus4]), 2, "clu")
    plus2 = shifted(jnp.stack([own, from_plus4]), -2, "clu")
    from_minus1 = shifted(four, 1, "clu")
    from_plus1 = shifted(four, -1, "clu")
    order = jnp.stack(
        [
            four,
            from_plus1,
            jnp.stack([plus2[0], plus2[1], minus2[1], minus2[0]]),
            jnp.concatenate([from_minus1[1:], from_minus1[:1]]),
        ],
        axis=1,
    )
    return order.reshape((lax.axis_size("clu"),) + own.shape)


def body(tokens, proj_weight, clusters):
    rows, depth = tokens.shape[1:]
    owners = lax.axis_size("clu")
    me = lax.axis_index("clu")
    x = lax.axis_index("x")
    heads = clusters.shape[2]
    shard = proj_weight.shape[0]
    width = 2 * proj_weight.shape[2]
    head_dim = proj_weight.shape[2] // heads
    capacity = 2 * rows // owners
    chips = lax.axis_size("x")
    dense = tuple(range(heads // 2))
    routed = tuple(range(heads // 2, heads))

    pieces = cut_tokens(tokens[0], lax.axis_index("core"), chips)
    pieces = lax.all_to_all(pieces, "x", split_axis=0, concat_axis=0, tiled=True)

    own = proj_weight.reshape(shard, 2, 2, width // 4).transpose(0, 2, 1, 3)
    ids = clusters[0].T.astype(BF16).reshape(-1, 128)
    ids = jnp.pad(ids, ((0, shard - ids.shape[0]), (0, 0)))
    own = jnp.concatenate([own.reshape(shard, width), ids], axis=1)
    blocks = gather_z(own)
    ring = jnp.roll(blocks[:, :, :width], me, axis=0).reshape(owners * shard, width)
    all_ids = jnp.roll(blocks[:, :16, width:], me, axis=0)
    other = lax.ppermute(ring, "core", [(0, 1), (1, 0)])

    slot_row, slot_col = routing(clusters[0], owners, capacity)
    steps = (2, 1, -1, 0)
    partials = []
    for g in range(2):
        sent = project(pieces, ring, other, x, steps, g * width // 2, width // 2)
        partials.append(
            [part if s == 0 else shifted(part, s, "x") for part, s in zip(sent, steps)]
        )

    here = add(partials[0])
    gathered = lax.all_gather(here, "clu", axis=0)
    outgoing = pack(partials[1], slot_row, routed, owners, capacity, head_dim)
    incoming = lax.all_to_all(outgoing, "clu", split_axis=0, concat_axis=0, tiled=True)
    mask = owned_mask(all_ids, me, routed, capacity)
    replies = attend(incoming, mask, capacity)
    returned = lax.all_to_all(replies, "clu", split_axis=0, concat_axis=0, tiled=True)
    attended = attend_all(gathered, here, all_ids, clusters[0], me, dense)
    return unpack(attended, returned, slot_col, routed, capacity)[None]


def solution(mesh):
    ctx, clu, tp = (mesh.shape[name] for name in mesh.axis_names)
    fine = jax.sharding.Mesh(
        mesh.devices.reshape(ctx // 2, 2, clu, tp), ("x", "core", "clu", "tp")
    )
    ctx_axes = ("x", "core")
    return jax.shard_map(
        body,
        mesh=fine,
        in_specs=(
            P(ctx_axes, "clu", None),
            P(ctx_axes + ("clu",), None, "tp"),
            P(ctx_axes, "clu", "tp"),
        ),
        out_specs=P(ctx_axes, "clu", "tp"),
        check_vma=False,
    )
```

time: 329 us -> 214 us (0.65)
  Pallas kernels: 111 us -> 19.2 us
  blocking collectives: 71 us -> 0 us
  starting transfers between devices: 55.5 us -> 84.1 us
  between operations: 0.3 us -> 13.8 us
  waiting for transfers between devices: 78.4 us -> 84 us
    pallas_call x5 -> x7, Pallas kernels: 107 us -> 15.3 us  [the longest x1 6.5 us: attend_all(): vmem_call(kernel, jax.ShapeDtypeStruct((rows, heads * head_dim), BF16), (...]
    all_to_all x2 -> x0, blocking collectives: 71 us -> none  [the longest x1 36.8 us: body(): lax.all_to_all(replies, CLU, split_axis=0, concat_axis=0, tiled=True)]
    all_gather x0 -> x1, waiting for transfers between devices: none -> 33.6 us  [body(): gathered = lax.all_gather(here, 'clu', axis=0)]
    ppermute x13, waiting for transfers between devices: 33.2 us -> 15.6 us  [shifted(): lax.ppermute(block, axis, [(i, (i + step) % size) for i in range(size)])]
    ppermute x13, starting transfers between devices: 48.9 us -> 63.4 us  [shifted(): lax.ppermute(block, axis, [(i, (i + step) % size) for i in range(size)])]
    all_to_all x1 -> x3, starting transfers between devices: 4.67 us -> 18.8 us  [the longest x1 7.62 us: body(): lax.all_to_all(outgoing, 'clu', split_axis=0, concat_axis=0, tiled=True)]
    all_to_all x1 -> x3, waiting for transfers between devices: 45.1 us -> 32 us  [the longest x1 32 us: body(): lax.all_to_all(outgoing, 'clu', split_axis=0, concat_axis=0, tiled=True)]
    unnamed x24 -> x8, local copies, waits for them, and re-layouts: 8.24 us -> 5.13 us
  transfers between devices with their start and end apart: 15 -> 18, of which waited for: 9 -> 9; matrix products, arithmetic and copies ran while one was open for 0% -> 2% of each run, Pallas kernels for 21% -> 7%
where the time goes in v6:
time: 214 us; the launch traced here: 212 us
  starting transfers between devices  84.1 us (39%)
  waiting for transfers between devices  84 us (39%)
  Pallas kernels  19.2 us (9%)
  between operations  13.8 us (6%)
  local copies, waits for them, and re-layouts  8.46 us (4%)
  other arithmetic  2.62 us (1%)
    ppermute x13, starting transfers between devices, shifted(): lax.ppermute(block, axis, [(i, (i + step) % size) for i in range(size)])  63.4 us
    all_gather x1, waiting for transfers between devices, body(): gathered = lax.all_gather(here, 'clu', axis=0)  33.6 us
    all_to_all x1, waiting for transfers between devices, body(): lax.all_to_all(outgoing, 'clu', split_axis=0, concat_axis=0, tiled=True)  32 us
    ppermute x13, waiting for transfers between devices, shifted(): lax.ppermute(block, axis, [(i, (i + step) % size) for i in range(size)])  15.6 us
    all_to_all x1, starting transfers between devices, body(): lax.all_to_all(outgoing, 'clu', split_axis=0, concat_axis=0, tiled=True)  7.62 us
    all_to_all x1, starting transfers between devices, body(): lax.all_to_all(replies, 'clu', split_axis=0, concat_axis=0, tiled=True)  6.84 us
    pallas_call x1, Pallas kernels, attend_all(): vmem_call(kernel, jax.ShapeDtypeStruct((rows, heads * head_dim), BF16), (...  6.5 us
    pallas_call x2, Pallas kernels, project(): vmem_call(kernel, (jax.ShapeDtypeStruct((rows, width), BF16),) * len(step...  5.54 us
  transfers between devices with their start and end apart: 18, of which 9 were waited for; matrix products, arithmetic and copies ran while one was open for 2% of the time, Pallas kernels for 7%

profile of v6, /device:TPU:24, one launch (start us, length us, event | category | flops | bytes accessed | tf_op | source)
XLA Modules:
  0.0 212.1 jit_solution(13379176301522008381)
XLA Ops:
  8.2 12.7 %collective-permute-start = (bf16[32,1152]{1,0:T(8,128)(2,1)S(1)}, bf16[32,1152]{1,0:T(8,128)(2,1)S(1)}, u32[]{:S(2)}, u32[]{:S(2)}) collective-permute-start(bf16[32,1152]{1,0:T(8,128)(2,1)S(1)} %get-tuple-element.32), channel_id=1, source_target_pairs={{0,48},{4,52},{8,56},{12,60},{16,0},{20,4},{24,8},{28,12},{32,16},... | collective-permute-start | bytes 221192 | tf_op jit(solution)/shard_map/ppermute | solution.py:302
  22.9 10.8 %collective-permute-start.1 = (bf16[32,1152]{1,0:T(8,128)(2,1)S(1)}, bf16[32,1152]{1,0:T(8,128)(2,1)S(1)}, u32[]{:S(2)}, u32[]{:S(2)}) collective-permute-start(bf16[32,1152]{1,0:T(8,128)(2,1)S(1)} %get-tuple-element.32), channel_id=1, source_target_pairs={{0,32},{4,36},{8,40},{12,44},{16,48},{20,52},{24,56},{28,60},{32,0... | collective-permute-start | bytes 221192 | tf_op jit(solution)/shard_map/ppermute | solution.py:302
  37.0 4.3 %all-to-all-start = ((bf16[4,256,1024]{2,1,0:T(8,128)(2,1)}), bf16[4,256,1024]{2,1,0:T(8,128)(2,1)S(1)}, u32[]{:S(2)}, u32[]{:S(2)}) async-start(bf16[4,256,1024]{2,1,0:T(8,128)(2,1)} %copy-done), calls=%async_computation | async-start | bytes 4194304 | tf_op jit(solution)/shard_map/all_to_all | solution.py:341
  41.3 3.4 %collective-permute-start.5 = (bf16[2,32,1152]{2,1,0:T(8,128)(2,1)S(1)}, bf16[2,32,1152]{2,1,0:T(8,128)(2,1)S(1)}, u32[]{:S(2)}, u32[]{:S(2)}) collective-permute-start(bf16[2,32,1152]{2,1,0:T(8,128)(2,1)S(1)} %get-tuple-element.30), channel_id=1, source_target_pairs={{0,8},{4,12},{8,16},{12,20},{16,24},{20,28},{24,32},{28,36},{32,40... | collective-permute-start | bytes 442376 | tf_op jit(solution)/shard_map/ppermute | solution.py:302
  44.8 4.1 %collective-permute-start.3 = (bf16[4,32,1152]{2,1,0:T(8,128)(2,1)S(1)}, bf16[4,32,1152]{2,1,0:T(8,128)(2,1)S(1)}, u32[]{:S(2)}, u32[]{:S(2)}) collective-permute-start(bf16[4,32,1152]{2,1,0:T(8,128)(2,1)S(1)} %get-tuple-element.26), channel_id=1, source_target_pairs={{0,60},{4,0},{8,4},{12,8},{16,12},{20,16},{24,20},{28,24},{32,28},... | collective-permute-start | bytes 884744 | tf_op jit(solution)/shard_map/ppermute | solution.py:302
  50.9 4.4 %collective-permute-start.4 = (bf16[2,32,1152]{2,1,0:T(8,128)(2,1)S(1)}, bf16[2,32,1152]{2,1,0:T(8,128)(2,1)S(1)}, u32[]{:S(2)}, u32[]{:S(2)}) collective-permute-start(bf16[2,32,1152]{2,1,0:T(8,128)(2,1)S(1)} %get-tuple-element.29), channel_id=1, source_target_pairs={{0,56},{4,60},{8,0},{12,4},{16,8},{20,12},{24,16},{28,20},{32,24},... | collective-permute-start | bytes 442376 | tf_op jit(solution)/shard_map/ppermute | solution.py:302
  55.3 5.5 %collective-permute-done.4 = bf16[2,32,1152]{2,1,0:T(8,128)(2,1)S(1)} collective-permute-done((bf16[2,32,1152]{2,1,0:T(8,128)(2,1)S(1)}, bf16[2,32,1152]{2,1,0:T(8,128)(2,1)S(1)}, u32[]{:S(2)}, u32[]{:S(2)}) %collective-permute-start.4) | collective-permute-done | bytes 147488 | tf_op jit(solution)/shard_map/ppermute | solution.py:302
  65.8 2.8 %collective-permute-done.7.other_ref = bf16[512,1024]{1,0:T(8,128)(2,1)} collective-permute-done((bf16[512,1024]{1,0:T(8,128)(2,1)S(1)}, bf16[512,1024]{1,0:T(8,128)(2,1)}, u32[]{:S(2)}, u32[]{:S(2)}) %collective-permute-start.7) | collective-permute-done | bytes 1048608 | tf_op jit(solution)/shard_map/ppermute | solution.py:350
  68.6 2.5 %shard_map.38 = (bf16[256,512]{1,0:T(8,128)(2,1)S(1)}, bf16[256,512]{1,0:T(8,128)(2,1)S(1)}, bf16[256,512]{1,0:T(8,128)(2,1)S(1)}, bf16[256,512]{1,0:T(8,128)(2,1)S(1)}) custom-call(s32[1]{0:T(128)} %bitcast.1.x_ref, bf16[4,256,1024]{2,1,0:T(8,128)(2,1)S(1)} %all-to-all-done.pieces_ref, bf16[512,1024]{1,0:T(8,128)(2,1)S(1)} %bitcast.32, ...), custom_call_target="tpu_custom_call" | custom-call | tf_op jit(solution)/shard_map/pallas_call | solution.py:148
  71.1 5.2 %collective-permute-start.8 = (bf16[256,512]{1,0:T(8,128)(2,1)S(1)}, bf16[256,512]{1,0:T(8,128)(2,1)S(1)}, u32[]{:S(2)}, u32[]{:S(2)}) collective-permute-start(bf16[256,512]{1,0:T(8,128)(2,1)S(1)} %get-tuple-element.15), channel_id=1, source_target_pairs={{0,256},{128,384},{256,0},{384,128},{1,257},{129,385},{257,1},{385... | collective-permute-start | bytes 786440 | tf_op jit(solution)/shard_map/ppermute | solution.py:302
  76.2 2.5 %collective-permute-start.9 = (bf16[256,512]{1,0:T(8,128)(2,1)S(1)}, bf16[256,512]{1,0:T(8,128)(2,1)S(1)}, u32[]{:S(2)}, u32[]{:S(2)}) collective-permute-start(bf16[256,512]{1,0:T(8,128)(2,1)S(1)} %get-tuple-element.16), channel_id=1, source_target_pairs={{0,128},{128,256},{256,384},{384,0},{1,129},{129,257},{257,385},{3... | collective-permute-start | bytes 786440 | tf_op jit(solution)/shard_map/ppermute | solution.py:302
  78.7 4.6 %collective-permute-start.10 = (bf16[256,512]{1,0:T(8,128)(2,1)S(1)}, bf16[256,512]{1,0:T(8,128)(2,1)S(1)}, u32[]{:S(2)}, u32[]{:S(2)}) collective-permute-start(bf16[256,512]{1,0:T(8,128)(2,1)S(1)} %get-tuple-element.17), channel_id=1, source_target_pairs={{0,384},{128,0},{256,128},{384,256},{1,385},{129,1},{257,129},{385... | collective-permute-start | bytes 786440 | tf_op jit(solution)/shard_map/ppermute | solution.py:302
  83.6 4.8 %collective-permute-done.9.refs_1_ = bf16[256,512]{1,0:T(8,128)(2,1)S(1)} collective-permute-done((bf16[256,512]{1,0:T(8,128)(2,1)S(1)}, bf16[256,512]{1,0:T(8,128)(2,1)S(1)}, u32[]{:S(2)}, u32[]{:S(2)}) %collective-permute-start.9) | collective-permute-done | bytes 262176 | tf_op jit(solution)/shard_map/ppermute | solution.py:302
  89.6 3.1 %shard_map.41 = (bf16[256,512]{1,0:T(8,128)(2,1)}, bf16[256,512]{1,0:T(8,128)(2,1)}, bf16[256,512]{1,0:T(8,128)(2,1)}, bf16[256,512]{1,0:T(8,128)(2,1)S(1)}) custom-call(s32[1]{0:T(128)} %bitcast.1.x_ref, bf16[4,256,1024]{2,1,0:T(8,128)(2,1)S(1)} %all-to-all-done.pieces_ref, bf16[512,1024]{1,0:T(8,128)(2,1)S(1)} %bitcast.33, ...), custom_call_target="tpu_custom_call" | custom-call | tf_op jit(solution)/shard_map/pallas_call | solution.py:148
  92.6 4.9 %collective-permute-start.11 = (bf16[256,512]{1,0:T(8,128)(2,1)}, bf16[256,512]{1,0:T(8,128)(2,1)S(1)}, u32[]{:S(2)}, u32[]{:S(2)}) collective-permute-start(bf16[256,512]{1,0:T(8,128)(2,1)} %get-tuple-element.19), channel_id=1, source_target_pairs={{0,256},{128,384},{256,0},{384,128},{1,257},{129,385},{257,1},{385... | collective-permute-start | bytes 786440 | tf_op jit(solution)/shard_map/ppermute | solution.py:302
  97.5 3.4 %collective-permute-start.12 = (bf16[256,512]{1,0:T(8,128)(2,1)}, bf16[256,512]{1,0:T(8,128)(2,1)S(1)}, u32[]{:S(2)}, u32[]{:S(2)}) collective-permute-start(bf16[256,512]{1,0:T(8,128)(2,1)} %get-tuple-element.20), channel_id=1, source_target_pairs={{0,128},{128,256},{256,384},{384,0},{1,129},{129,257},{257,385},{3... | collective-permute-start | bytes 786440 | tf_op jit(solution)/shard_map/ppermute | solution.py:302
  100.9 3.7 %collective-permute-start.13 = (bf16[256,512]{1,0:T(8,128)(2,1)}, bf16[256,512]{1,0:T(8,128)(2,1)S(1)}, u32[]{:S(2)}, u32[]{:S(2)}) collective-permute-start(bf16[256,512]{1,0:T(8,128)(2,1)} %get-tuple-element.21), channel_id=1, source_target_pairs={{0,384},{128,0},{256,128},{384,256},{1,385},{129,1},{257,129},{385... | collective-permute-start | bytes 786440 | tf_op jit(solution)/shard_map/ppermute | solution.py:302
  105.4 4.5 %collective-permute-done.12.refs_1_ = bf16[256,512]{1,0:T(8,128)(2,1)S(1)} collective-permute-done((bf16[256,512]{1,0:T(8,128)(2,1)}, bf16[256,512]{1,0:T(8,128)(2,1)S(1)}, u32[]{:S(2)}, u32[]{:S(2)}) %collective-permute-start.12) | collective-permute-done | bytes 262176 | tf_op jit(solution)/shard_map/ppermute | solution.py:302
  111.3 7.6 %all-to-all-start.1 = ((bf16[16,64,256]{2,1,0:T(8,128)(2,1)}), bf16[16,64,256]{2,1,0:T(8,128)(2,1)S(1)}, u32[]{:S(2)}, u32[]{:S(2)}) async-start(bf16[16,64,256]{2,1,0:T(8,128)(2,1)} %shard_map.43), calls=%async_computation.1 | async-start | bytes 1048576 | tf_op jit(solution)/shard_map/all_to_all | solution.py:364
  121.1 32.0 %all-to-all-done.1.block_ref = bf16[16,64,256]{2,1,0:T(8,128)(2,1)S(1)} async-done(((bf16[16,64,256]{2,1,0:T(8,128)(2,1)}), bf16[16,64,256]{2,1,0:T(8,128)(2,1)S(1)}, u32[]{:S(2)}, u32[]{:S(2)}) %all-to-all-start.1) | async-done | bytes 524320 | tf_op jit(solution)/shard_map/all_to_all | solution.py:364
  155.1 6.8 %all-to-all-start.2 = ((bf16[16,64,128]{2,1,0:T(8,128)(2,1)}), bf16[16,64,128]{2,1,0:T(8,128)(2,1)S(1)}, u32[]{:S(2)}, u32[]{:S(2)}) async-start(bf16[16,64,128]{2,1,0:T(8,128)(2,1)} %shard_map.45), calls=%async_computation.2 | async-start | bytes 524288 | tf_op jit(solution)/shard_map/all_to_all | solution.py:367
  162.0 33.6 %all-gather.3.cloned.1.call-done = bf16[4096,512]{1,0:T(8,128)(2,1)} async-done(((bf16[256,512]{1,0:T(8,128)(2,1)}), bf16[4096,512]{1,0:T(8,128)(2,1)}) %all-gather.3.cloned.1.call-update) | async-done | bytes 4194320 | tf_op jit(solution)/shard_map/all_gather | solution.py:362
  195.5 2.2 %copy-done.1 = bf16[4096,512]{1,0:T(8,128)(2,1)S(1)} copy-done((bf16[4096,512]{1,0:T(8,128)(2,1)S(1)}, bf16[4096,512]{1,0:T(8,128)(2,1)}, u32[]{:S(2)}) %copy-start.1) | copy-done | bytes 4194328
  197.7 6.5 %shard_map.40.dense_ref = bf16[256,256]{1,0:T(8,128)(2,1)S(1)} custom-call(s32[1]{0:T(128)} %bitcast.me_ref, bf16[16,256,512]{2,1,0:T(8,128)(2,1)S(1)} %bitcast.34, bf16[256,512]{1,0:T(8,128)(2,1)} %shard_map.39.own_ref, bf16[16,16,128]{2,1,0:T(8,128)(2,1)S(1)} %fusion.3.all_ids_ref.ids_ref, s32[256,4]{1,0:T(8,128)S(1)} %copy.8.ids_ref), custom_call_target="tpu_custom_call" | custom-call | tf_op jit(solution)/shard_map/pallas_call | solution.py:271
  (50 shorter events, 22.7 us)
Async XLA Ops:
  8.2 33.0 %collective-permute-start = (bf16[32,1152]{1,0:T(8,128)(2,1)S(1)}, bf16[32,1152]{1,0:T(8,128)(2,1)S(1)}, u32[]{:S(2)}, u32[]{:S(2)}) collective-permute-start(bf16[32,1152]{1,0:T(8,128)(2,1)S(1)} %get-tuple-element.32), channel_id=1, source_target_pairs={{0,48},{4,52},{8,56},{12,60},{16,0},{20,4},{24,8},{28,12},{32,16},... | collective-permute-start | bytes 221192 | tf_op jit(solution)/shard_map/ppermute | solution.py:302
  21.0 20.3 %collective-permute-start.2 = (bf16[32,1152]{1,0:T(8,128)(2,1)S(1)}, bf16[32,1152]{1,0:T(8,128)(2,1)S(1)}, u32[]{:S(2)}, u32[]{:S(2)}) collective-permute-start(bf16[32,1152]{1,0:T(8,128)(2,1)S(1)} %get-tuple-element.32), channel_id=1, source_target_pairs={{0,16},{4,20},{8,24},{12,28},{16,32},{20,36},{24,40},{28,44},{32,4... | collective-permute-start | bytes 221192 | tf_op jit(solution)/shard_map/ppermute | solution.py:302
  22.9 21.8 %collective-permute-start.1 = (bf16[32,1152]{1,0:T(8,128)(2,1)S(1)}, bf16[32,1152]{1,0:T(8,128)(2,1)S(1)}, u32[]{:S(2)}, u32[]{:S(2)}) collective-permute-start(bf16[32,1152]{1,0:T(8,128)(2,1)S(1)} %get-tuple-element.32), channel_id=1, source_target_pairs={{0,32},{4,36},{8,40},{12,44},{16,48},{20,52},{24,56},{28,60},{32,0... | collective-permute-start | bytes 221192 | tf_op jit(solution)/shard_map/ppermute | solution.py:302
  33.7 1.6 copy-start.2
  35.6 1.4 copy-start
  37.0 31.6 %all-to-all-start = ((bf16[4,256,1024]{2,1,0:T(8,128)(2,1)}), bf16[4,256,1024]{2,1,0:T(8,128)(2,1)S(1)}, u32[]{:S(2)}, u32[]{:S(2)}) async-start(bf16[4,256,1024]{2,1,0:T(8,128)(2,1)} %copy-done), calls=%async_computation | async-start | bytes 4194304 | tf_op jit(solution)/shard_map/all_to_all | solution.py:341
  41.3 154.2 %all-gather.3.cloned.1.call-start = ((), (), s32[]{:S(2)}) async-start(), calls=%async_computation.3 | async-start | bytes 4456448 | tf_op jit(solution)/shard_map/all_gather | solution.py:362
  41.3 13.9 %collective-permute-start.5 = (bf16[2,32,1152]{2,1,0:T(8,128)(2,1)S(1)}, bf16[2,32,1152]{2,1,0:T(8,128)(2,1)S(1)}, u32[]{:S(2)}, u32[]{:S(2)}) collective-permute-start(bf16[2,32,1152]{2,1,0:T(8,128)(2,1)S(1)} %get-tuple-element.30), channel_id=1, source_target_pairs={{0,8},{4,12},{8,16},{12,20},{16,24},{20,28},{24,32},{28,36},{32,40... | collective-permute-start | bytes 442376 | tf_op jit(solution)/shard_map/ppermute | solution.py:302
  44.8 16.1 %collective-permute-start.3 = (bf16[4,32,1152]{2,1,0:T(8,128)(2,1)S(1)}, bf16[4,32,1152]{2,1,0:T(8,128)(2,1)S(1)}, u32[]{:S(2)}, u32[]{:S(2)}) collective-permute-start(bf16[4,32,1152]{2,1,0:T(8,128)(2,1)S(1)} %get-tuple-element.26), channel_id=1, source_target_pairs={{0,60},{4,0},{8,4},{12,8},{16,12},{20,16},{24,20},{28,24},{32,28},... | collective-permute-start | bytes 884744 | tf_op jit(solution)/shard_map/ppermute | solution.py:302
  48.9 11.9 %collective-permute-start.6 = (bf16[4,32,1152]{2,1,0:T(8,128)(2,1)S(1)}, bf16[4,32,1152]{2,1,0:T(8,128)(2,1)S(1)}, u32[]{:S(2)}, u32[]{:S(2)}) collective-permute-start(bf16[4,32,1152]{2,1,0:T(8,128)(2,1)S(1)} %get-tuple-element.26), channel_id=1, source_target_pairs={{0,4},{4,8},{8,12},{12,16},{16,20},{20,24},{24,28},{28,32},{32,36}... | collective-permute-start | bytes 884744 | tf_op jit(solution)/shard_map/ppermute | solution.py:302
  50.9 9.9 %collective-permute-start.4 = (bf16[2,32,1152]{2,1,0:T(8,128)(2,1)S(1)}, bf16[2,32,1152]{2,1,0:T(8,128)(2,1)S(1)}, u32[]{:S(2)}, u32[]{:S(2)}) collective-permute-start(bf16[2,32,1152]{2,1,0:T(8,128)(2,1)S(1)} %get-tuple-element.29), channel_id=1, source_target_pairs={{0,56},{4,60},{8,0},{12,4},{16,8},{20,12},{24,16},{28,20},{32,24},... | collective-permute-start | bytes 442376 | tf_op jit(solution)/shard_map/ppermute | solution.py:302
  63.9 4.7 %collective-permute-start.7 = (bf16[512,1024]{1,0:T(8,128)(2,1)S(1)}, bf16[512,1024]{1,0:T(8,128)(2,1)}, u32[]{:S(2)}, u32[]{:S(2)}) collective-permute-start(bf16[512,1024]{1,0:T(8,128)(2,1)S(1)} %bitcast.31), channel_id=1, source_target_pairs={{0,64},{64,0},{1,65},{65,1},{2,66},{66,2},{3,67},{67,3},{4,68},{68... | collective-permute-start | bytes 3145736 | tf_op jit(solution)/shard_map/ppermute | solution.py:350
  71.1 12.5 %collective-permute-start.8 = (bf16[256,512]{1,0:T(8,128)(2,1)S(1)}, bf16[256,512]{1,0:T(8,128)(2,1)S(1)}, u32[]{:S(2)}, u32[]{:S(2)}) collective-permute-start(bf16[256,512]{1,0:T(8,128)(2,1)S(1)} %get-tuple-element.15), channel_id=1, source_target_pairs={{0,256},{128,384},{256,0},{384,128},{1,257},{129,385},{257,1},{385... | collective-permute-start | bytes 786440 | tf_op jit(solution)/shard_map/ppermute | solution.py:302
  76.2 12.2 %collective-permute-start.9 = (bf16[256,512]{1,0:T(8,128)(2,1)S(1)}, bf16[256,512]{1,0:T(8,128)(2,1)S(1)}, u32[]{:S(2)}, u32[]{:S(2)}) collective-permute-start(bf16[256,512]{1,0:T(8,128)(2,1)S(1)} %get-tuple-element.16), channel_id=1, source_target_pairs={{0,128},{128,256},{256,384},{384,0},{1,129},{129,257},{257,385},{3... | collective-permute-start | bytes 786440 | tf_op jit(solution)/shard_map/ppermute | solution.py:302
  78.7 10.0 %collective-permute-start.10 = (bf16[256,512]{1,0:T(8,128)(2,1)S(1)}, bf16[256,512]{1,0:T(8,128)(2,1)S(1)}, u32[]{:S(2)}, u32[]{:S(2)}) collective-permute-start(bf16[256,512]{1,0:T(8,128)(2,1)S(1)} %get-tuple-element.17), channel_id=1, source_target_pairs={{0,384},{128,0},{256,128},{384,256},{1,385},{129,1},{257,129},{385... | collective-permute-start | bytes 786440 | tf_op jit(solution)/shard_map/ppermute | solution.py:302
  89.6 15.0 %copy-start.3 = (s32[1,256,4]{1,2,0:T(4,128)S(1)}, s32[1,256,4]{1,2,0:T(4,128)}, u32[]{:S(2)}) copy-start(s32[1,256,4]{1,2,0:T(4,128)} %param.5) | copy-start | bytes 12292
  92.6 12.8 %collective-permute-start.11 = (bf16[256,512]{1,0:T(8,128)(2,1)}, bf16[256,512]{1,0:T(8,128)(2,1)S(1)}, u32[]{:S(2)}, u32[]{:S(2)}) collective-permute-start(bf16[256,512]{1,0:T(8,128)(2,1)} %get-tuple-element.19), channel_id=1, source_target_pairs={{0,256},{128,384},{256,0},{384,128},{1,257},{129,385},{257,1},{385... | collective-permute-start | bytes 786440 | tf_op jit(solution)/shard_map/ppermute | solution.py:302
  97.5 12.4 %collective-permute-start.12 = (bf16[256,512]{1,0:T(8,128)(2,1)}, bf16[256,512]{1,0:T(8,128)(2,1)S(1)}, u32[]{:S(2)}, u32[]{:S(2)}) collective-permute-start(bf16[256,512]{1,0:T(8,128)(2,1)} %get-tuple-element.20), channel_id=1, source_target_pairs={{0,128},{128,256},{256,384},{384,0},{1,129},{129,257},{257,385},{3... | collective-permute-start | bytes 786440 | tf_op jit(solution)/shard_map/ppermute | solution.py:302
  100.9 9.2 %collective-permute-start.13 = (bf16[256,512]{1,0:T(8,128)(2,1)}, bf16[256,512]{1,0:T(8,128)(2,1)S(1)}, u32[]{:S(2)}, u32[]{:S(2)}) collective-permute-start(bf16[256,512]{1,0:T(8,128)(2,1)} %get-tuple-element.21), channel_id=1, source_target_pairs={{0,384},{128,0},{256,128},{384,256},{1,385},{129,1},{257,129},{385... | collective-permute-start | bytes 786440 | tf_op jit(solution)/shard_map/ppermute | solution.py:302
  111.3 41.8 %all-to-all-start.1 = ((bf16[16,64,256]{2,1,0:T(8,128)(2,1)}), bf16[16,64,256]{2,1,0:T(8,128)(2,1)S(1)}, u32[]{:S(2)}, u32[]{:S(2)}) async-start(bf16[16,64,256]{2,1,0:T(8,128)(2,1)} %shard_map.43), calls=%async_computation.1 | async-start | bytes 1048576 | tf_op jit(solution)/shard_map/all_to_all | solution.py:364
  155.1 49.1 %all-to-all-start.2 = ((bf16[16,64,128]{2,1,0:T(8,128)(2,1)}), bf16[16,64,128]{2,1,0:T(8,128)(2,1)S(1)}, u32[]{:S(2)}, u32[]{:S(2)}) async-start(bf16[16,64,128]{2,1,0:T(8,128)(2,1)} %shard_map.45), calls=%async_computation.2 | async-start | bytes 524288 | tf_op jit(solution)/shard_map/all_to_all | solution.py:367
  195.5 2.2 %copy-start.1 = (bf16[4096,512]{1,0:T(8,128)(2,1)S(1)}, bf16[4096,512]{1,0:T(8,128)(2,1)}, u32[]{:S(2)}) copy-start(bf16[4096,512]{1,0:T(8,128)(2,1)} %all-gather.3.cloned.1.call-done) | copy-start | bytes 12582916
Sparse Core Ops, SparseCore 0:
  89.7 105.7 all-gather.2

commit v7 on v5

v7 whole, which is shorter than its diff:
```python
import jax
import jax.numpy as jnp
from jax import lax
from jax.experimental import pallas as pl
from jax.experimental.pallas import tpu as pltpu
from jax.sharding import PartitionSpec as P

CLUSTERS = 64
BF16 = jnp.bfloat16
F32 = jnp.float32
VMEM_LIMIT = 48 * 1024 * 1024


def vmem_call(kernel, out_shape, in_smem, **kwargs):
    vmem = pl.BlockSpec(memory_space=pltpu.VMEM)
    smem = pl.BlockSpec(memory_space=pltpu.SMEM)
    return pl.pallas_call(
        kernel,
        out_shape=out_shape,
        in_specs=[smem if flag else vmem for flag in in_smem],
        out_specs=jax.tree.map(lambda _: vmem, out_shape),
        compiler_params=pltpu.CompilerParams(vmem_limit_bytes=VMEM_LIMIT),
        **kwargs,
    )


def scalar(value):
    return jnp.reshape(value, (1,)).astype(jnp.int32)


def iota(shape, dim):
    return lax.broadcasted_iota(jnp.int32, shape, dim)


def routing(ids, owners, capacity):
    rows, heads = ids.shape
    per_owner = CLUSTERS // owners

    def kernel(ids_ref, ids_t_ref, slot_row_ref, slot_col_ref):
        before_col = (iota((rows, rows), 1) < iota((rows, rows), 0)).astype(BF16)
        before_row = (iota((rows, rows), 0) < iota((rows, rows), 1)).astype(BF16)
        for h in range(heads):
            owner_col = ids_ref[:, h : h + 1] // per_owner
            hot = owner_col == iota((rows, owners), 1)
            count = jnp.dot(before_col, hot.astype(BF16), preferred_element_type=F32)
            rank = jnp.sum(jnp.where(hot, count, 0.0), axis=1, keepdims=True)
            slot_col_ref[:, h : h + 1] = owner_col * capacity + rank.astype(jnp.int32)
            owner_row = ids_t_ref[h : h + 1, :] // per_owner
            hot = owner_row == iota((owners, rows), 0)
            count = jnp.dot(hot.astype(BF16), before_row, preferred_element_type=F32)
            rank = jnp.sum(jnp.where(hot, count, 0.0), axis=0, keepdims=True)
            slot_row_ref[h : h + 1, :] = owner_row * capacity + rank.astype(jnp.int32)

    return vmem_call(
        kernel,
        (
            jax.ShapeDtypeStruct((heads, rows), jnp.int32),
            jax.ShapeDtypeStruct((rows, heads), jnp.int32),
        ),
        (False, False),
    )(ids, ids.T)


def owned_members(all_ids, me, heads, capacity):
    sources, id_rows, lanes = all_ids.shape
    rows = sources * capacity // 2
    per_head = rows // lanes
    per_owner = CLUSTERS // sources
    slots = sources * capacity

    def kernel(me_ref, ids_ref, out_ref):
        before = (iota((rows, rows), 0) < iota((rows, rows), 1)).astype(BF16)
        place = iota((sources, capacity, rows), 1)
        kinds = iota((16, slots), 0) + 1
        column = iota((slots, lanes), 1)
        tags = jnp.zeros((slots, lanes), jnp.int32)
        for h in range(heads):
            ids = jnp.concatenate(
                [ids_ref[:, h * per_head + j, :] for j in range(per_head)], axis=1
            )
            ids = ids.astype(F32).astype(jnp.int32)
            owner = ids // per_owner
            mine = owner == me_ref[0]
            rank = jnp.dot(mine.astype(BF16), before, preferred_element_type=F32)
            rank = jnp.where(mine, rank.astype(jnp.int32), -1)
            tag = ids - owner * per_owner + 1
            placed = jnp.where(rank[:, None, :] == place, tag[:, None, :], 0)
            tag = jnp.sum(placed.reshape(slots, rows), axis=1, keepdims=True)
            tags = jnp.where(column == h, tag, tags)
        same_slot = (iota((slots, slots), 0) == iota((slots, slots), 1)).astype(BF16)
        tags = lax.dot_general(
            tags.astype(BF16), same_slot, (((0,), (0,)), ((), ())), preferred_element_type=F32
        ).astype(jnp.int32)
        for h in range(heads):
            out_ref[h] = (tags[h : h + 1, :] == kinds).astype(BF16)

    return vmem_call(kernel, jax.ShapeDtypeStruct((heads, 16, slots), BF16), (True, False))(
        scalar(me), all_ids
    )


def cut_tokens(local_rows, core, chips):
    rows, depth = local_rows.shape
    half = depth // chips // 2

    def kernel(core_ref, in_ref, own_ref, other_ref, sems):
        copies = []
        for p in range(chips):
            for j, out_ref in enumerate((own_ref, other_ref)):
                first = (2 * p + lax.rem(core_ref[0] + j, 2)) * half
                copies.append(
                    pltpu.make_async_copy(
                        in_ref.at[:, pl.ds(pl.multiple_of(first, half), half)],
                        out_ref.at[p],
                        sems.at[2 * p + j],
                    )
                )
        for copy in copies:
            copy.start()
        for copy in copies:
            copy.wait()

    vmem = pl.BlockSpec(memory_space=pltpu.VMEM)
    return pl.pallas_call(
        kernel,
        out_shape=(jax.ShapeDtypeStruct((chips, rows, half), BF16),) * 2,
        in_specs=[
            pl.BlockSpec(memory_space=pltpu.SMEM),
            pl.BlockSpec(memory_space=pl.ANY),
        ],
        out_specs=(vmem, vmem),
        scratch_shapes=[pltpu.SemaphoreType.DMA((2 * chips,))],
        compiler_params=pltpu.CompilerParams(vmem_limit_bytes=VMEM_LIMIT),
    )(scalar(core), local_rows)


def products(total, tokens, halves, steps, x, me, places, out_types):
    chips, rows, half = tokens[0].shape
    width = halves[0].shape[1]
    given = () if total is None else total
    shard = halves[0].shape[0] // len(places[0])
    classes = 4

    def kernel(x_ref, me_ref, *refs):
        total_refs = refs[: len(given)]
        token_refs = refs[len(given) : len(given) + 2]
        half_refs = refs[len(given) + 2 : -3]
        out_refs, weight_ref = refs[-3:-1], refs[-1]
        results = [ref[...] for ref in total_refs] if given else [0.0, 0.0]
        for n, step in enumerate(steps):
            for ref, blocks in zip(half_refs[2 * n : 2 * n + 2], places):
                for i, (kind, number) in enumerate(blocks):
                    device = lax.rem(me_ref[0] + kind, classes) + classes * number
                    at = pl.multiple_of(device * shard, shard)
                    weight_ref[pl.ds(at, shard), :] = ref[i * shard : (i + 1) * shard, :]
            chip = lax.rem(x_ref[0] + step + chips, chips)
            for i, token_ref in enumerate(token_refs):
                results[i] += jnp.dot(
                    token_ref[chip], weight_ref[...], preferred_element_type=F32
                )
        for result, out_ref in zip(results, out_refs):
            out_ref[...] = result.astype(out_ref.dtype)

    operands = tuple(given) + tuple(tokens) + tuple(halves)
    return vmem_call(
        kernel,
        tuple(jax.ShapeDtypeStruct((rows, width), t) for t in out_types),
        (True, True) + (False,) * len(operands),
        scratch_shapes=[pltpu.VMEM((half, width), BF16)],
    )(scalar(x), scalar(me), *operands)


def pack(own, received, slot_row, owners, capacity, head_dim):
    rows, width = own.shape
    heads = slot_row.shape[0]
    slots = owners * capacity

    def kernel(own_ref, received_ref, slot_ref, out_ref):
        for h in range(heads):
            place = iota((slots, rows), 0) == slot_ref[h : h + 1, :]
            place = place.astype(BF16)
            for m in range(2):
                cols = slice((m * heads + h) * head_dim, (m * heads + h + 1) * head_dim)
                total = own_ref[:, cols] + received_ref[:, cols].astype(F32)
                packed = jnp.dot(
                    place, total.astype(BF16), preferred_element_type=F32
                ).astype(BF16)
                out_ref[
                    :, h * capacity : (h + 1) * capacity, m * head_dim : (m + 1) * head_dim
                ] = packed.reshape(owners, capacity, head_dim)

    return vmem_call(
        kernel,
        jax.ShapeDtypeStruct((owners, heads * capacity, 2 * head_dim), BF16),
        (False,) * 3,
    )(own, received, slot_row)


def attend(blocks, members, capacity):
    sources, rows, width = blocks.shape
    head_dim = width // 2
    heads = rows // capacity
    slots = sources * capacity
    scale = head_dim ** (-0.5)

    def kernel(block_ref, member_ref, out_ref):
        query = iota((slots, slots), 0)
        key = iota((slots, slots), 1)
        for h in range(heads):
            here = slice(h * capacity, (h + 1) * capacity)
            keys = block_ref[:, here, :head_dim].reshape(slots, head_dim)
            values = block_ref[:, here, head_dim:].reshape(slots, head_dim)
            member = member_ref[h]
            same = lax.dot_general(
                member, member, (((0,), (0,)), ((), ())), preferred_element_type=F32
            )
            scores = lax.dot_general(
                keys, keys, (((1,), (1,)), ((), ())), preferred_element_type=F32
            )
            scores = jnp.where(query == key, -100000.0, scores * scale)
            scores = jnp.where((same > 0.5) & (key <= query), scores, -1e30)
            row_max = jnp.max(scores, axis=1, keepdims=True)
            weights = jnp.exp(scores - row_max)
            total = jnp.sum(weights, axis=1, keepdims=True)
            probabilities = (weights / total).astype(BF16)
            result = jnp.dot(probabilities, values, preferred_element_type=F32).astype(BF16)
            out_ref[:, here, :] = result.reshape(sources, capacity, head_dim)

    return vmem_call(
        kernel, jax.ShapeDtypeStruct((sources, rows, head_dim), BF16), (False, False)
    )(blocks, members)


def unpack(returned, slot_col, capacity):
    owners, height, head_dim = returned.shape
    rows, heads = slot_col.shape
    slots = owners * capacity

    def kernel(block_ref, slot_ref, out_ref):
        for h in range(heads):
            block = block_ref[:, h * capacity : (h + 1) * capacity, :].reshape(slots, head_dim)
            place = slot_ref[:, h : h + 1] == iota((rows, slots), 1)
            out_ref[:, h * head_dim : (h + 1) * head_dim] = jnp.dot(
                place.astype(BF16), block, preferred_element_type=F32
            ).astype(BF16)

    return vmem_call(
        kernel, jax.ShapeDtypeStruct((rows, heads * head_dim), BF16), (False, False)
    )(returned, slot_col)


CLU = ("zq", "zr")


def shifted(block, step, axis):
    size = lax.axis_size(axis)
    return lax.ppermute(block, axis, [(i, (i + step) % size) for i in range(size)])


def body(tokens, proj_weight, clusters):
    rows, depth = tokens.shape[1:]
    owners = lax.axis_size(CLU)
    me = lax.axis_index(CLU)
    x = lax.axis_index("x")
    heads = clusters.shape[2]
    shard = proj_weight.shape[0]
    width = 2 * proj_weight.shape[2]
    head_dim = proj_weight.shape[2] // heads
    capacity = 2 * rows // owners
    chips = lax.axis_size("x")

    ids = clusters[0].T.astype(BF16).reshape(-1, 128)
    ids = jnp.pad(ids, ((0, shard - ids.shape[0]), (0, 0)))
    own = jnp.concatenate([proj_weight.reshape(shard, width), ids], axis=1)
    four = lax.all_gather(own, "zq", axis=0)
    below = shifted(four, 1, CLU)
    above = shifted(four, -1, CLU)
    beyond = [shifted(four[:2], 2, CLU), shifted(four[2:], -2, CLU)]

    def weights_of(parts):
        parts = [part[:, :, :width].reshape(-1, width) for part in parts]
        return jnp.concatenate(parts, axis=0)

    first = weights_of([four, below])
    second = weights_of([above] + beyond)
    places = (
        [(0, j) for j in range(4)] + [(3, j) for j in range(4)],
        [(1, j) for j in range(4)] + [(2, j) for j in range(4)],
    )

    mine, send = cut_tokens(tokens[0], lax.axis_index("core"), chips)
    both = (mine, lax.ppermute(send, "core", [(0, 1), (1, 0)]))

    first_below, first_above = shifted(first, 1, "x"), shifted(first, -1, "x")
    second_below, second_above = shifted(second, 1, "x"), shifted(second, -1, "x")
    first_far, second_far = shifted(first_below, 1, "x"), shifted(second_above, -1, "x")
    total = products(
        None,
        both,
        [first, second, first_below, second_below, first_above, second_above],
        (0, -1, 1),
        x,
        me,
        places,
        (F32, F32),
    )
    kept, given = products(
        total, both, [first_far, second_far], (2,), x, me, places, (F32, BF16)
    )
    received = lax.ppermute(given, "core", [(0, 1), (1, 0)])

    slot_row, slot_col = routing(clusters[0], owners, capacity)
    outgoing = pack(kept, received, slot_row, owners, capacity, head_dim)
    incoming = lax.all_to_all(outgoing, CLU, split_axis=0, concat_axis=0, tiled=True)

    by_class = jnp.stack(
        [part[:, :16, width:] for part in (four, above, jnp.concatenate(beyond), below)]
    )
    by_class = jnp.roll(by_class, lax.axis_index("zr"), axis=0)
    all_ids = by_class.transpose(1, 0, 2, 3).reshape((owners,) + by_class.shape[2:])
    members = owned_members(all_ids, me, heads, capacity)
    replies = attend(incoming, members, capacity)
    returned = lax.all_to_all(replies, CLU, split_axis=0, concat_axis=0, tiled=True)
    return unpack(returned, slot_col, capacity)[None]


def solution(mesh):
    ctx, clu, tp = (mesh.shape[name] for name in mesh.axis_names)
    fine = jax.sharding.Mesh(
        mesh.devices.reshape(ctx // 2, 2, clu // 4, 4, tp), ("x", "core") + CLU + ("tp",)
    )
    ctx_axes = ("x", "core")
    return jax.shard_map(
        body,
        mesh=fine,
        in_specs=(
            P(ctx_axes, CLU, None),
            P(ctx_axes + CLU, None, "tp"),
            P(ctx_axes, CLU, "tp"),
        ),
        out_specs=P(ctx_axes, CLU, "tp"),
        check_vma=False,
    )
```

time: 206 us -> 200 us (0.971)
  waiting for transfers between devices: 47.8 us -> 66.3 us
  blocking collectives: 74.6 us -> 64 us
  local copies, waits for them, and re-layouts: 13.8 us -> 6.36 us
  Pallas kernels: 21.1 us -> 15.3 us
    ppermute x10, waiting for transfers between devices: 1.14 us -> 19.1 us  [shifted(): lax.ppermute(block, axis, [(i, (i + step) % size) for i in range(size)])]
    all_gather x1, blocking collectives: 37.6 us -> 27.1 us  [body(): four = lax.all_gather(own, 'zq', axis=0)]
    pallas_call x5 -> x4, Pallas kernels: 15.5 us -> 8.66 us  [the longest x2 6.33 us: products(): vmem_call(kernel, tuple((jax.ShapeDtypeStruct((rows, width), t) for t in...]
    slice x7 -> x6, local copies, waits for them, and re-layouts: 5.8 us -> 0.1 us  [the longest x5 0.08 us: weights_of(): parts = [part[:, :, :width].reshape(-1, width) for part in parts]]
    unnamed x26 -> x27, local copies, waits for them, and re-layouts: 7.84 us -> 5.38 us
  transfers between devices with their start and end apart: 13 -> 13, of which waited for: 3 -> 8; matrix products, arithmetic and copies ran while one was open for 3% -> 2% of each run, Pallas kernels for 6% -> 4%
where the time goes in v7:
time: 200 us
  waiting for transfers between devices  66.3 us (33%)
  blocking collectives  64 us (32%)
  starting transfers between devices  46.4 us (23%)
  Pallas kernels  15.3 us (8%)
  local copies, waits for them, and re-layouts  6.36 us (3%)
    all_to_all x1, waiting for transfers between devices, body(): lax.all_to_all(outgoing, CLU, split_axis=0, concat_axis=0, tiled=True)  46.1 us
    all_to_all x1, blocking collectives, body(): lax.all_to_all(replies, CLU, split_axis=0, concat_axis=0, tiled=True)  36.9 us
    ppermute x10, starting transfers between devices, shifted(): lax.ppermute(block, axis, [(i, (i + step) % size) for i in range(size)])  35.3 us
    all_gather x1, blocking collectives, body(): four = lax.all_gather(own, 'zq', axis=0)  27.1 us
    ppermute x10, waiting for transfers between devices, shifted(): lax.ppermute(block, axis, [(i, (i + step) % size) for i in range(size)])  19.1 us
    all_to_all x1, starting transfers between devices, body(): lax.all_to_all(outgoing, CLU, split_axis=0, concat_axis=0, tiled=True)  7.3 us
    pallas_call x2, Pallas kernels, products(): vmem_call(kernel, tuple((jax.ShapeDtypeStruct((rows, width), t) for t in...  6.33 us
    unnamed x27, local copies, waits for them, and re-layouts  5.38 us
  transfers between devices with their start and end apart: 13, of which 8 were waited for; matrix products, arithmetic and copies ran while one was open for 2% of the time, Pallas kernels for 4%

profile of v7, /device:TPU:24, one launch (start us, length us, event | category | flops | bytes accessed | tf_op | source)
XLA Modules:
  0.0 199.5 jit_solution(15809079735150510645)
XLA Ops:
  1.6 27.1 %all-gather = bf16[128,1152]{1,0:T(8,128)(2,1)S(1)} all-gather(bf16[32,1152]{1,0:T(8,128)(2,1)S(1)} %fusion.1), channel_id=2, replica_groups=mesh['x'=4,'core'=2,'zq'=4,'zr'=4,'tp'=4] {'zq'}, dimensions={0}, use_global_device_ids=true | all-gather | bytes 368640 | tf_op jit(solution)/shard_map/all_gather | solution.py:275
  28.7 4.2 %collective-permute-start.2 = (bf16[4,32,1152]{2,1,0:T(8,128)(2,1)S(1)}, bf16[4,32,1152]{2,1,0:T(8,128)(2,1)S(1)}, u32[]{:S(2)}, u32[]{:S(2)}) collective-permute-start(bf16[4,32,1152]{2,1,0:T(8,128)(2,1)S(1)} %bitcast.51), channel_id=1, source_target_pairs={{0,60},{4,0},{8,4},{12,8},{16,12},{20,16},{24,20},{28,24},{32,28},... | collective-permute-start | bytes 884744 | tf_op jit(solution)/shard_map/ppermute | solution.py:257
  32.9 2.0 collective-permute-start.1
  34.9 4.0 %collective-permute-start.3 = (bf16[2,32,1152]{2,1,0:T(8,128)(2,1)S(1)}, bf16[2,32,1152]{2,1,0:T(8,128)(2,1)S(1)}, u32[]{:S(2)}, u32[]{:S(2)}) collective-permute-start(bf16[2,32,1152]{2,1,0:T(8,128)(2,1)S(1)} %bitcast.63), channel_id=1, source_target_pairs={{0,8},{4,12},{8,16},{12,20},{16,24},{20,28},{24,32},{28,36},{32,40... | collective-permute-start | bytes 442376 | tf_op jit(solution)/shard_map/ppermute | solution.py:257
  39.0 3.9 %collective-permute-start.4 = (bf16[2,32,1152]{2,1,0:T(8,128)(2,1)S(1)}, bf16[2,32,1152]{2,1,0:T(8,128)(2,1)S(1)}, u32[]{:S(2)}, u32[]{:S(2)}) collective-permute-start(bf16[2,32,1152]{2,1,0:T(8,128)(2,1)S(1)} %bitcast.62), channel_id=1, source_target_pairs={{0,56},{4,60},{8,0},{12,4},{16,8},{20,12},{24,16},{28,20},{32,24},... | collective-permute-start | bytes 442376 | tf_op jit(solution)/shard_map/ppermute | solution.py:257
  42.9 1.6 copy-done.2
  45.7 1.9 collective-permute-start
  49.1 4.7 %collective-permute-start.8 = (bf16[256,1024]{1,0:T(8,128)(2,1)S(1)}, bf16[256,1024]{1,0:T(8,128)(2,1)S(1)}, u32[]{:S(2)}, u32[]{:S(2)}) collective-permute-start(bf16[256,1024]{1,0:T(8,128)(2,1)S(1)} %pad_maximum_fusion.1.refs_3_), channel_id=1, source_target_pairs={{0,384},{128,0},{256,128},{384,256},{1,385},{129,1},{257,129},{385... | collective-permute-start | bytes 1572872 | tf_op jit(solution)/shard_map/ppermute | solution.py:257
  53.9 1.9 collective-permute-start.5
  55.8 2.7 %collective-permute-start.6 = (bf16[256,1024]{1,0:T(8,128)(2,1)S(1)}, bf16[256,1024]{1,0:T(8,128)(2,1)S(1)}, u32[]{:S(2)}, u32[]{:S(2)}) collective-permute-start(bf16[256,1024]{1,0:T(8,128)(2,1)S(1)} %pad_maximum_fusion.1.refs_3_), channel_id=1, source_target_pairs={{0,128},{128,256},{256,384},{384,0},{1,129},{129,257},{257,385},{3... | collective-permute-start | bytes 1572872 | tf_op jit(solution)/shard_map/ppermute | solution.py:257
  58.5 4.4 %collective-permute-start.7 = (bf16[256,1024]{1,0:T(8,128)(2,1)S(1)}, bf16[256,1024]{1,0:T(8,128)(2,1)}, u32[]{:S(2)}, u32[]{:S(2)}) collective-permute-start(bf16[256,1024]{1,0:T(8,128)(2,1)S(1)} %pad_maximum_fusion.refs_2_), channel_id=1, source_target_pairs={{0,384},{128,0},{256,128},{384,256},{1,385},{129,1},{257,129},{385... | collective-permute-start | bytes 1572872 | tf_op jit(solution)/shard_map/ppermute | solution.py:257
  62.9 3.2 %collective-permute-done.8.refs_7_ = bf16[256,1024]{1,0:T(8,128)(2,1)S(1)} collective-permute-done((bf16[256,1024]{1,0:T(8,128)(2,1)S(1)}, bf16[256,1024]{1,0:T(8,128)(2,1)S(1)}, u32[]{:S(2)}, u32[]{:S(2)}) %collective-permute-start.8) | collective-permute-done | bytes 524320 | tf_op jit(solution)/shard_map/ppermute | solution.py:257
  66.1 5.6 %collective-permute-start.10 = (bf16[256,1024]{1,0:T(8,128)(2,1)S(1)}, bf16[256,1024]{1,0:T(8,128)(2,1)S(1)}, u32[]{:S(2)}, u32[]{:S(2)}) collective-permute-start(bf16[256,1024]{1,0:T(8,128)(2,1)S(1)} %collective-permute-done.8.refs_7_), channel_id=1, source_target_pairs={{0,384},{128,0},{256,128},{384,256},{1,385},{129,1},{257,129},{385... | collective-permute-start | bytes 1572872 | tf_op jit(solution)/shard_map/ppermute | solution.py:257
  71.8 1.9 collective-permute-start.9
  73.8 9.3 %collective-permute-done.6.refs_5_ = bf16[256,1024]{1,0:T(8,128)(2,1)S(1)} collective-permute-done((bf16[256,1024]{1,0:T(8,128)(2,1)S(1)}, bf16[256,1024]{1,0:T(8,128)(2,1)S(1)}, u32[]{:S(2)}, u32[]{:S(2)}) %collective-permute-start.6) | collective-permute-done | bytes 524320 | tf_op jit(solution)/shard_map/ppermute | solution.py:257
  83.1 4.1 %shard_map.38 = (f32[256,1024]{1,0:T(8,128)S(1)}, f32[256,1024]{1,0:T(8,128)S(1)}) custom-call(s32[1]{0:T(128)} %bitcast.x_ref, s32[1]{0:T(128)} %bitcast.1.me_ref, bf16[4,256,512]{2,1,0:T(8,128)(2,1)} %copy-done, bf16[4,256,512]{2,1,0:T(8,128)(2,1)} %collective-permute-done.refs_1_.refs_3_, bf16[256,1024]{1,0:T(8,128)(2,1)S(1)} %pad_maximum_fusion.refs_2_, ...), custom_call_target="tpu_custom_call" | custom-call | tf_op jit(solution)/shard_map/pallas_call | solution.py:165
  87.5 5.6 %collective-permute-done.9.refs_4_ = bf16[256,1024]{1,0:T(8,128)(2,1)} collective-permute-done((bf16[256,1024]{1,0:T(8,128)(2,1)S(1)}, bf16[256,1024]{1,0:T(8,128)(2,1)}, u32[]{:S(2)}, u32[]{:S(2)}) %collective-permute-start.9) | collective-permute-done | bytes 524320 | tf_op jit(solution)/shard_map/ppermute | solution.py:257
  93.1 2.2 %shard_map.39 = (f32[256,1024]{1,0:T(8,128)S(1)}, bf16[256,1024]{1,0:T(8,128)(2,1)S(1)}) custom-call(s32[1]{0:T(128)} %bitcast.x_ref, s32[1]{0:T(128)} %bitcast.1.me_ref, f32[256,1024]{1,0:T(8,128)S(1)} %get-tuple-element.15.refs_0_, f32[256,1024]{1,0:T(8,128)S(1)} %get-tuple-element.16.refs_1_, bf16[4,256,512]{2,1,0:T(8,128)(2,1)S(1)} %copy-done.1, ...), custom_call_target="tpu_custom_call" | custom-call | tf_op jit(solution)/shard_map/pallas_call | solution.py:165
  95.3 1.9 collective-permute-start.11
  99.1 1.7 shard_map.41
  100.8 7.3 %all-to-all-start = ((bf16[16,128,256]{2,1,0:T(8,128)(2,1)}), bf16[16,128,256]{2,1,0:T(8,128)(2,1)S(1)}, u32[]{:S(2)}, u32[]{:S(2)}) async-start(bf16[16,128,256]{2,1,0:T(8,128)(2,1)} %shard_map.41), calls=%async_computation | async-start | bytes 2097152 | tf_op jit(solution)/shard_map/all_to_all | solution.py:314
  112.2 46.1 %all-to-all-done.block_ref = bf16[16,128,256]{2,1,0:T(8,128)(2,1)S(1)} async-done(((bf16[16,128,256]{2,1,0:T(8,128)(2,1)}), bf16[16,128,256]{2,1,0:T(8,128)(2,1)S(1)}, u32[]{:S(2)}, u32[]{:S(2)}) %all-to-all-start) | async-done | bytes 1048608 | tf_op jit(solution)/shard_map/all_to_all | solution.py:314
  158.4 3.1 %shard_map.43 = bf16[16,128,128]{2,1,0:T(8,128)(2,1)S(1)} custom-call(bf16[16,128,256]{2,1,0:T(8,128)(2,1)S(1)} %all-to-all-done.block_ref, bf16[4,16,512]{2,1,0:T(8,128)(2,1)S(1)} %shard_map.42.member_ref), custom_call_target="tpu_custom_call" | custom-call | tf_op jit(solution)/shard_map/pallas_call | solution.py:229
  161.4 36.9 %all_to_all.10.block_ref = bf16[16,128,128]{2,1,0:T(8,128)(2,1)S(1)} all-to-all(bf16[16,128,128]{2,1,0:T(8,128)(2,1)S(1)} %shard_map.43), channel_id=1, replica_groups=mesh['x'=4,'core'=2,'zq'=4,'zr'=4,'tp'=4] {'zq','zr'}, dimensions={0} | all-to-all | bytes 1048576 | tf_op jit(solution)/shard_map/all_to_all | solution.py:323
  (54 shorter events, 11.9 us)
Async XLA Ops:
  28.7 19.6 %collective-permute-start.2 = (bf16[4,32,1152]{2,1,0:T(8,128)(2,1)S(1)}, bf16[4,32,1152]{2,1,0:T(8,128)(2,1)S(1)}, u32[]{:S(2)}, u32[]{:S(2)}) collective-permute-start(bf16[4,32,1152]{2,1,0:T(8,128)(2,1)S(1)} %bitcast.51), channel_id=1, source_target_pairs={{0,60},{4,0},{8,4},{12,8},{16,12},{20,16},{24,20},{28,24},{32,28},... | collective-permute-start | bytes 884744 | tf_op jit(solution)/shard_map/ppermute | solution.py:257
  32.9 20.9 %collective-permute-start.1 = (bf16[4,32,1152]{2,1,0:T(8,128)(2,1)S(1)}, bf16[4,32,1152]{2,1,0:T(8,128)(2,1)S(1)}, u32[]{:S(2)}, u32[]{:S(2)}) collective-permute-start(bf16[4,32,1152]{2,1,0:T(8,128)(2,1)S(1)} %bitcast.52), channel_id=1, source_target_pairs={{0,4},{4,8},{8,12},{12,16},{16,20},{20,24},{24,28},{28,32},{32,36}... | collective-permute-start | bytes 884744 | tf_op jit(solution)/shard_map/ppermute | solution.py:257
  34.9 12.8 %collective-permute-start.3 = (bf16[2,32,1152]{2,1,0:T(8,128)(2,1)S(1)}, bf16[2,32,1152]{2,1,0:T(8,128)(2,1)S(1)}, u32[]{:S(2)}, u32[]{:S(2)}) collective-permute-start(bf16[2,32,1152]{2,1,0:T(8,128)(2,1)S(1)} %bitcast.63), channel_id=1, source_target_pairs={{0,8},{4,12},{8,16},{12,20},{16,24},{20,28},{24,32},{28,36},{32,40... | collective-permute-start | bytes 442376 | tf_op jit(solution)/shard_map/ppermute | solution.py:257
  39.0 9.3 %collective-permute-start.4 = (bf16[2,32,1152]{2,1,0:T(8,128)(2,1)S(1)}, bf16[2,32,1152]{2,1,0:T(8,128)(2,1)S(1)}, u32[]{:S(2)}, u32[]{:S(2)}) collective-permute-start(bf16[2,32,1152]{2,1,0:T(8,128)(2,1)S(1)} %bitcast.62), channel_id=1, source_target_pairs={{0,56},{4,60},{8,0},{12,4},{16,8},{20,12},{24,16},{28,20},{32,24},... | collective-permute-start | bytes 442376 | tf_op jit(solution)/shard_map/ppermute | solution.py:257
  42.9 1.6 copy-start.2
  45.7 8.2 %copy-start = (bf16[4,256,512]{2,1,0:T(8,128)(2,1)}, bf16[4,256,512]{2,1,0:T(8,128)(2,1)S(1)}, u32[]{:S(2)}) copy-start(bf16[4,256,512]{2,1,0:T(8,128)(2,1)S(1)} %get-tuple-element.13.refs_0_.refs_2_) | copy-start | bytes 3145732
  45.7 37.3 %collective-permute-start = (bf16[4,256,512]{2,1,0:T(8,128)(2,1)}, bf16[4,256,512]{2,1,0:T(8,128)(2,1)}, u32[]{:S(2)}, u32[]{:S(2)}) collective-permute-start(bf16[4,256,512]{2,1,0:T(8,128)(2,1)} %get-tuple-element.14), channel_id=1, source_target_pairs={{0,64},{64,0},{1,65},{65,1},{2,66},{66,2},{3,67},{67,3},{4,68},{68... | collective-permute-start | bytes 3145736 | tf_op jit(solution)/shard_map/ppermute | solution.py:292
  47.7 6.1 %copy-start.4 = (bf16[2,32,1152]{2,1,0:T(8,128)(2,1)}, bf16[2,32,1152]{2,1,0:T(8,128)(2,1)S(1)}, u32[]{:S(2)}) copy-start(bf16[2,32,1152]{2,1,0:T(8,128)(2,1)S(1)} %collective-permute-done.3) | copy-start | bytes 442372
  48.3 5.5 %copy-start.6 = (bf16[2,32,1152]{2,1,0:T(8,128)(2,1)}, bf16[2,32,1152]{2,1,0:T(8,128)(2,1)S(1)}, u32[]{:S(2)}) copy-start(bf16[2,32,1152]{2,1,0:T(8,128)(2,1)S(1)} %collective-permute-done.4) | copy-start | bytes 442372
  48.3 0.7 copy-start.9
  49.1 17.0 %collective-permute-start.8 = (bf16[256,1024]{1,0:T(8,128)(2,1)S(1)}, bf16[256,1024]{1,0:T(8,128)(2,1)S(1)}, u32[]{:S(2)}, u32[]{:S(2)}) collective-permute-start(bf16[256,1024]{1,0:T(8,128)(2,1)S(1)} %pad_maximum_fusion.1.refs_3_), channel_id=1, source_target_pairs={{0,384},{128,0},{256,128},{384,256},{1,385},{129,1},{257,129},{385... | collective-permute-start | bytes 1572872 | tf_op jit(solution)/shard_map/ppermute | solution.py:257
  53.8 9.1 %copy-start.8 = (bf16[4,32,1152]{2,1,0:T(8,128)(2,1)}, bf16[4,32,1152]{2,1,0:T(8,128)(2,1)S(1)}, u32[]{:S(2)}) copy-start(bf16[4,32,1152]{2,1,0:T(8,128)(2,1)S(1)} %collective-permute-done.1) | copy-start | bytes 884740
  53.9 17.9 %collective-permute-start.5 = (bf16[256,1024]{1,0:T(8,128)(2,1)S(1)}, bf16[256,1024]{1,0:T(8,128)(2,1)S(1)}, u32[]{:S(2)}, u32[]{:S(2)}) collective-permute-start(bf16[256,1024]{1,0:T(8,128)(2,1)S(1)} %pad_maximum_fusion.refs_2_), channel_id=1, source_target_pairs={{0,128},{128,256},{256,384},{384,0},{1,129},{129,257},{257,385},{3... | collective-permute-start | bytes 1572872 | tf_op jit(solution)/shard_map/ppermute | solution.py:257
  55.8 27.2 %collective-permute-start.6 = (bf16[256,1024]{1,0:T(8,128)(2,1)S(1)}, bf16[256,1024]{1,0:T(8,128)(2,1)S(1)}, u32[]{:S(2)}, u32[]{:S(2)}) collective-permute-start(bf16[256,1024]{1,0:T(8,128)(2,1)S(1)} %pad_maximum_fusion.1.refs_3_), channel_id=1, source_target_pairs={{0,128},{128,256},{256,384},{384,0},{1,129},{129,257},{257,385},{3... | collective-permute-start | bytes 1572872 | tf_op jit(solution)/shard_map/ppermute | solution.py:257
  58.5 24.6 %collective-permute-start.7 = (bf16[256,1024]{1,0:T(8,128)(2,1)S(1)}, bf16[256,1024]{1,0:T(8,128)(2,1)}, u32[]{:S(2)}, u32[]{:S(2)}) collective-permute-start(bf16[256,1024]{1,0:T(8,128)(2,1)S(1)} %pad_maximum_fusion.refs_2_), channel_id=1, source_target_pairs={{0,384},{128,0},{256,128},{384,256},{1,385},{129,1},{257,129},{385... | collective-permute-start | bytes 1572872 | tf_op jit(solution)/shard_map/ppermute | solution.py:257
  66.1 21.5 %collective-permute-start.10 = (bf16[256,1024]{1,0:T(8,128)(2,1)S(1)}, bf16[256,1024]{1,0:T(8,128)(2,1)S(1)}, u32[]{:S(2)}, u32[]{:S(2)}) collective-permute-start(bf16[256,1024]{1,0:T(8,128)(2,1)S(1)} %collective-permute-done.8.refs_7_), channel_id=1, source_target_pairs={{0,384},{128,0},{256,128},{384,256},{1,385},{129,1},{257,129},{385... | collective-permute-start | bytes 1572872 | tf_op jit(solution)/shard_map/ppermute | solution.py:257
  71.8 21.2 %collective-permute-start.9 = (bf16[256,1024]{1,0:T(8,128)(2,1)S(1)}, bf16[256,1024]{1,0:T(8,128)(2,1)}, u32[]{:S(2)}, u32[]{:S(2)}) collective-permute-start(bf16[256,1024]{1,0:T(8,128)(2,1)S(1)} %collective-permute-done.5.refs_4_), channel_id=1, source_target_pairs={{0,128},{128,256},{256,384},{384,0},{1,129},{129,257},{257,385},{3... | collective-permute-start | bytes 1572872 | tf_op jit(solution)/shard_map/ppermute | solution.py:257
  83.1 10.0 %copy-start.1 = (bf16[4,256,512]{2,1,0:T(8,128)(2,1)S(1)}, bf16[4,256,512]{2,1,0:T(8,128)(2,1)}, u32[]{:S(2)}) copy-start(bf16[4,256,512]{2,1,0:T(8,128)(2,1)} %copy-done) | copy-start | bytes 3145732
  93.1 4.2 %copy-start.3 = (s32[1,256,4]{1,2,0:T(4,128)S(1)}, s32[1,256,4]{1,2,0:T(4,128)}, u32[]{:S(2)}) copy-start(s32[1,256,4]{1,2,0:T(4,128)} %param.5) | copy-start | bytes 12292
  95.3 3.8 %collective-permute-start.11 = (bf16[256,1024]{1,0:T(8,128)(2,1)S(1)}, bf16[256,1024]{1,0:T(8,128)(2,1)S(1)}, u32[]{:S(2)}, u32[]{:S(2)}) collective-permute-start(bf16[256,1024]{1,0:T(8,128)(2,1)S(1)} %get-tuple-element.18), channel_id=1, source_target_pairs={{0,64},{64,0},{1,65},{65,1},{2,66},{66,2},{3,67},{67,3},{4,68},{68... | collective-permute-start | bytes 1572872 | tf_op jit(solution)/shard_map/ppermute | solution.py:310
  99.1 9.8 %copy-start.5 = (bf16[2,32,1152]{2,1,0:T(8,128)(2,1)S(1)}, bf16[2,32,1152]{2,1,0:T(8,128)(2,1)}, u32[]{:S(2)}) copy-start(bf16[2,32,1152]{2,1,0:T(8,128)(2,1)} %copy-done.4) | copy-start | bytes 442372
  99.1 9.8 %copy-start.7 = (bf16[2,32,1152]{2,1,0:T(8,128)(2,1)S(1)}, bf16[2,32,1152]{2,1,0:T(8,128)(2,1)}, u32[]{:S(2)}) copy-start(bf16[2,32,1152]{2,1,0:T(8,128)(2,1)} %copy-done.6) | copy-start | bytes 442372
  100.8 57.5 %all-to-all-start = ((bf16[16,128,256]{2,1,0:T(8,128)(2,1)}), bf16[16,128,256]{2,1,0:T(8,128)(2,1)S(1)}, u32[]{:S(2)}, u32[]{:S(2)}) async-start(bf16[16,128,256]{2,1,0:T(8,128)(2,1)} %shard_map.41), calls=%async_computation | async-start | bytes 2097152 | tf_op jit(solution)/shard_map/all_to_all | solution.py:314

commit v8 on v7

--- a/solution.py
+++ b/solution.py
@@ -6,6 +6,7 @@
 from jax.sharding import PartitionSpec as P
 
 CLUSTERS = 64
+GROUPS = 2
 BF16 = jnp.bfloat16
 F32 = jnp.float32
 VMEM_LIMIT = 48 * 1024 * 1024
@@ -152,11 +153,11 @@
                 for i, (kind, number) in enumerate(blocks):
                     device = lax.rem(me_ref[0] + kind, classes) + classes * number
                     at = pl.multiple_of(device * shard, shard)
-                    weight_ref[pl.ds(at, shard), :] = ref[i * shard : (i + 1) * shard, :]
+                    weight_ref[n, pl.ds(at, shard), :] = ref[i * shard : (i + 1) * shard, :]
             chip = lax.rem(x_ref[0] + step + chips, chips)
             for i, token_ref in enumerate(token_refs):
                 results[i] += jnp.dot(
-                    token_ref[chip], weight_ref[...], preferred_element_type=F32
+                    token_ref[chip], weight_ref[n], preferred_element_type=F32
                 )
         for result, out_ref in zip(results, out_refs):
             out_ref[...] = result.astype(out_ref.dtype)
@@ -166,27 +167,27 @@
         kernel,
         tuple(jax.ShapeDtypeStruct((rows, width), t) for t in out_types),
         (True, True) + (False,) * len(operands),
-        scratch_shapes=[pltpu.VMEM((half, width), BF16)],
+        scratch_shapes=[pltpu.VMEM((len(steps), half, width), BF16)],
     )(scalar(x), scalar(me), *operands)
 
 
-def pack(own, received, slot_row, owners, capacity, head_dim):
+def pack(own, received, slot_row, chosen, owners, capacity, head_dim):
     rows, width = own.shape
-    heads = slot_row.shape[0]
+    heads = len(chosen)
     slots = owners * capacity
 
     def kernel(own_ref, received_ref, slot_ref, out_ref):
-        for h in range(heads):
+        for i, h in enumerate(chosen):
             place = iota((slots, rows), 0) == slot_ref[h : h + 1, :]
             place = place.astype(BF16)
             for m in range(2):
-                cols = slice((m * heads + h) * head_dim, (m * heads + h + 1) * head_dim)
+                cols = slice((m * heads + i) * head_dim, (m * heads + i + 1) * head_dim)
                 total = own_ref[:, cols] + received_ref[:, cols].astype(F32)
                 packed = jnp.dot(
                     place, total.astype(BF16), preferred_element_type=F32
                 ).astype(BF16)
                 out_ref[
-                    :, h * capacity : (h + 1) * capacity, m * head_dim : (m + 1) * head_dim
+                    :, i * capacity : (i + 1) * capacity, m * head_dim : (m + 1) * head_dim
                 ] = packed.reshape(owners, capacity, head_dim)
 
     return vmem_call(
@@ -196,18 +197,23 @@
     )(own, received, slot_row)
 
 
-def attend(blocks, members, capacity):
+def attend(blocks, members, chosen, before, capacity):
     sources, rows, width = blocks.shape
     head_dim = width // 2
-    heads = rows // capacity
     slots = sources * capacity
     scale = head_dim ** (-0.5)
-
-    def kernel(block_ref, member_ref, out_ref):
+    done = 0 if before is None else before.shape[1]
+    given = () if before is None else (before,)
+
+    def kernel(*refs):
+        block_ref, member_ref = refs[:2]
+        out_ref = refs[-1]
+        if given:
+            out_ref[:, :done, :] = refs[2][...]
         query = iota((slots, slots), 0)
         key = iota((slots, slots), 1)
-        for h in range(heads):
-            here = slice(h * capacity, (h + 1) * capacity)
+        for i, h in enumerate(chosen):
+            here = slice(i * capacity, (i + 1) * capacity)
             keys = block_ref[:, here, :head_dim].reshape(slots, head_dim)
             values = block_ref[:, here, head_dim:].reshape(slots, head_dim)
             member = member_ref[h]
@@ -224,11 +230,14 @@
             total = jnp.sum(weights, axis=1, keepdims=True)
             probabilities = (weights / total).astype(BF16)
             result = jnp.dot(probabilities, values, preferred_element_type=F32).astype(BF16)
-            out_ref[:, here, :] = result.reshape(sources, capacity, head_dim)
-
-    return vmem_call(
-        kernel, jax.ShapeDtypeStruct((sources, rows, head_dim), BF16), (False, False)
-    )(blocks, members)
+            there = slice(done + i * capacity, done + (i + 1) * capacity)
+            out_ref[:, there, :] = result.reshape(sources, capacity, head_dim)
+
+    return vmem_call(
+        kernel,
+        jax.ShapeDtypeStruct((sources, done + rows, head_dim), BF16),
+        (False,) * (2 + len(given)),
+    )(blocks, members, *given)
 
 
 def unpack(returned, slot_col, capacity):
@@ -269,20 +278,14 @@
     capacity = 2 * rows // owners
     chips = lax.axis_size("x")
 
+    own = proj_weight.reshape(shard, 2, GROUPS, -1).transpose(0, 2, 1, 3)
     ids = clusters[0].T.astype(BF16).reshape(-1, 128)
     ids = jnp.pad(ids, ((0, shard - ids.shape[0]), (0, 0)))
-    own = jnp.concatenate([proj_weight.reshape(shard, width), ids], axis=1)
+    own = jnp.concatenate([own.reshape(shard, width), ids], axis=1)
     four = lax.all_gather(own, "zq", axis=0)
     below = shifted(four, 1, CLU)
     above = shifted(four, -1, CLU)
     beyond = [shifted(four[:2], 2, CLU), shifted(four[2:], -2, CLU)]
-
-    def weights_of(parts):
-        parts = [part[:, :, :width].reshape(-1, width) for part in parts]
-        return jnp.concatenate(parts, axis=0)
-
-    first = weights_of([four, below])
-    second = weights_of([above] + beyond)
     places = (
         [(0, j) for j in range(4)] + [(3, j) for j in range(4)],
         [(1, j) for j in range(4)] + [(2, j) for j in range(4)],
@@ -290,28 +293,45 @@
 
     mine, send = cut_tokens(tokens[0], lax.axis_index("core"), chips)
     both = (mine, lax.ppermute(send, "core", [(0, 1), (1, 0)]))
-
-    first_below, first_above = shifted(first, 1, "x"), shifted(first, -1, "x")
-    second_below, second_above = shifted(second, 1, "x"), shifted(second, -1, "x")
-    first_far, second_far = shifted(first_below, 1, "x"), shifted(second_above, -1, "x")
-    total = products(
-        None,
-        both,
-        [first, second, first_below, second_below, first_above, second_above],
-        (0, -1, 1),
-        x,
-        me,
-        places,
-        (F32, F32),
-    )
-    kept, given = products(
-        total, both, [first_far, second_far], (2,), x, me, places, (F32, BF16)
-    )
-    received = lax.ppermute(given, "core", [(0, 1), (1, 0)])
-
     slot_row, slot_col = routing(clusters[0], owners, capacity)
-    outgoing = pack(kept, received, slot_row, owners, capacity, head_dim)
-    incoming = lax.all_to_all(outgoing, CLU, split_axis=0, concat_axis=0, tiled=True)
+
+    def partial_sums(first, second):
+        first_below, first_above = shifted(first, 1, "x"), shifted(first, -1, "x")
+        second_below, second_above = shifted(second, 1, "x"), shifted(second, -1, "x")
+        first_far, second_far = shifted(first_below, 1, "x"), shifted(second_above, -1, "x")
+        total = products(
+            None,
+            both,
+            [first, second, first_below, second_below, first_above, second_above],
+            (0, -1, 1),
+            x,
+            me,
+            places,
+            (F32, F32),
+        )
+        kept, given = products(
+            total, both, [first_far, second_far], (2,), x, me, places, (F32, BF16)
+        )
+        return kept, lax.ppermute(given, "core", [(0, 1), (1, 0)])
+
+    incoming = []
+    outgoing = None
+    for g in range(GROUPS):
+        group_width = width // GROUPS
+        cols = slice(g * group_width, (g + 1) * group_width)
+        chosen = range(g * heads // GROUPS, (g + 1) * heads // GROUPS)
+        parts = (four, below, above, *beyond)
+        if outgoing is not None:
+            parts, outgoing = lax.optimization_barrier((parts, outgoing))
+            incoming.append(
+                lax.all_to_all(outgoing, CLU, split_axis=0, concat_axis=0, tiled=True)
+            )
+        parts = [part[:, :, cols].reshape(-1, group_width) for part in parts]
+        kept, received = partial_sums(
+            jnp.concatenate(parts[:2], axis=0), jnp.concatenate(parts[2:], axis=0)
+        )
+        outgoing = pack(kept, received, slot_row, chosen, owners, capacity, head_dim)
+    incoming.append(lax.all_to_all(outgoing, CLU, split_axis=0, concat_axis=0, tiled=True))
 
     by_class = jnp.stack(
         [part[:, :16, width:] for part in (four, above, jnp.concatenate(beyond), below)]
@@ -319,7 +339,10 @@
     by_class = jnp.roll(by_class, lax.axis_index("zr"), axis=0)
     all_ids = by_class.transpose(1, 0, 2, 3).reshape((owners,) + by_class.shape[2:])
     members = owned_members(all_ids, me, heads, capacity)
-    replies = attend(incoming, members, capacity)
+    replies = None
+    for g in range(GROUPS):
+        chosen = range(g * heads // GROUPS, (g + 1) * heads // GROUPS)
+        replies = attend(incoming[g], members, chosen, replies, capacity)
     returned = lax.all_to_all(replies, CLU, split_axis=0, concat_axis=0, tiled=True)
     return unpack(returned, slot_col, capacity)[None]
 

time: 200 us -> 213 us (1.065)
  starting transfers between devices: 46.4 us -> 77.1 us
  waiting for transfers between devices: 66.3 us -> 43 us
  local copies, waits for them, and re-layouts: 6.36 us -> 11.4 us
    all_to_all x1 -> x2, waiting for transfers between devices: 46.1 us -> 22 us  [body(): lax.all_to_all(outgoing, CLU, split_axis=0, concat_axis=0, tiled=True)]
    ppermute x10 -> x16, starting transfers between devices: 35.3 us -> 52.4 us  [shifted(): lax.ppermute(block, axis, [(i, (i + step) % size) for i in range(size)])]
    all_to_all x1 -> x2, starting transfers between devices: 7.3 us -> 18.7 us  [body(): lax.all_to_all(outgoing, CLU, split_axis=0, concat_axis=0, tiled=True)]
    slice x5 -> x11, local copies, waits for them, and re-layouts: 0.08 us -> 3.7 us  [body(): parts = [part[:, :, cols].reshape(-1, group_width) for part in parts]]
    ppermute x1 -> x2, starting transfers between devices: 1.92 us -> 4.09 us  [partial_sums(): return (kept, lax.ppermute(given, 'core', [(0, 1), (1, 0)]))]
    unnamed x27 -> x18, local copies, waits for them, and re-layouts: 5.38 us -> 5.97 us
    pallas_call x2 -> x4, Pallas kernels: 6.33 us -> 5.76 us  [products(): vmem_call(kernel, tuple((jax.ShapeDtypeStruct((rows, width), t) for t in...]
    ppermute x10 -> x16, waiting for transfers between devices: 19.1 us -> 18.7 us  [shifted(): lax.ppermute(block, axis, [(i, (i + step) % size) for i in range(size)])]
  transfers between devices with their start and end apart: 13 -> 21, of which waited for: 8 -> 11; matrix products, arithmetic and copies ran while one was open for 2% -> 4% of each run, Pallas kernels for 4% -> 5%
where the time goes in v8:
time: 213 us; the launch traced here: 211 us
  starting transfers between devices  77.1 us (36%)
  blocking collectives  62.5 us (29%)
  waiting for transfers between devices  43 us (20%)
  Pallas kernels  16 us (8%)
  local copies, waits for them, and re-layouts  11.4 us (5%)
    ppermute x16, starting transfers between devices, shifted(): lax.ppermute(block, axis, [(i, (i + step) % size) for i in range(size)])  52.4 us
    all_to_all x1, blocking collectives, body(): lax.all_to_all(replies, CLU, split_axis=0, concat_axis=0, tiled=True)  35.4 us
    all_gather x1, blocking collectives, body(): four = lax.all_gather(own, 'zq', axis=0)  27.1 us
    all_to_all x2, waiting for transfers between devices, body(): lax.all_to_all(outgoing, CLU, split_axis=0, concat_axis=0, tiled=True)  22 us
    ppermute x16, waiting for transfers between devices, shifted(): lax.ppermute(block, axis, [(i, (i + step) % size) for i in range(size)])  18.7 us
    all_to_all x2, starting transfers between devices, body(): lax.all_to_all(outgoing, CLU, split_axis=0, concat_axis=0, tiled=True)  18.7 us
    unnamed x18, local copies, waits for them, and re-layouts  5.97 us
    pallas_call x4, Pallas kernels, products(): vmem_call(kernel, tuple((jax.ShapeDtypeStruct((rows, width), t) for t in...  5.76 us
  transfers between devices with their start and end apart: 21, of which 11 were waited for; matrix products, arithmetic and copies ran while one was open for 4% of the time, Pallas kernels for 5%

profile of v8, /device:TPU:24, one launch (start us, length us, event | category | flops | bytes accessed | tf_op | source)
XLA Modules:
  0.0 211.3 jit_solution(3031261449698066513)
XLA Ops:
  1.6 27.1 %all-gather = bf16[128,1152]{1,0:T(8,128)(2,1)S(1)} all-gather(bf16[32,1152]{1,0:T(8,128)(2,1)S(1)} %fusion.1), channel_id=2, replica_groups=mesh['x'=4,'core'=2,'zq'=4,'zr'=4,'tp'=4] {'zq'}, dimensions={0}, use_global_device_ids=true | all-gather | bytes 368640 | tf_op jit(solution)/shard_map/all_gather | solution.py:285
  28.7 4.2 %collective-permute-start.2 = (bf16[4,32,1152]{2,1,0:T(8,128)(2,1)S(1)}, bf16[4,32,1152]{2,1,0:T(8,128)(2,1)S(1)}, u32[]{:S(2)}, u32[]{:S(2)}) collective-permute-start(bf16[4,32,1152]{2,1,0:T(8,128)(2,1)S(1)} %bitcast.57), channel_id=1, source_target_pairs={{0,60},{4,0},{8,4},{12,8},{16,12},{20,16},{24,20},{28,24},{32,28},... | collective-permute-start | bytes 884744 | tf_op jit(solution)/shard_map/ppermute | solution.py:266
  39.7 4.0 %collective-permute-start.3 = (bf16[2,32,1152]{2,1,0:T(8,128)(2,1)S(1)}, bf16[2,32,1152]{2,1,0:T(8,128)(2,1)S(1)}, u32[]{:S(2)}, u32[]{:S(2)}) collective-permute-start(bf16[2,32,1152]{2,1,0:T(8,128)(2,1)S(1)} %bitcast.74), channel_id=1, source_target_pairs={{0,8},{4,12},{8,16},{12,20},{16,24},{20,28},{24,32},{28,36},{32,40... | collective-permute-start | bytes 442376 | tf_op jit(solution)/shard_map/ppermute | solution.py:266
  43.7 3.9 %collective-permute-start.4 = (bf16[2,32,1152]{2,1,0:T(8,128)(2,1)S(1)}, bf16[2,32,1152]{2,1,0:T(8,128)(2,1)S(1)}, u32[]{:S(2)}, u32[]{:S(2)}) collective-permute-start(bf16[2,32,1152]{2,1,0:T(8,128)(2,1)S(1)} %bitcast.73), channel_id=1, source_target_pairs={{0,56},{4,60},{8,0},{12,4},{16,8},{20,12},{24,16},{28,20},{32,24},... | collective-permute-start | bytes 442376 | tf_op jit(solution)/shard_map/ppermute | solution.py:266
  47.7 5.5 %collective-permute-done.3 = bf16[2,32,1152]{2,1,0:T(8,128)(2,1)S(1)} collective-permute-done((bf16[2,32,1152]{2,1,0:T(8,128)(2,1)S(1)}, bf16[2,32,1152]{2,1,0:T(8,128)(2,1)S(1)}, u32[]{:S(2)}, u32[]{:S(2)}) %collective-permute-start.3) | collective-permute-done | bytes 147488 | tf_op jit(solution)/shard_map/ppermute | solution.py:266
  53.2 2.6 %collective-permute-done.4 = bf16[2,32,1152]{2,1,0:T(8,128)(2,1)S(1)} collective-permute-done((bf16[2,32,1152]{2,1,0:T(8,128)(2,1)S(1)}, bf16[2,32,1152]{2,1,0:T(8,128)(2,1)S(1)}, u32[]{:S(2)}, u32[]{:S(2)}) %collective-permute-start.4) | collective-permute-done | bytes 147488 | tf_op jit(solution)/shard_map/ppermute | solution.py:266
  56.5 4.7 %collective-permute-start.8 = (bf16[256,512]{1,0:T(8,128)(2,1)S(1)}, bf16[256,512]{1,0:T(8,128)(2,1)S(1)}, u32[]{:S(2)}, u32[]{:S(2)}) collective-permute-start(bf16[256,512]{1,0:T(8,128)(2,1)S(1)} %pad_maximum_fusion.1.refs_3_), channel_id=1, source_target_pairs={{0,384},{128,0},{256,128},{384,256},{1,385},{129,1},{257,129},{385... | collective-permute-start | bytes 786440 | tf_op jit(solution)/shard_map/ppermute | solution.py:266
  64.1 2.7 %collective-permute-start.6 = (bf16[256,512]{1,0:T(8,128)(2,1)S(1)}, bf16[256,512]{1,0:T(8,128)(2,1)}, u32[]{:S(2)}, u32[]{:S(2)}) collective-permute-start(bf16[256,512]{1,0:T(8,128)(2,1)S(1)} %pad_maximum_fusion.1.refs_3_), channel_id=1, source_target_pairs={{0,128},{128,256},{256,384},{384,0},{1,129},{129,257},{257,385},{3... | collective-permute-start | bytes 786440 | tf_op jit(solution)/shard_map/ppermute | solution.py:266
  66.8 4.4 %collective-permute-start.7 = (bf16[256,512]{1,0:T(8,128)(2,1)S(1)}, bf16[256,512]{1,0:T(8,128)(2,1)}, u32[]{:S(2)}, u32[]{:S(2)}) collective-permute-start(bf16[256,512]{1,0:T(8,128)(2,1)S(1)} %pad_maximum_fusion.refs_2_), channel_id=1, source_target_pairs={{0,384},{128,0},{256,128},{384,256},{1,385},{129,1},{257,129},{385... | collective-permute-start | bytes 786440 | tf_op jit(solution)/shard_map/ppermute | solution.py:266
  71.2 3.9 %collective-permute-start.10 = (bf16[256,512]{1,0:T(8,128)(2,1)S(1)}, bf16[256,512]{1,0:T(8,128)(2,1)S(1)}, u32[]{:S(2)}, u32[]{:S(2)}) collective-permute-start(bf16[256,512]{1,0:T(8,128)(2,1)S(1)} %collective-permute-done.8.refs_7_), channel_id=1, source_target_pairs={{0,384},{128,0},{256,128},{384,256},{1,385},{129,1},{257,129},{385... | collective-permute-start | bytes 786440 | tf_op jit(solution)/shard_map/ppermute | solution.py:266
  77.8 2.1 shard_map.38
  80.6 4.0 %collective-permute-done.9.refs_4_ = bf16[256,512]{1,0:T(8,128)(2,1)} collective-permute-done((bf16[256,512]{1,0:T(8,128)(2,1)S(1)}, bf16[256,512]{1,0:T(8,128)(2,1)}, u32[]{:S(2)}, u32[]{:S(2)}) %collective-permute-start.9) | collective-permute-done | bytes 262176 | tf_op jit(solution)/shard_map/ppermute | solution.py:266
  84.7 2.1 %shard_map.39 = (f32[256,512]{1,0:T(8,128)S(1)}, bf16[256,512]{1,0:T(8,128)(2,1)}) custom-call(s32[1]{0:T(128)} %bitcast.x_ref, s32[1]{0:T(128)} %bitcast.1.me_ref, f32[256,512]{1,0:T(8,128)S(1)} %get-tuple-element.25.refs_0_, f32[256,512]{1,0:T(8,128)S(1)} %get-tuple-element.26.refs_1_, bf16[4,256,512]{2,1,0:T(8,128)(2,1)S(1)} %get-tuple-element.23.refs_0_.refs_2_, ...), custom_call_target="tpu_custom_call" | custom-call | tf_op jit(solution)/shard_map/pallas_call | solution.py:166
  91.8 6.9 %all-to-all-start.1 = ((bf16[16,64,256]{2,1,0:T(8,128)(2,1)}), bf16[16,64,256]{2,1,0:T(8,128)(2,1)S(1)}, u32[]{:S(2)}, u32[]{:S(2)}) async-start(bf16[16,64,256]{2,1,0:T(8,128)(2,1)} %shard_map.41), calls=%async_computation.1 | async-start | bytes 1048576 | tf_op jit(solution)/shard_map/all_to_all | solution.py:327
  99.8 2.3 %collective-permute-start.15 = (bf16[256,512]{1,0:T(8,128)(2,1)S(1)}, bf16[256,512]{1,0:T(8,128)(2,1)S(1)}, u32[]{:S(2)}, u32[]{:S(2)}) collective-permute-start(bf16[256,512]{1,0:T(8,128)(2,1)S(1)} %pad_maximum_fusion.3.refs_3_), channel_id=1, source_target_pairs={{0,384},{128,0},{256,128},{384,256},{1,385},{129,1},{257,129},{385... | collective-permute-start | bytes 786440 | tf_op jit(solution)/shard_map/ppermute | solution.py:266
  103.9 3.6 %collective-permute-start.12 = (bf16[256,512]{1,0:T(8,128)(2,1)S(1)}, bf16[256,512]{1,0:T(8,128)(2,1)S(1)}, u32[]{:S(2)}, u32[]{:S(2)}) collective-permute-start(bf16[256,512]{1,0:T(8,128)(2,1)S(1)} %pad_maximum_fusion.2.refs_2_), channel_id=1, source_target_pairs={{0,128},{128,256},{256,384},{384,0},{1,129},{129,257},{257,385},{3... | collective-permute-start | bytes 786440 | tf_op jit(solution)/shard_map/ppermute | solution.py:266
  109.4 5.1 %collective-permute-start.14 = (bf16[256,512]{1,0:T(8,128)(2,1)S(1)}, bf16[256,512]{1,0:T(8,128)(2,1)S(1)}, u32[]{:S(2)}, u32[]{:S(2)}) collective-permute-start(bf16[256,512]{1,0:T(8,128)(2,1)S(1)} %pad_maximum_fusion.2.refs_2_), channel_id=1, source_target_pairs={{0,384},{128,0},{256,128},{384,256},{1,385},{129,1},{257,129},{385... | collective-permute-start | bytes 786440 | tf_op jit(solution)/shard_map/ppermute | solution.py:266
  114.6 2.3 %collective-permute-start.17 = (bf16[256,512]{1,0:T(8,128)(2,1)S(1)}, bf16[256,512]{1,0:T(8,128)(2,1)S(1)}, u32[]{:S(2)}, u32[]{:S(2)}) collective-permute-start(bf16[256,512]{1,0:T(8,128)(2,1)S(1)} %collective-permute-done.15.refs_7_), channel_id=1, source_target_pairs={{0,384},{128,0},{256,128},{384,256},{1,385},{129,1},{257,129},{385... | collective-permute-start | bytes 786440 | tf_op jit(solution)/shard_map/ppermute | solution.py:266
  116.9 3.6 %collective-permute-start.16 = (bf16[256,512]{1,0:T(8,128)(2,1)S(1)}, bf16[256,512]{1,0:T(8,128)(2,1)S(1)}, u32[]{:S(2)}, u32[]{:S(2)}) collective-permute-start(bf16[256,512]{1,0:T(8,128)(2,1)S(1)} %collective-permute-done.12.refs_4_), channel_id=1, source_target_pairs={{0,128},{128,256},{256,384},{384,0},{1,129},{129,257},{257,385},{3... | collective-permute-start | bytes 786440 | tf_op jit(solution)/shard_map/ppermute | solution.py:266
  122.4 2.5 %collective-permute-done.17.refs_5_ = bf16[256,512]{1,0:T(8,128)(2,1)S(1)} collective-permute-done((bf16[256,512]{1,0:T(8,128)(2,1)S(1)}, bf16[256,512]{1,0:T(8,128)(2,1)S(1)}, u32[]{:S(2)}, u32[]{:S(2)}) %collective-permute-start.17) | collective-permute-done | bytes 262176 | tf_op jit(solution)/shard_map/ppermute | solution.py:266
  127.1 2.1 collective-permute-start.18
  131.9 11.7 %all-to-all-start = ((bf16[16,64,256]{2,1,0:T(8,128)(2,1)}), bf16[16,64,256]{2,1,0:T(8,128)(2,1)S(1)}, u32[]{:S(2)}, u32[]{:S(2)}) async-start(bf16[16,64,256]{2,1,0:T(8,128)(2,1)} %shard_map.44), calls=%async_computation | async-start | bytes 1048576 | tf_op jit(solution)/shard_map/all_to_all | solution.py:334
  151.0 22.0 %all-to-all-done.refs_0_ = bf16[16,64,256]{2,1,0:T(8,128)(2,1)S(1)} async-done(((bf16[16,64,256]{2,1,0:T(8,128)(2,1)}), bf16[16,64,256]{2,1,0:T(8,128)(2,1)S(1)}, u32[]{:S(2)}, u32[]{:S(2)}) %all-to-all-start) | async-done | bytes 524320 | tf_op jit(solution)/shard_map/all_to_all | solution.py:334
  174.7 35.4 %all_to_all.15.block_ref = bf16[16,128,128]{2,1,0:T(8,128)(2,1)S(1)} all-to-all(bf16[16,128,128]{2,1,0:T(8,128)(2,1)S(1)} %shard_map.47), channel_id=1, replica_groups=mesh['x'=4,'core'=2,'zq'=4,'zr'=4,'tp'=4] {'zq','zr'}, dimensions={0} | all-to-all | bytes 1048576 | tf_op jit(solution)/shard_map/all_to_all | solution.py:346
  (74 shorter events, 42.2 us)
Async XLA Ops:
  28.7 33.4 %copy-start.2 = (bf16[128,1152]{1,0:T(8,128)(2,1)}, bf16[128,1152]{1,0:T(8,128)(2,1)S(1)}, u32[]{:S(2)}) copy-start(bf16[128,1152]{1,0:T(8,128)(2,1)S(1)} %all-gather) | copy-start | bytes 884740
  28.7 27.0 %collective-permute-start.2 = (bf16[4,32,1152]{2,1,0:T(8,128)(2,1)S(1)}, bf16[4,32,1152]{2,1,0:T(8,128)(2,1)S(1)}, u32[]{:S(2)}, u32[]{:S(2)}) collective-permute-start(bf16[4,32,1152]{2,1,0:T(8,128)(2,1)S(1)} %bitcast.57), channel_id=1, source_target_pairs={{0,60},{4,0},{8,4},{12,8},{16,12},{20,16},{24,20},{28,24},{32,28},... | collective-permute-start | bytes 884744 | tf_op jit(solution)/shard_map/ppermute | solution.py:266
  32.9 28.3 %collective-permute-start.1 = (bf16[4,32,1152]{2,1,0:T(8,128)(2,1)S(1)}, bf16[4,32,1152]{2,1,0:T(8,128)(2,1)}, u32[]{:S(2)}, u32[]{:S(2)}) collective-permute-start(bf16[4,32,1152]{2,1,0:T(8,128)(2,1)S(1)} %bitcast.58), channel_id=1, source_target_pairs={{0,4},{4,8},{8,12},{12,16},{16,20},{20,24},{24,28},{28,32},{32,36}... | collective-permute-start | bytes 884744 | tf_op jit(solution)/shard_map/ppermute | solution.py:266
  37.7 40.1 %collective-permute-start = (bf16[4,256,512]{2,1,0:T(8,128)(2,1)}, bf16[4,256,512]{2,1,0:T(8,128)(2,1)S(1)}, u32[]{:S(2)}, u32[]{:S(2)}) collective-permute-start(bf16[4,256,512]{2,1,0:T(8,128)(2,1)} %get-tuple-element.24), channel_id=1, source_target_pairs={{0,64},{64,0},{1,65},{65,1},{2,66},{66,2},{3,67},{67,3},{4,68},{68... | collective-permute-start | bytes 3145736 | tf_op jit(solution)/shard_map/ppermute | solution.py:295
  39.7 13.5 %collective-permute-start.3 = (bf16[2,32,1152]{2,1,0:T(8,128)(2,1)S(1)}, bf16[2,32,1152]{2,1,0:T(8,128)(2,1)S(1)}, u32[]{:S(2)}, u32[]{:S(2)}) collective-permute-start(bf16[2,32,1152]{2,1,0:T(8,128)(2,1)S(1)} %bitcast.74), channel_id=1, source_target_pairs={{0,8},{4,12},{8,16},{12,20},{16,24},{20,28},{24,32},{28,36},{32,40... | collective-permute-start | bytes 442376 | tf_op jit(solution)/shard_map/ppermute | solution.py:266
  43.7 12.0 %collective-permute-start.4 = (bf16[2,32,1152]{2,1,0:T(8,128)(2,1)S(1)}, bf16[2,32,1152]{2,1,0:T(8,128)(2,1)S(1)}, u32[]{:S(2)}, u32[]{:S(2)}) collective-permute-start(bf16[2,32,1152]{2,1,0:T(8,128)(2,1)S(1)} %bitcast.73), channel_id=1, source_target_pairs={{0,56},{4,60},{8,0},{12,4},{16,8},{20,12},{24,16},{28,20},{32,24},... | collective-permute-start | bytes 442376 | tf_op jit(solution)/shard_map/ppermute | solution.py:266
  56.5 14.7 %collective-permute-start.8 = (bf16[256,512]{1,0:T(8,128)(2,1)S(1)}, bf16[256,512]{1,0:T(8,128)(2,1)S(1)}, u32[]{:S(2)}, u32[]{:S(2)}) collective-permute-start(bf16[256,512]{1,0:T(8,128)(2,1)S(1)} %pad_maximum_fusion.1.refs_3_), channel_id=1, source_target_pairs={{0,384},{128,0},{256,128},{384,256},{1,385},{129,1},{257,129},{385... | collective-permute-start | bytes 786440 | tf_op jit(solution)/shard_map/ppermute | solution.py:266
  62.1 12.9 %collective-permute-start.5 = (bf16[256,512]{1,0:T(8,128)(2,1)S(1)}, bf16[256,512]{1,0:T(8,128)(2,1)S(1)}, u32[]{:S(2)}, u32[]{:S(2)}) collective-permute-start(bf16[256,512]{1,0:T(8,128)(2,1)S(1)} %pad_maximum_fusion.refs_2_), channel_id=1, source_target_pairs={{0,128},{128,256},{256,384},{384,0},{1,129},{129,257},{257,385},{3... | collective-permute-start | bytes 786440 | tf_op jit(solution)/shard_map/ppermute | solution.py:266
  64.1 13.0 %collective-permute-start.6 = (bf16[256,512]{1,0:T(8,128)(2,1)S(1)}, bf16[256,512]{1,0:T(8,128)(2,1)}, u32[]{:S(2)}, u32[]{:S(2)}) collective-permute-start(bf16[256,512]{1,0:T(8,128)(2,1)S(1)} %pad_maximum_fusion.1.refs_3_), channel_id=1, source_target_pairs={{0,128},{128,256},{256,384},{384,0},{1,129},{129,257},{257,385},{3... | collective-permute-start | bytes 786440 | tf_op jit(solution)/shard_map/ppermute | solution.py:266
  66.8 11.1 %collective-permute-start.7 = (bf16[256,512]{1,0:T(8,128)(2,1)S(1)}, bf16[256,512]{1,0:T(8,128)(2,1)}, u32[]{:S(2)}, u32[]{:S(2)}) collective-permute-start(bf16[256,512]{1,0:T(8,128)(2,1)S(1)} %pad_maximum_fusion.refs_2_), channel_id=1, source_target_pairs={{0,384},{128,0},{256,128},{384,256},{1,385},{129,1},{257,129},{385... | collective-permute-start | bytes 786440 | tf_op jit(solution)/shard_map/ppermute | solution.py:266
  71.2 9.5 %collective-permute-start.10 = (bf16[256,512]{1,0:T(8,128)(2,1)S(1)}, bf16[256,512]{1,0:T(8,128)(2,1)S(1)}, u32[]{:S(2)}, u32[]{:S(2)}) collective-permute-start(bf16[256,512]{1,0:T(8,128)(2,1)S(1)} %collective-permute-done.8.refs_7_), channel_id=1, source_target_pairs={{0,384},{128,0},{256,128},{384,256},{1,385},{129,1},{257,129},{385... | collective-permute-start | bytes 786440 | tf_op jit(solution)/shard_map/ppermute | solution.py:266
  75.1 9.6 %collective-permute-start.9 = (bf16[256,512]{1,0:T(8,128)(2,1)S(1)}, bf16[256,512]{1,0:T(8,128)(2,1)}, u32[]{:S(2)}, u32[]{:S(2)}) collective-permute-start(bf16[256,512]{1,0:T(8,128)(2,1)S(1)} %collective-permute-done.5.refs_4_), channel_id=1, source_target_pairs={{0,128},{128,256},{256,384},{384,0},{1,129},{129,257},{257,385},{3... | collective-permute-start | bytes 786440 | tf_op jit(solution)/shard_map/ppermute | solution.py:266
  86.8 12.9 %slice-start = ((bf16[2,32,1152]{2,1,0:T(8,128)(2,1)}), bf16[2,32,512]{2,1,0:T(8,128)(2,1)S(1)}, s32[]{:S(2)}) async-start(bf16[2,32,1152]{2,1,0:T(8,128)(2,1)} %copy-done.3), calls=%async_computation.3 | async-start | bytes 131072 | tf_op jit(solution)/shard_map/slice | solution.py:329
  86.8 3.8 %collective-permute-start.11 = (bf16[256,512]{1,0:T(8,128)(2,1)}, bf16[256,512]{1,0:T(8,128)(2,1)S(1)}, u32[]{:S(2)}, u32[]{:S(2)}) collective-permute-start(bf16[256,512]{1,0:T(8,128)(2,1)} %get-tuple-element.28), channel_id=1, source_target_pairs={{0,64},{64,0},{1,65},{65,1},{2,66},{66,2},{3,67},{67,3},{4,68},{68... | collective-permute-start | bytes 786440 | tf_op jit(solution)/shard_map/ppermute | solution.py:315
  91.8 40.1 %all-to-all-start.1 = ((bf16[16,64,256]{2,1,0:T(8,128)(2,1)}), bf16[16,64,256]{2,1,0:T(8,128)(2,1)S(1)}, u32[]{:S(2)}, u32[]{:S(2)}) async-start(bf16[16,64,256]{2,1,0:T(8,128)(2,1)} %shard_map.41), calls=%async_computation.1 | async-start | bytes 1048576 | tf_op jit(solution)/shard_map/all_to_all | solution.py:327
  99.8 14.8 %collective-permute-start.15 = (bf16[256,512]{1,0:T(8,128)(2,1)S(1)}, bf16[256,512]{1,0:T(8,128)(2,1)S(1)}, u32[]{:S(2)}, u32[]{:S(2)}) collective-permute-start(bf16[256,512]{1,0:T(8,128)(2,1)S(1)} %pad_maximum_fusion.3.refs_3_), channel_id=1, source_target_pairs={{0,384},{128,0},{256,128},{384,256},{1,385},{129,1},{257,129},{385... | collective-permute-start | bytes 786440 | tf_op jit(solution)/shard_map/ppermute | solution.py:266
  103.9 12.9 %collective-permute-start.12 = (bf16[256,512]{1,0:T(8,128)(2,1)S(1)}, bf16[256,512]{1,0:T(8,128)(2,1)S(1)}, u32[]{:S(2)}, u32[]{:S(2)}) collective-permute-start(bf16[256,512]{1,0:T(8,128)(2,1)S(1)} %pad_maximum_fusion.2.refs_2_), channel_id=1, source_target_pairs={{0,128},{128,256},{256,384},{384,0},{1,129},{129,257},{257,385},{3... | collective-permute-start | bytes 786440 | tf_op jit(solution)/shard_map/ppermute | solution.py:266
  107.5 13.0 %collective-permute-start.13 = (bf16[256,512]{1,0:T(8,128)(2,1)S(1)}, bf16[256,512]{1,0:T(8,128)(2,1)S(1)}, u32[]{:S(2)}, u32[]{:S(2)}) collective-permute-start(bf16[256,512]{1,0:T(8,128)(2,1)S(1)} %pad_maximum_fusion.3.refs_3_), channel_id=1, source_target_pairs={{0,128},{128,256},{256,384},{384,0},{1,129},{129,257},{257,385},{3... | collective-permute-start | bytes 786440 | tf_op jit(solution)/shard_map/ppermute | solution.py:266
  109.4 11.9 %collective-permute-start.14 = (bf16[256,512]{1,0:T(8,128)(2,1)S(1)}, bf16[256,512]{1,0:T(8,128)(2,1)S(1)}, u32[]{:S(2)}, u32[]{:S(2)}) collective-permute-start(bf16[256,512]{1,0:T(8,128)(2,1)S(1)} %pad_maximum_fusion.2.refs_2_), channel_id=1, source_target_pairs={{0,384},{128,0},{256,128},{384,256},{1,385},{129,1},{257,129},{385... | collective-permute-start | bytes 786440 | tf_op jit(solution)/shard_map/ppermute | solution.py:266
  114.6 10.3 %collective-permute-start.17 = (bf16[256,512]{1,0:T(8,128)(2,1)S(1)}, bf16[256,512]{1,0:T(8,128)(2,1)S(1)}, u32[]{:S(2)}, u32[]{:S(2)}) collective-permute-start(bf16[256,512]{1,0:T(8,128)(2,1)S(1)} %collective-permute-done.15.refs_7_), channel_id=1, source_target_pairs={{0,384},{128,0},{256,128},{384,256},{1,385},{129,1},{257,129},{385... | collective-permute-start | bytes 786440 | tf_op jit(solution)/shard_map/ppermute | solution.py:266
  116.9 9.8 %collective-permute-start.16 = (bf16[256,512]{1,0:T(8,128)(2,1)S(1)}, bf16[256,512]{1,0:T(8,128)(2,1)S(1)}, u32[]{:S(2)}, u32[]{:S(2)}) collective-permute-start(bf16[256,512]{1,0:T(8,128)(2,1)S(1)} %collective-permute-done.12.refs_4_), channel_id=1, source_target_pairs={{0,128},{128,256},{256,384},{384,0},{1,129},{129,257},{257,385},{3... | collective-permute-start | bytes 786440 | tf_op jit(solution)/shard_map/ppermute | solution.py:266
  127.1 18.0 %copy-start.4 = (bf16[2,32,1152]{2,1,0:T(8,128)(2,1)S(1)}, bf16[2,32,1152]{2,1,0:T(8,128)(2,1)}, u32[]{:S(2)}) copy-start(bf16[2,32,1152]{2,1,0:T(8,128)(2,1)} %copy-done.3) | copy-start | bytes 442372
  127.1 3.6 %collective-permute-start.18 = (bf16[256,512]{1,0:T(8,128)(2,1)S(1)}, bf16[256,512]{1,0:T(8,128)(2,1)S(1)}, u32[]{:S(2)}, u32[]{:S(2)}) collective-permute-start(bf16[256,512]{1,0:T(8,128)(2,1)S(1)} %get-tuple-element.38), channel_id=1, source_target_pairs={{0,64},{64,0},{1,65},{65,1},{2,66},{66,2},{3,67},{67,3},{4,68},{68... | collective-permute-start | bytes 786440 | tf_op jit(solution)/shard_map/ppermute | solution.py:315
  131.9 41.0 %all-to-all-start = ((bf16[16,64,256]{2,1,0:T(8,128)(2,1)}), bf16[16,64,256]{2,1,0:T(8,128)(2,1)S(1)}, u32[]{:S(2)}, u32[]{:S(2)}) async-start(bf16[16,64,256]{2,1,0:T(8,128)(2,1)} %shard_map.44), calls=%async_computation | async-start | bytes 1048576 | tf_op jit(solution)/shard_map/all_to_all | solution.py:334
  (4 other events, 17.7 us)

commit v9 on v7

--- a/solution.py
+++ b/solution.py
@@ -103,15 +103,15 @@
     rows, depth = local_rows.shape
     half = depth // chips // 2
 
-    def kernel(core_ref, in_ref, own_ref, other_ref, sems):
+    def kernel(core_ref, in_ref, out_ref, sems):
         copies = []
         for p in range(chips):
-            for j, out_ref in enumerate((own_ref, other_ref)):
+            for j in range(2):
                 first = (2 * p + lax.rem(core_ref[0] + j, 2)) * half
                 copies.append(
                     pltpu.make_async_copy(
                         in_ref.at[:, pl.ds(pl.multiple_of(first, half), half)],
-                        out_ref.at[p],
+                        out_ref.at[p, :, j * half : (j + 1) * half],
                         sems.at[2 * p + j],
                     )
                 )
@@ -120,68 +120,58 @@
         for copy in copies:
             copy.wait()
 
-    vmem = pl.BlockSpec(memory_space=pltpu.VMEM)
     return pl.pallas_call(
         kernel,
-        out_shape=(jax.ShapeDtypeStruct((chips, rows, half), BF16),) * 2,
+        out_shape=jax.ShapeDtypeStruct((chips, rows, 2 * half), BF16),
         in_specs=[
             pl.BlockSpec(memory_space=pltpu.SMEM),
             pl.BlockSpec(memory_space=pl.ANY),
         ],
-        out_specs=(vmem, vmem),
+        out_specs=pl.BlockSpec(memory_space=pltpu.VMEM),
         scratch_shapes=[pltpu.SemaphoreType.DMA((2 * chips,))],
         compiler_params=pltpu.CompilerParams(vmem_limit_bytes=VMEM_LIMIT),
     )(scalar(core), local_rows)
 
 
-def products(total, tokens, halves, steps, x, me, places, out_types):
-    chips, rows, half = tokens[0].shape
-    width = halves[0].shape[1]
-    given = () if total is None else total
-    shard = halves[0].shape[0] // len(places[0])
+def project(pieces, ring, other, me, places):
+    chips, rows, depth = pieces.shape
+    half, width = ring.shape
+    shard = half // len(places)
     classes = 4
 
-    def kernel(x_ref, me_ref, *refs):
-        total_refs = refs[: len(given)]
-        token_refs = refs[len(given) : len(given) + 2]
-        half_refs = refs[len(given) + 2 : -3]
-        out_refs, weight_ref = refs[-3:-1], refs[-1]
-        results = [ref[...] for ref in total_refs] if given else [0.0, 0.0]
-        for n, step in enumerate(steps):
-            for ref, blocks in zip(half_refs[2 * n : 2 * n + 2], places):
-                for i, (kind, number) in enumerate(blocks):
-                    device = lax.rem(me_ref[0] + kind, classes) + classes * number
-                    at = pl.multiple_of(device * shard, shard)
-                    weight_ref[pl.ds(at, shard), :] = ref[i * shard : (i + 1) * shard, :]
-            chip = lax.rem(x_ref[0] + step + chips, chips)
-            for i, token_ref in enumerate(token_refs):
-                results[i] += jnp.dot(
-                    token_ref[chip], weight_ref[...], preferred_element_type=F32
-                )
-        for result, out_ref in zip(results, out_refs):
-            out_ref[...] = result.astype(out_ref.dtype)
-
-    operands = tuple(given) + tuple(tokens) + tuple(halves)
-    return vmem_call(
-        kernel,
-        tuple(jax.ShapeDtypeStruct((rows, width), t) for t in out_types),
-        (True, True) + (False,) * len(operands),
-        scratch_shapes=[pltpu.VMEM((half, width), BF16)],
-    )(scalar(x), scalar(me), *operands)
-
-
-def pack(own, received, slot_row, owners, capacity, head_dim):
-    rows, width = own.shape
+    def kernel(me_ref, pieces_ref, ring_ref, other_ref, out_ref, weight_ref):
+        for j, ref in enumerate((ring_ref, other_ref)):
+            for i, (kind, number) in enumerate(places):
+                device = lax.rem(me_ref[0] + kind, classes) + classes * number
+                at = pl.multiple_of(j * half + device * shard, shard)
+                weight_ref[pl.ds(at, shard), :] = ref[i * shard : (i + 1) * shard, :]
+        for p in range(chips):
+            out_ref[p] = jnp.dot(
+                pieces_ref[p], weight_ref[...], preferred_element_type=F32
+            ).astype(BF16)
+
+    return vmem_call(
+        kernel,
+        jax.ShapeDtypeStruct((chips, rows, width), BF16),
+        (True, False, False, False),
+        scratch_shapes=[pltpu.VMEM((depth, width), BF16)],
+    )(scalar(me), pieces, ring, other)
+
+
+def pack(partial, slot_row, owners, capacity, head_dim):
+    parts, rows, width = partial.shape
     heads = slot_row.shape[0]
     slots = owners * capacity
 
-    def kernel(own_ref, received_ref, slot_ref, out_ref):
+    def kernel(partial_ref, slot_ref, out_ref):
         for h in range(heads):
             place = iota((slots, rows), 0) == slot_ref[h : h + 1, :]
             place = place.astype(BF16)
             for m in range(2):
                 cols = slice((m * heads + h) * head_dim, (m * heads + h + 1) * head_dim)
-                total = own_ref[:, cols] + received_ref[:, cols].astype(F32)
+                total = partial_ref[0, :, cols].astype(F32)
+                for p in range(1, parts):
+                    total += partial_ref[p, :, cols].astype(F32)
                 packed = jnp.dot(
                     place, total.astype(BF16), preferred_element_type=F32
                 ).astype(BF16)
@@ -192,8 +182,8 @@
     return vmem_call(
         kernel,
         jax.ShapeDtypeStruct((owners, heads * capacity, 2 * head_dim), BF16),
-        (False,) * 3,
-    )(own, received, slot_row)
+        (False,) * 2,
+    )(partial, slot_row)
 
 
 def attend(blocks, members, capacity):
@@ -261,7 +251,6 @@
     rows, depth = tokens.shape[1:]
     owners = lax.axis_size(CLU)
     me = lax.axis_index(CLU)
-    x = lax.axis_index("x")
     heads = clusters.shape[2]
     shard = proj_weight.shape[0]
     width = 2 * proj_weight.shape[2]
@@ -269,48 +258,27 @@
     capacity = 2 * rows // owners
     chips = lax.axis_size("x")
 
+    pieces = cut_tokens(tokens[0], lax.axis_index("core"), chips)
     ids = clusters[0].T.astype(BF16).reshape(-1, 128)
     ids = jnp.pad(ids, ((0, shard - ids.shape[0]), (0, 0)))
     own = jnp.concatenate([proj_weight.reshape(shard, width), ids], axis=1)
+    own, pieces = lax.optimization_barrier((own, pieces))
+    pieces = lax.all_to_all(pieces, "x", split_axis=0, concat_axis=0, tiled=True)
+
     four = lax.all_gather(own, "zq", axis=0)
     below = shifted(four, 1, CLU)
     above = shifted(four, -1, CLU)
     beyond = [shifted(four[:2], 2, CLU), shifted(four[2:], -2, CLU)]
-
-    def weights_of(parts):
-        parts = [part[:, :, :width].reshape(-1, width) for part in parts]
-        return jnp.concatenate(parts, axis=0)
-
-    first = weights_of([four, below])
-    second = weights_of([above] + beyond)
-    places = (
-        [(0, j) for j in range(4)] + [(3, j) for j in range(4)],
-        [(1, j) for j in range(4)] + [(2, j) for j in range(4)],
-    )
-
-    mine, send = cut_tokens(tokens[0], lax.axis_index("core"), chips)
-    both = (mine, lax.ppermute(send, "core", [(0, 1), (1, 0)]))
-
-    first_below, first_above = shifted(first, 1, "x"), shifted(first, -1, "x")
-    second_below, second_above = shifted(second, 1, "x"), shifted(second, -1, "x")
-    first_far, second_far = shifted(first_below, 1, "x"), shifted(second_above, -1, "x")
-    total = products(
-        None,
-        both,
-        [first, second, first_below, second_below, first_above, second_above],
-        (0, -1, 1),
-        x,
-        me,
-        places,
-        (F32, F32),
-    )
-    kept, given = products(
-        total, both, [first_far, second_far], (2,), x, me, places, (F32, BF16)
-    )
-    received = lax.ppermute(given, "core", [(0, 1), (1, 0)])
+    ring = jnp.concatenate(
+        [part[:, :, :width].reshape(-1, width) for part in (four, below, above, *beyond)], axis=0
+    )
+    other = lax.ppermute(ring, "core", [(0, 1), (1, 0)])
+    places = [(kind, j) for kind in (0, 3, 1, 2) for j in range(4)]
+    partial = project(pieces, ring, other, me, places)
+    partial = lax.all_to_all(partial, "x", split_axis=0, concat_axis=0, tiled=True)
 
     slot_row, slot_col = routing(clusters[0], owners, capacity)
-    outgoing = pack(kept, received, slot_row, owners, capacity, head_dim)
+    outgoing = pack(partial, slot_row, owners, capacity, head_dim)
     incoming = lax.all_to_all(outgoing, CLU, split_axis=0, concat_axis=0, tiled=True)
 
     by_class = jnp.stack(

time: 200 us -> 198 us (0.990)
  waiting for transfers between devices: 66.3 us -> 83.9 us
  starting transfers between devices: 46.4 us -> 31 us
  local copies, waits for them, and re-layouts: 6.36 us -> 2.85 us
    all_to_all x0 -> x2, waiting for transfers between devices: none -> 38.7 us  [the longest x1 21.3 us: body(): lax.all_to_all(partial, 'x', split_axis=0, concat_axis=0, tiled=True)]
    ppermute x10 -> x4, starting transfers between devices: 35.3 us -> 14.2 us  [shifted(): lax.ppermute(block, axis, [(i, (i + step) % size) for i in range(size)])]
    ppermute x10 -> x4, waiting for transfers between devices: 19.1 us -> 0.87 us  [shifted(): lax.ppermute(block, axis, [(i, (i + step) % size) for i in range(size)])]
    all_to_all x0 -> x2, starting transfers between devices: none -> 8.19 us  [the longest x1 4.45 us: body(): lax.all_to_all(pieces, 'x', split_axis=0, concat_axis=0, tiled=True)]
    all_to_all x1, waiting for transfers between devices: 46.1 us -> 41.8 us  [body(): lax.all_to_all(outgoing, CLU, split_axis=0, concat_axis=0, tiled=True)]
    unnamed x27 -> x15, local copies, waits for them, and re-layouts: 5.38 us -> 2.57 us
    pallas_call x3 -> x2, Pallas kernels: 7.56 us -> 7.05 us  [the longest x1 5.46 us: project(): vmem_call(kernel, jax.ShapeDtypeStruct((chips, rows, width), BF16), (True...]
  transfers between devices with their start and end apart: 13 -> 8, of which waited for: 8 -> 5; matrix products, arithmetic and copies ran while one was open for 2% -> 0% of each run, Pallas kernels for 4% -> 1%
where the time goes in v9:
time: 198 us; the launch traced here: 197 us
  waiting for transfers between devices  83.9 us (42%)
  blocking collectives  63 us (32%)
  starting transfers between devices  31 us (16%)
  Pallas kernels  14.8 us (7%)
  local copies, waits for them, and re-layouts  2.85 us (1%)
    all_to_all x1, waiting for transfers between devices, body(): lax.all_to_all(outgoing, CLU, split_axis=0, concat_axis=0, tiled=True)  41.8 us
    all_to_all x1, blocking collectives, body(): lax.all_to_all(replies, CLU, split_axis=0, concat_axis=0, tiled=True)  35.9 us
    all_gather x1, blocking collectives, body(): four = lax.all_gather(own, 'zq', axis=0)  27.1 us
    all_to_all x1, waiting for transfers between devices, body(): lax.all_to_all(partial, 'x', split_axis=0, concat_axis=0, tiled=True)  21.3 us
    all_to_all x1, waiting for transfers between devices, body(): lax.all_to_all(pieces, 'x', split_axis=0, concat_axis=0, tiled=True)  17.4 us
    ppermute x4, starting transfers between devices, shifted(): lax.ppermute(block, axis, [(i, (i + step) % size) for i in range(size)])  14.2 us
    all_to_all x1, starting transfers between devices, body(): lax.all_to_all(outgoing, CLU, split_axis=0, concat_axis=0, tiled=True)  6.73 us
    pallas_call x1, Pallas kernels, project(): vmem_call(kernel, jax.ShapeDtypeStruct((chips, rows, width), BF16), (True...  5.46 us
  transfers between devices with their start and end apart: 8, of which 5 were waited for; matrix products, arithmetic and copies ran while one was open for 0% of the time, Pallas kernels for 1%

profile of v9, /device:TPU:24, one launch (start us, length us, event | category | flops | bytes accessed | tf_op | source)
XLA Modules:
  0.0 196.6 jit_solution(10358783079768392333)
XLA Ops:
  0.0 0.8 copy.9
  0.9 0.7 bitcast_convert_fusion
  1.6 1.6 copy-done
  3.1 1.6 shard_map.37
  4.8 27.1 %all-gather = bf16[128,1152]{1,0:T(8,128)(2,1)S(1)} all-gather(bf16[32,1152]{1,0:T(8,128)(2,1)S(1)} %fusion.1), channel_id=2, replica_groups=mesh['x'=4,'core'=2,'zq'=4,'zr'=4,'tp'=4] {'zq'}, dimensions={0}, use_global_device_ids=true | all-gather | bytes 368640 | tf_op jit(solution)/shard_map/all_gather | solution.py:268
  31.9 4.2 %collective-permute-start.1 = (bf16[4,32,1152]{2,1,0:T(8,128)(2,1)S(1)}, bf16[4,32,1152]{2,1,0:T(8,128)(2,1)S(1)}, u32[]{:S(2)}, u32[]{:S(2)}) collective-permute-start(bf16[4,32,1152]{2,1,0:T(8,128)(2,1)S(1)} %bitcast.50), channel_id=1, source_target_pairs={{0,60},{4,0},{8,4},{12,8},{16,12},{20,16},{24,20},{28,24},{32,28},... | collective-permute-start | bytes 884744 | tf_op jit(solution)/shard_map/ppermute | solution.py:247
  36.1 2.0 %collective-permute-start = (bf16[4,32,1152]{2,1,0:T(8,128)(2,1)S(1)}, bf16[4,32,1152]{2,1,0:T(8,128)(2,1)S(1)}, u32[]{:S(2)}, u32[]{:S(2)}) collective-permute-start(bf16[4,32,1152]{2,1,0:T(8,128)(2,1)S(1)} %bitcast.51), channel_id=1, source_target_pairs={{0,4},{4,8},{8,12},{12,16},{16,20},{20,24},{24,28},{28,32},{32,36}... | collective-permute-start | bytes 884744 | tf_op jit(solution)/shard_map/ppermute | solution.py:247
  38.1 4.0 %collective-permute-start.2 = (bf16[2,32,1152]{2,1,0:T(8,128)(2,1)S(1)}, bf16[2,32,1152]{2,1,0:T(8,128)(2,1)S(1)}, u32[]{:S(2)}, u32[]{:S(2)}) collective-permute-start(bf16[2,32,1152]{2,1,0:T(8,128)(2,1)S(1)} %bitcast.62), channel_id=1, source_target_pairs={{0,8},{4,12},{8,16},{12,20},{16,24},{20,28},{24,32},{28,36},{32,40... | collective-permute-start | bytes 442376 | tf_op jit(solution)/shard_map/ppermute | solution.py:247
  42.2 3.9 %collective-permute-start.3 = (bf16[2,32,1152]{2,1,0:T(8,128)(2,1)S(1)}, bf16[2,32,1152]{2,1,0:T(8,128)(2,1)S(1)}, u32[]{:S(2)}, u32[]{:S(2)}) collective-permute-start(bf16[2,32,1152]{2,1,0:T(8,128)(2,1)S(1)} %bitcast.61), channel_id=1, source_target_pairs={{0,56},{4,60},{8,0},{12,4},{16,8},{20,12},{24,16},{28,20},{32,24},... | collective-permute-start | bytes 442376 | tf_op jit(solution)/shard_map/ppermute | solution.py:247
  46.1 4.5 %all-to-all-start = ((bf16[4,256,1024]{2,1,0:T(8,128)(2,1)}), bf16[4,256,1024]{2,1,0:T(8,128)(2,1)}, u32[]{:S(2)}, u32[]{:S(2)}) async-start(bf16[4,256,1024]{2,1,0:T(8,128)(2,1)} %shard_map.37), calls=%async_computation | async-start | bytes 4194304 | tf_op jit(solution)/shard_map/all_to_all | solution.py:266
  50.6 0.9 collective-permute-done.3
  51.7 1.9 collective-permute-start.4
  53.6 2.6 %collective-permute-done.4.other_ref = bf16[512,1024]{1,0:T(8,128)(2,1)S(1)} collective-permute-done((bf16[512,1024]{1,0:T(8,128)(2,1)S(1)}, bf16[512,1024]{1,0:T(8,128)(2,1)S(1)}, u32[]{:S(2)}, u32[]{:S(2)}) %collective-permute-start.4) | collective-permute-done | bytes 1048608 | tf_op jit(solution)/shard_map/ppermute | solution.py:275
  56.2 17.4 %all-to-all-done.pieces_ref = bf16[4,256,1024]{2,1,0:T(8,128)(2,1)} async-done(((bf16[4,256,1024]{2,1,0:T(8,128)(2,1)}), bf16[4,256,1024]{2,1,0:T(8,128)(2,1)}, u32[]{:S(2)}, u32[]{:S(2)}) %all-to-all-start) | async-done | bytes 2097184 | tf_op jit(solution)/shard_map/all_to_all | solution.py:266
  73.6 5.5 %shard_map.38 = bf16[4,256,1024]{2,1,0:T(8,128)(2,1)} custom-call(s32[1]{0:T(128)} %bitcast.me_ref, bf16[4,256,1024]{2,1,0:T(8,128)(2,1)} %all-to-all-done.pieces_ref, bf16[512,1024]{1,0:T(8,128)(2,1)S(1)} %constant_dynamic-update-slice_fusion.ring_ref, bf16[512,1024]{1,0:T(8,128)(2,1)S(1)} %collective-permute-done.4.other_ref), custom_call_target="tpu_custom_call" | custom-call | tf_op jit(solution)/shard_map/pallas_call | solution.py:153
  79.1 3.7 %all-to-all-start.1 = ((bf16[4,256,1024]{2,1,0:T(8,128)(2,1)}), bf16[4,256,1024]{2,1,0:T(8,128)(2,1)S(1)}, u32[]{:S(2)}, u32[]{:S(2)}) async-start(bf16[4,256,1024]{2,1,0:T(8,128)(2,1)} %shard_map.38), calls=%async_computation.1 | async-start | bytes 4194304 | tf_op jit(solution)/shard_map/all_to_all | solution.py:278
  83.7 21.3 %all-to-all-done.1.partial_ref = bf16[4,256,1024]{2,1,0:T(8,128)(2,1)S(1)} async-done(((bf16[4,256,1024]{2,1,0:T(8,128)(2,1)}), bf16[4,256,1024]{2,1,0:T(8,128)(2,1)S(1)}, u32[]{:S(2)}, u32[]{:S(2)}) %all-to-all-start.1) | async-done | bytes 2097184 | tf_op jit(solution)/shard_map/all_to_all | solution.py:278
  104.9 1.7 shard_map.40
  106.7 6.7 %all-to-all-start.2 = ((bf16[16,128,256]{2,1,0:T(8,128)(2,1)}), bf16[16,128,256]{2,1,0:T(8,128)(2,1)S(1)}, u32[]{:S(2)}, u32[]{:S(2)}) async-start(bf16[16,128,256]{2,1,0:T(8,128)(2,1)} %shard_map.40), calls=%async_computation.2 | async-start | bytes 2097152 | tf_op jit(solution)/shard_map/all_to_all | solution.py:282
  113.6 1.1 shard_map.41.member_ref
  114.7 41.8 %all-to-all-done.2.block_ref = bf16[16,128,256]{2,1,0:T(8,128)(2,1)S(1)} async-done(((bf16[16,128,256]{2,1,0:T(8,128)(2,1)}), bf16[16,128,256]{2,1,0:T(8,128)(2,1)S(1)}, u32[]{:S(2)}, u32[]{:S(2)}) %all-to-all-start.2) | async-done | bytes 1048608 | tf_op jit(solution)/shard_map/all_to_all | solution.py:282
  156.4 3.1 %shard_map.42 = bf16[16,128,128]{2,1,0:T(8,128)(2,1)S(1)} custom-call(bf16[16,128,256]{2,1,0:T(8,128)(2,1)S(1)} %all-to-all-done.2.block_ref, bf16[4,16,512]{2,1,0:T(8,128)(2,1)S(1)} %shard_map.41.member_ref), custom_call_target="tpu_custom_call" | custom-call | tf_op jit(solution)/shard_map/pallas_call | solution.py:219
  159.5 35.9 %all_to_all.20.block_ref = bf16[16,128,128]{2,1,0:T(8,128)(2,1)S(1)} all-to-all(bf16[16,128,128]{2,1,0:T(8,128)(2,1)S(1)} %shard_map.42), channel_id=1, replica_groups=mesh['x'=4,'core'=2,'zq'=4,'zr'=4,'tp'=4] {'zq','zr'}, dimensions={0} | all-to-all | bytes 1048576 | tf_op jit(solution)/shard_map/all_to_all | solution.py:291
  195.4 1.2 shard_map.43
  (30 shorter events, 1.1 us)
Async XLA Ops:
  1.6 1.6 copy-start
  31.9 19.7 %collective-permute-start.1 = (bf16[4,32,1152]{2,1,0:T(8,128)(2,1)S(1)}, bf16[4,32,1152]{2,1,0:T(8,128)(2,1)S(1)}, u32[]{:S(2)}, u32[]{:S(2)}) collective-permute-start(bf16[4,32,1152]{2,1,0:T(8,128)(2,1)S(1)} %bitcast.50), channel_id=1, source_target_pairs={{0,60},{4,0},{8,4},{12,8},{16,12},{20,16},{24,20},{28,24},{32,28},... | collective-permute-start | bytes 884744 | tf_op jit(solution)/shard_map/ppermute | solution.py:247
  36.1 15.4 %collective-permute-start = (bf16[4,32,1152]{2,1,0:T(8,128)(2,1)S(1)}, bf16[4,32,1152]{2,1,0:T(8,128)(2,1)S(1)}, u32[]{:S(2)}, u32[]{:S(2)}) collective-permute-start(bf16[4,32,1152]{2,1,0:T(8,128)(2,1)S(1)} %bitcast.51), channel_id=1, source_target_pairs={{0,4},{4,8},{8,12},{12,16},{16,20},{20,24},{24,28},{28,32},{32,36}... | collective-permute-start | bytes 884744 | tf_op jit(solution)/shard_map/ppermute | solution.py:247
  38.1 12.5 %collective-permute-start.2 = (bf16[2,32,1152]{2,1,0:T(8,128)(2,1)S(1)}, bf16[2,32,1152]{2,1,0:T(8,128)(2,1)S(1)}, u32[]{:S(2)}, u32[]{:S(2)}) collective-permute-start(bf16[2,32,1152]{2,1,0:T(8,128)(2,1)S(1)} %bitcast.62), channel_id=1, source_target_pairs={{0,8},{4,12},{8,16},{12,20},{16,24},{20,28},{24,32},{28,36},{32,40... | collective-permute-start | bytes 442376 | tf_op jit(solution)/shard_map/ppermute | solution.py:247
  42.2 9.3 %collective-permute-start.3 = (bf16[2,32,1152]{2,1,0:T(8,128)(2,1)S(1)}, bf16[2,32,1152]{2,1,0:T(8,128)(2,1)S(1)}, u32[]{:S(2)}, u32[]{:S(2)}) collective-permute-start(bf16[2,32,1152]{2,1,0:T(8,128)(2,1)S(1)} %bitcast.61), channel_id=1, source_target_pairs={{0,56},{4,60},{8,0},{12,4},{16,8},{20,12},{24,16},{28,20},{32,24},... | collective-permute-start | bytes 442376 | tf_op jit(solution)/shard_map/ppermute | solution.py:247
  46.1 27.6 %all-to-all-start = ((bf16[4,256,1024]{2,1,0:T(8,128)(2,1)}), bf16[4,256,1024]{2,1,0:T(8,128)(2,1)}, u32[]{:S(2)}, u32[]{:S(2)}) async-start(bf16[4,256,1024]{2,1,0:T(8,128)(2,1)} %shard_map.37), calls=%async_computation | async-start | bytes 4194304 | tf_op jit(solution)/shard_map/all_to_all | solution.py:266
  51.7 4.6 %collective-permute-start.4 = (bf16[512,1024]{1,0:T(8,128)(2,1)S(1)}, bf16[512,1024]{1,0:T(8,128)(2,1)S(1)}, u32[]{:S(2)}, u32[]{:S(2)}) collective-permute-start(bf16[512,1024]{1,0:T(8,128)(2,1)S(1)} %constant_dynamic-update-slice_fusion.ring_ref), channel_id=1, source_target_pairs={{0,64},{64,0},{1,65},{65,1},{2,66},{66,2},{3,67},{67,3},{4,68},{68... | collective-permute-start | bytes 3145736 | tf_op jit(solution)/shard_map/ppermute | solution.py:275
  79.1 3.8 %copy-start.1 = (s32[1,256,4]{1,2,0:T(4,128)S(1)}, s32[1,256,4]{1,2,0:T(4,128)}, u32[]{:S(2)}) copy-start(s32[1,256,4]{1,2,0:T(4,128)} %param.5) | copy-start | bytes 12292
  79.1 25.8 %all-to-all-start.1 = ((bf16[4,256,1024]{2,1,0:T(8,128)(2,1)}), bf16[4,256,1024]{2,1,0:T(8,128)(2,1)S(1)}, u32[]{:S(2)}, u32[]{:S(2)}) async-start(bf16[4,256,1024]{2,1,0:T(8,128)(2,1)} %shard_map.38), calls=%async_computation.1 | async-start | bytes 4194304 | tf_op jit(solution)/shard_map/all_to_all | solution.py:278
  106.7 49.8 %all-to-all-start.2 = ((bf16[16,128,256]{2,1,0:T(8,128)(2,1)}), bf16[16,128,256]{2,1,0:T(8,128)(2,1)S(1)}, u32[]{:S(2)}, u32[]{:S(2)}) async-start(bf16[16,128,256]{2,1,0:T(8,128)(2,1)} %shard_map.40), calls=%async_computation.2 | async-start | bytes 2097152 | tf_op jit(solution)/shard_map/all_to_all | solution.py:282

commit v10 on v9

--- a/solution.py
+++ b/solution.py
@@ -268,7 +268,8 @@
     four = lax.all_gather(own, "zq", axis=0)
     below = shifted(four, 1, CLU)
     above = shifted(four, -1, CLU)
-    beyond = [shifted(four[:2], 2, CLU), shifted(four[2:], -2, CLU)]
+    later, pieces = lax.optimization_barrier((four, pieces))
+    beyond = [shifted(later[:2], 2, CLU), shifted(later[2:], -2, CLU)]
     ring = jnp.concatenate(
         [part[:, :, :width].reshape(-1, width) for part in (four, below, above, *beyond)], axis=0
     )

time: 198 us -> 205 us (1.035)
  local copies, waits for them, and re-layouts: 2.85 us -> 9.67 us
  starting transfers between devices: 31 us -> 33.8 us
  waiting for transfers between devices: 83.9 us -> 81.3 us
    all_to_all x1, waiting for transfers between devices: 17.4 us -> 0.01 us  [body(): lax.all_to_all(pieces, 'x', split_axis=0, concat_axis=0, tiled=True)]
    ppermute x4, waiting for transfers between devices: 0.87 us -> 7.81 us  [shifted(): lax.ppermute(block, axis, [(i, (i + step) % size) for i in range(size)])]
    all_to_all x1, waiting for transfers between devices: 21.3 us -> 25.8 us  [body(): lax.all_to_all(partial, 'x', split_axis=0, concat_axis=0, tiled=True)]
    unnamed x15 -> x27, local copies, waits for them, and re-layouts: 2.57 us -> 7.02 us
    all_to_all x1, waiting for transfers between devices: 41.8 us -> 45.1 us  [body(): lax.all_to_all(outgoing, CLU, split_axis=0, concat_axis=0, tiled=True)]
  transfers between devices with their start and end apart: 8 -> 8, of which waited for: 5 -> 6; matrix products, arithmetic and copies ran while one was open for 0% -> 3% of each run, Pallas kernels for 1% -> 1%
where the time goes in v10:
time: 205 us; the launch traced here: 204 us
  waiting for transfers between devices  81.3 us (40%)
  blocking collectives  63.4 us (31%)
  starting transfers between devices  33.8 us (16%)
  Pallas kernels  14.8 us (7%)
  local copies, waits for them, and re-layouts  9.67 us (5%)
    all_to_all x1, waiting for transfers between devices, body(): lax.all_to_all(outgoing, CLU, split_axis=0, concat_axis=0, tiled=True)  45.1 us
    all_to_all x1, blocking collectives, body(): lax.all_to_all(replies, CLU, split_axis=0, concat_axis=0, tiled=True)  36.8 us
    all_gather x1, blocking collectives, body(): four = lax.all_gather(own, 'zq', axis=0)  26.6 us
    all_to_all x1, waiting for transfers between devices, body(): lax.all_to_all(partial, 'x', split_axis=0, concat_axis=0, tiled=True)  25.8 us
    ppermute x4, starting transfers between devices, shifted(): lax.ppermute(block, axis, [(i, (i + step) % size) for i in range(size)])  15 us
    ppermute x4, waiting for transfers between devices, shifted(): lax.ppermute(block, axis, [(i, (i + step) % size) for i in range(size)])  7.81 us
    all_to_all x1, starting transfers between devices, body(): lax.all_to_all(outgoing, CLU, split_axis=0, concat_axis=0, tiled=True)  7.77 us
    unnamed x27, local copies, waits for them, and re-layouts  7.02 us
  transfers between devices with their start and end apart: 8, of which 6 were waited for; matrix products, arithmetic and copies ran while one was open for 3% of the time, Pallas kernels for 1%

profile of v10, /device:TPU:24, one launch (start us, length us, event | category | flops | bytes accessed | tf_op | source)
XLA Modules:
  0.0 204.0 jit_solution(923452197845434135)
XLA Ops:
  1.6 1.6 copy-done
  3.1 1.6 shard_map.37
  4.8 4.3 %all-to-all-start = ((bf16[4,256,1024]{2,1,0:T(8,128)(2,1)}), bf16[4,256,1024]{2,1,0:T(8,128)(2,1)S(1)}, u32[]{:S(2)}, u32[]{:S(2)}) async-start(bf16[4,256,1024]{2,1,0:T(8,128)(2,1)} %shard_map.37), calls=%async_computation | async-start | bytes 4194304 | tf_op jit(solution)/shard_map/all_to_all | solution.py:266
  9.1 26.6 %all-gather = bf16[128,1152]{1,0:T(8,128)(2,1)S(1)} all-gather(bf16[32,1152]{1,0:T(8,128)(2,1)S(1)} %fusion.1), channel_id=2, replica_groups=mesh['x'=4,'core'=2,'zq'=4,'zr'=4,'tp'=4] {'zq'}, dimensions={0}, use_global_device_ids=true | all-gather | bytes 368640 | tf_op jit(solution)/shard_map/all_gather | solution.py:268
  35.7 4.4 %collective-permute-start = (bf16[4,32,1152]{2,1,0:T(8,128)(2,1)S(1)}, bf16[4,32,1152]{2,1,0:T(8,128)(2,1)S(1)}, u32[]{:S(2)}, u32[]{:S(2)}) collective-permute-start(bf16[4,32,1152]{2,1,0:T(8,128)(2,1)S(1)} %bitcast.50), channel_id=1, source_target_pairs={{0,4},{4,8},{8,12},{12,16},{16,20},{20,24},{24,28},{28,32},{32,36}... | collective-permute-start | bytes 884744 | tf_op jit(solution)/shard_map/ppermute | solution.py:247
  40.0 2.7 %collective-permute-start.1 = (bf16[4,32,1152]{2,1,0:T(8,128)(2,1)S(1)}, bf16[4,32,1152]{2,1,0:T(8,128)(2,1)}, u32[]{:S(2)}, u32[]{:S(2)}) collective-permute-start(bf16[4,32,1152]{2,1,0:T(8,128)(2,1)S(1)} %bitcast.51), channel_id=1, source_target_pairs={{0,60},{4,0},{8,4},{12,8},{16,12},{20,16},{24,20},{28,24},{32,28},... | collective-permute-start | bytes 884744 | tf_op jit(solution)/shard_map/ppermute | solution.py:247
  42.8 2.7 %collective-permute-done = bf16[4,32,1152]{2,1,0:T(8,128)(2,1)S(1)} collective-permute-done((bf16[4,32,1152]{2,1,0:T(8,128)(2,1)S(1)}, bf16[4,32,1152]{2,1,0:T(8,128)(2,1)S(1)}, u32[]{:S(2)}, u32[]{:S(2)}) %collective-permute-start) | collective-permute-done | bytes 294944 | tf_op jit(solution)/shard_map/ppermute | solution.py:247
  47.0 3.6 %collective-permute-start.2 = (bf16[2,32,1152]{2,1,0:T(8,128)(2,1)S(1)}, bf16[2,32,1152]{2,1,0:T(8,128)(2,1)S(1)}, u32[]{:S(2)}, u32[]{:S(2)}) collective-permute-start(bf16[2,32,1152]{2,1,0:T(8,128)(2,1)S(1)} %get-tuple-element.20), channel_id=1, source_target_pairs={{0,8},{4,12},{8,16},{12,20},{16,24},{20,28},{24,32},{28,36},{32,40... | collective-permute-start | bytes 442376 | tf_op jit(solution)/shard_map/ppermute | solution.py:247
  50.5 1.0 constant_dynamic-update-slice_fusion.3
  51.5 1.0 slice.46
  52.5 4.4 %collective-permute-start.3 = (bf16[2,32,1152]{2,1,0:T(8,128)(2,1)S(1)}, bf16[2,32,1152]{2,1,0:T(8,128)(2,1)S(1)}, u32[]{:S(2)}, u32[]{:S(2)}) collective-permute-start(bf16[2,32,1152]{2,1,0:T(8,128)(2,1)S(1)} %get-tuple-element.19), channel_id=1, source_target_pairs={{0,56},{4,60},{8,0},{12,4},{16,8},{20,12},{24,16},{28,20},{32,24},... | collective-permute-start | bytes 442376 | tf_op jit(solution)/shard_map/ppermute | solution.py:247
  57.5 4.5 %collective-permute-done.3 = bf16[2,32,1152]{2,1,0:T(8,128)(2,1)S(1)} collective-permute-done((bf16[2,32,1152]{2,1,0:T(8,128)(2,1)S(1)}, bf16[2,32,1152]{2,1,0:T(8,128)(2,1)S(1)}, u32[]{:S(2)}, u32[]{:S(2)}) %collective-permute-start.3) | collective-permute-done | bytes 147488 | tf_op jit(solution)/shard_map/ppermute | solution.py:247
  62.7 1.9 collective-permute-start.4
  64.6 2.6 %collective-permute-done.4.other_ref = bf16[512,1024]{1,0:T(8,128)(2,1)S(1)} collective-permute-done((bf16[512,1024]{1,0:T(8,128)(2,1)S(1)}, bf16[512,1024]{1,0:T(8,128)(2,1)S(1)}, u32[]{:S(2)}, u32[]{:S(2)}) %collective-permute-start.4) | collective-permute-done | bytes 1048608 | tf_op jit(solution)/shard_map/ppermute | solution.py:276
  67.3 5.4 %shard_map.38 = bf16[4,256,1024]{2,1,0:T(8,128)(2,1)} custom-call(s32[1]{0:T(128)} %bitcast.me_ref, bf16[4,256,1024]{2,1,0:T(8,128)(2,1)} %copy-done.2, bf16[512,1024]{1,0:T(8,128)(2,1)S(1)} %constant_dynamic-update-slice_fusion.ring_ref, bf16[512,1024]{1,0:T(8,128)(2,1)S(1)} %collective-permute-done.4.other_ref), custom_call_target="tpu_custom_call" | custom-call | tf_op jit(solution)/shard_map/pallas_call | solution.py:153
  72.7 4.8 %all-to-all-start.1 = ((bf16[4,256,1024]{2,1,0:T(8,128)(2,1)}), bf16[4,256,1024]{2,1,0:T(8,128)(2,1)S(1)}, u32[]{:S(2)}, u32[]{:S(2)}) async-start(bf16[4,256,1024]{2,1,0:T(8,128)(2,1)} %shard_map.38), calls=%async_computation.1 | async-start | bytes 4194304 | tf_op jit(solution)/shard_map/all_to_all | solution.py:279
  78.4 25.8 %all-to-all-done.1.partial_ref = bf16[4,256,1024]{2,1,0:T(8,128)(2,1)S(1)} async-done(((bf16[4,256,1024]{2,1,0:T(8,128)(2,1)}), bf16[4,256,1024]{2,1,0:T(8,128)(2,1)S(1)}, u32[]{:S(2)}, u32[]{:S(2)}) %all-to-all-start.1) | async-done | bytes 2097184 | tf_op jit(solution)/shard_map/all_to_all | solution.py:279
  104.2 1.7 shard_map.40
  105.9 7.8 %all-to-all-start.2 = ((bf16[16,128,256]{2,1,0:T(8,128)(2,1)}), bf16[16,128,256]{2,1,0:T(8,128)(2,1)S(1)}, u32[]{:S(2)}, u32[]{:S(2)}) async-start(bf16[16,128,256]{2,1,0:T(8,128)(2,1)} %shard_map.40), calls=%async_computation.2 | async-start | bytes 2097152 | tf_op jit(solution)/shard_map/all_to_all | solution.py:283
  116.7 1.1 shard_map.41.member_ref
  117.8 45.1 %all-to-all-done.2.block_ref = bf16[16,128,256]{2,1,0:T(8,128)(2,1)S(1)} async-done(((bf16[16,128,256]{2,1,0:T(8,128)(2,1)}), bf16[16,128,256]{2,1,0:T(8,128)(2,1)S(1)}, u32[]{:S(2)}, u32[]{:S(2)}) %all-to-all-start.2) | async-done | bytes 1048608 | tf_op jit(solution)/shard_map/all_to_all | solution.py:283
  162.9 3.1 %shard_map.42 = bf16[16,128,128]{2,1,0:T(8,128)(2,1)S(1)} custom-call(bf16[16,128,256]{2,1,0:T(8,128)(2,1)S(1)} %all-to-all-done.2.block_ref, bf16[4,16,512]{2,1,0:T(8,128)(2,1)S(1)} %shard_map.41.member_ref), custom_call_target="tpu_custom_call" | custom-call | tf_op jit(solution)/shard_map/pallas_call | solution.py:219
  165.9 36.8 %all_to_all.20.block_ref = bf16[16,128,128]{2,1,0:T(8,128)(2,1)S(1)} all-to-all(bf16[16,128,128]{2,1,0:T(8,128)(2,1)S(1)} %shard_map.42), channel_id=1, replica_groups=mesh['x'=4,'core'=2,'zq'=4,'zr'=4,'tp'=4] {'zq','zr'}, dimensions={0} | all-to-all | bytes 1048576 | tf_op jit(solution)/shard_map/all_to_all | solution.py:292
  202.8 1.2 shard_map.43
  (42 shorter events, 8.1 us)
Async XLA Ops:
  1.6 1.6 copy-start
  4.8 42.1 %all-to-all-start = ((bf16[4,256,1024]{2,1,0:T(8,128)(2,1)}), bf16[4,256,1024]{2,1,0:T(8,128)(2,1)S(1)}, u32[]{:S(2)}, u32[]{:S(2)}) async-start(bf16[4,256,1024]{2,1,0:T(8,128)(2,1)} %shard_map.37), calls=%async_computation | async-start | bytes 4194304 | tf_op jit(solution)/shard_map/all_to_all | solution.py:266
  35.7 9.8 %collective-permute-start = (bf16[4,32,1152]{2,1,0:T(8,128)(2,1)S(1)}, bf16[4,32,1152]{2,1,0:T(8,128)(2,1)S(1)}, u32[]{:S(2)}, u32[]{:S(2)}) collective-permute-start(bf16[4,32,1152]{2,1,0:T(8,128)(2,1)S(1)} %bitcast.50), channel_id=1, source_target_pairs={{0,4},{4,8},{8,12},{12,16},{16,20},{20,24},{24,28},{28,32},{32,36}... | collective-permute-start | bytes 884744 | tf_op jit(solution)/shard_map/ppermute | solution.py:247
  40.0 11.5 %collective-permute-start.1 = (bf16[4,32,1152]{2,1,0:T(8,128)(2,1)S(1)}, bf16[4,32,1152]{2,1,0:T(8,128)(2,1)}, u32[]{:S(2)}, u32[]{:S(2)}) collective-permute-start(bf16[4,32,1152]{2,1,0:T(8,128)(2,1)S(1)} %bitcast.51), channel_id=1, source_target_pairs={{0,60},{4,0},{8,4},{12,8},{16,12},{20,16},{24,20},{28,24},{32,28},... | collective-permute-start | bytes 884744 | tf_op jit(solution)/shard_map/ppermute | solution.py:247
  45.5 0.7 copy-start.7
  46.9 15.1 %copy-start.2 = (bf16[4,256,1024]{2,1,0:T(8,128)(2,1)}, bf16[4,256,1024]{2,1,0:T(8,128)(2,1)S(1)}, u32[]{:S(2)}) copy-start(bf16[4,256,1024]{2,1,0:T(8,128)(2,1)S(1)} %all-to-all-done.pieces_ref) | copy-start | bytes 6291460
  47.0 10.5 %collective-permute-start.2 = (bf16[2,32,1152]{2,1,0:T(8,128)(2,1)S(1)}, bf16[2,32,1152]{2,1,0:T(8,128)(2,1)S(1)}, u32[]{:S(2)}, u32[]{:S(2)}) collective-permute-start(bf16[2,32,1152]{2,1,0:T(8,128)(2,1)S(1)} %get-tuple-element.20), channel_id=1, source_target_pairs={{0,8},{4,12},{8,16},{12,20},{16,24},{20,28},{24,32},{28,36},{32,40... | collective-permute-start | bytes 442376 | tf_op jit(solution)/shard_map/ppermute | solution.py:247
  52.5 9.6 %collective-permute-start.3 = (bf16[2,32,1152]{2,1,0:T(8,128)(2,1)S(1)}, bf16[2,32,1152]{2,1,0:T(8,128)(2,1)S(1)}, u32[]{:S(2)}, u32[]{:S(2)}) collective-permute-start(bf16[2,32,1152]{2,1,0:T(8,128)(2,1)S(1)} %get-tuple-element.19), channel_id=1, source_target_pairs={{0,56},{4,60},{8,0},{12,4},{16,8},{20,12},{24,16},{28,20},{32,24},... | collective-permute-start | bytes 442376 | tf_op jit(solution)/shard_map/ppermute | solution.py:247
  57.5 4.6 %copy-start.3 = (bf16[2,32,1152]{2,1,0:T(8,128)(2,1)}, bf16[2,32,1152]{2,1,0:T(8,128)(2,1)S(1)}, u32[]{:S(2)}) copy-start(bf16[2,32,1152]{2,1,0:T(8,128)(2,1)S(1)} %collective-permute-done.2) | copy-start | bytes 442372
  62.1 0.7 copy-start.5
  62.7 4.5 %collective-permute-start.4 = (bf16[512,1024]{1,0:T(8,128)(2,1)S(1)}, bf16[512,1024]{1,0:T(8,128)(2,1)S(1)}, u32[]{:S(2)}, u32[]{:S(2)}) collective-permute-start(bf16[512,1024]{1,0:T(8,128)(2,1)S(1)} %constant_dynamic-update-slice_fusion.ring_ref), channel_id=1, source_target_pairs={{0,64},{64,0},{1,65},{65,1},{2,66},{66,2},{3,67},{67,3},{4,68},{68... | collective-permute-start | bytes 3145736 | tf_op jit(solution)/shard_map/ppermute | solution.py:276
  72.7 4.9 %copy-start.1 = (s32[1,256,4]{1,2,0:T(4,128)S(1)}, s32[1,256,4]{1,2,0:T(4,128)}, u32[]{:S(2)}) copy-start(s32[1,256,4]{1,2,0:T(4,128)} %param.5) | copy-start | bytes 12292
  72.7 31.5 %all-to-all-start.1 = ((bf16[4,256,1024]{2,1,0:T(8,128)(2,1)}), bf16[4,256,1024]{2,1,0:T(8,128)(2,1)S(1)}, u32[]{:S(2)}, u32[]{:S(2)}) async-start(bf16[4,256,1024]{2,1,0:T(8,128)(2,1)} %shard_map.38), calls=%async_computation.1 | async-start | bytes 4194304 | tf_op jit(solution)/shard_map/all_to_all | solution.py:279
  104.2 10.3 %copy-start.4 = (bf16[2,32,1152]{2,1,0:T(8,128)(2,1)S(1)}, bf16[2,32,1152]{2,1,0:T(8,128)(2,1)}, u32[]{:S(2)}) copy-start(bf16[2,32,1152]{2,1,0:T(8,128)(2,1)} %copy-done.3) | copy-start | bytes 442372
  104.2 10.3 %copy-start.6 = (bf16[2,32,1152]{2,1,0:T(8,128)(2,1)S(1)}, bf16[2,32,1152]{2,1,0:T(8,128)(2,1)}, u32[]{:S(2)}) copy-start(bf16[2,32,1152]{2,1,0:T(8,128)(2,1)} %copy-done.5) | copy-start | bytes 442372
  105.9 56.9 %all-to-all-start.2 = ((bf16[16,128,256]{2,1,0:T(8,128)(2,1)}), bf16[16,128,256]{2,1,0:T(8,128)(2,1)S(1)}, u32[]{:S(2)}, u32[]{:S(2)}) async-start(bf16[16,128,256]{2,1,0:T(8,128)(2,1)} %shard_map.40), calls=%async_computation.2 | async-start | bytes 2097152 | tf_op jit(solution)/shard_map/all_to_all | solution.py:283

commit v11 on v9

--- a/solution.py
+++ b/solution.py
@@ -267,7 +267,8 @@
 
     four = lax.all_gather(own, "zq", axis=0)
     below = shifted(four, 1, CLU)
-    above = shifted(four, -1, CLU)
+    later, pieces = lax.optimization_barrier((four, pieces))
+    above = shifted(later, -1, CLU)
     beyond = [shifted(four[:2], 2, CLU), shifted(four[2:], -2, CLU)]
     ring = jnp.concatenate(
         [part[:, :, :width].reshape(-1, width) for part in (four, below, above, *beyond)], axis=0

time: 198 us -> 202 us (1.020)
  starting transfers between devices: 31 us -> 37.7 us
  waiting for transfers between devices: 83.9 us -> 80.9 us
    all_to_all x1, waiting for transfers between devices: 17.4 us -> 0.01 us  [body(): lax.all_to_all(pieces, 'x', split_axis=0, concat_axis=0, tiled=True)]
    all_to_all x1, waiting for transfers between devices: 41.8 us -> 48.1 us  [body(): lax.all_to_all(outgoing, CLU, split_axis=0, concat_axis=0, tiled=True)]
    ppermute x4, starting transfers between devices: 14.2 us -> 19.1 us  [shifted(): lax.ppermute(block, axis, [(i, (i + step) % size) for i in range(size)])]
    all_to_all x1, waiting for transfers between devices: 21.3 us -> 26.1 us  [body(): lax.all_to_all(partial, 'x', split_axis=0, concat_axis=0, tiled=True)]
    ppermute x4, waiting for transfers between devices: 0.87 us -> 4.08 us  [shifted(): lax.ppermute(block, axis, [(i, (i + step) % size) for i in range(size)])]
where the time goes in v11:
time: 202 us; the launch traced here: 201 us
  waiting for transfers between devices  80.9 us (40%)
  blocking collectives  63.5 us (31%)
  starting transfers between devices  37.7 us (19%)
  Pallas kernels  14.8 us (7%)
  local copies, waits for them, and re-layouts  2.86 us (1%)
    all_to_all x1, waiting for transfers between devices, body(): lax.all_to_all(outgoing, CLU, split_axis=0, concat_axis=0, tiled=True)  48.1 us
    all_to_all x1, blocking collectives, body(): lax.all_to_all(replies, CLU, split_axis=0, concat_axis=0, tiled=True)  37 us
    all_gather x1, blocking collectives, body(): four = lax.all_gather(own, 'zq', axis=0)  26.5 us
    all_to_all x1, waiting for transfers between devices, body(): lax.all_to_all(partial, 'x', split_axis=0, concat_axis=0, tiled=True)  26.1 us
    ppermute x4, starting transfers between devices, shifted(): lax.ppermute(block, axis, [(i, (i + step) % size) for i in range(size)])  19.1 us
    all_to_all x1, starting transfers between devices, body(): lax.all_to_all(outgoing, CLU, split_axis=0, concat_axis=0, tiled=True)  8.66 us
    pallas_call x1, Pallas kernels, project(): vmem_call(kernel, jax.ShapeDtypeStruct((chips, rows, width), BF16), (True...  5.47 us
    all_to_all x1, starting transfers between devices, body(): lax.all_to_all(pieces, 'x', split_axis=0, concat_axis=0, tiled=True)  4.3 us
  transfers between devices with their start and end apart: 8, of which 5 were waited for; matrix products, arithmetic and copies ran while one was open for 0% of the time, Pallas kernels for 1%

profile of v11, /device:TPU:24, one launch (start us, length us, event | category | flops | bytes accessed | tf_op | source)
XLA Modules:
  0.0 200.8 jit_solution(18368939224499876632)
XLA Ops:
  0.0 0.8 copy.9
  0.9 0.7 bitcast_convert_fusion
  1.6 1.6 copy-done
  3.1 1.6 shard_map.37
  4.8 4.3 %all-to-all-start = ((bf16[4,256,1024]{2,1,0:T(8,128)(2,1)}), bf16[4,256,1024]{2,1,0:T(8,128)(2,1)S(1)}, u32[]{:S(2)}, u32[]{:S(2)}) async-start(bf16[4,256,1024]{2,1,0:T(8,128)(2,1)} %shard_map.37), calls=%async_computation | async-start | bytes 4194304 | tf_op jit(solution)/shard_map/all_to_all | solution.py:266
  9.1 26.5 %all-gather = bf16[128,1152]{1,0:T(8,128)(2,1)S(1)} all-gather(bf16[32,1152]{1,0:T(8,128)(2,1)S(1)} %fusion.1), channel_id=2, replica_groups=mesh['x'=4,'core'=2,'zq'=4,'zr'=4,'tp'=4] {'zq'}, dimensions={0}, use_global_device_ids=true | all-gather | bytes 368640 | tf_op jit(solution)/shard_map/all_gather | solution.py:268
  35.6 4.1 %collective-permute-start = (bf16[4,32,1152]{2,1,0:T(8,128)(2,1)S(1)}, bf16[4,32,1152]{2,1,0:T(8,128)(2,1)S(1)}, u32[]{:S(2)}, u32[]{:S(2)}) collective-permute-start(bf16[4,32,1152]{2,1,0:T(8,128)(2,1)S(1)} %bitcast.50), channel_id=1, source_target_pairs={{0,4},{4,8},{8,12},{12,16},{16,20},{20,24},{24,28},{28,32},{32,36}... | collective-permute-start | bytes 884744 | tf_op jit(solution)/shard_map/ppermute | solution.py:247
  39.8 7.0 %collective-permute-start.1 = (bf16[4,32,1152]{2,1,0:T(8,128)(2,1)S(1)}, bf16[4,32,1152]{2,1,0:T(8,128)(2,1)S(1)}, u32[]{:S(2)}, u32[]{:S(2)}) collective-permute-start(bf16[4,32,1152]{2,1,0:T(8,128)(2,1)S(1)} %bitcast.51), channel_id=1, source_target_pairs={{0,60},{4,0},{8,4},{12,8},{16,12},{20,16},{24,20},{28,24},{32,28},... | collective-permute-start | bytes 884744 | tf_op jit(solution)/shard_map/ppermute | solution.py:247
  46.8 1.9 collective-permute-start.2
  48.8 6.0 %collective-permute-start.3 = (bf16[2,32,1152]{2,1,0:T(8,128)(2,1)S(1)}, bf16[2,32,1152]{2,1,0:T(8,128)(2,1)S(1)}, u32[]{:S(2)}, u32[]{:S(2)}) collective-permute-start(bf16[2,32,1152]{2,1,0:T(8,128)(2,1)S(1)} %bitcast.61), channel_id=1, source_target_pairs={{0,56},{4,60},{8,0},{12,4},{16,8},{20,12},{24,16},{28,20},{32,24},... | collective-permute-start | bytes 442376 | tf_op jit(solution)/shard_map/ppermute | solution.py:247
  54.9 2.7 %collective-permute-done.2 = bf16[2,32,1152]{2,1,0:T(8,128)(2,1)S(1)} collective-permute-done((bf16[2,32,1152]{2,1,0:T(8,128)(2,1)S(1)}, bf16[2,32,1152]{2,1,0:T(8,128)(2,1)S(1)}, u32[]{:S(2)}, u32[]{:S(2)}) %collective-permute-start.2) | collective-permute-done | bytes 147488 | tf_op jit(solution)/shard_map/ppermute | solution.py:247
  57.6 1.4 collective-permute-done.3
  59.1 1.9 collective-permute-start.4
  61.1 2.6 %collective-permute-done.4.other_ref = bf16[512,1024]{1,0:T(8,128)(2,1)S(1)} collective-permute-done((bf16[512,1024]{1,0:T(8,128)(2,1)S(1)}, bf16[512,1024]{1,0:T(8,128)(2,1)S(1)}, u32[]{:S(2)}, u32[]{:S(2)}) %collective-permute-start.4) | collective-permute-done | bytes 1048608 | tf_op jit(solution)/shard_map/ppermute | solution.py:276
  63.7 5.5 %shard_map.38 = bf16[4,256,1024]{2,1,0:T(8,128)(2,1)} custom-call(s32[1]{0:T(128)} %bitcast.me_ref, bf16[4,256,1024]{2,1,0:T(8,128)(2,1)} %copy-done.2, bf16[512,1024]{1,0:T(8,128)(2,1)S(1)} %constant_dynamic-update-slice_fusion.ring_ref, bf16[512,1024]{1,0:T(8,128)(2,1)S(1)} %collective-permute-done.4.other_ref), custom_call_target="tpu_custom_call" | custom-call | tf_op jit(solution)/shard_map/pallas_call | solution.py:153
  69.2 3.7 %all-to-all-start.1 = ((bf16[4,256,1024]{2,1,0:T(8,128)(2,1)}), bf16[4,256,1024]{2,1,0:T(8,128)(2,1)S(1)}, u32[]{:S(2)}, u32[]{:S(2)}) async-start(bf16[4,256,1024]{2,1,0:T(8,128)(2,1)} %shard_map.38), calls=%async_computation.1 | async-start | bytes 4194304 | tf_op jit(solution)/shard_map/all_to_all | solution.py:279
  73.7 26.1 %all-to-all-done.1.partial_ref = bf16[4,256,1024]{2,1,0:T(8,128)(2,1)S(1)} async-done(((bf16[4,256,1024]{2,1,0:T(8,128)(2,1)}), bf16[4,256,1024]{2,1,0:T(8,128)(2,1)S(1)}, u32[]{:S(2)}, u32[]{:S(2)}) %all-to-all-start.1) | async-done | bytes 2097184 | tf_op jit(solution)/shard_map/all_to_all | solution.py:279
  99.8 1.7 shard_map.40
  101.5 8.7 %all-to-all-start.2 = ((bf16[16,128,256]{2,1,0:T(8,128)(2,1)}), bf16[16,128,256]{2,1,0:T(8,128)(2,1)S(1)}, u32[]{:S(2)}, u32[]{:S(2)}) async-start(bf16[16,128,256]{2,1,0:T(8,128)(2,1)} %shard_map.40), calls=%async_computation.2 | async-start | bytes 2097152 | tf_op jit(solution)/shard_map/all_to_all | solution.py:283
  110.4 1.1 shard_map.41.member_ref
  111.5 48.1 %all-to-all-done.2.block_ref = bf16[16,128,256]{2,1,0:T(8,128)(2,1)S(1)} async-done(((bf16[16,128,256]{2,1,0:T(8,128)(2,1)}), bf16[16,128,256]{2,1,0:T(8,128)(2,1)S(1)}, u32[]{:S(2)}, u32[]{:S(2)}) %all-to-all-start.2) | async-done | bytes 1048608 | tf_op jit(solution)/shard_map/all_to_all | solution.py:283
  159.6 3.1 %shard_map.42 = bf16[16,128,128]{2,1,0:T(8,128)(2,1)S(1)} custom-call(bf16[16,128,256]{2,1,0:T(8,128)(2,1)S(1)} %all-to-all-done.2.block_ref, bf16[4,16,512]{2,1,0:T(8,128)(2,1)S(1)} %shard_map.41.member_ref), custom_call_target="tpu_custom_call" | custom-call | tf_op jit(solution)/shard_map/pallas_call | solution.py:219
  162.6 37.0 %all_to_all.20.block_ref = bf16[16,128,128]{2,1,0:T(8,128)(2,1)S(1)} all-to-all(bf16[16,128,128]{2,1,0:T(8,128)(2,1)S(1)} %shard_map.42), channel_id=1, replica_groups=mesh['x'=4,'core'=2,'zq'=4,'zr'=4,'tp'=4] {'zq','zr'}, dimensions={0} | all-to-all | bytes 1048576 | tf_op jit(solution)/shard_map/all_to_all | solution.py:292
  199.6 1.2 shard_map.43
  (32 shorter events, 1.1 us)
Async XLA Ops:
  1.6 1.6 copy-start
  4.8 35.0 %all-to-all-start = ((bf16[4,256,1024]{2,1,0:T(8,128)(2,1)}), bf16[4,256,1024]{2,1,0:T(8,128)(2,1)S(1)}, u32[]{:S(2)}, u32[]{:S(2)}) async-start(bf16[4,256,1024]{2,1,0:T(8,128)(2,1)} %shard_map.37), calls=%async_computation | async-start | bytes 4194304 | tf_op jit(solution)/shard_map/all_to_all | solution.py:266
  35.6 23.4 %collective-permute-start = (bf16[4,32,1152]{2,1,0:T(8,128)(2,1)S(1)}, bf16[4,32,1152]{2,1,0:T(8,128)(2,1)S(1)}, u32[]{:S(2)}, u32[]{:S(2)}) collective-permute-start(bf16[4,32,1152]{2,1,0:T(8,128)(2,1)S(1)} %bitcast.50), channel_id=1, source_target_pairs={{0,4},{4,8},{8,12},{12,16},{16,20},{20,24},{24,28},{28,32},{32,36}... | collective-permute-start | bytes 884744 | tf_op jit(solution)/shard_map/ppermute | solution.py:247
  39.8 15.1 %copy-start.2 = (bf16[4,256,1024]{2,1,0:T(8,128)(2,1)}, bf16[4,256,1024]{2,1,0:T(8,128)(2,1)S(1)}, u32[]{:S(2)}) copy-start(bf16[4,256,1024]{2,1,0:T(8,128)(2,1)S(1)} %all-to-all-done.pieces_ref) | copy-start | bytes 6291460
  39.8 19.3 %collective-permute-start.1 = (bf16[4,32,1152]{2,1,0:T(8,128)(2,1)S(1)}, bf16[4,32,1152]{2,1,0:T(8,128)(2,1)S(1)}, u32[]{:S(2)}, u32[]{:S(2)}) collective-permute-start(bf16[4,32,1152]{2,1,0:T(8,128)(2,1)S(1)} %bitcast.51), channel_id=1, source_target_pairs={{0,60},{4,0},{8,4},{12,8},{16,12},{20,16},{24,20},{28,24},{32,28},... | collective-permute-start | bytes 884744 | tf_op jit(solution)/shard_map/ppermute | solution.py:247
  46.8 10.8 %collective-permute-start.2 = (bf16[2,32,1152]{2,1,0:T(8,128)(2,1)S(1)}, bf16[2,32,1152]{2,1,0:T(8,128)(2,1)S(1)}, u32[]{:S(2)}, u32[]{:S(2)}) collective-permute-start(bf16[2,32,1152]{2,1,0:T(8,128)(2,1)S(1)} %bitcast.62), channel_id=1, source_target_pairs={{0,8},{4,12},{8,16},{12,20},{16,24},{20,28},{24,32},{28,36},{32,40... | collective-permute-start | bytes 442376 | tf_op jit(solution)/shard_map/ppermute | solution.py:247
  48.8 10.2 %collective-permute-start.3 = (bf16[2,32,1152]{2,1,0:T(8,128)(2,1)S(1)}, bf16[2,32,1152]{2,1,0:T(8,128)(2,1)S(1)}, u32[]{:S(2)}, u32[]{:S(2)}) collective-permute-start(bf16[2,32,1152]{2,1,0:T(8,128)(2,1)S(1)} %bitcast.61), channel_id=1, source_target_pairs={{0,56},{4,60},{8,0},{12,4},{16,8},{20,12},{24,16},{28,20},{32,24},... | collective-permute-start | bytes 442376 | tf_op jit(solution)/shard_map/ppermute | solution.py:247
  59.1 4.6 %collective-permute-start.4 = (bf16[512,1024]{1,0:T(8,128)(2,1)S(1)}, bf16[512,1024]{1,0:T(8,128)(2,1)S(1)}, u32[]{:S(2)}, u32[]{:S(2)}) collective-permute-start(bf16[512,1024]{1,0:T(8,128)(2,1)S(1)} %constant_dynamic-update-slice_fusion.ring_ref), channel_id=1, source_target_pairs={{0,64},{64,0},{1,65},{65,1},{2,66},{66,2},{3,67},{67,3},{4,68},{68... | collective-permute-start | bytes 3145736 | tf_op jit(solution)/shard_map/ppermute | solution.py:276
  69.2 3.8 %copy-start.1 = (s32[1,256,4]{1,2,0:T(4,128)S(1)}, s32[1,256,4]{1,2,0:T(4,128)}, u32[]{:S(2)}) copy-start(s32[1,256,4]{1,2,0:T(4,128)} %param.5) | copy-start | bytes 12292
  69.2 30.6 %all-to-all-start.1 = ((bf16[4,256,1024]{2,1,0:T(8,128)(2,1)}), bf16[4,256,1024]{2,1,0:T(8,128)(2,1)S(1)}, u32[]{:S(2)}, u32[]{:S(2)}) async-start(bf16[4,256,1024]{2,1,0:T(8,128)(2,1)} %shard_map.38), calls=%async_computation.1 | async-start | bytes 4194304 | tf_op jit(solution)/shard_map/all_to_all | solution.py:279
  101.5 58.0 %all-to-all-start.2 = ((bf16[16,128,256]{2,1,0:T(8,128)(2,1)}), bf16[16,128,256]{2,1,0:T(8,128)(2,1)S(1)}, u32[]{:S(2)}, u32[]{:S(2)}) async-start(bf16[16,128,256]{2,1,0:T(8,128)(2,1)} %shard_map.40), calls=%async_computation.2 | async-start | bytes 2097152 | tf_op jit(solution)/shard_map/all_to_all | solution.py:283

commit v12 on v11

--- a/solution.py
+++ b/solution.py
@@ -125,7 +125,7 @@
         out_shape=jax.ShapeDtypeStruct((chips, rows, 2 * half), BF16),
         in_specs=[
             pl.BlockSpec(memory_space=pltpu.SMEM),
-            pl.BlockSpec(memory_space=pl.ANY),
+            pl.BlockSpec(memory_space=pltpu.HBM),
         ],
         out_specs=pl.BlockSpec(memory_space=pltpu.VMEM),
         scratch_shapes=[pltpu.SemaphoreType.DMA((2 * chips,))],
@@ -133,45 +133,62 @@
     )(scalar(core), local_rows)
 
 
-def project(pieces, ring, other, me, places):
+def project(pieces, ring, other, x, me, steps, places):
     chips, rows, depth = pieces.shape
     half, width = ring.shape
     shard = half // len(places)
     classes = 4
 
-    def kernel(me_ref, pieces_ref, ring_ref, other_ref, out_ref, weight_ref):
+    def kernel(x_ref, me_ref, pieces_ref, ring_ref, other_ref, *refs):
+        out_refs, weight_ref = refs[:-1], refs[-1]
         for j, ref in enumerate((ring_ref, other_ref)):
             for i, (kind, number) in enumerate(places):
                 device = lax.rem(me_ref[0] + kind, classes) + classes * number
                 at = pl.multiple_of(j * half + device * shard, shard)
                 weight_ref[pl.ds(at, shard), :] = ref[i * shard : (i + 1) * shard, :]
-        for p in range(chips):
-            out_ref[p] = jnp.dot(
+        for step, out_ref in zip(steps, out_refs):
+            p = lax.rem(x_ref[0] + step + chips, chips)
+            out_ref[...] = jnp.dot(
                 pieces_ref[p], weight_ref[...], preferred_element_type=F32
             ).astype(BF16)
 
     return vmem_call(
         kernel,
-        jax.ShapeDtypeStruct((chips, rows, width), BF16),
-        (True, False, False, False),
+        (jax.ShapeDtypeStruct((rows, width), BF16),) * len(steps),
+        (True, True, False, False, False),
         scratch_shapes=[pltpu.VMEM((depth, width), BF16)],
-    )(scalar(me), pieces, ring, other)
-
-
-def pack(partial, slot_row, owners, capacity, head_dim):
-    parts, rows, width = partial.shape
+    )(scalar(x), scalar(me), pieces, ring, other)
+
+
+def exchange_x(parts, steps):
+    chips = lax.axis_size("x")
+    received = []
+    for core in (1, 0):
+        for i, step in enumerate(steps):
+            pairs = [(2 * x + core, (x + step) % chips * 2 + core) for x in range(chips)]
+            received.append(lax.ppermute(parts[i], ("x", "core"), pairs))
+        if core == 1:
+            ready = sum(part[:16, :128] for part in received)
+            ready = lax.ppermute(ready, "core", [(1, 0)])
+            parts, ready = lax.optimization_barrier((parts, ready))
+    return received, ready
+
+
+def pack(partials, ready, slot_row, owners, capacity, head_dim):
+    rows, width = partials[0].shape
     heads = slot_row.shape[0]
     slots = owners * capacity
 
-    def kernel(partial_ref, slot_ref, out_ref):
+    def kernel(*refs):
+        slot_ref, _, out_ref = refs[-3:]
         for h in range(heads):
             place = iota((slots, rows), 0) == slot_ref[h : h + 1, :]
             place = place.astype(BF16)
             for m in range(2):
                 cols = slice((m * heads + h) * head_dim, (m * heads + h + 1) * head_dim)
-                total = partial_ref[0, :, cols].astype(F32)
-                for p in range(1, parts):
-                    total += partial_ref[p, :, cols].astype(F32)
+                total = refs[0][:, cols].astype(F32)
+                for ref in refs[1:-3]:
+                    total += ref[:, cols].astype(F32)
                 packed = jnp.dot(
                     place, total.astype(BF16), preferred_element_type=F32
                 ).astype(BF16)
@@ -182,8 +199,8 @@
     return vmem_call(
         kernel,
         jax.ShapeDtypeStruct((owners, heads * capacity, 2 * head_dim), BF16),
-        (False,) * 2,
-    )(partial, slot_row)
+        (False,) * (len(partials) + 2),
+    )(*partials, slot_row, ready)
 
 
 def attend(blocks, members, capacity):
@@ -275,11 +292,13 @@
     )
     other = lax.ppermute(ring, "core", [(0, 1), (1, 0)])
     places = [(kind, j) for kind in (0, 3, 1, 2) for j in range(4)]
-    partial = project(pieces, ring, other, me, places)
-    partial = lax.all_to_all(partial, "x", split_axis=0, concat_axis=0, tiled=True)
+    steps = (2, 1, -1, 0)
+    sent = project(pieces, ring, other, lax.axis_index("x"), me, steps, places)
+    received, ready = exchange_x(sent[:-1], steps[:-1])
+    partials = [sent[-1]] + received
 
     slot_row, slot_col = routing(clusters[0], owners, capacity)
-    outgoing = pack(partial, slot_row, owners, capacity, head_dim)
+    outgoing = pack(partials, ready, slot_row, owners, capacity, head_dim)
     incoming = lax.all_to_all(outgoing, CLU, split_axis=0, concat_axis=0, tiled=True)
 
     by_class = jnp.stack(

time: 202 us -> 188 us (0.931)
  waiting for transfers between devices: 80.9 us -> 61.4 us
  starting transfers between devices: 37.7 us -> 46.5 us
  blocking collectives: 63.5 us -> 54.9 us
  local copies, waits for them, and re-layouts: 2.86 us -> 7.81 us
    all_to_all x1 -> x0, waiting for transfers between devices: 26.1 us -> none  [body(): lax.all_to_all(partial, 'x', split_axis=0, concat_axis=0, tiled=True)]
    ppermute x0 -> x7, waiting for transfers between devices: none -> 26 us  [the longest x1 15.9 us: exchange_x(): ready = lax.ppermute(ready, 'core', [(1, 0)])]
    all_to_all x1, waiting for transfers between devices: 48.1 us -> 28.6 us  [body(): lax.all_to_all(outgoing, CLU, split_axis=0, concat_axis=0, tiled=True)]
    ppermute x0 -> x7, starting transfers between devices: none -> 12.3 us  [the longest x6 11 us: exchange_x(): received.append(lax.ppermute(parts[i], ('x', 'core'), pairs))]
    all_to_all x1, blocking collectives: 37 us -> 28.4 us  [body(): lax.all_to_all(replies, CLU, split_axis=0, concat_axis=0, tiled=True)]
    unnamed x17 -> x31, local copies, waits for them, and re-layouts: 2.57 us -> 6.82 us
    all_to_all x1 -> x0, starting transfers between devices: 3.74 us -> none  [body(): lax.all_to_all(partial, 'x', split_axis=0, concat_axis=0, tiled=True)]
  transfers between devices with their start and end apart: 8 -> 14, of which waited for: 5 -> 8; matrix products, arithmetic and copies ran while one was open for 0% -> 2% of each run, Pallas kernels for 1% -> 1%
where the time goes in v12:
time: 188 us; the launch traced here: 187 us
  waiting for transfers between devices  61.4 us (33%)
  blocking collectives  54.9 us (29%)
  starting transfers between devices  46.5 us (25%)
  Pallas kernels  14.9 us (8%)
  local copies, waits for them, and re-layouts  7.81 us (4%)
    all_to_all x1, waiting for transfers between devices, body(): lax.all_to_all(outgoing, CLU, split_axis=0, concat_axis=0, tiled=True)  28.6 us
    all_to_all x1, blocking collectives, body(): lax.all_to_all(replies, CLU, split_axis=0, concat_axis=0, tiled=True)  28.4 us
    all_gather x1, blocking collectives, body(): four = lax.all_gather(own, 'zq', axis=0)  26.5 us
    ppermute x4, starting transfers between devices, shifted(): lax.ppermute(block, axis, [(i, (i + step) % size) for i in range(size)])  19.1 us
    ppermute x1, waiting for transfers between devices, exchange_x(): ready = lax.ppermute(ready, 'core', [(1, 0)])  15.9 us
    ppermute x6, starting transfers between devices, exchange_x(): received.append(lax.ppermute(parts[i], ('x', 'core'), pairs))  11 us
    ppermute x6, waiting for transfers between devices, exchange_x(): received.append(lax.ppermute(parts[i], ('x', 'core'), pairs))  10.2 us
    all_to_all x1, starting transfers between devices, body(): lax.all_to_all(outgoing, CLU, split_axis=0, concat_axis=0, tiled=True)  8.81 us
  transfers between devices with their start and end apart: 14, of which 8 were waited for; matrix products, arithmetic and copies ran while one was open for 2% of the time, Pallas kernels for 1%

profile of v12, /device:TPU:24, one launch (start us, length us, event | category | flops | bytes accessed | tf_op | source)
XLA Modules:
  0.0 186.6 jit_solution(1309219272395353828)
XLA Ops:
  1.6 1.6 copy-done
  3.1 1.6 shard_map.37
  4.8 4.3 %all-to-all-start = ((bf16[4,256,1024]{2,1,0:T(8,128)(2,1)}), bf16[4,256,1024]{2,1,0:T(8,128)(2,1)S(1)}, u32[]{:S(2)}, u32[]{:S(2)}) async-start(bf16[4,256,1024]{2,1,0:T(8,128)(2,1)} %shard_map.37), calls=%async_computation | async-start | bytes 4194304 | tf_op jit(solution)/shard_map/all_to_all | solution.py:283
  9.1 26.5 %all-gather = bf16[128,1152]{1,0:T(8,128)(2,1)S(1)} all-gather(bf16[32,1152]{1,0:T(8,128)(2,1)S(1)} %fusion.1), channel_id=2, replica_groups=mesh['x'=4,'core'=2,'zq'=4,'zr'=4,'tp'=4] {'zq'}, dimensions={0}, use_global_device_ids=true | all-gather | bytes 368640 | tf_op jit(solution)/shard_map/all_gather | solution.py:285
  35.6 4.1 %collective-permute-start = (bf16[4,32,1152]{2,1,0:T(8,128)(2,1)S(1)}, bf16[4,32,1152]{2,1,0:T(8,128)(2,1)S(1)}, u32[]{:S(2)}, u32[]{:S(2)}) collective-permute-start(bf16[4,32,1152]{2,1,0:T(8,128)(2,1)S(1)} %bitcast.51), channel_id=1, source_target_pairs={{0,4},{4,8},{8,12},{12,16},{16,20},{20,24},{24,28},{28,32},{32,36}... | collective-permute-start | bytes 884744 | tf_op jit(solution)/shard_map/ppermute | solution.py:264
  39.8 7.0 %collective-permute-start.1 = (bf16[4,32,1152]{2,1,0:T(8,128)(2,1)S(1)}, bf16[4,32,1152]{2,1,0:T(8,128)(2,1)S(1)}, u32[]{:S(2)}, u32[]{:S(2)}) collective-permute-start(bf16[4,32,1152]{2,1,0:T(8,128)(2,1)S(1)} %bitcast.52), channel_id=1, source_target_pairs={{0,60},{4,0},{8,4},{12,8},{16,12},{20,16},{24,20},{28,24},{32,28},... | collective-permute-start | bytes 884744 | tf_op jit(solution)/shard_map/ppermute | solution.py:264
  46.9 1.9 %collective-permute-start.2 = (bf16[2,32,1152]{2,1,0:T(8,128)(2,1)S(1)}, bf16[2,32,1152]{2,1,0:T(8,128)(2,1)S(1)}, u32[]{:S(2)}, u32[]{:S(2)}) collective-permute-start(bf16[2,32,1152]{2,1,0:T(8,128)(2,1)S(1)} %bitcast.63), channel_id=1, source_target_pairs={{0,8},{4,12},{8,16},{12,20},{16,24},{20,28},{24,32},{28,36},{32,40... | collective-permute-start | bytes 442376 | tf_op jit(solution)/shard_map/ppermute | solution.py:264
  48.8 6.0 %collective-permute-start.3 = (bf16[2,32,1152]{2,1,0:T(8,128)(2,1)S(1)}, bf16[2,32,1152]{2,1,0:T(8,128)(2,1)S(1)}, u32[]{:S(2)}, u32[]{:S(2)}) collective-permute-start(bf16[2,32,1152]{2,1,0:T(8,128)(2,1)S(1)} %bitcast.62), channel_id=1, source_target_pairs={{0,56},{4,60},{8,0},{12,4},{16,8},{20,12},{24,16},{28,20},{32,24},... | collective-permute-start | bytes 442376 | tf_op jit(solution)/shard_map/ppermute | solution.py:264
  54.9 2.7 %collective-permute-done.2 = bf16[2,32,1152]{2,1,0:T(8,128)(2,1)S(1)} collective-permute-done((bf16[2,32,1152]{2,1,0:T(8,128)(2,1)S(1)}, bf16[2,32,1152]{2,1,0:T(8,128)(2,1)S(1)}, u32[]{:S(2)}, u32[]{:S(2)}) %collective-permute-start.2) | collective-permute-done | bytes 147488 | tf_op jit(solution)/shard_map/ppermute | solution.py:264
  57.6 1.4 collective-permute-done.3
  59.8 1.9 %collective-permute-start.4 = (bf16[512,1024]{1,0:T(8,128)(2,1)S(1)}, bf16[512,1024]{1,0:T(8,128)(2,1)S(1)}, u32[]{:S(2)}, u32[]{:S(2)}) collective-permute-start(bf16[512,1024]{1,0:T(8,128)(2,1)S(1)} %constant_dynamic-update-slice_fusion.ring_ref), channel_id=1, source_target_pairs={{0,64},{64,0},{1,65},{65,1},{2,66},{66,2},{3,67},{67,3},{4,68},{68... | collective-permute-start | bytes 3145736 | tf_op jit(solution)/shard_map/ppermute | solution.py:293
  61.8 2.6 %collective-permute-done.4.other_ref = bf16[512,1024]{1,0:T(8,128)(2,1)S(1)} collective-permute-done((bf16[512,1024]{1,0:T(8,128)(2,1)S(1)}, bf16[512,1024]{1,0:T(8,128)(2,1)S(1)}, u32[]{:S(2)}, u32[]{:S(2)}) %collective-permute-start.4) | collective-permute-done | bytes 1048608 | tf_op jit(solution)/shard_map/ppermute | solution.py:293
  64.4 4.4 %shard_map.38 = (bf16[256,1024]{1,0:T(8,128)(2,1)}, bf16[256,1024]{1,0:T(8,128)(2,1)}, bf16[256,1024]{1,0:T(8,128)(2,1)}, bf16[256,1024]{1,0:T(8,128)(2,1)S(1)}) custom-call(s32[1]{0:T(128)} %bitcast.x_ref, s32[1]{0:T(128)} %bitcast.1.me_ref, bf16[4,256,1024]{2,1,0:T(8,128)(2,1)} %copy-done.2, ...), custom_call_target="tpu_custom_call" | custom-call | tf_op jit(solution)/shard_map/pallas_call | solution.py:155
  72.2 15.9 %collective-permute-done.8.refs_8_ = bf16[16,128]{1,0:T(8,128)(2,1)S(1)} collective-permute-done((bf16[16,128]{1,0:T(8,128)(2,1)S(1)}, bf16[16,128]{1,0:T(8,128)(2,1)S(1)}, u32[]{:S(2)}, u32[]{:S(2)}) %collective-permute-start.8) | collective-permute-done | bytes 4128 | tf_op jit(solution)/shard_map/ppermute | solution.py:172
  88.1 2.1 %collective-permute-start.10 = (bf16[256,1024]{1,0:T(8,128)(2,1)}, bf16[256,1024]{1,0:T(8,128)(2,1)S(1)}, u32[]{:S(2)}, u32[]{:S(2)}) collective-permute-start(bf16[256,1024]{1,0:T(8,128)(2,1)} %get-tuple-element.28), channel_id=1, source_target_pairs={{0,128},{128,256},{256,384},{384,0},{1,129},{129,257},{257,385},{3... | collective-permute-start | bytes 1572872 | tf_op jit(solution)/shard_map/ppermute | solution.py:169
  90.2 4.9 %collective-permute-start.11 = (bf16[256,1024]{1,0:T(8,128)(2,1)}, bf16[256,1024]{1,0:T(8,128)(2,1)S(1)}, u32[]{:S(2)}, u32[]{:S(2)}) collective-permute-start(bf16[256,1024]{1,0:T(8,128)(2,1)} %get-tuple-element.29), channel_id=1, source_target_pairs={{0,384},{128,0},{256,128},{384,256},{1,385},{129,1},{257,129},{385... | collective-permute-start | bytes 1572872 | tf_op jit(solution)/shard_map/ppermute | solution.py:169
  95.2 1.9 %collective-permute-start.9 = (bf16[256,1024]{1,0:T(8,128)(2,1)}, bf16[256,1024]{1,0:T(8,128)(2,1)}, u32[]{:S(2)}, u32[]{:S(2)}) collective-permute-start(bf16[256,1024]{1,0:T(8,128)(2,1)} %get-tuple-element.27), channel_id=1, source_target_pairs={{0,256},{128,384},{256,0},{384,128},{1,257},{129,385},{257,1},{385... | collective-permute-start | bytes 1572872 | tf_op jit(solution)/shard_map/ppermute | solution.py:169
  97.9 2.7 %collective-permute-done.10.refs_5_ = bf16[256,1024]{1,0:T(8,128)(2,1)S(1)} collective-permute-done((bf16[256,1024]{1,0:T(8,128)(2,1)}, bf16[256,1024]{1,0:T(8,128)(2,1)S(1)}, u32[]{:S(2)}, u32[]{:S(2)}) %collective-permute-start.10) | collective-permute-done | bytes 524320 | tf_op jit(solution)/shard_map/ppermute | solution.py:169
  100.6 7.2 %collective-permute-done.11.refs_6_ = bf16[256,1024]{1,0:T(8,128)(2,1)S(1)} collective-permute-done((bf16[256,1024]{1,0:T(8,128)(2,1)}, bf16[256,1024]{1,0:T(8,128)(2,1)S(1)}, u32[]{:S(2)}, u32[]{:S(2)}) %collective-permute-start.11) | collective-permute-done | bytes 524320 | tf_op jit(solution)/shard_map/ppermute | solution.py:169
  108.1 2.9 %shard_map.40 = bf16[16,128,256]{2,1,0:T(8,128)(2,1)} custom-call(bf16[256,1024]{1,0:T(8,128)(2,1)S(1)} %get-tuple-element.23.refs_0_, bf16[256,1024]{1,0:T(8,128)(2,1)S(1)} %collective-permute-done.5.refs_1_, bf16[256,1024]{1,0:T(8,128)(2,1)S(1)} %collective-permute-done.6.refs_2_, bf16[256,1024]{1,0:T(8,128)(2,1)S(1)} %collective-permute-done.7.refs_3_, ...), custom_call_target="tpu_custom_call" | custom-call | tf_op jit(solution)/shard_map/pallas_call | solution.py:199
  111.0 8.8 %all-to-all-start.1 = ((bf16[16,128,256]{2,1,0:T(8,128)(2,1)}), bf16[16,128,256]{2,1,0:T(8,128)(2,1)S(1)}, u32[]{:S(2)}, u32[]{:S(2)}) async-start(bf16[16,128,256]{2,1,0:T(8,128)(2,1)} %shard_map.40), calls=%async_computation.1 | async-start | bytes 2097152 | tf_op jit(solution)/shard_map/all_to_all | solution.py:302
  125.3 28.6 %all-to-all-done.1.block_ref = bf16[16,128,256]{2,1,0:T(8,128)(2,1)S(1)} async-done(((bf16[16,128,256]{2,1,0:T(8,128)(2,1)}), bf16[16,128,256]{2,1,0:T(8,128)(2,1)S(1)}, u32[]{:S(2)}, u32[]{:S(2)}) %all-to-all-start.1) | async-done | bytes 1048608 | tf_op jit(solution)/shard_map/all_to_all | solution.py:302
  153.9 3.1 %shard_map.42 = bf16[16,128,128]{2,1,0:T(8,128)(2,1)S(1)} custom-call(bf16[16,128,256]{2,1,0:T(8,128)(2,1)S(1)} %all-to-all-done.1.block_ref, bf16[4,16,512]{2,1,0:T(8,128)(2,1)S(1)} %shard_map.41.member_ref), custom_call_target="tpu_custom_call" | custom-call | tf_op jit(solution)/shard_map/pallas_call | solution.py:236
  157.0 28.4 %all_to_all.15.block_ref = bf16[16,128,128]{2,1,0:T(8,128)(2,1)S(1)} all-to-all(bf16[16,128,128]{2,1,0:T(8,128)(2,1)S(1)} %shard_map.42), channel_id=1, replica_groups=mesh['x'=4,'core'=2,'zq'=4,'zr'=4,'tp'=4] {'zq','zr'}, dimensions={0} | all-to-all | bytes 1048576 | tf_op jit(solution)/shard_map/all_to_all | solution.py:311
  (59 shorter events, 13.5 us)
Async XLA Ops:
  1.6 1.6 copy-start
  4.8 35.0 %all-to-all-start = ((bf16[4,256,1024]{2,1,0:T(8,128)(2,1)}), bf16[4,256,1024]{2,1,0:T(8,128)(2,1)S(1)}, u32[]{:S(2)}, u32[]{:S(2)}) async-start(bf16[4,256,1024]{2,1,0:T(8,128)(2,1)} %shard_map.37), calls=%async_computation | async-start | bytes 4194304 | tf_op jit(solution)/shard_map/all_to_all | solution.py:283
  35.6 23.5 %copy-start.3 = (bf16[128,1152]{1,0:T(8,128)(2,1)}, bf16[128,1152]{1,0:T(8,128)(2,1)S(1)}, u32[]{:S(2)}) copy-start(bf16[128,1152]{1,0:T(8,128)(2,1)S(1)} %all-gather) | copy-start | bytes 884740
  35.6 23.4 %collective-permute-start = (bf16[4,32,1152]{2,1,0:T(8,128)(2,1)S(1)}, bf16[4,32,1152]{2,1,0:T(8,128)(2,1)S(1)}, u32[]{:S(2)}, u32[]{:S(2)}) collective-permute-start(bf16[4,32,1152]{2,1,0:T(8,128)(2,1)S(1)} %bitcast.51), channel_id=1, source_target_pairs={{0,4},{4,8},{8,12},{12,16},{16,20},{20,24},{24,28},{28,32},{32,36}... | collective-permute-start | bytes 884744 | tf_op jit(solution)/shard_map/ppermute | solution.py:264
  39.8 15.1 %copy-start.2 = (bf16[4,256,1024]{2,1,0:T(8,128)(2,1)}, bf16[4,256,1024]{2,1,0:T(8,128)(2,1)S(1)}, u32[]{:S(2)}) copy-start(bf16[4,256,1024]{2,1,0:T(8,128)(2,1)S(1)} %all-to-all-done.pieces_ref) | copy-start | bytes 6291460
  39.8 19.3 %collective-permute-start.1 = (bf16[4,32,1152]{2,1,0:T(8,128)(2,1)S(1)}, bf16[4,32,1152]{2,1,0:T(8,128)(2,1)S(1)}, u32[]{:S(2)}, u32[]{:S(2)}) collective-permute-start(bf16[4,32,1152]{2,1,0:T(8,128)(2,1)S(1)} %bitcast.52), channel_id=1, source_target_pairs={{0,60},{4,0},{8,4},{12,8},{16,12},{20,16},{24,20},{28,24},{32,28},... | collective-permute-start | bytes 884744 | tf_op jit(solution)/shard_map/ppermute | solution.py:264
  46.9 10.8 %collective-permute-start.2 = (bf16[2,32,1152]{2,1,0:T(8,128)(2,1)S(1)}, bf16[2,32,1152]{2,1,0:T(8,128)(2,1)S(1)}, u32[]{:S(2)}, u32[]{:S(2)}) collective-permute-start(bf16[2,32,1152]{2,1,0:T(8,128)(2,1)S(1)} %bitcast.63), channel_id=1, source_target_pairs={{0,8},{4,12},{8,16},{12,20},{16,24},{20,28},{24,32},{28,36},{32,40... | collective-permute-start | bytes 442376 | tf_op jit(solution)/shard_map/ppermute | solution.py:264
  48.8 10.2 %collective-permute-start.3 = (bf16[2,32,1152]{2,1,0:T(8,128)(2,1)S(1)}, bf16[2,32,1152]{2,1,0:T(8,128)(2,1)S(1)}, u32[]{:S(2)}, u32[]{:S(2)}) collective-permute-start(bf16[2,32,1152]{2,1,0:T(8,128)(2,1)S(1)} %bitcast.62), channel_id=1, source_target_pairs={{0,56},{4,60},{8,0},{12,4},{16,8},{20,12},{24,16},{28,20},{32,24},... | collective-permute-start | bytes 442376 | tf_op jit(solution)/shard_map/ppermute | solution.py:264
  57.6 1.6 copy-start.4
  59.0 0.7 copy-start.6
  59.0 5.4 %copy-start.8 = (bf16[4,32,1152]{2,1,0:T(8,128)(2,1)}, bf16[4,32,1152]{2,1,0:T(8,128)(2,1)S(1)}, u32[]{:S(2)}) copy-start(bf16[4,32,1152]{2,1,0:T(8,128)(2,1)S(1)} %collective-permute-done) | copy-start | bytes 884740
  59.1 0.8 copy-start.9
  59.8 4.5 %collective-permute-start.4 = (bf16[512,1024]{1,0:T(8,128)(2,1)S(1)}, bf16[512,1024]{1,0:T(8,128)(2,1)S(1)}, u32[]{:S(2)}, u32[]{:S(2)}) collective-permute-start(bf16[512,1024]{1,0:T(8,128)(2,1)S(1)} %constant_dynamic-update-slice_fusion.ring_ref), channel_id=1, source_target_pairs={{0,64},{64,0},{1,65},{65,1},{2,66},{66,2},{3,67},{67,3},{4,68},{68... | collective-permute-start | bytes 3145736 | tf_op jit(solution)/shard_map/ppermute | solution.py:293
  64.4 32.7 %copy-start.1 = (s32[1,256,4]{1,2,0:T(4,128)S(1)}, s32[1,256,4]{1,2,0:T(4,128)}, u32[]{:S(2)}) copy-start(s32[1,256,4]{1,2,0:T(4,128)} %param.5) | copy-start | bytes 12292
  68.8 2.1 %collective-permute-start.5 = (bf16[256,1024]{1,0:T(8,128)(2,1)}, bf16[256,1024]{1,0:T(8,128)(2,1)S(1)}, u32[]{:S(2)}, u32[]{:S(2)}) collective-permute-start(bf16[256,1024]{1,0:T(8,128)(2,1)} %get-tuple-element.27), channel_id=1, source_target_pairs={{64,320},{192,448},{320,64},{448,192},{65,321},{193,449},{321,65},... | collective-permute-start | bytes 1572872 | tf_op jit(solution)/shard_map/ppermute | solution.py:169
  69.5 1.4 collective-permute-start.6
  70.2 0.7 collective-permute-start.7
  70.9 17.2 %collective-permute-start.8 = (bf16[16,128]{1,0:T(8,128)(2,1)S(1)}, bf16[16,128]{1,0:T(8,128)(2,1)S(1)}, u32[]{:S(2)}, u32[]{:S(2)}) collective-permute-start(bf16[16,128]{1,0:T(8,128)(2,1)S(1)} %slice_add_fusion), channel_id=1, source_target_pairs={{64,0},{65,1},{66,2},{67,3},{68,4},{69,5},{70,6},{71,7},{72,8},{73... | collective-permute-start | bytes 12296 | tf_op jit(solution)/shard_map/ppermute | solution.py:172
  88.1 12.5 %collective-permute-start.10 = (bf16[256,1024]{1,0:T(8,128)(2,1)}, bf16[256,1024]{1,0:T(8,128)(2,1)S(1)}, u32[]{:S(2)}, u32[]{:S(2)}) collective-permute-start(bf16[256,1024]{1,0:T(8,128)(2,1)} %get-tuple-element.28), channel_id=1, source_target_pairs={{0,128},{128,256},{256,384},{384,0},{1,129},{129,257},{257,385},{3... | collective-permute-start | bytes 1572872 | tf_op jit(solution)/shard_map/ppermute | solution.py:169
  90.2 17.6 %collective-permute-start.11 = (bf16[256,1024]{1,0:T(8,128)(2,1)}, bf16[256,1024]{1,0:T(8,128)(2,1)S(1)}, u32[]{:S(2)}, u32[]{:S(2)}) collective-permute-start(bf16[256,1024]{1,0:T(8,128)(2,1)} %get-tuple-element.29), channel_id=1, source_target_pairs={{0,384},{128,0},{256,128},{384,256},{1,385},{129,1},{257,129},{385... | collective-permute-start | bytes 1572872 | tf_op jit(solution)/shard_map/ppermute | solution.py:169
  95.2 12.9 %collective-permute-start.9 = (bf16[256,1024]{1,0:T(8,128)(2,1)}, bf16[256,1024]{1,0:T(8,128)(2,1)}, u32[]{:S(2)}, u32[]{:S(2)}) collective-permute-start(bf16[256,1024]{1,0:T(8,128)(2,1)} %get-tuple-element.27), channel_id=1, source_target_pairs={{0,256},{128,384},{256,0},{384,128},{1,257},{129,385},{257,1},{385... | collective-permute-start | bytes 1572872 | tf_op jit(solution)/shard_map/ppermute | solution.py:169
  111.0 10.3 %copy-start.5 = (bf16[2,32,1152]{2,1,0:T(8,128)(2,1)S(1)}, bf16[2,32,1152]{2,1,0:T(8,128)(2,1)}, u32[]{:S(2)}) copy-start(bf16[2,32,1152]{2,1,0:T(8,128)(2,1)} %copy-done.4) | copy-start | bytes 442372
  111.0 10.3 %copy-start.7 = (bf16[2,32,1152]{2,1,0:T(8,128)(2,1)S(1)}, bf16[2,32,1152]{2,1,0:T(8,128)(2,1)}, u32[]{:S(2)}) copy-start(bf16[2,32,1152]{2,1,0:T(8,128)(2,1)} %copy-done.6) | copy-start | bytes 442372
  111.0 42.9 %all-to-all-start.1 = ((bf16[16,128,256]{2,1,0:T(8,128)(2,1)}), bf16[16,128,256]{2,1,0:T(8,128)(2,1)S(1)}, u32[]{:S(2)}, u32[]{:S(2)}) async-start(bf16[16,128,256]{2,1,0:T(8,128)(2,1)} %shard_map.40), calls=%async_computation.1 | async-start | bytes 2097152 | tf_op jit(solution)/shard_map/all_to_all | solution.py:302

commit v13 on v12

--- a/solution.py
+++ b/solution.py
@@ -125,39 +125,50 @@
         out_shape=jax.ShapeDtypeStruct((chips, rows, 2 * half), BF16),
         in_specs=[
             pl.BlockSpec(memory_space=pltpu.SMEM),
-            pl.BlockSpec(memory_space=pltpu.HBM),
+            pl.BlockSpec(memory_space=pltpu.VMEM),
         ],
-        out_specs=pl.BlockSpec(memory_space=pltpu.VMEM),
+        out_specs=pl.BlockSpec(memory_space=pl.ANY),
         scratch_shapes=[pltpu.SemaphoreType.DMA((2 * chips,))],
         compiler_params=pltpu.CompilerParams(vmem_limit_bytes=VMEM_LIMIT),
     )(scalar(core), local_rows)
 
 
-def project(pieces, ring, other, x, me, steps, places):
+def assemble(parts, places, me, width):
+    shard = parts[0].shape[1]
+    count = sum(part.shape[0] for part in parts)
+    classes = 4
+
+    def kernel(me_ref, *refs):
+        out_ref = refs[-1]
+        for ref, (kind, first) in zip(refs, places):
+            device = lax.rem(me_ref[0] + kind, classes) + classes * first
+            for j in range(ref.shape[0]):
+                at = pl.multiple_of((device + classes * j) * shard, shard)
+                out_ref[pl.ds(at, shard), :] = ref[j, :, :width]
+
+    return vmem_call(
+        kernel,
+        jax.ShapeDtypeStruct((count * shard, width), BF16),
+        (True,) + (False,) * len(parts),
+    )(scalar(me), *parts)
+
+
+def project(pieces, ring, other, x, steps):
     chips, rows, depth = pieces.shape
     half, width = ring.shape
-    shard = half // len(places)
-    classes = 4
-
-    def kernel(x_ref, me_ref, pieces_ref, ring_ref, other_ref, *refs):
-        out_refs, weight_ref = refs[:-1], refs[-1]
-        for j, ref in enumerate((ring_ref, other_ref)):
-            for i, (kind, number) in enumerate(places):
-                device = lax.rem(me_ref[0] + kind, classes) + classes * number
-                at = pl.multiple_of(j * half + device * shard, shard)
-                weight_ref[pl.ds(at, shard), :] = ref[i * shard : (i + 1) * shard, :]
+
+    def kernel(x_ref, pieces_ref, ring_ref, other_ref, *out_refs):
         for step, out_ref in zip(steps, out_refs):
             p = lax.rem(x_ref[0] + step + chips, chips)
-            out_ref[...] = jnp.dot(
-                pieces_ref[p], weight_ref[...], preferred_element_type=F32
-            ).astype(BF16)
+            total = jnp.dot(pieces_ref[p, :, :half], ring_ref[...], preferred_element_type=F32)
+            total += jnp.dot(pieces_ref[p, :, half:], other_ref[...], preferred_element_type=F32)
+            out_ref[...] = total.astype(BF16)
 
     return vmem_call(
         kernel,
         (jax.ShapeDtypeStruct((rows, width), BF16),) * len(steps),
-        (True, True, False, False, False),
-        scratch_shapes=[pltpu.VMEM((depth, width), BF16)],
-    )(scalar(x), scalar(me), pieces, ring, other)
+        (True, False, False, False),
+    )(scalar(x), pieces, ring, other)
 
 
 def exchange_x(parts, steps):
@@ -174,33 +185,44 @@
     return received, ready
 
 
-def pack(partials, ready, slot_row, owners, capacity, head_dim):
-    rows, width = partials[0].shape
+def pack(own, received, ready, slot_row, core, owners, capacity, head_dim):
+    rows, width = own.shape
     heads = slot_row.shape[0]
     slots = owners * capacity
-
-    def kernel(*refs):
+    count = len(received) // 2
+
+    def kernel(core_ref, own_ref, *refs):
         slot_ref, _, out_ref = refs[-3:]
-        for h in range(heads):
-            place = iota((slots, rows), 0) == slot_ref[h : h + 1, :]
-            place = place.astype(BF16)
-            for m in range(2):
-                cols = slice((m * heads + h) * head_dim, (m * heads + h + 1) * head_dim)
-                total = refs[0][:, cols].astype(F32)
-                for ref in refs[1:-3]:
-                    total += ref[:, cols].astype(F32)
-                packed = jnp.dot(
-                    place, total.astype(BF16), preferred_element_type=F32
-                ).astype(BF16)
-                out_ref[
-                    :, h * capacity : (h + 1) * capacity, m * head_dim : (m + 1) * head_dim
-                ] = packed.reshape(owners, capacity, head_dim)
+
+        def place_sums(part_refs):
+            for h in range(heads):
+                place = iota((slots, rows), 0) == slot_ref[h : h + 1, :]
+                place = place.astype(BF16)
+                for m in range(2):
+                    cols = slice((m * heads + h) * head_dim, (m * heads + h + 1) * head_dim)
+                    total = own_ref[:, cols].astype(F32)
+                    for ref in part_refs:
+                        total += ref[:, cols].astype(F32)
+                    packed = jnp.dot(
+                        place, total.astype(BF16), preferred_element_type=F32
+                    ).astype(BF16)
+                    out_ref[
+                        :, h * capacity : (h + 1) * capacity, m * head_dim : (m + 1) * head_dim
+                    ] = packed.reshape(owners, capacity, head_dim)
+
+        @pl.when(core_ref[0] == 1)
+        def _():
+            place_sums(refs[:count])
+
+        @pl.when(core_ref[0] == 0)
+        def _():
+            place_sums(refs[count : 2 * count])
 
     return vmem_call(
         kernel,
         jax.ShapeDtypeStruct((owners, heads * capacity, 2 * head_dim), BF16),
-        (False,) * (len(partials) + 2),
-    )(*partials, slot_row, ready)
+        (True,) + (False,) * (len(received) + 3),
+    )(scalar(core), own, *received, slot_row, ready)
 
 
 def attend(blocks, members, capacity):
@@ -284,25 +306,25 @@
 
     four = lax.all_gather(own, "zq", axis=0)
     below = shifted(four, 1, CLU)
-    later, pieces = lax.optimization_barrier((four, pieces))
-    above = shifted(later, -1, CLU)
-    beyond = [shifted(four[:2], 2, CLU), shifted(four[2:], -2, CLU)]
-    ring = jnp.concatenate(
-        [part[:, :, :width].reshape(-1, width) for part in (four, below, above, *beyond)], axis=0
-    )
+    above = shifted(four, -1, CLU)
+    low = shifted(four[:2], 2, CLU)
+    later, pieces = lax.optimization_barrier((four[2:], pieces))
+    high = shifted(later, -2, CLU)
+    parts = [four, below, above, low, high]
+    ring = assemble(parts, [(0, 0), (3, 0), (1, 0), (2, 0), (2, 2)], me, width)
+    slot_row, slot_col = routing(clusters[0], owners, capacity)
+    ring, slot_row = lax.optimization_barrier((ring, slot_row))
     other = lax.ppermute(ring, "core", [(0, 1), (1, 0)])
-    places = [(kind, j) for kind in (0, 3, 1, 2) for j in range(4)]
     steps = (2, 1, -1, 0)
-    sent = project(pieces, ring, other, lax.axis_index("x"), me, steps, places)
-    received, ready = exchange_x(sent[:-1], steps[:-1])
-    partials = [sent[-1]] + received
-
-    slot_row, slot_col = routing(clusters[0], owners, capacity)
-    outgoing = pack(partials, ready, slot_row, owners, capacity, head_dim)
+    *sent, kept = project(pieces, ring, other, lax.axis_index("x"), steps)
+    received, ready = exchange_x(sent, steps[:-1])
+    outgoing = pack(
+        kept, received, ready, slot_row, lax.axis_index("core"), owners, capacity, head_dim
+    )
     incoming = lax.all_to_all(outgoing, CLU, split_axis=0, concat_axis=0, tiled=True)
 
     by_class = jnp.stack(
-        [part[:, :16, width:] for part in (four, above, jnp.concatenate(beyond), below)]
+        [part[:, :16, width:] for part in (four, above, jnp.concatenate([low, high]), below)]
     )
     by_class = jnp.roll(by_class, lax.axis_index("zr"), axis=0)
     all_ids = by_class.transpose(1, 0, 2, 3).reshape((owners,) + by_class.shape[2:])

time: 188 us -> 178 us (0.947)
  local copies, waits for them, and re-layouts: 7.81 us -> 2.7 us
  starting transfers between devices: 46.5 us -> 42.7 us
    ppermute x4, starting transfers between devices: 19.1 us -> 14.2 us  [shifted(): lax.ppermute(block, axis, [(i, (i + step) % size) for i in range(size)])]
    unnamed x31 -> x11, local copies, waits for them, and re-layouts: 6.82 us -> 2.5 us
    all_to_all x1, waiting for transfers between devices: 28.6 us -> 32.2 us  [body(): lax.all_to_all(outgoing, CLU, split_axis=0, concat_axis=0, tiled=True)]
    ppermute x6, starting transfers between devices: 11 us -> 13.8 us  [exchange_x(): received.append(lax.ppermute(parts[i], ('x', 'core'), pairs))]
    ppermute x6, waiting for transfers between devices: 10.2 us -> 7.37 us  [exchange_x(): received.append(lax.ppermute(parts[i], ('x', 'core'), pairs))]
  transfers between devices with their start and end apart: 14 -> 14, of which waited for: 8 -> 9; matrix products, arithmetic and copies ran while one was open for 2% -> 0% of each run, Pallas kernels for 1% -> 1%
where the time goes in v13:
time: 178 us; the launch traced here: 176 us
  waiting for transfers between devices  62.8 us (35%)
  blocking collectives  53.9 us (30%)
  starting transfers between devices  42.7 us (24%)
  Pallas kernels  13.1 us (7%)
  local copies, waits for them, and re-layouts  2.7 us (2%)
    all_to_all x1, waiting for transfers between devices, body(): lax.all_to_all(outgoing, CLU, split_axis=0, concat_axis=0, tiled=True)  32.2 us
    all_gather x1, blocking collectives, body(): four = lax.all_gather(own, 'zq', axis=0)  27.1 us
    all_to_all x1, blocking collectives, body(): lax.all_to_all(replies, CLU, split_axis=0, concat_axis=0, tiled=True)  26.8 us
    ppermute x1, waiting for transfers between devices, exchange_x(): ready = lax.ppermute(ready, 'core', [(1, 0)])  16 us
    ppermute x4, starting transfers between devices, shifted(): lax.ppermute(block, axis, [(i, (i + step) % size) for i in range(size)])  14.2 us
    ppermute x6, starting transfers between devices, exchange_x(): received.append(lax.ppermute(parts[i], ('x', 'core'), pairs))  13.8 us
    ppermute x6, waiting for transfers between devices, exchange_x(): received.append(lax.ppermute(parts[i], ('x', 'core'), pairs))  7.37 us
    all_to_all x1, starting transfers between devices, body(): lax.all_to_all(outgoing, CLU, split_axis=0, concat_axis=0, tiled=True)  7.01 us
  transfers between devices with their start and end apart: 14, of which 9 were waited for; matrix products, arithmetic and copies ran while one was open for 0% of the time, Pallas kernels for 1%

profile of v13, /device:TPU:24, one launch (start us, length us, event | category | flops | bytes accessed | tf_op | source)
XLA Modules:
  0.0 176.3 jit_solution(3963639921234613979)
XLA Ops:
  1.6 1.6 copy-done
  3.2 1.4 shard_map.37
  4.6 4.5 %all-to-all-start = ((bf16[4,256,1024]{2,1,0:T(8,128)(2,1)}), bf16[4,256,1024]{2,1,0:T(8,128)(2,1)}, u32[]{:S(2)}, u32[]{:S(2)}) async-start(bf16[4,256,1024]{2,1,0:T(8,128)(2,1)} %shard_map.37), calls=%async_computation | async-start | bytes 4194304 | tf_op jit(solution)/shard_map/all_to_all | solution.py:305
  9.0 27.1 %all-gather = bf16[128,1152]{1,0:T(8,128)(2,1)S(1)} all-gather(bf16[32,1152]{1,0:T(8,128)(2,1)S(1)} %fusion.1), channel_id=2, replica_groups=mesh['x'=4,'core'=2,'zq'=4,'zr'=4,'tp'=4] {'zq'}, dimensions={0}, use_global_device_ids=true | all-gather | bytes 368640 | tf_op jit(solution)/shard_map/all_gather | solution.py:307
  36.1 4.2 %collective-permute-start.1 = (bf16[4,32,1152]{2,1,0:T(8,128)(2,1)S(1)}, bf16[4,32,1152]{2,1,0:T(8,128)(2,1)S(1)}, u32[]{:S(2)}, u32[]{:S(2)}) collective-permute-start(bf16[4,32,1152]{2,1,0:T(8,128)(2,1)S(1)} %bitcast.38), channel_id=1, source_target_pairs={{0,60},{4,0},{8,4},{12,8},{16,12},{20,16},{24,20},{28,24},{32,28},... | collective-permute-start | bytes 884744 | tf_op jit(solution)/shard_map/ppermute | solution.py:286
  40.4 2.0 %collective-permute-start = (bf16[4,32,1152]{2,1,0:T(8,128)(2,1)S(1)}, bf16[4,32,1152]{2,1,0:T(8,128)(2,1)S(1)}, u32[]{:S(2)}, u32[]{:S(2)}) collective-permute-start(bf16[4,32,1152]{2,1,0:T(8,128)(2,1)S(1)} %bitcast.39), channel_id=1, source_target_pairs={{0,4},{4,8},{8,12},{12,16},{16,20},{20,24},{24,28},{28,32},{32,36}... | collective-permute-start | bytes 884744 | tf_op jit(solution)/shard_map/ppermute | solution.py:286
  42.4 4.0 %collective-permute-start.2 = (bf16[2,32,1152]{2,1,0:T(8,128)(2,1)S(1)}, bf16[2,32,1152]{2,1,0:T(8,128)(2,1)S(1)}, u32[]{:S(2)}, u32[]{:S(2)}) collective-permute-start(bf16[2,32,1152]{2,1,0:T(8,128)(2,1)S(1)} %bitcast.49), channel_id=1, source_target_pairs={{0,8},{4,12},{8,16},{12,20},{16,24},{20,28},{24,32},{28,36},{32,40... | collective-permute-start | bytes 442376 | tf_op jit(solution)/shard_map/ppermute | solution.py:286
  46.4 3.9 %collective-permute-start.3 = (bf16[2,32,1152]{2,1,0:T(8,128)(2,1)S(1)}, bf16[2,32,1152]{2,1,0:T(8,128)(2,1)S(1)}, u32[]{:S(2)}, u32[]{:S(2)}) collective-permute-start(bf16[2,32,1152]{2,1,0:T(8,128)(2,1)S(1)} %bitcast.48), channel_id=1, source_target_pairs={{0,56},{4,60},{8,0},{12,4},{16,8},{20,12},{24,16},{28,20},{32,24},... | collective-permute-start | bytes 442376 | tf_op jit(solution)/shard_map/ppermute | solution.py:286
  51.2 2.7 %collective-permute-done.2.refs_3_ = bf16[2,32,1152]{2,1,0:T(8,128)(2,1)S(1)} collective-permute-done((bf16[2,32,1152]{2,1,0:T(8,128)(2,1)S(1)}, bf16[2,32,1152]{2,1,0:T(8,128)(2,1)S(1)}, u32[]{:S(2)}, u32[]{:S(2)}) %collective-permute-start.2) | collective-permute-done | bytes 147488 | tf_op jit(solution)/shard_map/ppermute | solution.py:286
  54.0 1.8 %collective-permute-done.3.refs_4_ = bf16[2,32,1152]{2,1,0:T(8,128)(2,1)S(1)} collective-permute-done((bf16[2,32,1152]{2,1,0:T(8,128)(2,1)S(1)}, bf16[2,32,1152]{2,1,0:T(8,128)(2,1)S(1)}, u32[]{:S(2)}, u32[]{:S(2)}) %collective-permute-start.3) | collective-permute-done | bytes 147488 | tf_op jit(solution)/shard_map/ppermute | solution.py:286
  55.8 1.9 %collective-permute-start.4 = (bf16[512,1024]{1,0:T(8,128)(2,1)S(1)}, bf16[512,1024]{1,0:T(8,128)(2,1)S(1)}, u32[]{:S(2)}, u32[]{:S(2)}) collective-permute-start(bf16[512,1024]{1,0:T(8,128)(2,1)S(1)} %shard_map.38.ring_ref), channel_id=1, source_target_pairs={{0,64},{64,0},{1,65},{65,1},{2,66},{66,2},{3,67},{67,3},{4,68},{68... | collective-permute-start | bytes 3145736 | tf_op jit(solution)/shard_map/ppermute | solution.py:317
  57.8 2.6 %collective-permute-done.4.other_ref = bf16[512,1024]{1,0:T(8,128)(2,1)S(1)} collective-permute-done((bf16[512,1024]{1,0:T(8,128)(2,1)S(1)}, bf16[512,1024]{1,0:T(8,128)(2,1)S(1)}, u32[]{:S(2)}, u32[]{:S(2)}) %collective-permute-start.4) | collective-permute-done | bytes 1048608 | tf_op jit(solution)/shard_map/ppermute | solution.py:317
  60.4 3.9 %shard_map.40 = (bf16[256,1024]{1,0:T(8,128)(2,1)S(1)}, bf16[256,1024]{1,0:T(8,128)(2,1)S(1)}, bf16[256,1024]{1,0:T(8,128)(2,1)S(1)}, bf16[256,1024]{1,0:T(8,128)(2,1)S(1)}) custom-call(s32[1]{0:T(128)} %bitcast.1.x_ref, bf16[4,256,1024]{2,1,0:T(8,128)(2,1)} %all-to-all-done.pieces_ref, bf16[512,1024]{1,0:T(8,128)(2,1)S(1)} %shard_map.38.ring_ref, ...), custom_call_target="tpu_custom_call" | custom-call | tf_op jit(solution)/shard_map/pallas_call | solution.py:167
  66.5 1.3 collective-permute-start.8
  67.8 16.0 %collective-permute-done.8.refs_7_ = bf16[16,128]{1,0:T(8,128)(2,1)S(1)} collective-permute-done((bf16[16,128]{1,0:T(8,128)(2,1)S(1)}, bf16[16,128]{1,0:T(8,128)(2,1)S(1)}, u32[]{:S(2)}, u32[]{:S(2)}) %collective-permute-start.8) | collective-permute-done | bytes 4128 | tf_op jit(solution)/shard_map/ppermute | solution.py:183
  83.8 4.7 %collective-permute-start.9 = (bf16[256,1024]{1,0:T(8,128)(2,1)S(1)}, bf16[256,1024]{1,0:T(8,128)(2,1)S(1)}, u32[]{:S(2)}, u32[]{:S(2)}) collective-permute-start(bf16[256,1024]{1,0:T(8,128)(2,1)S(1)} %get-tuple-element.31), channel_id=1, source_target_pairs={{0,256},{128,384},{256,0},{384,128},{1,257},{129,385},{257,1},{385... | collective-permute-start | bytes 1572872 | tf_op jit(solution)/shard_map/ppermute | solution.py:180
  88.5 3.3 %collective-permute-start.10 = (bf16[256,1024]{1,0:T(8,128)(2,1)S(1)}, bf16[256,1024]{1,0:T(8,128)(2,1)S(1)}, u32[]{:S(2)}, u32[]{:S(2)}) collective-permute-start(bf16[256,1024]{1,0:T(8,128)(2,1)S(1)} %get-tuple-element.32), channel_id=1, source_target_pairs={{0,128},{128,256},{256,384},{384,0},{1,129},{129,257},{257,385},{3... | collective-permute-start | bytes 1572872 | tf_op jit(solution)/shard_map/ppermute | solution.py:180
  91.9 3.7 %collective-permute-start.11 = (bf16[256,1024]{1,0:T(8,128)(2,1)S(1)}, bf16[256,1024]{1,0:T(8,128)(2,1)S(1)}, u32[]{:S(2)}, u32[]{:S(2)}) collective-permute-start(bf16[256,1024]{1,0:T(8,128)(2,1)S(1)} %get-tuple-element.33), channel_id=1, source_target_pairs={{0,384},{128,0},{256,128},{384,256},{1,385},{129,1},{257,129},{385... | collective-permute-start | bytes 1572872 | tf_op jit(solution)/shard_map/ppermute | solution.py:180
  96.5 5.5 %collective-permute-done.10.refs_4_ = bf16[256,1024]{1,0:T(8,128)(2,1)S(1)} collective-permute-done((bf16[256,1024]{1,0:T(8,128)(2,1)S(1)}, bf16[256,1024]{1,0:T(8,128)(2,1)S(1)}, u32[]{:S(2)}, u32[]{:S(2)}) %collective-permute-start.10) | collective-permute-done | bytes 524320 | tf_op jit(solution)/shard_map/ppermute | solution.py:180
  103.0 1.7 shard_map.41
  104.7 7.0 %all-to-all-start.1 = ((bf16[16,128,256]{2,1,0:T(8,128)(2,1)}), bf16[16,128,256]{2,1,0:T(8,128)(2,1)S(1)}, u32[]{:S(2)}, u32[]{:S(2)}) async-start(bf16[16,128,256]{2,1,0:T(8,128)(2,1)} %shard_map.41), calls=%async_computation.1 | async-start | bytes 2097152 | tf_op jit(solution)/shard_map/all_to_all | solution.py:324
  113.0 32.2 %all-to-all-done.1.block_ref = bf16[16,128,256]{2,1,0:T(8,128)(2,1)S(1)} async-done(((bf16[16,128,256]{2,1,0:T(8,128)(2,1)}), bf16[16,128,256]{2,1,0:T(8,128)(2,1)S(1)}, u32[]{:S(2)}, u32[]{:S(2)}) %all-to-all-start.1) | async-done | bytes 1048608 | tf_op jit(solution)/shard_map/all_to_all | solution.py:324
  145.2 3.1 %shard_map.43 = bf16[16,128,128]{2,1,0:T(8,128)(2,1)S(1)} custom-call(bf16[16,128,256]{2,1,0:T(8,128)(2,1)S(1)} %all-to-all-done.1.block_ref, bf16[4,16,512]{2,1,0:T(8,128)(2,1)S(1)} %shard_map.42.member_ref), custom_call_target="tpu_custom_call" | custom-call | tf_op jit(solution)/shard_map/pallas_call | solution.py:258
  148.3 26.8 %all_to_all.15.block_ref = bf16[16,128,128]{2,1,0:T(8,128)(2,1)S(1)} all-to-all(bf16[16,128,128]{2,1,0:T(8,128)(2,1)S(1)} %shard_map.43), channel_id=1, replica_groups=mesh['x'=4,'core'=2,'zq'=4,'zr'=4,'tp'=4] {'zq','zr'}, dimensions={0} | all-to-all | bytes 1048576 | tf_op jit(solution)/shard_map/all_to_all | solution.py:333
  (35 shorter events, 8.9 us)
Async XLA Ops:
  1.6 1.6 copy-start
  4.5 45.8 %copy-start.1 = (s32[1,256,4]{1,2,0:T(4,128)S(1)}, s32[1,256,4]{1,2,0:T(4,128)}, u32[]{:S(2)}) copy-start(s32[1,256,4]{1,2,0:T(4,128)} %param.5) | copy-start | bytes 12292
  4.6 41.9 %all-to-all-start = ((bf16[4,256,1024]{2,1,0:T(8,128)(2,1)}), bf16[4,256,1024]{2,1,0:T(8,128)(2,1)}, u32[]{:S(2)}, u32[]{:S(2)}) async-start(bf16[4,256,1024]{2,1,0:T(8,128)(2,1)} %shard_map.37), calls=%async_computation | async-start | bytes 4194304 | tf_op jit(solution)/shard_map/all_to_all | solution.py:305
  36.1 17.8 %collective-permute-start.1 = (bf16[4,32,1152]{2,1,0:T(8,128)(2,1)S(1)}, bf16[4,32,1152]{2,1,0:T(8,128)(2,1)S(1)}, u32[]{:S(2)}, u32[]{:S(2)}) collective-permute-start(bf16[4,32,1152]{2,1,0:T(8,128)(2,1)S(1)} %bitcast.38), channel_id=1, source_target_pairs={{0,60},{4,0},{8,4},{12,8},{16,12},{20,16},{24,20},{28,24},{32,28},... | collective-permute-start | bytes 884744 | tf_op jit(solution)/shard_map/ppermute | solution.py:286
  40.4 13.7 %collective-permute-start = (bf16[4,32,1152]{2,1,0:T(8,128)(2,1)S(1)}, bf16[4,32,1152]{2,1,0:T(8,128)(2,1)S(1)}, u32[]{:S(2)}, u32[]{:S(2)}) collective-permute-start(bf16[4,32,1152]{2,1,0:T(8,128)(2,1)S(1)} %bitcast.39), channel_id=1, source_target_pairs={{0,4},{4,8},{8,12},{12,16},{16,20},{20,24},{24,28},{28,32},{32,36}... | collective-permute-start | bytes 884744 | tf_op jit(solution)/shard_map/ppermute | solution.py:286
  42.4 11.5 %collective-permute-start.2 = (bf16[2,32,1152]{2,1,0:T(8,128)(2,1)S(1)}, bf16[2,32,1152]{2,1,0:T(8,128)(2,1)S(1)}, u32[]{:S(2)}, u32[]{:S(2)}) collective-permute-start(bf16[2,32,1152]{2,1,0:T(8,128)(2,1)S(1)} %bitcast.49), channel_id=1, source_target_pairs={{0,8},{4,12},{8,16},{12,20},{16,24},{20,28},{24,32},{28,36},{32,40... | collective-permute-start | bytes 442376 | tf_op jit(solution)/shard_map/ppermute | solution.py:286
  46.4 9.3 %collective-permute-start.3 = (bf16[2,32,1152]{2,1,0:T(8,128)(2,1)S(1)}, bf16[2,32,1152]{2,1,0:T(8,128)(2,1)S(1)}, u32[]{:S(2)}, u32[]{:S(2)}) collective-permute-start(bf16[2,32,1152]{2,1,0:T(8,128)(2,1)S(1)} %bitcast.48), channel_id=1, source_target_pairs={{0,56},{4,60},{8,0},{12,4},{16,8},{20,12},{24,16},{28,20},{32,24},... | collective-permute-start | bytes 442376 | tf_op jit(solution)/shard_map/ppermute | solution.py:286
  55.8 4.6 %collective-permute-start.4 = (bf16[512,1024]{1,0:T(8,128)(2,1)S(1)}, bf16[512,1024]{1,0:T(8,128)(2,1)S(1)}, u32[]{:S(2)}, u32[]{:S(2)}) collective-permute-start(bf16[512,1024]{1,0:T(8,128)(2,1)S(1)} %shard_map.38.ring_ref), channel_id=1, source_target_pairs={{0,64},{64,0},{1,65},{65,1},{2,66},{66,2},{3,67},{67,3},{4,68},{68... | collective-permute-start | bytes 3145736 | tf_op jit(solution)/shard_map/ppermute | solution.py:317
  64.3 2.1 %collective-permute-start.5 = (bf16[256,1024]{1,0:T(8,128)(2,1)S(1)}, bf16[256,1024]{1,0:T(8,128)(2,1)S(1)}, u32[]{:S(2)}, u32[]{:S(2)}) collective-permute-start(bf16[256,1024]{1,0:T(8,128)(2,1)S(1)} %get-tuple-element.31), channel_id=1, source_target_pairs={{64,320},{192,448},{320,64},{448,192},{65,321},{193,449},{321,65},... | collective-permute-start | bytes 1572872 | tf_op jit(solution)/shard_map/ppermute | solution.py:180
  65.0 1.4 collective-permute-start.6
  65.7 0.7 collective-permute-start.7
  66.5 17.3 %collective-permute-start.8 = (bf16[16,128]{1,0:T(8,128)(2,1)S(1)}, bf16[16,128]{1,0:T(8,128)(2,1)S(1)}, u32[]{:S(2)}, u32[]{:S(2)}) collective-permute-start(bf16[16,128]{1,0:T(8,128)(2,1)S(1)} %slice_add_fusion), channel_id=1, source_target_pairs={{64,0},{65,1},{66,2},{67,3},{68,4},{69,5},{70,6},{71,7},{72,8},{73... | collective-permute-start | bytes 12296 | tf_op jit(solution)/shard_map/ppermute | solution.py:183
  83.8 12.7 %collective-permute-start.9 = (bf16[256,1024]{1,0:T(8,128)(2,1)S(1)}, bf16[256,1024]{1,0:T(8,128)(2,1)S(1)}, u32[]{:S(2)}, u32[]{:S(2)}) collective-permute-start(bf16[256,1024]{1,0:T(8,128)(2,1)S(1)} %get-tuple-element.31), channel_id=1, source_target_pairs={{0,256},{128,384},{256,0},{384,128},{1,257},{129,385},{257,1},{385... | collective-permute-start | bytes 1572872 | tf_op jit(solution)/shard_map/ppermute | solution.py:180
  88.5 13.5 %collective-permute-start.10 = (bf16[256,1024]{1,0:T(8,128)(2,1)S(1)}, bf16[256,1024]{1,0:T(8,128)(2,1)S(1)}, u32[]{:S(2)}, u32[]{:S(2)}) collective-permute-start(bf16[256,1024]{1,0:T(8,128)(2,1)S(1)} %get-tuple-element.32), channel_id=1, source_target_pairs={{0,128},{128,256},{256,384},{384,0},{1,129},{129,257},{257,385},{3... | collective-permute-start | bytes 1572872 | tf_op jit(solution)/shard_map/ppermute | solution.py:180
  91.9 11.1 %collective-permute-start.11 = (bf16[256,1024]{1,0:T(8,128)(2,1)S(1)}, bf16[256,1024]{1,0:T(8,128)(2,1)S(1)}, u32[]{:S(2)}, u32[]{:S(2)}) collective-permute-start(bf16[256,1024]{1,0:T(8,128)(2,1)S(1)} %get-tuple-element.33), channel_id=1, source_target_pairs={{0,384},{128,0},{256,128},{384,256},{1,385},{129,1},{257,129},{385... | collective-permute-start | bytes 1572872 | tf_op jit(solution)/shard_map/ppermute | solution.py:180
  104.7 40.5 %all-to-all-start.1 = ((bf16[16,128,256]{2,1,0:T(8,128)(2,1)}), bf16[16,128,256]{2,1,0:T(8,128)(2,1)S(1)}, u32[]{:S(2)}, u32[]{:S(2)}) async-start(bf16[16,128,256]{2,1,0:T(8,128)(2,1)} %shard_map.41), calls=%async_computation.1 | async-start | bytes 2097152 | tf_op jit(solution)/shard_map/all_to_all | solution.py:324

commit v14 on v13

--- a/solution.py
+++ b/solution.py
@@ -9,6 +9,7 @@
 BF16 = jnp.bfloat16
 F32 = jnp.float32
 VMEM_LIMIT = 48 * 1024 * 1024
+CUT_LIMIT = 62 * 1024 * 1024
 
 
 def vmem_call(kernel, out_shape, in_smem, **kwargs):
@@ -103,33 +104,45 @@
     rows, depth = local_rows.shape
     half = depth // chips // 2
 
-    def kernel(core_ref, in_ref, out_ref, sems):
-        copies = []
-        for p in range(chips):
-            for j in range(2):
-                first = (2 * p + lax.rem(core_ref[0] + j, 2)) * half
-                copies.append(
-                    pltpu.make_async_copy(
-                        in_ref.at[:, pl.ds(pl.multiple_of(first, half), half)],
-                        out_ref.at[p, :, j * half : (j + 1) * half],
-                        sems.at[2 * p + j],
-                    )
+    def kernel(core_ref, in_ref, out_ref, block_ref, in_sems, out_sems):
+        blocks = [(p, j) for p in range(chips) for j in range(2)]
+        reads, writes = [], []
+        for i, (p, j) in enumerate(blocks):
+            first = (2 * p + lax.rem(core_ref[0] + j, 2)) * half
+            reads.append(
+                pltpu.make_async_copy(
+                    in_ref.at[:, pl.ds(pl.multiple_of(first, half), half)],
+                    block_ref.at[i],
+                    in_sems.at[i],
                 )
-        for copy in copies:
-            copy.start()
-        for copy in copies:
-            copy.wait()
+            )
+            writes.append(
+                pltpu.make_async_copy(
+                    block_ref.at[i], out_ref.at[p, :, j * half : (j + 1) * half], out_sems.at[i]
+                )
+            )
+        for read in reads:
+            read.start()
+        for read, write in zip(reads, writes):
+            read.wait()
+            write.start()
+        for write in writes:
+            write.wait()
 
     return pl.pallas_call(
         kernel,
         out_shape=jax.ShapeDtypeStruct((chips, rows, 2 * half), BF16),
         in_specs=[
             pl.BlockSpec(memory_space=pltpu.SMEM),
-            pl.BlockSpec(memory_space=pltpu.VMEM),
+            pl.BlockSpec(memory_space=pl.ANY),
         ],
         out_specs=pl.BlockSpec(memory_space=pl.ANY),
-        scratch_shapes=[pltpu.SemaphoreType.DMA((2 * chips,))],
-        compiler_params=pltpu.CompilerParams(vmem_limit_bytes=VMEM_LIMIT),
+        scratch_shapes=[
+            pltpu.VMEM((2 * chips, rows, half), BF16),
+            pltpu.SemaphoreType.DMA((2 * chips,)),
+            pltpu.SemaphoreType.DMA((2 * chips,)),
+        ],
+        compiler_params=pltpu.CompilerParams(vmem_limit_bytes=CUT_LIMIT),
     )(scalar(core), local_rows)
 
 
@@ -179,8 +192,7 @@
             pairs = [(2 * x + core, (x + step) % chips * 2 + core) for x in range(chips)]
             received.append(lax.ppermute(parts[i], ("x", "core"), pairs))
         if core == 1:
-            ready = sum(part[:16, :128] for part in received)
-            ready = lax.ppermute(ready, "core", [(1, 0)])
+            ready = lax.ppermute(received[0][:16, :128], "core", [(1, 0)])
             parts, ready = lax.optimization_barrier((parts, ready))
     return received, ready
 

time: 178 us -> 199 us (1.12)
  blocking collectives: 53.9 us -> 64 us
  waiting for transfers between devices: 62.8 us -> 71.9 us
    all_to_all x1, waiting for transfers between devices: 32.2 us -> 42.8 us  [body(): lax.all_to_all(outgoing, CLU, split_axis=0, concat_axis=0, tiled=True)]
    all_to_all x1, blocking collectives: 26.8 us -> 36.9 us  [body(): lax.all_to_all(replies, CLU, split_axis=0, concat_axis=0, tiled=True)]
    ppermute x1, waiting for transfers between devices: 16 us -> 10.1 us  [exchange_x(): ready = lax.ppermute(received[0][:16, :128], 'core', [(1, 0)])]
    ppermute x6, waiting for transfers between devices: 7.37 us -> 11.8 us  [exchange_x(): received.append(lax.ppermute(parts[i], ('x', 'core'), pairs))]
where the time goes in v14:
time: 199 us; the launch traced here: 195 us
  waiting for transfers between devices  71.9 us (36%)
  blocking collectives  64 us (32%)
  starting transfers between devices  43 us (22%)
  Pallas kernels  14.2 us (7%)
    all_to_all x1, waiting for transfers between devices, body(): lax.all_to_all(outgoing, CLU, split_axis=0, concat_axis=0, tiled=True)  42.8 us
    all_to_all x1, blocking collectives, body(): lax.all_to_all(replies, CLU, split_axis=0, concat_axis=0, tiled=True)  36.9 us
    all_gather x1, blocking collectives, body(): four = lax.all_gather(own, 'zq', axis=0)  27.1 us
    ppermute x6, starting transfers between devices, exchange_x(): received.append(lax.ppermute(parts[i], ('x', 'core'), pairs))  14.2 us
    ppermute x4, starting transfers between devices, shifted(): lax.ppermute(block, axis, [(i, (i + step) % size) for i in range(size)])  14.2 us
    ppermute x6, waiting for transfers between devices, exchange_x(): received.append(lax.ppermute(parts[i], ('x', 'core'), pairs))  11.8 us
    ppermute x1, waiting for transfers between devices, exchange_x(): ready = lax.ppermute(received[0][:16, :128], 'core', [(1, 0)])  10.1 us
    all_to_all x1, starting transfers between devices, body(): lax.all_to_all(outgoing, CLU, split_axis=0, concat_axis=0, tiled=True)  7.01 us
  transfers between devices with their start and end apart: 14, of which 9 were waited for; matrix products, arithmetic and copies ran while one was open for 0% of the time, Pallas kernels for 1%

profile of v14, /device:TPU:24, one launch (start us, length us, event | category | flops | bytes accessed | tf_op | source)
XLA Modules:
  0.0 195.3 jit_solution(4011792403156114839)
XLA Ops:
  1.6 2.4 %shard_map.37 = bf16[4,256,1024]{2,1,0:T(8,128)(2,1)} custom-call(s32[1]{0:T(128)} %bitcast.core_ref, bf16[256,4096]{1,0:T(8,128)(2,1)} %bitcast.46), custom_call_target="tpu_custom_call" | custom-call | tf_op jit(solution)/shard_map/pallas_call | solution.py:132
  4.0 4.5 %all-to-all-start = ((bf16[4,256,1024]{2,1,0:T(8,128)(2,1)}), bf16[4,256,1024]{2,1,0:T(8,128)(2,1)}, u32[]{:S(2)}, u32[]{:S(2)}) async-start(bf16[4,256,1024]{2,1,0:T(8,128)(2,1)} %shard_map.37), calls=%async_computation | async-start | bytes 4194304 | tf_op jit(solution)/shard_map/all_to_all | solution.py:317
  8.5 27.1 %all-gather = bf16[128,1152]{1,0:T(8,128)(2,1)S(1)} all-gather(bf16[32,1152]{1,0:T(8,128)(2,1)S(1)} %fusion.1), channel_id=2, replica_groups=mesh['x'=4,'core'=2,'zq'=4,'zr'=4,'tp'=4] {'zq'}, dimensions={0}, use_global_device_ids=true | all-gather | bytes 368640 | tf_op jit(solution)/shard_map/all_gather | solution.py:319
  35.6 4.2 %collective-permute-start.1 = (bf16[4,32,1152]{2,1,0:T(8,128)(2,1)S(1)}, bf16[4,32,1152]{2,1,0:T(8,128)(2,1)S(1)}, u32[]{:S(2)}, u32[]{:S(2)}) collective-permute-start(bf16[4,32,1152]{2,1,0:T(8,128)(2,1)S(1)} %bitcast.38), channel_id=1, source_target_pairs={{0,60},{4,0},{8,4},{12,8},{16,12},{20,16},{24,20},{28,24},{32,28},... | collective-permute-start | bytes 884744 | tf_op jit(solution)/shard_map/ppermute | solution.py:298
  39.8 2.0 %collective-permute-start = (bf16[4,32,1152]{2,1,0:T(8,128)(2,1)S(1)}, bf16[4,32,1152]{2,1,0:T(8,128)(2,1)S(1)}, u32[]{:S(2)}, u32[]{:S(2)}) collective-permute-start(bf16[4,32,1152]{2,1,0:T(8,128)(2,1)S(1)} %bitcast.39), channel_id=1, source_target_pairs={{0,4},{4,8},{8,12},{12,16},{16,20},{20,24},{24,28},{28,32},{32,36}... | collective-permute-start | bytes 884744 | tf_op jit(solution)/shard_map/ppermute | solution.py:298
  41.8 4.0 %collective-permute-start.2 = (bf16[2,32,1152]{2,1,0:T(8,128)(2,1)S(1)}, bf16[2,32,1152]{2,1,0:T(8,128)(2,1)S(1)}, u32[]{:S(2)}, u32[]{:S(2)}) collective-permute-start(bf16[2,32,1152]{2,1,0:T(8,128)(2,1)S(1)} %bitcast.49), channel_id=1, source_target_pairs={{0,8},{4,12},{8,16},{12,20},{16,24},{20,28},{24,32},{28,36},{32,40... | collective-permute-start | bytes 442376 | tf_op jit(solution)/shard_map/ppermute | solution.py:298
  45.9 3.9 %collective-permute-start.3 = (bf16[2,32,1152]{2,1,0:T(8,128)(2,1)S(1)}, bf16[2,32,1152]{2,1,0:T(8,128)(2,1)S(1)}, u32[]{:S(2)}, u32[]{:S(2)}) collective-permute-start(bf16[2,32,1152]{2,1,0:T(8,128)(2,1)S(1)} %bitcast.48), channel_id=1, source_target_pairs={{0,56},{4,60},{8,0},{12,4},{16,8},{20,12},{24,16},{28,20},{32,24},... | collective-permute-start | bytes 442376 | tf_op jit(solution)/shard_map/ppermute | solution.py:298
  50.6 2.7 %collective-permute-done.2.refs_3_ = bf16[2,32,1152]{2,1,0:T(8,128)(2,1)S(1)} collective-permute-done((bf16[2,32,1152]{2,1,0:T(8,128)(2,1)S(1)}, bf16[2,32,1152]{2,1,0:T(8,128)(2,1)S(1)}, u32[]{:S(2)}, u32[]{:S(2)}) %collective-permute-start.2) | collective-permute-done | bytes 147488 | tf_op jit(solution)/shard_map/ppermute | solution.py:298
  53.4 1.8 collective-permute-done.3.refs_4_
  55.3 1.9 collective-permute-start.4
  57.2 2.6 %collective-permute-done.4.other_ref = bf16[512,1024]{1,0:T(8,128)(2,1)S(1)} collective-permute-done((bf16[512,1024]{1,0:T(8,128)(2,1)S(1)}, bf16[512,1024]{1,0:T(8,128)(2,1)S(1)}, u32[]{:S(2)}, u32[]{:S(2)}) %collective-permute-start.4) | collective-permute-done | bytes 1048608 | tf_op jit(solution)/shard_map/ppermute | solution.py:329
  59.8 4.0 %shard_map.40 = (bf16[256,1024]{1,0:T(8,128)(2,1)S(1)}, bf16[256,1024]{1,0:T(8,128)(2,1)S(1)}, bf16[256,1024]{1,0:T(8,128)(2,1)S(1)}, bf16[256,1024]{1,0:T(8,128)(2,1)S(1)}) custom-call(s32[1]{0:T(128)} %bitcast.1.x_ref, bf16[4,256,1024]{2,1,0:T(8,128)(2,1)} %all-to-all-done.pieces_ref, bf16[512,1024]{1,0:T(8,128)(2,1)S(1)} %shard_map.38.ring_ref, ...), custom_call_target="tpu_custom_call" | custom-call | tf_op jit(solution)/shard_map/pallas_call | solution.py:180
  67.2 10.1 %collective-permute-done.8.refs_7_ = bf16[16,128]{1,0:T(8,128)(2,1)S(1)} collective-permute-done((bf16[16,128]{1,0:T(8,128)(2,1)S(1)}, bf16[16,128]{1,0:T(8,128)(2,1)S(1)}, u32[]{:S(2)}, u32[]{:S(2)}) %collective-permute-start.8) | collective-permute-done | bytes 4128 | tf_op jit(solution)/shard_map/ppermute | solution.py:195
  77.3 5.1 %collective-permute-start.9 = (bf16[256,1024]{1,0:T(8,128)(2,1)S(1)}, bf16[256,1024]{1,0:T(8,128)(2,1)S(1)}, u32[]{:S(2)}, u32[]{:S(2)}) collective-permute-start(bf16[256,1024]{1,0:T(8,128)(2,1)S(1)} %get-tuple-element.31), channel_id=1, source_target_pairs={{0,256},{128,384},{256,0},{384,128},{1,257},{129,385},{257,1},{385... | collective-permute-start | bytes 1572872 | tf_op jit(solution)/shard_map/ppermute | solution.py:193
  82.4 2.5 %collective-permute-start.10 = (bf16[256,1024]{1,0:T(8,128)(2,1)S(1)}, bf16[256,1024]{1,0:T(8,128)(2,1)S(1)}, u32[]{:S(2)}, u32[]{:S(2)}) collective-permute-start(bf16[256,1024]{1,0:T(8,128)(2,1)S(1)} %get-tuple-element.32), channel_id=1, source_target_pairs={{0,128},{128,256},{256,384},{384,0},{1,129},{129,257},{257,385},{3... | collective-permute-start | bytes 1572872 | tf_op jit(solution)/shard_map/ppermute | solution.py:193
  84.8 4.6 %collective-permute-start.11 = (bf16[256,1024]{1,0:T(8,128)(2,1)S(1)}, bf16[256,1024]{1,0:T(8,128)(2,1)S(1)}, u32[]{:S(2)}, u32[]{:S(2)}) collective-permute-start(bf16[256,1024]{1,0:T(8,128)(2,1)S(1)} %get-tuple-element.33), channel_id=1, source_target_pairs={{0,384},{128,0},{256,128},{384,256},{1,385},{129,1},{257,129},{385... | collective-permute-start | bytes 1572872 | tf_op jit(solution)/shard_map/ppermute | solution.py:193
  89.5 5.3 %collective-permute-done.9.refs_3_ = bf16[256,1024]{1,0:T(8,128)(2,1)S(1)} collective-permute-done((bf16[256,1024]{1,0:T(8,128)(2,1)S(1)}, bf16[256,1024]{1,0:T(8,128)(2,1)S(1)}, u32[]{:S(2)}, u32[]{:S(2)}) %collective-permute-start.9) | collective-permute-done | bytes 524320 | tf_op jit(solution)/shard_map/ppermute | solution.py:193
  94.8 4.5 %collective-permute-done.10.refs_4_ = bf16[256,1024]{1,0:T(8,128)(2,1)S(1)} collective-permute-done((bf16[256,1024]{1,0:T(8,128)(2,1)S(1)}, bf16[256,1024]{1,0:T(8,128)(2,1)S(1)}, u32[]{:S(2)}, u32[]{:S(2)}) %collective-permute-start.10) | collective-permute-done | bytes 524320 | tf_op jit(solution)/shard_map/ppermute | solution.py:193
  99.2 2.1 %collective-permute-done.11.refs_5_ = bf16[256,1024]{1,0:T(8,128)(2,1)S(1)} collective-permute-done((bf16[256,1024]{1,0:T(8,128)(2,1)S(1)}, bf16[256,1024]{1,0:T(8,128)(2,1)S(1)}, u32[]{:S(2)}, u32[]{:S(2)}) %collective-permute-start.11) | collective-permute-done | bytes 524320 | tf_op jit(solution)/shard_map/ppermute | solution.py:193
  101.3 1.8 shard_map.41
  103.0 7.0 %all-to-all-start.1 = ((bf16[16,128,256]{2,1,0:T(8,128)(2,1)}), bf16[16,128,256]{2,1,0:T(8,128)(2,1)S(1)}, u32[]{:S(2)}, u32[]{:S(2)}) async-start(bf16[16,128,256]{2,1,0:T(8,128)(2,1)} %shard_map.41), calls=%async_computation.1 | async-start | bytes 2097152 | tf_op jit(solution)/shard_map/all_to_all | solution.py:336
  111.3 42.8 %all-to-all-done.1.block_ref = bf16[16,128,256]{2,1,0:T(8,128)(2,1)S(1)} async-done(((bf16[16,128,256]{2,1,0:T(8,128)(2,1)}), bf16[16,128,256]{2,1,0:T(8,128)(2,1)S(1)}, u32[]{:S(2)}, u32[]{:S(2)}) %all-to-all-start.1) | async-done | bytes 1048608 | tf_op jit(solution)/shard_map/all_to_all | solution.py:336
  154.1 3.1 %shard_map.43 = bf16[16,128,128]{2,1,0:T(8,128)(2,1)S(1)} custom-call(bf16[16,128,256]{2,1,0:T(8,128)(2,1)S(1)} %all-to-all-done.1.block_ref, bf16[4,16,512]{2,1,0:T(8,128)(2,1)S(1)} %shard_map.42.member_ref), custom_call_target="tpu_custom_call" | custom-call | tf_op jit(solution)/shard_map/pallas_call | solution.py:270
  157.2 36.9 %all_to_all.15.block_ref = bf16[16,128,128]{2,1,0:T(8,128)(2,1)S(1)} all-to-all(bf16[16,128,128]{2,1,0:T(8,128)(2,1)S(1)} %shard_map.43), channel_id=1, replica_groups=mesh['x'=4,'core'=2,'zq'=4,'zr'=4,'tp'=4] {'zq','zr'}, dimensions={0} | all-to-all | bytes 1048576 | tf_op jit(solution)/shard_map/all_to_all | solution.py:345
  (33 shorter events, 8.3 us)
Async XLA Ops:
  4.0 45.8 %copy-start = (s32[1,256,4]{1,2,0:T(4,128)S(1)}, s32[1,256,4]{1,2,0:T(4,128)}, u32[]{:S(2)}) copy-start(s32[1,256,4]{1,2,0:T(4,128)} %param.5) | copy-start | bytes 12292
  4.0 41.9 %all-to-all-start = ((bf16[4,256,1024]{2,1,0:T(8,128)(2,1)}), bf16[4,256,1024]{2,1,0:T(8,128)(2,1)}, u32[]{:S(2)}, u32[]{:S(2)}) async-start(bf16[4,256,1024]{2,1,0:T(8,128)(2,1)} %shard_map.37), calls=%async_computation | async-start | bytes 4194304 | tf_op jit(solution)/shard_map/all_to_all | solution.py:317
  35.6 17.8 %collective-permute-start.1 = (bf16[4,32,1152]{2,1,0:T(8,128)(2,1)S(1)}, bf16[4,32,1152]{2,1,0:T(8,128)(2,1)S(1)}, u32[]{:S(2)}, u32[]{:S(2)}) collective-permute-start(bf16[4,32,1152]{2,1,0:T(8,128)(2,1)S(1)} %bitcast.38), channel_id=1, source_target_pairs={{0,60},{4,0},{8,4},{12,8},{16,12},{20,16},{24,20},{28,24},{32,28},... | collective-permute-start | bytes 884744 | tf_op jit(solution)/shard_map/ppermute | solution.py:298
  39.8 13.7 %collective-permute-start = (bf16[4,32,1152]{2,1,0:T(8,128)(2,1)S(1)}, bf16[4,32,1152]{2,1,0:T(8,128)(2,1)S(1)}, u32[]{:S(2)}, u32[]{:S(2)}) collective-permute-start(bf16[4,32,1152]{2,1,0:T(8,128)(2,1)S(1)} %bitcast.39), channel_id=1, source_target_pairs={{0,4},{4,8},{8,12},{12,16},{16,20},{20,24},{24,28},{28,32},{32,36}... | collective-permute-start | bytes 884744 | tf_op jit(solution)/shard_map/ppermute | solution.py:298
  41.8 11.5 %collective-permute-start.2 = (bf16[2,32,1152]{2,1,0:T(8,128)(2,1)S(1)}, bf16[2,32,1152]{2,1,0:T(8,128)(2,1)S(1)}, u32[]{:S(2)}, u32[]{:S(2)}) collective-permute-start(bf16[2,32,1152]{2,1,0:T(8,128)(2,1)S(1)} %bitcast.49), channel_id=1, source_target_pairs={{0,8},{4,12},{8,16},{12,20},{16,24},{20,28},{24,32},{28,36},{32,40... | collective-permute-start | bytes 442376 | tf_op jit(solution)/shard_map/ppermute | solution.py:298
  45.9 9.3 %collective-permute-start.3 = (bf16[2,32,1152]{2,1,0:T(8,128)(2,1)S(1)}, bf16[2,32,1152]{2,1,0:T(8,128)(2,1)S(1)}, u32[]{:S(2)}, u32[]{:S(2)}) collective-permute-start(bf16[2,32,1152]{2,1,0:T(8,128)(2,1)S(1)} %bitcast.48), channel_id=1, source_target_pairs={{0,56},{4,60},{8,0},{12,4},{16,8},{20,12},{24,16},{28,20},{32,24},... | collective-permute-start | bytes 442376 | tf_op jit(solution)/shard_map/ppermute | solution.py:298
  55.3 4.6 %collective-permute-start.4 = (bf16[512,1024]{1,0:T(8,128)(2,1)S(1)}, bf16[512,1024]{1,0:T(8,128)(2,1)S(1)}, u32[]{:S(2)}, u32[]{:S(2)}) collective-permute-start(bf16[512,1024]{1,0:T(8,128)(2,1)S(1)} %shard_map.38.ring_ref), channel_id=1, source_target_pairs={{0,64},{64,0},{1,65},{65,1},{2,66},{66,2},{3,67},{67,3},{4,68},{68... | collective-permute-start | bytes 3145736 | tf_op jit(solution)/shard_map/ppermute | solution.py:329
  63.8 0.7 collective-permute-start.5
  64.5 12.8 %collective-permute-start.8 = (bf16[16,128]{1,0:T(8,128)(2,1)S(1)}, bf16[16,128]{1,0:T(8,128)(2,1)S(1)}, u32[]{:S(2)}, u32[]{:S(2)}) collective-permute-start(bf16[16,128]{1,0:T(8,128)(2,1)S(1)} %slice.32), channel_id=1, source_target_pairs={{64,0},{65,1},{66,2},{67,3},{68,4},{69,5},{70,6},{71,7},{72,8},{73... | collective-permute-start | bytes 12296 | tf_op jit(solution)/shard_map/ppermute | solution.py:195
  65.8 23.6 %collective-permute-start.6 = (bf16[256,1024]{1,0:T(8,128)(2,1)S(1)}, bf16[256,1024]{1,0:T(8,128)(2,1)S(1)}, u32[]{:S(2)}, u32[]{:S(2)}) collective-permute-start(bf16[256,1024]{1,0:T(8,128)(2,1)S(1)} %get-tuple-element.32), channel_id=1, source_target_pairs={{64,192},{192,320},{320,448},{448,64},{65,193},{193,321},{321,449}... | collective-permute-start | bytes 1572872 | tf_op jit(solution)/shard_map/ppermute | solution.py:193
  66.5 22.9 %collective-permute-start.7 = (bf16[256,1024]{1,0:T(8,128)(2,1)S(1)}, bf16[256,1024]{1,0:T(8,128)(2,1)S(1)}, u32[]{:S(2)}, u32[]{:S(2)}) collective-permute-start(bf16[256,1024]{1,0:T(8,128)(2,1)S(1)} %get-tuple-element.33), channel_id=1, source_target_pairs={{64,448},{192,64},{320,192},{448,320},{65,449},{193,65},{321,193},... | collective-permute-start | bytes 1572872 | tf_op jit(solution)/shard_map/ppermute | solution.py:193
  77.3 17.5 %collective-permute-start.9 = (bf16[256,1024]{1,0:T(8,128)(2,1)S(1)}, bf16[256,1024]{1,0:T(8,128)(2,1)S(1)}, u32[]{:S(2)}, u32[]{:S(2)}) collective-permute-start(bf16[256,1024]{1,0:T(8,128)(2,1)S(1)} %get-tuple-element.31), channel_id=1, source_target_pairs={{0,256},{128,384},{256,0},{384,128},{1,257},{129,385},{257,1},{385... | collective-permute-start | bytes 1572872 | tf_op jit(solution)/shard_map/ppermute | solution.py:193
  82.4 16.8 %collective-permute-start.10 = (bf16[256,1024]{1,0:T(8,128)(2,1)S(1)}, bf16[256,1024]{1,0:T(8,128)(2,1)S(1)}, u32[]{:S(2)}, u32[]{:S(2)}) collective-permute-start(bf16[256,1024]{1,0:T(8,128)(2,1)S(1)} %get-tuple-element.32), channel_id=1, source_target_pairs={{0,128},{128,256},{256,384},{384,0},{1,129},{129,257},{257,385},{3... | collective-permute-start | bytes 1572872 | tf_op jit(solution)/shard_map/ppermute | solution.py:193
  84.8 16.4 %collective-permute-start.11 = (bf16[256,1024]{1,0:T(8,128)(2,1)S(1)}, bf16[256,1024]{1,0:T(8,128)(2,1)S(1)}, u32[]{:S(2)}, u32[]{:S(2)}) collective-permute-start(bf16[256,1024]{1,0:T(8,128)(2,1)S(1)} %get-tuple-element.33), channel_id=1, source_target_pairs={{0,384},{128,0},{256,128},{384,256},{1,385},{129,1},{257,129},{385... | collective-permute-start | bytes 1572872 | tf_op jit(solution)/shard_map/ppermute | solution.py:193
  103.0 51.1 %all-to-all-start.1 = ((bf16[16,128,256]{2,1,0:T(8,128)(2,1)}), bf16[16,128,256]{2,1,0:T(8,128)(2,1)S(1)}, u32[]{:S(2)}, u32[]{:S(2)}) async-start(bf16[16,128,256]{2,1,0:T(8,128)(2,1)} %shard_map.41), calls=%async_computation.1 | async-start | bytes 2097152 | tf_op jit(solution)/shard_map/all_to_all | solution.py:336

commit v15 on v14

--- a/solution.py
+++ b/solution.py
@@ -192,7 +192,8 @@
             pairs = [(2 * x + core, (x + step) % chips * 2 + core) for x in range(chips)]
             received.append(lax.ppermute(parts[i], ("x", "core"), pairs))
         if core == 1:
-            ready = lax.ppermute(received[0][:16, :128], "core", [(1, 0)])
+            ready = sum(part[:16, :128] for part in received)
+            ready = lax.ppermute(ready, "core", [(1, 0)])
             parts, ready = lax.optimization_barrier((parts, ready))
     return received, ready
 
@@ -203,38 +204,52 @@
     slots = owners * capacity
     count = len(received) // 2
 
-    def kernel(core_ref, own_ref, *refs):
-        slot_ref, _, out_ref = refs[-3:]
-
-        def place_sums(part_refs):
-            for h in range(heads):
-                place = iota((slots, rows), 0) == slot_ref[h : h + 1, :]
-                place = place.astype(BF16)
-                for m in range(2):
-                    cols = slice((m * heads + h) * head_dim, (m * heads + h + 1) * head_dim)
-                    total = own_ref[:, cols].astype(F32)
-                    for ref in part_refs:
-                        total += ref[:, cols].astype(F32)
-                    packed = jnp.dot(
-                        place, total.astype(BF16), preferred_element_type=F32
-                    ).astype(BF16)
-                    out_ref[
-                        :, h * capacity : (h + 1) * capacity, m * head_dim : (m + 1) * head_dim
-                    ] = packed.reshape(owners, capacity, head_dim)
-
-        @pl.when(core_ref[0] == 1)
-        def _():
-            place_sums(refs[:count])
-
-        @pl.when(core_ref[0] == 0)
-        def _():
-            place_sums(refs[count : 2 * count])
-
-    return vmem_call(
-        kernel,
-        jax.ShapeDtypeStruct((owners, heads * capacity, 2 * head_dim), BF16),
-        (True,) + (False,) * (len(received) + 3),
-    )(scalar(core), own, *received, slot_row, ready)
+    def kernel(core_ref, slot_ref, own_ref, *refs):
+        out_ref, part_ref, sems = refs[-3:]
+
+        def copies(part_refs):
+            return [
+                pltpu.make_async_copy(ref, part_ref.at[i], sems.at[i])
+                for i, ref in enumerate((own_ref,) + part_refs)
+            ]
+
+        for number, first in ((1, 0), (0, count)):
+
+            @pl.when(core_ref[0] == number)
+            def _():
+                for copy in copies(refs[first : first + count]):
+                    copy.start()
+                for copy in copies(refs[first : first + count]):
+                    copy.wait()
+
+        for h in range(heads):
+            place = iota((slots, rows), 0) == slot_ref[h : h + 1, :]
+            place = place.astype(BF16)
+            for m in range(2):
+                cols = slice((m * heads + h) * head_dim, (m * heads + h + 1) * head_dim)
+                total = part_ref[0, :, cols].astype(F32)
+                for i in range(1, count + 1):
+                    total += part_ref[i, :, cols].astype(F32)
+                packed = jnp.dot(
+                    place, total.astype(BF16), preferred_element_type=F32
+                ).astype(BF16)
+                out_ref[
+                    :, h * capacity : (h + 1) * capacity, m * head_dim : (m + 1) * head_dim
+                ] = packed.reshape(owners, capacity, head_dim)
+
+    vmem = pl.BlockSpec(memory_space=pltpu.VMEM)
+    whole = pl.BlockSpec(memory_space=pl.ANY)
+    return pl.pallas_call(
+        kernel,
+        out_shape=jax.ShapeDtypeStruct((owners, heads * capacity, 2 * head_dim), BF16),
+        in_specs=[pl.BlockSpec(memory_space=pltpu.SMEM), vmem] + [whole] * (len(received) + 2),
+        out_specs=vmem,
+        scratch_shapes=[
+            pltpu.VMEM((count + 1, rows, width), BF16),
+            pltpu.SemaphoreType.DMA((count + 1,)),
+        ],
+        compiler_params=pltpu.CompilerParams(vmem_limit_bytes=VMEM_LIMIT),
+    )(scalar(core), slot_row, own, *received, ready)
 
 
 def attend(blocks, members, capacity):

time: 199 us -> 178 us (0.89)
  blocking collectives: 64 us -> 53.9 us
  waiting for transfers between devices: 71.9 us -> 62.8 us
    all_to_all x1, waiting for transfers between devices: 42.8 us -> 32.2 us  [body(): lax.all_to_all(outgoing, CLU, split_axis=0, concat_axis=0, tiled=True)]
    all_to_all x1, blocking collectives: 36.9 us -> 26.8 us  [body(): lax.all_to_all(replies, CLU, split_axis=0, concat_axis=0, tiled=True)]
    ppermute x1, waiting for transfers between devices: 10.1 us -> 16 us  [exchange_x(): ready = lax.ppermute(ready, 'core', [(1, 0)])]
    ppermute x6, waiting for transfers between devices: 11.8 us -> 7.37 us  [exchange_x(): received.append(lax.ppermute(parts[i], ('x', 'core'), pairs))]
where the time goes in v15:
time: 178 us; the launch traced here: 176 us
  waiting for transfers between devices  62.8 us (35%)
  blocking collectives  53.9 us (30%)
  starting transfers between devices  42.7 us (24%)
  Pallas kernels  14.4 us (8%)
    all_to_all x1, waiting for transfers between devices, body(): lax.all_to_all(outgoing, CLU, split_axis=0, concat_axis=0, tiled=True)  32.2 us
    all_gather x1, blocking collectives, body(): four = lax.all_gather(own, 'zq', axis=0)  27.1 us
    all_to_all x1, blocking collectives, body(): lax.all_to_all(replies, CLU, split_axis=0, concat_axis=0, tiled=True)  26.8 us
    ppermute x1, waiting for transfers between devices, exchange_x(): ready = lax.ppermute(ready, 'core', [(1, 0)])  16 us
    ppermute x4, starting transfers between devices, shifted(): lax.ppermute(block, axis, [(i, (i + step) % size) for i in range(size)])  14.2 us
    ppermute x6, starting transfers between devices, exchange_x(): received.append(lax.ppermute(parts[i], ('x', 'core'), pairs))  13.8 us
    ppermute x6, waiting for transfers between devices, exchange_x(): received.append(lax.ppermute(parts[i], ('x', 'core'), pairs))  7.37 us
    all_to_all x1, starting transfers between devices, body(): lax.all_to_all(outgoing, CLU, split_axis=0, concat_axis=0, tiled=True)  7.02 us
  transfers between devices with their start and end apart: 14, of which 9 were waited for; matrix products, arithmetic and copies ran while one was open for 0% of the time, Pallas kernels for 1%

profile of v15, /device:TPU:24, one launch (start us, length us, event | category | flops | bytes accessed | tf_op | source)
XLA Modules:
  0.0 176.0 jit_solution(16322074864587559572)
XLA Ops:
  1.6 2.4 %shard_map.37 = bf16[4,256,1024]{2,1,0:T(8,128)(2,1)} custom-call(s32[1]{0:T(128)} %bitcast.core_ref, bf16[256,4096]{1,0:T(8,128)(2,1)} %bitcast.46), custom_call_target="tpu_custom_call" | custom-call | tf_op jit(solution)/shard_map/pallas_call | solution.py:132
  4.0 4.5 %all-to-all-start = ((bf16[4,256,1024]{2,1,0:T(8,128)(2,1)}), bf16[4,256,1024]{2,1,0:T(8,128)(2,1)}, u32[]{:S(2)}, u32[]{:S(2)}) async-start(bf16[4,256,1024]{2,1,0:T(8,128)(2,1)} %shard_map.37), calls=%async_computation | async-start | bytes 4194304 | tf_op jit(solution)/shard_map/all_to_all | solution.py:332
  8.5 27.1 %all-gather = bf16[128,1152]{1,0:T(8,128)(2,1)S(1)} all-gather(bf16[32,1152]{1,0:T(8,128)(2,1)S(1)} %fusion.1), channel_id=2, replica_groups=mesh['x'=4,'core'=2,'zq'=4,'zr'=4,'tp'=4] {'zq'}, dimensions={0}, use_global_device_ids=true | all-gather | bytes 368640 | tf_op jit(solution)/shard_map/all_gather | solution.py:334
  35.6 4.2 %collective-permute-start.1 = (bf16[4,32,1152]{2,1,0:T(8,128)(2,1)S(1)}, bf16[4,32,1152]{2,1,0:T(8,128)(2,1)S(1)}, u32[]{:S(2)}, u32[]{:S(2)}) collective-permute-start(bf16[4,32,1152]{2,1,0:T(8,128)(2,1)S(1)} %bitcast.38), channel_id=1, source_target_pairs={{0,60},{4,0},{8,4},{12,8},{16,12},{20,16},{24,20},{28,24},{32,28},... | collective-permute-start | bytes 884744 | tf_op jit(solution)/shard_map/ppermute | solution.py:313
  39.8 2.0 %collective-permute-start = (bf16[4,32,1152]{2,1,0:T(8,128)(2,1)S(1)}, bf16[4,32,1152]{2,1,0:T(8,128)(2,1)S(1)}, u32[]{:S(2)}, u32[]{:S(2)}) collective-permute-start(bf16[4,32,1152]{2,1,0:T(8,128)(2,1)S(1)} %bitcast.39), channel_id=1, source_target_pairs={{0,4},{4,8},{8,12},{12,16},{16,20},{20,24},{24,28},{28,32},{32,36}... | collective-permute-start | bytes 884744 | tf_op jit(solution)/shard_map/ppermute | solution.py:313
  41.8 4.0 %collective-permute-start.2 = (bf16[2,32,1152]{2,1,0:T(8,128)(2,1)S(1)}, bf16[2,32,1152]{2,1,0:T(8,128)(2,1)S(1)}, u32[]{:S(2)}, u32[]{:S(2)}) collective-permute-start(bf16[2,32,1152]{2,1,0:T(8,128)(2,1)S(1)} %bitcast.49), channel_id=1, source_target_pairs={{0,8},{4,12},{8,16},{12,20},{16,24},{20,28},{24,32},{28,36},{32,40... | collective-permute-start | bytes 442376 | tf_op jit(solution)/shard_map/ppermute | solution.py:313
  45.9 3.9 %collective-permute-start.3 = (bf16[2,32,1152]{2,1,0:T(8,128)(2,1)S(1)}, bf16[2,32,1152]{2,1,0:T(8,128)(2,1)S(1)}, u32[]{:S(2)}, u32[]{:S(2)}) collective-permute-start(bf16[2,32,1152]{2,1,0:T(8,128)(2,1)S(1)} %bitcast.48), channel_id=1, source_target_pairs={{0,56},{4,60},{8,0},{12,4},{16,8},{20,12},{24,16},{28,20},{32,24},... | collective-permute-start | bytes 442376 | tf_op jit(solution)/shard_map/ppermute | solution.py:313
  50.6 2.7 %collective-permute-done.2.refs_3_ = bf16[2,32,1152]{2,1,0:T(8,128)(2,1)S(1)} collective-permute-done((bf16[2,32,1152]{2,1,0:T(8,128)(2,1)S(1)}, bf16[2,32,1152]{2,1,0:T(8,128)(2,1)S(1)}, u32[]{:S(2)}, u32[]{:S(2)}) %collective-permute-start.2) | collective-permute-done | bytes 147488 | tf_op jit(solution)/shard_map/ppermute | solution.py:313
  53.4 1.8 %collective-permute-done.3.refs_4_ = bf16[2,32,1152]{2,1,0:T(8,128)(2,1)S(1)} collective-permute-done((bf16[2,32,1152]{2,1,0:T(8,128)(2,1)S(1)}, bf16[2,32,1152]{2,1,0:T(8,128)(2,1)S(1)}, u32[]{:S(2)}, u32[]{:S(2)}) %collective-permute-start.3) | collective-permute-done | bytes 147488 | tf_op jit(solution)/shard_map/ppermute | solution.py:313
  55.3 1.9 %collective-permute-start.4 = (bf16[512,1024]{1,0:T(8,128)(2,1)S(1)}, bf16[512,1024]{1,0:T(8,128)(2,1)S(1)}, u32[]{:S(2)}, u32[]{:S(2)}) collective-permute-start(bf16[512,1024]{1,0:T(8,128)(2,1)S(1)} %shard_map.38.ring_ref), channel_id=1, source_target_pairs={{0,64},{64,0},{1,65},{65,1},{2,66},{66,2},{3,67},{67,3},{4,68},{68... | collective-permute-start | bytes 3145736 | tf_op jit(solution)/shard_map/ppermute | solution.py:344
  57.2 2.6 %collective-permute-done.4.other_ref = bf16[512,1024]{1,0:T(8,128)(2,1)S(1)} collective-permute-done((bf16[512,1024]{1,0:T(8,128)(2,1)S(1)}, bf16[512,1024]{1,0:T(8,128)(2,1)S(1)}, u32[]{:S(2)}, u32[]{:S(2)}) %collective-permute-start.4) | collective-permute-done | bytes 1048608 | tf_op jit(solution)/shard_map/ppermute | solution.py:344
  59.8 4.0 %shard_map.40 = (bf16[256,1024]{1,0:T(8,128)(2,1)S(1)}, bf16[256,1024]{1,0:T(8,128)(2,1)S(1)}, bf16[256,1024]{1,0:T(8,128)(2,1)S(1)}, bf16[256,1024]{1,0:T(8,128)(2,1)S(1)}) custom-call(s32[1]{0:T(128)} %bitcast.9.x_ref, bf16[4,256,1024]{2,1,0:T(8,128)(2,1)} %all-to-all-done.pieces_ref, bf16[512,1024]{1,0:T(8,128)(2,1)S(1)} %shard_map.38.ring_ref, ...), custom_call_target="tpu_custom_call" | custom-call | tf_op jit(solution)/shard_map/pallas_call | solution.py:180
  66.0 1.3 collective-permute-start.8
  67.3 16.0 %collective-permute-done.8.refs_6_ = bf16[16,128]{1,0:T(8,128)(2,1)S(1)} collective-permute-done((bf16[16,128]{1,0:T(8,128)(2,1)S(1)}, bf16[16,128]{1,0:T(8,128)(2,1)S(1)}, u32[]{:S(2)}, u32[]{:S(2)}) %collective-permute-start.8) | collective-permute-done | bytes 4128 | tf_op jit(solution)/shard_map/ppermute | solution.py:196
  83.3 4.7 %collective-permute-start.9 = (bf16[256,1024]{1,0:T(8,128)(2,1)S(1)}, bf16[256,1024]{1,0:T(8,128)(2,1)S(1)}, u32[]{:S(2)}, u32[]{:S(2)}) collective-permute-start(bf16[256,1024]{1,0:T(8,128)(2,1)S(1)} %get-tuple-element.32), channel_id=1, source_target_pairs={{0,256},{128,384},{256,0},{384,128},{1,257},{129,385},{257,1},{385... | collective-permute-start | bytes 1572872 | tf_op jit(solution)/shard_map/ppermute | solution.py:193
  88.0 3.3 %collective-permute-start.10 = (bf16[256,1024]{1,0:T(8,128)(2,1)S(1)}, bf16[256,1024]{1,0:T(8,128)(2,1)S(1)}, u32[]{:S(2)}, u32[]{:S(2)}) collective-permute-start(bf16[256,1024]{1,0:T(8,128)(2,1)S(1)} %get-tuple-element.33), channel_id=1, source_target_pairs={{0,128},{128,256},{256,384},{384,0},{1,129},{129,257},{257,385},{3... | collective-permute-start | bytes 1572872 | tf_op jit(solution)/shard_map/ppermute | solution.py:193
  91.4 3.7 %collective-permute-start.11 = (bf16[256,1024]{1,0:T(8,128)(2,1)S(1)}, bf16[256,1024]{1,0:T(8,128)(2,1)S(1)}, u32[]{:S(2)}, u32[]{:S(2)}) collective-permute-start(bf16[256,1024]{1,0:T(8,128)(2,1)S(1)} %get-tuple-element.34), channel_id=1, source_target_pairs={{0,384},{128,0},{256,128},{384,256},{1,385},{129,1},{257,129},{385... | collective-permute-start | bytes 1572872 | tf_op jit(solution)/shard_map/ppermute | solution.py:193
  96.0 5.5 %collective-permute-done.10.refs_4_ = bf16[256,1024]{1,0:T(8,128)(2,1)S(1)} collective-permute-done((bf16[256,1024]{1,0:T(8,128)(2,1)S(1)}, bf16[256,1024]{1,0:T(8,128)(2,1)S(1)}, u32[]{:S(2)}, u32[]{:S(2)}) %collective-permute-start.10) | collective-permute-done | bytes 524320 | tf_op jit(solution)/shard_map/ppermute | solution.py:193
  102.4 1.9 %shard_map.41 = bf16[16,128,256]{2,1,0:T(8,128)(2,1)} custom-call(s32[1]{0:T(128)} %bitcast.core_ref, s32[4,256]{1,0:T(4,128)S(1)} %get-tuple-element.25.slot_ref, bf16[256,1024]{1,0:T(8,128)(2,1)S(1)} %get-tuple-element.28.own_ref, bf16[256,1024]{1,0:T(8,128)(2,1)S(1)} %collective-permute-done.5.refs_0_, ...), custom_call_target="tpu_custom_call" | custom-call | tf_op jit(solution)/shard_map/pallas_call | solution.py:242
  104.4 7.0 %all-to-all-start.1 = ((bf16[16,128,256]{2,1,0:T(8,128)(2,1)}), bf16[16,128,256]{2,1,0:T(8,128)(2,1)S(1)}, u32[]{:S(2)}, u32[]{:S(2)}) async-start(bf16[16,128,256]{2,1,0:T(8,128)(2,1)} %shard_map.41), calls=%async_computation.1 | async-start | bytes 2097152 | tf_op jit(solution)/shard_map/all_to_all | solution.py:351
  112.7 32.2 %all-to-all-done.1.block_ref = bf16[16,128,256]{2,1,0:T(8,128)(2,1)S(1)} async-done(((bf16[16,128,256]{2,1,0:T(8,128)(2,1)}), bf16[16,128,256]{2,1,0:T(8,128)(2,1)S(1)}, u32[]{:S(2)}, u32[]{:S(2)}) %all-to-all-start.1) | async-done | bytes 1048608 | tf_op jit(solution)/shard_map/all_to_all | solution.py:351
  144.9 3.1 %shard_map.43 = bf16[16,128,128]{2,1,0:T(8,128)(2,1)S(1)} custom-call(bf16[16,128,256]{2,1,0:T(8,128)(2,1)S(1)} %all-to-all-done.1.block_ref, bf16[4,16,512]{2,1,0:T(8,128)(2,1)S(1)} %shard_map.42.member_ref), custom_call_target="tpu_custom_call" | custom-call | tf_op jit(solution)/shard_map/pallas_call | solution.py:285
  148.0 26.8 %all_to_all.15.block_ref = bf16[16,128,128]{2,1,0:T(8,128)(2,1)S(1)} all-to-all(bf16[16,128,128]{2,1,0:T(8,128)(2,1)S(1)} %shard_map.43), channel_id=1, replica_groups=mesh['x'=4,'core'=2,'zq'=4,'zr'=4,'tp'=4] {'zq','zr'}, dimensions={0} | all-to-all | bytes 1048576 | tf_op jit(solution)/shard_map/all_to_all | solution.py:360
  174.8 1.2 shard_map.44
  (33 shorter events, 7.7 us)
Async XLA Ops:
  4.0 45.8 %copy-start = (s32[1,256,4]{1,2,0:T(4,128)S(1)}, s32[1,256,4]{1,2,0:T(4,128)}, u32[]{:S(2)}) copy-start(s32[1,256,4]{1,2,0:T(4,128)} %param.5) | copy-start | bytes 12292
  4.0 41.9 %all-to-all-start = ((bf16[4,256,1024]{2,1,0:T(8,128)(2,1)}), bf16[4,256,1024]{2,1,0:T(8,128)(2,1)}, u32[]{:S(2)}, u32[]{:S(2)}) async-start(bf16[4,256,1024]{2,1,0:T(8,128)(2,1)} %shard_map.37), calls=%async_computation | async-start | bytes 4194304 | tf_op jit(solution)/shard_map/all_to_all | solution.py:332
  35.6 17.8 %collective-permute-start.1 = (bf16[4,32,1152]{2,1,0:T(8,128)(2,1)S(1)}, bf16[4,32,1152]{2,1,0:T(8,128)(2,1)S(1)}, u32[]{:S(2)}, u32[]{:S(2)}) collective-permute-start(bf16[4,32,1152]{2,1,0:T(8,128)(2,1)S(1)} %bitcast.38), channel_id=1, source_target_pairs={{0,60},{4,0},{8,4},{12,8},{16,12},{20,16},{24,20},{28,24},{32,28},... | collective-permute-start | bytes 884744 | tf_op jit(solution)/shard_map/ppermute | solution.py:313
  39.8 13.7 %collective-permute-start = (bf16[4,32,1152]{2,1,0:T(8,128)(2,1)S(1)}, bf16[4,32,1152]{2,1,0:T(8,128)(2,1)S(1)}, u32[]{:S(2)}, u32[]{:S(2)}) collective-permute-start(bf16[4,32,1152]{2,1,0:T(8,128)(2,1)S(1)} %bitcast.39), channel_id=1, source_target_pairs={{0,4},{4,8},{8,12},{12,16},{16,20},{20,24},{24,28},{28,32},{32,36}... | collective-permute-start | bytes 884744 | tf_op jit(solution)/shard_map/ppermute | solution.py:313
  41.8 11.5 %collective-permute-start.2 = (bf16[2,32,1152]{2,1,0:T(8,128)(2,1)S(1)}, bf16[2,32,1152]{2,1,0:T(8,128)(2,1)S(1)}, u32[]{:S(2)}, u32[]{:S(2)}) collective-permute-start(bf16[2,32,1152]{2,1,0:T(8,128)(2,1)S(1)} %bitcast.49), channel_id=1, source_target_pairs={{0,8},{4,12},{8,16},{12,20},{16,24},{20,28},{24,32},{28,36},{32,40... | collective-permute-start | bytes 442376 | tf_op jit(solution)/shard_map/ppermute | solution.py:313
  45.9 9.3 %collective-permute-start.3 = (bf16[2,32,1152]{2,1,0:T(8,128)(2,1)S(1)}, bf16[2,32,1152]{2,1,0:T(8,128)(2,1)S(1)}, u32[]{:S(2)}, u32[]{:S(2)}) collective-permute-start(bf16[2,32,1152]{2,1,0:T(8,128)(2,1)S(1)} %bitcast.48), channel_id=1, source_target_pairs={{0,56},{4,60},{8,0},{12,4},{16,8},{20,12},{24,16},{28,20},{32,24},... | collective-permute-start | bytes 442376 | tf_op jit(solution)/shard_map/ppermute | solution.py:313
  55.3 4.6 %collective-permute-start.4 = (bf16[512,1024]{1,0:T(8,128)(2,1)S(1)}, bf16[512,1024]{1,0:T(8,128)(2,1)S(1)}, u32[]{:S(2)}, u32[]{:S(2)}) collective-permute-start(bf16[512,1024]{1,0:T(8,128)(2,1)S(1)} %shard_map.38.ring_ref), channel_id=1, source_target_pairs={{0,64},{64,0},{1,65},{65,1},{2,66},{66,2},{3,67},{67,3},{4,68},{68... | collective-permute-start | bytes 3145736 | tf_op jit(solution)/shard_map/ppermute | solution.py:344
  63.8 2.1 %collective-permute-start.5 = (bf16[256,1024]{1,0:T(8,128)(2,1)S(1)}, bf16[256,1024]{1,0:T(8,128)(2,1)S(1)}, u32[]{:S(2)}, u32[]{:S(2)}) collective-permute-start(bf16[256,1024]{1,0:T(8,128)(2,1)S(1)} %get-tuple-element.32), channel_id=1, source_target_pairs={{64,320},{192,448},{320,64},{448,192},{65,321},{193,449},{321,65},... | collective-permute-start | bytes 1572872 | tf_op jit(solution)/shard_map/ppermute | solution.py:193
  64.5 1.4 collective-permute-start.6
  65.2 0.7 collective-permute-start.7
  66.0 17.3 %collective-permute-start.8 = (bf16[16,128]{1,0:T(8,128)(2,1)S(1)}, bf16[16,128]{1,0:T(8,128)(2,1)S(1)}, u32[]{:S(2)}, u32[]{:S(2)}) collective-permute-start(bf16[16,128]{1,0:T(8,128)(2,1)S(1)} %slice_add_fusion), channel_id=1, source_target_pairs={{64,0},{65,1},{66,2},{67,3},{68,4},{69,5},{70,6},{71,7},{72,8},{73... | collective-permute-start | bytes 12296 | tf_op jit(solution)/shard_map/ppermute | solution.py:196
  83.3 12.7 %collective-permute-start.9 = (bf16[256,1024]{1,0:T(8,128)(2,1)S(1)}, bf16[256,1024]{1,0:T(8,128)(2,1)S(1)}, u32[]{:S(2)}, u32[]{:S(2)}) collective-permute-start(bf16[256,1024]{1,0:T(8,128)(2,1)S(1)} %get-tuple-element.32), channel_id=1, source_target_pairs={{0,256},{128,384},{256,0},{384,128},{1,257},{129,385},{257,1},{385... | collective-permute-start | bytes 1572872 | tf_op jit(solution)/shard_map/ppermute | solution.py:193
  88.0 13.5 %collective-permute-start.10 = (bf16[256,1024]{1,0:T(8,128)(2,1)S(1)}, bf16[256,1024]{1,0:T(8,128)(2,1)S(1)}, u32[]{:S(2)}, u32[]{:S(2)}) collective-permute-start(bf16[256,1024]{1,0:T(8,128)(2,1)S(1)} %get-tuple-element.33), channel_id=1, source_target_pairs={{0,128},{128,256},{256,384},{384,0},{1,129},{129,257},{257,385},{3... | collective-permute-start | bytes 1572872 | tf_op jit(solution)/shard_map/ppermute | solution.py:193
  91.4 11.1 %collective-permute-start.11 = (bf16[256,1024]{1,0:T(8,128)(2,1)S(1)}, bf16[256,1024]{1,0:T(8,128)(2,1)S(1)}, u32[]{:S(2)}, u32[]{:S(2)}) collective-permute-start(bf16[256,1024]{1,0:T(8,128)(2,1)S(1)} %get-tuple-element.34), channel_id=1, source_target_pairs={{0,384},{128,0},{256,128},{384,256},{1,385},{129,1},{257,129},{385... | collective-permute-start | bytes 1572872 | tf_op jit(solution)/shard_map/ppermute | solution.py:193
  104.4 40.5 %all-to-all-start.1 = ((bf16[16,128,256]{2,1,0:T(8,128)(2,1)}), bf16[16,128,256]{2,1,0:T(8,128)(2,1)S(1)}, u32[]{:S(2)}, u32[]{:S(2)}) async-start(bf16[16,128,256]{2,1,0:T(8,128)(2,1)} %shard_map.41), calls=%async_computation.1 | async-start | bytes 2097152 | tf_op jit(solution)/shard_map/all_to_all | solution.py:351

commit v16 on v15

--- a/solution.py
+++ b/solution.py
@@ -184,36 +184,45 @@
     )(scalar(x), pieces, ring, other)
 
 
-def exchange_x(parts, steps):
+def exchange_x(parts, steps, both):
     chips = lax.axis_size("x")
-    received = []
+
+    def send(part, step, cores):
+        pairs = [
+            (2 * x + core, (x + step) % chips * 2 + core) for x in range(chips) for core in cores
+        ]
+        return lax.ppermute(part, ("x", "core"), pairs)
+
+    received = [[], []]
     for core in (1, 0):
         for i, step in enumerate(steps):
-            pairs = [(2 * x + core, (x + step) % chips * 2 + core) for x in range(chips)]
-            received.append(lax.ppermute(parts[i], ("x", "core"), pairs))
+            if step != both:
+                received[core].append(send(parts[i], step, (core,)))
         if core == 1:
-            ready = sum(part[:16, :128] for part in received)
+            common = send(parts[steps.index(both)], both, (0, 1))
+            ready = sum(part[:16, :128] for part in received[1] + [common])
             ready = lax.ppermute(ready, "core", [(1, 0)])
             parts, ready = lax.optimization_barrier((parts, ready))
-    return received, ready
-
-
-def pack(own, received, ready, slot_row, core, owners, capacity, head_dim):
+    return common, received, ready
+
+
+def pack(own, common, received, ready, slot_row, core, owners, capacity, head_dim):
     rows, width = own.shape
     heads = slot_row.shape[0]
     slots = owners * capacity
-    count = len(received) // 2
-
-    def kernel(core_ref, slot_ref, own_ref, *refs):
+    count = len(received[0])
+    total_count = count + 2
+
+    def kernel(core_ref, slot_ref, own_ref, common_ref, *refs):
         out_ref, part_ref, sems = refs[-3:]
 
         def copies(part_refs):
             return [
                 pltpu.make_async_copy(ref, part_ref.at[i], sems.at[i])
-                for i, ref in enumerate((own_ref,) + part_refs)
+                for i, ref in enumerate((own_ref, common_ref) + part_refs)
             ]
 
-        for number, first in ((1, 0), (0, count)):
+        for number, first in ((0, 0), (1, count)):
 
             @pl.when(core_ref[0] == number)
             def _():
@@ -228,7 +237,7 @@
             for m in range(2):
                 cols = slice((m * heads + h) * head_dim, (m * heads + h + 1) * head_dim)
                 total = part_ref[0, :, cols].astype(F32)
-                for i in range(1, count + 1):
+                for i in range(1, total_count):
                     total += part_ref[i, :, cols].astype(F32)
                 packed = jnp.dot(
                     place, total.astype(BF16), preferred_element_type=F32
@@ -242,14 +251,14 @@
     return pl.pallas_call(
         kernel,
         out_shape=jax.ShapeDtypeStruct((owners, heads * capacity, 2 * head_dim), BF16),
-        in_specs=[pl.BlockSpec(memory_space=pltpu.SMEM), vmem] + [whole] * (len(received) + 2),
+        in_specs=[pl.BlockSpec(memory_space=pltpu.SMEM), vmem] + [whole] * (2 * count + 3),
         out_specs=vmem,
         scratch_shapes=[
-            pltpu.VMEM((count + 1, rows, width), BF16),
-            pltpu.SemaphoreType.DMA((count + 1,)),
+            pltpu.VMEM((total_count, rows, width), BF16),
+            pltpu.SemaphoreType.DMA((total_count,)),
         ],
         compiler_params=pltpu.CompilerParams(vmem_limit_bytes=VMEM_LIMIT),
-    )(scalar(core), slot_row, own, *received, ready)
+    )(scalar(core), slot_row, own, common, *received[0], *received[1], ready)
 
 
 def attend(blocks, members, capacity):
@@ -344,9 +353,9 @@
     other = lax.ppermute(ring, "core", [(0, 1), (1, 0)])
     steps = (2, 1, -1, 0)
     *sent, kept = project(pieces, ring, other, lax.axis_index("x"), steps)
-    received, ready = exchange_x(sent, steps[:-1])
+    common, received, ready = exchange_x(sent, steps[:-1], -1)
     outgoing = pack(
-        kept, received, ready, slot_row, lax.axis_index("core"), owners, capacity, head_dim
+        kept, common, received, ready, slot_row, lax.axis_index("core"), owners, capacity, head_dim
     )
     incoming = lax.all_to_all(outgoing, CLU, split_axis=0, concat_axis=0, tiled=True)
 

time: 178 us -> 185 us (1.039)
  the two profiles are of different devices: /device:TPU:24 before, /device:TPU:14 now
where the time goes in v16:
time: 185 us; the launch traced here: 184 us
  waiting for transfers between devices  74.2 us (40%)
  blocking collectives  56.6 us (31%)
  starting transfers between devices  37.1 us (20%)
  Pallas kernels  14.4 us (8%)
    all_to_all x1, waiting for transfers between devices, body(): lax.all_to_all(outgoing, CLU, split_axis=0, concat_axis=0, tiled=True)  35.1 us
    all_to_all x1, blocking collectives, body(): lax.all_to_all(replies, CLU, split_axis=0, concat_axis=0, tiled=True)  30.1 us
    ppermute x5, waiting for transfers between devices, send(): return lax.ppermute(part, ('x', 'core'), pairs)  29.8 us
    all_gather x1, blocking collectives, body(): four = lax.all_gather(own, 'zq', axis=0)  26.5 us
    ppermute x4, starting transfers between devices, shifted(): lax.ppermute(block, axis, [(i, (i + step) % size) for i in range(size)])  14 us
    ppermute x5, starting transfers between devices, send(): return lax.ppermute(part, ('x', 'core'), pairs)  7.98 us
    all_to_all x1, starting transfers between devices, body(): lax.all_to_all(outgoing, CLU, split_axis=0, concat_axis=0, tiled=True)  7.01 us
    ppermute x4, waiting for transfers between devices, shifted(): lax.ppermute(block, axis, [(i, (i + step) % size) for i in range(size)])  4.99 us
  transfers between devices with their start and end apart: 13, of which 9 were waited for; matrix products, arithmetic and copies ran while one was open for 0% of the time, Pallas kernels for 1%

profile of v16, /device:TPU:14, one launch (start us, length us, event | category | flops | bytes accessed | tf_op | source)
XLA Modules:
  0.0 184.4 jit_solution(16169234089005107146)
XLA Ops:
  1.6 2.4 %shard_map.37 = bf16[4,256,1024]{2,1,0:T(8,128)(2,1)} custom-call(s32[1]{0:T(128)} %bitcast.core_ref, bf16[256,4096]{1,0:T(8,128)(2,1)} %bitcast.46), custom_call_target="tpu_custom_call" | custom-call | tf_op jit(solution)/shard_map/pallas_call | solution.py:132
  4.0 4.9 %all-to-all-start = ((bf16[4,256,1024]{2,1,0:T(8,128)(2,1)}), bf16[4,256,1024]{2,1,0:T(8,128)(2,1)}, u32[]{:S(2)}, u32[]{:S(2)}) async-start(bf16[4,256,1024]{2,1,0:T(8,128)(2,1)} %shard_map.37), calls=%async_computation | async-start | bytes 4194304 | tf_op jit(solution)/shard_map/all_to_all | solution.py:341
  8.9 26.5 %all-gather = bf16[128,1152]{1,0:T(8,128)(2,1)S(1)} all-gather(bf16[32,1152]{1,0:T(8,128)(2,1)S(1)} %fusion.1), channel_id=2, replica_groups=mesh['x'=4,'core'=2,'zq'=4,'zr'=4,'tp'=4] {'zq'}, dimensions={0}, use_global_device_ids=true | all-gather | bytes 368640 | tf_op jit(solution)/shard_map/all_gather | solution.py:343
  35.5 4.0 %collective-permute-start.1 = (bf16[4,32,1152]{2,1,0:T(8,128)(2,1)S(1)}, bf16[4,32,1152]{2,1,0:T(8,128)(2,1)S(1)}, u32[]{:S(2)}, u32[]{:S(2)}) collective-permute-start(bf16[4,32,1152]{2,1,0:T(8,128)(2,1)S(1)} %bitcast.38), channel_id=1, source_target_pairs={{0,60},{4,0},{8,4},{12,8},{16,12},{20,16},{24,20},{28,24},{32,28},... | collective-permute-start | bytes 884744 | tf_op jit(solution)/shard_map/ppermute | solution.py:322
  39.5 2.0 %collective-permute-start = (bf16[4,32,1152]{2,1,0:T(8,128)(2,1)S(1)}, bf16[4,32,1152]{2,1,0:T(8,128)(2,1)S(1)}, u32[]{:S(2)}, u32[]{:S(2)}) collective-permute-start(bf16[4,32,1152]{2,1,0:T(8,128)(2,1)S(1)} %bitcast.39), channel_id=1, source_target_pairs={{0,4},{4,8},{8,12},{12,16},{16,20},{20,24},{24,28},{28,32},{32,36}... | collective-permute-start | bytes 884744 | tf_op jit(solution)/shard_map/ppermute | solution.py:322
  41.5 4.3 %collective-permute-start.2 = (bf16[2,32,1152]{2,1,0:T(8,128)(2,1)S(1)}, bf16[2,32,1152]{2,1,0:T(8,128)(2,1)S(1)}, u32[]{:S(2)}, u32[]{:S(2)}) collective-permute-start(bf16[2,32,1152]{2,1,0:T(8,128)(2,1)S(1)} %bitcast.49), channel_id=1, source_target_pairs={{0,8},{4,12},{8,16},{12,20},{16,24},{20,28},{24,32},{28,36},{32,40... | collective-permute-start | bytes 442376 | tf_op jit(solution)/shard_map/ppermute | solution.py:322
  45.9 3.6 %collective-permute-start.3 = (bf16[2,32,1152]{2,1,0:T(8,128)(2,1)S(1)}, bf16[2,32,1152]{2,1,0:T(8,128)(2,1)S(1)}, u32[]{:S(2)}, u32[]{:S(2)}) collective-permute-start(bf16[2,32,1152]{2,1,0:T(8,128)(2,1)S(1)} %bitcast.48), channel_id=1, source_target_pairs={{0,56},{4,60},{8,0},{12,4},{16,8},{20,12},{24,16},{28,20},{32,24},... | collective-permute-start | bytes 442376 | tf_op jit(solution)/shard_map/ppermute | solution.py:322
  50.3 2.8 %collective-permute-done.2.refs_3_ = bf16[2,32,1152]{2,1,0:T(8,128)(2,1)S(1)} collective-permute-done((bf16[2,32,1152]{2,1,0:T(8,128)(2,1)S(1)}, bf16[2,32,1152]{2,1,0:T(8,128)(2,1)S(1)}, u32[]{:S(2)}, u32[]{:S(2)}) %collective-permute-start.2) | collective-permute-done | bytes 147488 | tf_op jit(solution)/shard_map/ppermute | solution.py:322
  53.4 1.9 %collective-permute-done.3.refs_4_ = bf16[2,32,1152]{2,1,0:T(8,128)(2,1)S(1)} collective-permute-done((bf16[2,32,1152]{2,1,0:T(8,128)(2,1)S(1)}, bf16[2,32,1152]{2,1,0:T(8,128)(2,1)S(1)}, u32[]{:S(2)}, u32[]{:S(2)}) %collective-permute-start.3) | collective-permute-done | bytes 147488 | tf_op jit(solution)/shard_map/ppermute | solution.py:322
  55.4 1.9 %collective-permute-start.4 = (bf16[512,1024]{1,0:T(8,128)(2,1)S(1)}, bf16[512,1024]{1,0:T(8,128)(2,1)S(1)}, u32[]{:S(2)}, u32[]{:S(2)}) collective-permute-start(bf16[512,1024]{1,0:T(8,128)(2,1)S(1)} %shard_map.38.ring_ref), channel_id=1, source_target_pairs={{0,64},{64,0},{1,65},{65,1},{2,66},{66,2},{3,67},{67,3},{4,68},{68... | collective-permute-start | bytes 3145736 | tf_op jit(solution)/shard_map/ppermute | solution.py:353
  57.3 2.6 %collective-permute-done.4.other_ref = bf16[512,1024]{1,0:T(8,128)(2,1)S(1)} collective-permute-done((bf16[512,1024]{1,0:T(8,128)(2,1)S(1)}, bf16[512,1024]{1,0:T(8,128)(2,1)S(1)}, u32[]{:S(2)}, u32[]{:S(2)}) %collective-permute-start.4) | collective-permute-done | bytes 1048608 | tf_op jit(solution)/shard_map/ppermute | solution.py:353
  60.0 4.0 %shard_map.40 = (bf16[256,1024]{1,0:T(8,128)(2,1)S(1)}, bf16[256,1024]{1,0:T(8,128)(2,1)S(1)}, bf16[256,1024]{1,0:T(8,128)(2,1)S(1)}, bf16[256,1024]{1,0:T(8,128)(2,1)S(1)}) custom-call(s32[1]{0:T(128)} %bitcast.9.x_ref, bf16[4,256,1024]{2,1,0:T(8,128)(2,1)} %all-to-all-done.pieces_ref, bf16[512,1024]{1,0:T(8,128)(2,1)S(1)} %shard_map.38.ring_ref, ...), custom_call_target="tpu_custom_call" | custom-call | tf_op jit(solution)/shard_map/pallas_call | solution.py:180
  63.9 2.8 %collective-permute-start.5 = (bf16[256,1024]{1,0:T(8,128)(2,1)S(1)}, bf16[256,1024]{1,0:T(8,128)(2,1)S(1)}, u32[]{:S(2)}, u32[]{:S(2)}) collective-permute-start(bf16[256,1024]{1,0:T(8,128)(2,1)S(1)} %get-tuple-element.28), channel_id=1, source_target_pairs={{0,384},{64,448},{128,0},{192,64},{256,128},{320,192},{384,256},{4... | collective-permute-start | bytes 1572872 | tf_op jit(solution)/shard_map/ppermute | solution.py:194
  68.1 18.5 %collective-permute-done.5.common_ref = bf16[256,1024]{1,0:T(8,128)(2,1)S(1)} collective-permute-done((bf16[256,1024]{1,0:T(8,128)(2,1)S(1)}, bf16[256,1024]{1,0:T(8,128)(2,1)S(1)}, u32[]{:S(2)}, u32[]{:S(2)}) %collective-permute-start.5) | collective-permute-done | bytes 524320 | tf_op jit(solution)/shard_map/ppermute | solution.py:194
  87.9 1.8 collective-permute-done.8.refs_4_
  89.7 1.9 %collective-permute-start.9 = (bf16[256,1024]{1,0:T(8,128)(2,1)S(1)}, bf16[256,1024]{1,0:T(8,128)(2,1)S(1)}, u32[]{:S(2)}, u32[]{:S(2)}) collective-permute-start(bf16[256,1024]{1,0:T(8,128)(2,1)S(1)} %get-tuple-element.31), channel_id=1, source_target_pairs={{0,256},{128,384},{256,0},{384,128},{1,257},{129,385},{257,1},{385... | collective-permute-start | bytes 1572872 | tf_op jit(solution)/shard_map/ppermute | solution.py:194
  91.6 1.9 %collective-permute-start.10 = (bf16[256,1024]{1,0:T(8,128)(2,1)S(1)}, bf16[256,1024]{1,0:T(8,128)(2,1)S(1)}, u32[]{:S(2)}, u32[]{:S(2)}) collective-permute-start(bf16[256,1024]{1,0:T(8,128)(2,1)S(1)} %get-tuple-element.32), channel_id=1, source_target_pairs={{0,128},{128,256},{256,384},{384,0},{1,129},{129,257},{257,385},{3... | collective-permute-start | bytes 1572872 | tf_op jit(solution)/shard_map/ppermute | solution.py:194
  93.5 8.7 %collective-permute-done.9.refs_0_ = bf16[256,1024]{1,0:T(8,128)(2,1)S(1)} collective-permute-done((bf16[256,1024]{1,0:T(8,128)(2,1)S(1)}, bf16[256,1024]{1,0:T(8,128)(2,1)S(1)}, u32[]{:S(2)}, u32[]{:S(2)}) %collective-permute-start.9) | collective-permute-done | bytes 524320 | tf_op jit(solution)/shard_map/ppermute | solution.py:194
  102.3 2.5 %collective-permute-done.10.refs_1_ = bf16[256,1024]{1,0:T(8,128)(2,1)S(1)} collective-permute-done((bf16[256,1024]{1,0:T(8,128)(2,1)S(1)}, bf16[256,1024]{1,0:T(8,128)(2,1)S(1)}, u32[]{:S(2)}, u32[]{:S(2)}) %collective-permute-start.10) | collective-permute-done | bytes 524320 | tf_op jit(solution)/shard_map/ppermute | solution.py:194
  104.8 1.9 %shard_map.41 = bf16[16,128,256]{2,1,0:T(8,128)(2,1)} custom-call(s32[1]{0:T(128)} %bitcast.core_ref, s32[4,256]{1,0:T(4,128)S(1)} %get-tuple-element.24.slot_ref, bf16[256,1024]{1,0:T(8,128)(2,1)S(1)} %get-tuple-element.27.own_ref, bf16[256,1024]{1,0:T(8,128)(2,1)S(1)} %collective-permute-done.5.common_ref, ...), custom_call_target="tpu_custom_call" | custom-call | tf_op jit(solution)/shard_map/pallas_call | solution.py:251
  106.7 7.0 %all-to-all-start.1 = ((bf16[16,128,256]{2,1,0:T(8,128)(2,1)}), bf16[16,128,256]{2,1,0:T(8,128)(2,1)S(1)}, u32[]{:S(2)}, u32[]{:S(2)}) async-start(bf16[16,128,256]{2,1,0:T(8,128)(2,1)} %shard_map.41), calls=%async_computation.1 | async-start | bytes 2097152 | tf_op jit(solution)/shard_map/all_to_all | solution.py:360
  115.0 35.1 %all-to-all-done.1.block_ref = bf16[16,128,256]{2,1,0:T(8,128)(2,1)S(1)} async-done(((bf16[16,128,256]{2,1,0:T(8,128)(2,1)}), bf16[16,128,256]{2,1,0:T(8,128)(2,1)S(1)}, u32[]{:S(2)}, u32[]{:S(2)}) %all-to-all-start.1) | async-done | bytes 1048608 | tf_op jit(solution)/shard_map/all_to_all | solution.py:360
  150.1 3.1 %shard_map.43 = bf16[16,128,128]{2,1,0:T(8,128)(2,1)S(1)} custom-call(bf16[16,128,256]{2,1,0:T(8,128)(2,1)S(1)} %all-to-all-done.1.block_ref, bf16[4,16,512]{2,1,0:T(8,128)(2,1)S(1)} %shard_map.42.member_ref), custom_call_target="tpu_custom_call" | custom-call | tf_op jit(solution)/shard_map/pallas_call | solution.py:294
  153.2 30.1 %all_to_all.15.block_ref = bf16[16,128,128]{2,1,0:T(8,128)(2,1)S(1)} all-to-all(bf16[16,128,128]{2,1,0:T(8,128)(2,1)S(1)} %shard_map.43), channel_id=1, replica_groups=mesh['x'=4,'core'=2,'zq'=4,'zr'=4,'tp'=4] {'zq','zr'}, dimensions={0} | all-to-all | bytes 1048576 | tf_op jit(solution)/shard_map/all_to_all | solution.py:369
  (31 shorter events, 7.8 us)
Async XLA Ops:
  4.0 45.5 %copy-start = (s32[1,256,4]{1,2,0:T(4,128)S(1)}, s32[1,256,4]{1,2,0:T(4,128)}, u32[]{:S(2)}) copy-start(s32[1,256,4]{1,2,0:T(4,128)} %param.5) | copy-start | bytes 12292
  4.0 41.9 %all-to-all-start = ((bf16[4,256,1024]{2,1,0:T(8,128)(2,1)}), bf16[4,256,1024]{2,1,0:T(8,128)(2,1)}, u32[]{:S(2)}, u32[]{:S(2)}) async-start(bf16[4,256,1024]{2,1,0:T(8,128)(2,1)} %shard_map.37), calls=%async_computation | async-start | bytes 4194304 | tf_op jit(solution)/shard_map/all_to_all | solution.py:341
  35.5 17.7 %collective-permute-start.1 = (bf16[4,32,1152]{2,1,0:T(8,128)(2,1)S(1)}, bf16[4,32,1152]{2,1,0:T(8,128)(2,1)S(1)}, u32[]{:S(2)}, u32[]{:S(2)}) collective-permute-start(bf16[4,32,1152]{2,1,0:T(8,128)(2,1)S(1)} %bitcast.38), channel_id=1, source_target_pairs={{0,60},{4,0},{8,4},{12,8},{16,12},{20,16},{24,20},{28,24},{32,28},... | collective-permute-start | bytes 884744 | tf_op jit(solution)/shard_map/ppermute | solution.py:322
  39.5 13.9 %collective-permute-start = (bf16[4,32,1152]{2,1,0:T(8,128)(2,1)S(1)}, bf16[4,32,1152]{2,1,0:T(8,128)(2,1)S(1)}, u32[]{:S(2)}, u32[]{:S(2)}) collective-permute-start(bf16[4,32,1152]{2,1,0:T(8,128)(2,1)S(1)} %bitcast.39), channel_id=1, source_target_pairs={{0,4},{4,8},{8,12},{12,16},{16,20},{20,24},{24,28},{28,32},{32,36}... | collective-permute-start | bytes 884744 | tf_op jit(solution)/shard_map/ppermute | solution.py:322
  41.5 11.6 %collective-permute-start.2 = (bf16[2,32,1152]{2,1,0:T(8,128)(2,1)S(1)}, bf16[2,32,1152]{2,1,0:T(8,128)(2,1)S(1)}, u32[]{:S(2)}, u32[]{:S(2)}) collective-permute-start(bf16[2,32,1152]{2,1,0:T(8,128)(2,1)S(1)} %bitcast.49), channel_id=1, source_target_pairs={{0,8},{4,12},{8,16},{12,20},{16,24},{20,28},{24,32},{28,36},{32,40... | collective-permute-start | bytes 442376 | tf_op jit(solution)/shard_map/ppermute | solution.py:322
  45.9 9.5 %collective-permute-start.3 = (bf16[2,32,1152]{2,1,0:T(8,128)(2,1)S(1)}, bf16[2,32,1152]{2,1,0:T(8,128)(2,1)S(1)}, u32[]{:S(2)}, u32[]{:S(2)}) collective-permute-start(bf16[2,32,1152]{2,1,0:T(8,128)(2,1)S(1)} %bitcast.48), channel_id=1, source_target_pairs={{0,56},{4,60},{8,0},{12,4},{16,8},{20,12},{24,16},{28,20},{32,24},... | collective-permute-start | bytes 442376 | tf_op jit(solution)/shard_map/ppermute | solution.py:322
  55.4 4.6 %collective-permute-start.4 = (bf16[512,1024]{1,0:T(8,128)(2,1)S(1)}, bf16[512,1024]{1,0:T(8,128)(2,1)S(1)}, u32[]{:S(2)}, u32[]{:S(2)}) collective-permute-start(bf16[512,1024]{1,0:T(8,128)(2,1)S(1)} %shard_map.38.ring_ref), channel_id=1, source_target_pairs={{0,64},{64,0},{1,65},{65,1},{2,66},{66,2},{3,67},{67,3},{4,68},{68... | collective-permute-start | bytes 3145736 | tf_op jit(solution)/shard_map/ppermute | solution.py:353
  63.9 22.7 %collective-permute-start.5 = (bf16[256,1024]{1,0:T(8,128)(2,1)S(1)}, bf16[256,1024]{1,0:T(8,128)(2,1)S(1)}, u32[]{:S(2)}, u32[]{:S(2)}) collective-permute-start(bf16[256,1024]{1,0:T(8,128)(2,1)S(1)} %get-tuple-element.28), channel_id=1, source_target_pairs={{0,384},{64,448},{128,0},{192,64},{256,128},{320,192},{384,256},{4... | collective-permute-start | bytes 1572872 | tf_op jit(solution)/shard_map/ppermute | solution.py:194
  66.7 19.9 %collective-permute-start.6 = (bf16[256,1024]{1,0:T(8,128)(2,1)S(1)}, bf16[256,1024]{1,0:T(8,128)(2,1)S(1)}, u32[]{:S(2)}, u32[]{:S(2)}) collective-permute-start(bf16[256,1024]{1,0:T(8,128)(2,1)S(1)} %get-tuple-element.31), channel_id=1, source_target_pairs={{64,320},{192,448},{320,64},{448,192},{65,321},{193,449},{321,65},... | collective-permute-start | bytes 1572872 | tf_op jit(solution)/shard_map/ppermute | solution.py:194
  67.4 19.2 %collective-permute-start.7 = (bf16[256,1024]{1,0:T(8,128)(2,1)S(1)}, bf16[256,1024]{1,0:T(8,128)(2,1)S(1)}, u32[]{:S(2)}, u32[]{:S(2)}) collective-permute-start(bf16[256,1024]{1,0:T(8,128)(2,1)S(1)} %get-tuple-element.32), channel_id=1, source_target_pairs={{64,192},{192,320},{320,448},{448,64},{65,193},{193,321},{321,449}... | collective-permute-start | bytes 1572872 | tf_op jit(solution)/shard_map/ppermute | solution.py:194
  86.6 3.1 %collective-permute-start.8 = (bf16[16,128]{1,0:T(8,128)(2,1)S(1)}, bf16[16,128]{1,0:T(8,128)(2,1)S(1)}, u32[]{:S(2)}, u32[]{:S(2)}) collective-permute-start(bf16[16,128]{1,0:T(8,128)(2,1)S(1)} %slice_add_fusion), channel_id=1, source_target_pairs={{64,0},{65,1},{66,2},{67,3},{68,4},{69,5},{70,6},{71,7},{72,8},{73... | collective-permute-start | bytes 12296 | tf_op jit(solution)/shard_map/ppermute | solution.py:204
  89.7 12.6 %collective-permute-start.9 = (bf16[256,1024]{1,0:T(8,128)(2,1)S(1)}, bf16[256,1024]{1,0:T(8,128)(2,1)S(1)}, u32[]{:S(2)}, u32[]{:S(2)}) collective-permute-start(bf16[256,1024]{1,0:T(8,128)(2,1)S(1)} %get-tuple-element.31), channel_id=1, source_target_pairs={{0,256},{128,384},{256,0},{384,128},{1,257},{129,385},{257,1},{385... | collective-permute-start | bytes 1572872 | tf_op jit(solution)/shard_map/ppermute | solution.py:194
  91.6 13.2 %collective-permute-start.10 = (bf16[256,1024]{1,0:T(8,128)(2,1)S(1)}, bf16[256,1024]{1,0:T(8,128)(2,1)S(1)}, u32[]{:S(2)}, u32[]{:S(2)}) collective-permute-start(bf16[256,1024]{1,0:T(8,128)(2,1)S(1)} %get-tuple-element.32), channel_id=1, source_target_pairs={{0,128},{128,256},{256,384},{384,0},{1,129},{129,257},{257,385},{3... | collective-permute-start | bytes 1572872 | tf_op jit(solution)/shard_map/ppermute | solution.py:194
  106.7 43.4 %all-to-all-start.1 = ((bf16[16,128,256]{2,1,0:T(8,128)(2,1)}), bf16[16,128,256]{2,1,0:T(8,128)(2,1)S(1)}, u32[]{:S(2)}, u32[]{:S(2)}) async-start(bf16[16,128,256]{2,1,0:T(8,128)(2,1)} %shard_map.41), calls=%async_computation.1 | async-start | bytes 2097152 | tf_op jit(solution)/shard_map/all_to_all | solution.py:360

commit v17 on v15

--- a/solution.py
+++ b/solution.py
@@ -170,17 +170,34 @@
     chips, rows, depth = pieces.shape
     half, width = ring.shape
 
-    def kernel(x_ref, pieces_ref, ring_ref, other_ref, *out_refs):
-        for step, out_ref in zip(steps, out_refs):
-            p = lax.rem(x_ref[0] + step + chips, chips)
-            total = jnp.dot(pieces_ref[p, :, :half], ring_ref[...], preferred_element_type=F32)
-            total += jnp.dot(pieces_ref[p, :, half:], other_ref[...], preferred_element_type=F32)
+    def kernel(x_ref, pieces_ref, ring_ref, other_ref, *refs):
+        out_refs, (piece_ref, sems) = refs[:-2], refs[-2:]
+        copies = [
+            pltpu.make_async_copy(
+                pieces_ref.at[lax.rem(x_ref[0] + step + chips, chips)], piece_ref.at[i], sems.at[i]
+            )
+            for i, step in enumerate(steps)
+        ]
+        for copy in copies:
+            copy.start()
+        for i, out_ref in enumerate(out_refs):
+            copies[i].wait()
+            total = jnp.dot(piece_ref[i, :, :half], ring_ref[...], preferred_element_type=F32)
+            total += jnp.dot(piece_ref[i, :, half:], other_ref[...], preferred_element_type=F32)
             out_ref[...] = total.astype(BF16)
 
-    return vmem_call(
-        kernel,
-        (jax.ShapeDtypeStruct((rows, width), BF16),) * len(steps),
-        (True, False, False, False),
+    smem = pl.BlockSpec(memory_space=pltpu.SMEM)
+    vmem = pl.BlockSpec(memory_space=pltpu.VMEM)
+    return pl.pallas_call(
+        kernel,
+        out_shape=(jax.ShapeDtypeStruct((rows, width), BF16),) * len(steps),
+        in_specs=[smem, pl.BlockSpec(memory_space=pl.ANY), vmem, vmem],
+        out_specs=(vmem,) * len(steps),
+        scratch_shapes=[
+            pltpu.VMEM((len(steps), rows, depth), BF16),
+            pltpu.SemaphoreType.DMA((len(steps),)),
+        ],
+        compiler_params=pltpu.CompilerParams(vmem_limit_bytes=VMEM_LIMIT),
     )(scalar(x), pieces, ring, other)
 
 
@@ -207,29 +224,41 @@
     def kernel(core_ref, slot_ref, own_ref, *refs):
         out_ref, part_ref, sems = refs[-3:]
 
-        def copies(part_refs):
+        def columns(h, m):
+            return slice((m * heads + h) * head_dim, (m * heads + h + 1) * head_dim)
+
+        def copies(part_refs, h):
             return [
-                pltpu.make_async_copy(ref, part_ref.at[i], sems.at[i])
+                pltpu.make_async_copy(
+                    ref.at[:, columns(h, m)], part_ref.at[i, :, columns(h, m)], sems.at[h, m, i]
+                )
+                for m in range(2)
                 for i, ref in enumerate((own_ref,) + part_refs)
             ]
 
-        for number, first in ((1, 0), (0, count)):
+        chosen = [(1, refs[:count]), (0, refs[count : 2 * count])]
+        for number, part_refs in chosen:
 
             @pl.when(core_ref[0] == number)
             def _():
-                for copy in copies(refs[first : first + count]):
-                    copy.start()
-                for copy in copies(refs[first : first + count]):
-                    copy.wait()
-
-        for h in range(heads):
+                for h in range(heads):
+                    for copy in copies(part_refs, h):
+                        copy.start()
+
+        for h in range(heads):
+            for number, part_refs in chosen:
+
+                @pl.when(core_ref[0] == number)
+                def _():
+                    for copy in copies(part_refs, h):
+                        copy.wait()
+
             place = iota((slots, rows), 0) == slot_ref[h : h + 1, :]
             place = place.astype(BF16)
             for m in range(2):
-                cols = slice((m * heads + h) * head_dim, (m * heads + h + 1) * head_dim)
-                total = part_ref[0, :, cols].astype(F32)
+                total = part_ref[0, :, columns(h, m)].astype(F32)
                 for i in range(1, count + 1):
-                    total += part_ref[i, :, cols].astype(F32)
+                    total += part_ref[i, :, columns(h, m)].astype(F32)
                 packed = jnp.dot(
                     place, total.astype(BF16), preferred_element_type=F32
                 ).astype(BF16)
@@ -246,7 +275,7 @@
         out_specs=vmem,
         scratch_shapes=[
             pltpu.VMEM((count + 1, rows, width), BF16),
-            pltpu.SemaphoreType.DMA((count + 1,)),
+            pltpu.SemaphoreType.DMA((heads, 2, count + 1)),
         ],
         compiler_params=pltpu.CompilerParams(vmem_limit_bytes=VMEM_LIMIT),
     )(scalar(core), slot_row, own, *received, ready)

time: 178 us -> 179 us (level)
  no operation moved by 1% of the time
where the time goes in v17:
time: 179 us; the launch traced here: 176 us
  waiting for transfers between devices  62.8 us (35%)
  blocking collectives  52.9 us (30%)
  starting transfers between devices  42.7 us (24%)
  Pallas kernels  15.7 us (9%)
    all_to_all x1, waiting for transfers between devices, body(): lax.all_to_all(outgoing, CLU, split_axis=0, concat_axis=0, tiled=True)  32.2 us
    all_gather x1, blocking collectives, body(): four = lax.all_gather(own, 'zq', axis=0)  27.1 us
    all_to_all x1, blocking collectives, body(): lax.all_to_all(replies, CLU, split_axis=0, concat_axis=0, tiled=True)  25.8 us
    ppermute x1, waiting for transfers between devices, exchange_x(): ready = lax.ppermute(ready, 'core', [(1, 0)])  16 us
    ppermute x4, starting transfers between devices, shifted(): lax.ppermute(block, axis, [(i, (i + step) % size) for i in range(size)])  14.2 us
    ppermute x6, starting transfers between devices, exchange_x(): received.append(lax.ppermute(parts[i], ('x', 'core'), pairs))  13.8 us
    ppermute x6, waiting for transfers between devices, exchange_x(): received.append(lax.ppermute(parts[i], ('x', 'core'), pairs))  7.37 us
    all_to_all x1, starting transfers between devices, body(): lax.all_to_all(outgoing, CLU, split_axis=0, concat_axis=0, tiled=True)  7.03 us
  transfers between devices with their start and end apart: 14, of which 9 were waited for; matrix products, arithmetic and copies ran while one was open for 0% of the time, Pallas kernels for 1%

profile of v17, /device:TPU:24, one launch (start us, length us, event | category | flops | bytes accessed | tf_op | source)
XLA Modules:
  0.0 176.3 jit_solution(6466248486072623818)
XLA Ops:
  1.6 2.4 %shard_map.37 = bf16[4,256,1024]{2,1,0:T(8,128)(2,1)} custom-call(s32[1]{0:T(128)} %bitcast.core_ref, bf16[256,4096]{1,0:T(8,128)(2,1)} %bitcast.46), custom_call_target="tpu_custom_call" | custom-call | tf_op jit(solution)/shard_map/pallas_call | solution.py:132
  4.0 4.5 %all-to-all-start = ((bf16[4,256,1024]{2,1,0:T(8,128)(2,1)}), bf16[4,256,1024]{2,1,0:T(8,128)(2,1)}, u32[]{:S(2)}, u32[]{:S(2)}) async-start(bf16[4,256,1024]{2,1,0:T(8,128)(2,1)} %shard_map.37), calls=%async_computation | async-start | bytes 4194304 | tf_op jit(solution)/shard_map/all_to_all | solution.py:361
  8.5 27.1 %all-gather = bf16[128,1152]{1,0:T(8,128)(2,1)S(1)} all-gather(bf16[32,1152]{1,0:T(8,128)(2,1)S(1)} %fusion.1), channel_id=2, replica_groups=mesh['x'=4,'core'=2,'zq'=4,'zr'=4,'tp'=4] {'zq'}, dimensions={0}, use_global_device_ids=true | all-gather | bytes 368640 | tf_op jit(solution)/shard_map/all_gather | solution.py:363
  35.6 4.2 %collective-permute-start.1 = (bf16[4,32,1152]{2,1,0:T(8,128)(2,1)S(1)}, bf16[4,32,1152]{2,1,0:T(8,128)(2,1)S(1)}, u32[]{:S(2)}, u32[]{:S(2)}) collective-permute-start(bf16[4,32,1152]{2,1,0:T(8,128)(2,1)S(1)} %bitcast.38), channel_id=1, source_target_pairs={{0,60},{4,0},{8,4},{12,8},{16,12},{20,16},{24,20},{28,24},{32,28},... | collective-permute-start | bytes 884744 | tf_op jit(solution)/shard_map/ppermute | solution.py:342
  39.8 2.0 %collective-permute-start = (bf16[4,32,1152]{2,1,0:T(8,128)(2,1)S(1)}, bf16[4,32,1152]{2,1,0:T(8,128)(2,1)S(1)}, u32[]{:S(2)}, u32[]{:S(2)}) collective-permute-start(bf16[4,32,1152]{2,1,0:T(8,128)(2,1)S(1)} %bitcast.39), channel_id=1, source_target_pairs={{0,4},{4,8},{8,12},{12,16},{16,20},{20,24},{24,28},{28,32},{32,36}... | collective-permute-start | bytes 884744 | tf_op jit(solution)/shard_map/ppermute | solution.py:342
  41.8 4.0 %collective-permute-start.2 = (bf16[2,32,1152]{2,1,0:T(8,128)(2,1)S(1)}, bf16[2,32,1152]{2,1,0:T(8,128)(2,1)S(1)}, u32[]{:S(2)}, u32[]{:S(2)}) collective-permute-start(bf16[2,32,1152]{2,1,0:T(8,128)(2,1)S(1)} %bitcast.49), channel_id=1, source_target_pairs={{0,8},{4,12},{8,16},{12,20},{16,24},{20,28},{24,32},{28,36},{32,40... | collective-permute-start | bytes 442376 | tf_op jit(solution)/shard_map/ppermute | solution.py:342
  45.9 3.9 %collective-permute-start.3 = (bf16[2,32,1152]{2,1,0:T(8,128)(2,1)S(1)}, bf16[2,32,1152]{2,1,0:T(8,128)(2,1)S(1)}, u32[]{:S(2)}, u32[]{:S(2)}) collective-permute-start(bf16[2,32,1152]{2,1,0:T(8,128)(2,1)S(1)} %bitcast.48), channel_id=1, source_target_pairs={{0,56},{4,60},{8,0},{12,4},{16,8},{20,12},{24,16},{28,20},{32,24},... | collective-permute-start | bytes 442376 | tf_op jit(solution)/shard_map/ppermute | solution.py:342
  50.6 2.7 %collective-permute-done.2.refs_3_ = bf16[2,32,1152]{2,1,0:T(8,128)(2,1)S(1)} collective-permute-done((bf16[2,32,1152]{2,1,0:T(8,128)(2,1)S(1)}, bf16[2,32,1152]{2,1,0:T(8,128)(2,1)S(1)}, u32[]{:S(2)}, u32[]{:S(2)}) %collective-permute-start.2) | collective-permute-done | bytes 147488 | tf_op jit(solution)/shard_map/ppermute | solution.py:342
  53.4 1.8 %collective-permute-done.3.refs_4_ = bf16[2,32,1152]{2,1,0:T(8,128)(2,1)S(1)} collective-permute-done((bf16[2,32,1152]{2,1,0:T(8,128)(2,1)S(1)}, bf16[2,32,1152]{2,1,0:T(8,128)(2,1)S(1)}, u32[]{:S(2)}, u32[]{:S(2)}) %collective-permute-start.3) | collective-permute-done | bytes 147488 | tf_op jit(solution)/shard_map/ppermute | solution.py:342
  55.3 1.9 %collective-permute-start.4 = (bf16[512,1024]{1,0:T(8,128)(2,1)S(1)}, bf16[512,1024]{1,0:T(8,128)(2,1)S(1)}, u32[]{:S(2)}, u32[]{:S(2)}) collective-permute-start(bf16[512,1024]{1,0:T(8,128)(2,1)S(1)} %shard_map.38.ring_ref), channel_id=1, source_target_pairs={{0,64},{64,0},{1,65},{65,1},{2,66},{66,2},{3,67},{67,3},{4,68},{68... | collective-permute-start | bytes 3145736 | tf_op jit(solution)/shard_map/ppermute | solution.py:373
  57.2 2.6 %collective-permute-done.4.other_ref = bf16[512,1024]{1,0:T(8,128)(2,1)S(1)} collective-permute-done((bf16[512,1024]{1,0:T(8,128)(2,1)S(1)}, bf16[512,1024]{1,0:T(8,128)(2,1)S(1)}, u32[]{:S(2)}, u32[]{:S(2)}) %collective-permute-start.4) | collective-permute-done | bytes 1048608 | tf_op jit(solution)/shard_map/ppermute | solution.py:373
  59.8 3.9 %shard_map.40 = (bf16[256,1024]{1,0:T(8,128)(2,1)S(1)}, bf16[256,1024]{1,0:T(8,128)(2,1)S(1)}, bf16[256,1024]{1,0:T(8,128)(2,1)S(1)}, bf16[256,1024]{1,0:T(8,128)(2,1)S(1)}) custom-call(s32[1]{0:T(128)} %bitcast.9.x_ref, bf16[4,256,1024]{2,1,0:T(8,128)(2,1)} %all-to-all-done.pieces_ref, bf16[512,1024]{1,0:T(8,128)(2,1)S(1)} %shard_map.38.ring_ref, ...), custom_call_target="tpu_custom_call" | custom-call | tf_op jit(solution)/shard_map/pallas_call | solution.py:191
  65.9 1.3 collective-permute-start.8
  67.2 16.0 %collective-permute-done.8.refs_6_ = bf16[16,128]{1,0:T(8,128)(2,1)S(1)} collective-permute-done((bf16[16,128]{1,0:T(8,128)(2,1)S(1)}, bf16[16,128]{1,0:T(8,128)(2,1)S(1)}, u32[]{:S(2)}, u32[]{:S(2)}) %collective-permute-start.8) | collective-permute-done | bytes 4128 | tf_op jit(solution)/shard_map/ppermute | solution.py:213
  83.3 4.7 %collective-permute-start.9 = (bf16[256,1024]{1,0:T(8,128)(2,1)S(1)}, bf16[256,1024]{1,0:T(8,128)(2,1)S(1)}, u32[]{:S(2)}, u32[]{:S(2)}) collective-permute-start(bf16[256,1024]{1,0:T(8,128)(2,1)S(1)} %get-tuple-element.32), channel_id=1, source_target_pairs={{0,256},{128,384},{256,0},{384,128},{1,257},{129,385},{257,1},{385... | collective-permute-start | bytes 1572872 | tf_op jit(solution)/shard_map/ppermute | solution.py:210
  88.0 3.3 %collective-permute-start.10 = (bf16[256,1024]{1,0:T(8,128)(2,1)S(1)}, bf16[256,1024]{1,0:T(8,128)(2,1)S(1)}, u32[]{:S(2)}, u32[]{:S(2)}) collective-permute-start(bf16[256,1024]{1,0:T(8,128)(2,1)S(1)} %get-tuple-element.33), channel_id=1, source_target_pairs={{0,128},{128,256},{256,384},{384,0},{1,129},{129,257},{257,385},{3... | collective-permute-start | bytes 1572872 | tf_op jit(solution)/shard_map/ppermute | solution.py:210
  91.3 3.7 %collective-permute-start.11 = (bf16[256,1024]{1,0:T(8,128)(2,1)S(1)}, bf16[256,1024]{1,0:T(8,128)(2,1)S(1)}, u32[]{:S(2)}, u32[]{:S(2)}) collective-permute-start(bf16[256,1024]{1,0:T(8,128)(2,1)S(1)} %get-tuple-element.34), channel_id=1, source_target_pairs={{0,384},{128,0},{256,128},{384,256},{1,385},{129,1},{257,129},{385... | collective-permute-start | bytes 1572872 | tf_op jit(solution)/shard_map/ppermute | solution.py:210
  95.9 5.5 %collective-permute-done.10.refs_4_ = bf16[256,1024]{1,0:T(8,128)(2,1)S(1)} collective-permute-done((bf16[256,1024]{1,0:T(8,128)(2,1)S(1)}, bf16[256,1024]{1,0:T(8,128)(2,1)S(1)}, u32[]{:S(2)}, u32[]{:S(2)}) %collective-permute-start.10) | collective-permute-done | bytes 524320 | tf_op jit(solution)/shard_map/ppermute | solution.py:210
  102.4 3.3 %shard_map.41 = bf16[16,128,256]{2,1,0:T(8,128)(2,1)} custom-call(s32[1]{0:T(128)} %bitcast.core_ref, s32[4,256]{1,0:T(4,128)S(1)} %get-tuple-element.25.slot_ref, bf16[256,1024]{1,0:T(8,128)(2,1)S(1)} %get-tuple-element.28.own_ref, bf16[256,1024]{1,0:T(8,128)(2,1)S(1)} %collective-permute-done.5.refs_0_, ...), custom_call_target="tpu_custom_call" | custom-call | tf_op jit(solution)/shard_map/pallas_call | solution.py:271
  105.7 7.0 %all-to-all-start.1 = ((bf16[16,128,256]{2,1,0:T(8,128)(2,1)}), bf16[16,128,256]{2,1,0:T(8,128)(2,1)S(1)}, u32[]{:S(2)}, u32[]{:S(2)}) async-start(bf16[16,128,256]{2,1,0:T(8,128)(2,1)} %shard_map.41), calls=%async_computation.1 | async-start | bytes 2097152 | tf_op jit(solution)/shard_map/all_to_all | solution.py:380
  114.0 32.2 %all-to-all-done.1.block_ref = bf16[16,128,256]{2,1,0:T(8,128)(2,1)S(1)} async-done(((bf16[16,128,256]{2,1,0:T(8,128)(2,1)}), bf16[16,128,256]{2,1,0:T(8,128)(2,1)S(1)}, u32[]{:S(2)}, u32[]{:S(2)}) %all-to-all-start.1) | async-done | bytes 1048608 | tf_op jit(solution)/shard_map/all_to_all | solution.py:380
  146.2 3.1 %shard_map.43 = bf16[16,128,128]{2,1,0:T(8,128)(2,1)S(1)} custom-call(bf16[16,128,256]{2,1,0:T(8,128)(2,1)S(1)} %all-to-all-done.1.block_ref, bf16[4,16,512]{2,1,0:T(8,128)(2,1)S(1)} %shard_map.42.member_ref), custom_call_target="tpu_custom_call" | custom-call | tf_op jit(solution)/shard_map/pallas_call | solution.py:314
  149.3 25.8 %all_to_all.15.block_ref = bf16[16,128,128]{2,1,0:T(8,128)(2,1)S(1)} all-to-all(bf16[16,128,128]{2,1,0:T(8,128)(2,1)S(1)} %shard_map.43), channel_id=1, replica_groups=mesh['x'=4,'core'=2,'zq'=4,'zr'=4,'tp'=4] {'zq','zr'}, dimensions={0} | all-to-all | bytes 1048576 | tf_op jit(solution)/shard_map/all_to_all | solution.py:389
  175.1 1.2 shard_map.44
  (33 shorter events, 7.7 us)
Async XLA Ops:
  4.0 45.8 %copy-start = (s32[1,256,4]{1,2,0:T(4,128)S(1)}, s32[1,256,4]{1,2,0:T(4,128)}, u32[]{:S(2)}) copy-start(s32[1,256,4]{1,2,0:T(4,128)} %param.5) | copy-start | bytes 12292
  4.0 41.9 %all-to-all-start = ((bf16[4,256,1024]{2,1,0:T(8,128)(2,1)}), bf16[4,256,1024]{2,1,0:T(8,128)(2,1)}, u32[]{:S(2)}, u32[]{:S(2)}) async-start(bf16[4,256,1024]{2,1,0:T(8,128)(2,1)} %shard_map.37), calls=%async_computation | async-start | bytes 4194304 | tf_op jit(solution)/shard_map/all_to_all | solution.py:361
  35.6 17.8 %collective-permute-start.1 = (bf16[4,32,1152]{2,1,0:T(8,128)(2,1)S(1)}, bf16[4,32,1152]{2,1,0:T(8,128)(2,1)S(1)}, u32[]{:S(2)}, u32[]{:S(2)}) collective-permute-start(bf16[4,32,1152]{2,1,0:T(8,128)(2,1)S(1)} %bitcast.38), channel_id=1, source_target_pairs={{0,60},{4,0},{8,4},{12,8},{16,12},{20,16},{24,20},{28,24},{32,28},... | collective-permute-start | bytes 884744 | tf_op jit(solution)/shard_map/ppermute | solution.py:342
  39.8 13.7 %collective-permute-start = (bf16[4,32,1152]{2,1,0:T(8,128)(2,1)S(1)}, bf16[4,32,1152]{2,1,0:T(8,128)(2,1)S(1)}, u32[]{:S(2)}, u32[]{:S(2)}) collective-permute-start(bf16[4,32,1152]{2,1,0:T(8,128)(2,1)S(1)} %bitcast.39), channel_id=1, source_target_pairs={{0,4},{4,8},{8,12},{12,16},{16,20},{20,24},{24,28},{28,32},{32,36}... | collective-permute-start | bytes 884744 | tf_op jit(solution)/shard_map/ppermute | solution.py:342
  41.8 11.5 %collective-permute-start.2 = (bf16[2,32,1152]{2,1,0:T(8,128)(2,1)S(1)}, bf16[2,32,1152]{2,1,0:T(8,128)(2,1)S(1)}, u32[]{:S(2)}, u32[]{:S(2)}) collective-permute-start(bf16[2,32,1152]{2,1,0:T(8,128)(2,1)S(1)} %bitcast.49), channel_id=1, source_target_pairs={{0,8},{4,12},{8,16},{12,20},{16,24},{20,28},{24,32},{28,36},{32,40... | collective-permute-start | bytes 442376 | tf_op jit(solution)/shard_map/ppermute | solution.py:342
  45.9 9.3 %collective-permute-start.3 = (bf16[2,32,1152]{2,1,0:T(8,128)(2,1)S(1)}, bf16[2,32,1152]{2,1,0:T(8,128)(2,1)S(1)}, u32[]{:S(2)}, u32[]{:S(2)}) collective-permute-start(bf16[2,32,1152]{2,1,0:T(8,128)(2,1)S(1)} %bitcast.48), channel_id=1, source_target_pairs={{0,56},{4,60},{8,0},{12,4},{16,8},{20,12},{24,16},{28,20},{32,24},... | collective-permute-start | bytes 442376 | tf_op jit(solution)/shard_map/ppermute | solution.py:342
  55.3 4.6 %collective-permute-start.4 = (bf16[512,1024]{1,0:T(8,128)(2,1)S(1)}, bf16[512,1024]{1,0:T(8,128)(2,1)S(1)}, u32[]{:S(2)}, u32[]{:S(2)}) collective-permute-start(bf16[512,1024]{1,0:T(8,128)(2,1)S(1)} %shard_map.38.ring_ref), channel_id=1, source_target_pairs={{0,64},{64,0},{1,65},{65,1},{2,66},{66,2},{3,67},{67,3},{4,68},{68... | collective-permute-start | bytes 3145736 | tf_op jit(solution)/shard_map/ppermute | solution.py:373
  63.8 2.1 %collective-permute-start.5 = (bf16[256,1024]{1,0:T(8,128)(2,1)S(1)}, bf16[256,1024]{1,0:T(8,128)(2,1)S(1)}, u32[]{:S(2)}, u32[]{:S(2)}) collective-permute-start(bf16[256,1024]{1,0:T(8,128)(2,1)S(1)} %get-tuple-element.32), channel_id=1, source_target_pairs={{64,320},{192,448},{320,64},{448,192},{65,321},{193,449},{321,65},... | collective-permute-start | bytes 1572872 | tf_op jit(solution)/shard_map/ppermute | solution.py:210
  64.5 1.4 collective-permute-start.6
  65.2 0.7 collective-permute-start.7
  65.9 17.3 %collective-permute-start.8 = (bf16[16,128]{1,0:T(8,128)(2,1)S(1)}, bf16[16,128]{1,0:T(8,128)(2,1)S(1)}, u32[]{:S(2)}, u32[]{:S(2)}) collective-permute-start(bf16[16,128]{1,0:T(8,128)(2,1)S(1)} %slice_add_fusion), channel_id=1, source_target_pairs={{64,0},{65,1},{66,2},{67,3},{68,4},{69,5},{70,6},{71,7},{72,8},{73... | collective-permute-start | bytes 12296 | tf_op jit(solution)/shard_map/ppermute | solution.py:213
  83.3 12.7 %collective-permute-start.9 = (bf16[256,1024]{1,0:T(8,128)(2,1)S(1)}, bf16[256,1024]{1,0:T(8,128)(2,1)S(1)}, u32[]{:S(2)}, u32[]{:S(2)}) collective-permute-start(bf16[256,1024]{1,0:T(8,128)(2,1)S(1)} %get-tuple-element.32), channel_id=1, source_target_pairs={{0,256},{128,384},{256,0},{384,128},{1,257},{129,385},{257,1},{385... | collective-permute-start | bytes 1572872 | tf_op jit(solution)/shard_map/ppermute | solution.py:210
  88.0 13.5 %collective-permute-start.10 = (bf16[256,1024]{1,0:T(8,128)(2,1)S(1)}, bf16[256,1024]{1,0:T(8,128)(2,1)S(1)}, u32[]{:S(2)}, u32[]{:S(2)}) collective-permute-start(bf16[256,1024]{1,0:T(8,128)(2,1)S(1)} %get-tuple-element.33), channel_id=1, source_target_pairs={{0,128},{128,256},{256,384},{384,0},{1,129},{129,257},{257,385},{3... | collective-permute-start | bytes 1572872 | tf_op jit(solution)/shard_map/ppermute | solution.py:210
  91.3 11.1 %collective-permute-start.11 = (bf16[256,1024]{1,0:T(8,128)(2,1)S(1)}, bf16[256,1024]{1,0:T(8,128)(2,1)S(1)}, u32[]{:S(2)}, u32[]{:S(2)}) collective-permute-start(bf16[256,1024]{1,0:T(8,128)(2,1)S(1)} %get-tuple-element.34), channel_id=1, source_target_pairs={{0,384},{128,0},{256,128},{384,256},{1,385},{129,1},{257,129},{385... | collective-permute-start | bytes 1572872 | tf_op jit(solution)/shard_map/ppermute | solution.py:210
  105.7 40.5 %all-to-all-start.1 = ((bf16[16,128,256]{2,1,0:T(8,128)(2,1)}), bf16[16,128,256]{2,1,0:T(8,128)(2,1)S(1)}, u32[]{:S(2)}, u32[]{:S(2)}) async-start(bf16[16,128,256]{2,1,0:T(8,128)(2,1)} %shard_map.41), calls=%async_computation.1 | async-start | bytes 2097152 | tf_op jit(solution)/shard_map/all_to_all | solution.py:380

commit v18 on v14

--- a/solution.py
+++ b/solution.py
@@ -184,17 +184,20 @@
     )(scalar(x), pieces, ring, other)
 
 
-def exchange_x(parts, steps):
+def exchange_x(parts, steps, free):
     chips = lax.axis_size("x")
-    received = []
-    for core in (1, 0):
-        for i, step in enumerate(steps):
-            pairs = [(2 * x + core, (x + step) % chips * 2 + core) for x in range(chips)]
-            received.append(lax.ppermute(parts[i], ("x", "core"), pairs))
-        if core == 1:
-            ready = lax.ppermute(received[0][:16, :128], "core", [(1, 0)])
-            parts, ready = lax.optimization_barrier((parts, ready))
-    return received, ready
+
+    def send(part, step, core):
+        pairs = [(2 * x + core, (x + step) % chips * 2 + core) for x in range(chips)]
+        return lax.ppermute(part, ("x", "core"), pairs)
+
+    first = [send(part, step, 1) for part, step in zip(parts, steps)]
+    second = [send(parts[steps.index(free)], free, 0)]
+    ready = sum(part[:16, :128] for part in first)
+    ready = lax.ppermute(ready, "core", [(1, 0)])
+    parts, ready = lax.optimization_barrier((parts, ready))
+    second += [send(part, step, 0) for part, step in zip(parts, steps) if step != free]
+    return first + second, ready
 
 
 def pack(own, received, ready, slot_row, core, owners, capacity, head_dim):
@@ -329,7 +332,7 @@
     other = lax.ppermute(ring, "core", [(0, 1), (1, 0)])
     steps = (2, 1, -1, 0)
     *sent, kept = project(pieces, ring, other, lax.axis_index("x"), steps)
-    received, ready = exchange_x(sent, steps[:-1])
+    received, ready = exchange_x(sent, steps[:-1], -1)
     outgoing = pack(
         kept, received, ready, slot_row, lax.axis_index("core"), owners, capacity, head_dim
     )

time: 199 us -> 185 us (0.930)
  the two profiles are of different devices: /device:TPU:24 before, /device:TPU:14 now
where the time goes in v18:
time: 185 us; the launch traced here: 184 us
  waiting for transfers between devices  71.4 us (39%)
  blocking collectives  56.4 us (30%)
  starting transfers between devices  39.7 us (21%)
  Pallas kernels  14.2 us (8%)
    all_to_all x1, waiting for transfers between devices, body(): lax.all_to_all(outgoing, CLU, split_axis=0, concat_axis=0, tiled=True)  34.9 us
    all_to_all x1, blocking collectives, body(): lax.all_to_all(replies, CLU, split_axis=0, concat_axis=0, tiled=True)  29.9 us
    all_gather x1, blocking collectives, body(): four = lax.all_gather(own, 'zq', axis=0)  26.5 us
    ppermute x1, waiting for transfers between devices, exchange_x(): ready = lax.ppermute(ready, 'core', [(1, 0)])  19.2 us
    ppermute x4, starting transfers between devices, shifted(): lax.ppermute(block, axis, [(i, (i + step) % size) for i in range(size)])  14 us
    ppermute x6, starting transfers between devices, send(): return lax.ppermute(part, ('x', 'core'), pairs)  10.6 us
    ppermute x6, waiting for transfers between devices, send(): return lax.ppermute(part, ('x', 'core'), pairs)  9.67 us
    all_to_all x1, starting transfers between devices, body(): lax.all_to_all(outgoing, CLU, split_axis=0, concat_axis=0, tiled=True)  7 us
  transfers between devices with their start and end apart: 14, of which 8 were waited for; matrix products, arithmetic and copies ran while one was open for 0% of the time, Pallas kernels for 1%

profile of v18, /device:TPU:14, one launch (start us, length us, event | category | flops | bytes accessed | tf_op | source)
XLA Modules:
  0.0 183.9 jit_solution(12990337044482090872)
XLA Ops:
  1.6 2.4 %shard_map.37 = bf16[4,256,1024]{2,1,0:T(8,128)(2,1)} custom-call(s32[1]{0:T(128)} %bitcast.core_ref, bf16[256,4096]{1,0:T(8,128)(2,1)} %bitcast.46), custom_call_target="tpu_custom_call" | custom-call | tf_op jit(solution)/shard_map/pallas_call | solution.py:132
  4.0 4.9 %all-to-all-start = ((bf16[4,256,1024]{2,1,0:T(8,128)(2,1)}), bf16[4,256,1024]{2,1,0:T(8,128)(2,1)}, u32[]{:S(2)}, u32[]{:S(2)}) async-start(bf16[4,256,1024]{2,1,0:T(8,128)(2,1)} %shard_map.37), calls=%async_computation | async-start | bytes 4194304 | tf_op jit(solution)/shard_map/all_to_all | solution.py:320
  8.9 26.5 %all-gather = bf16[128,1152]{1,0:T(8,128)(2,1)S(1)} all-gather(bf16[32,1152]{1,0:T(8,128)(2,1)S(1)} %fusion.1), channel_id=2, replica_groups=mesh['x'=4,'core'=2,'zq'=4,'zr'=4,'tp'=4] {'zq'}, dimensions={0}, use_global_device_ids=true | all-gather | bytes 368640 | tf_op jit(solution)/shard_map/all_gather | solution.py:322
  35.4 4.0 %collective-permute-start.1 = (bf16[4,32,1152]{2,1,0:T(8,128)(2,1)S(1)}, bf16[4,32,1152]{2,1,0:T(8,128)(2,1)S(1)}, u32[]{:S(2)}, u32[]{:S(2)}) collective-permute-start(bf16[4,32,1152]{2,1,0:T(8,128)(2,1)S(1)} %bitcast.38), channel_id=1, source_target_pairs={{0,60},{4,0},{8,4},{12,8},{16,12},{20,16},{24,20},{28,24},{32,28},... | collective-permute-start | bytes 884744 | tf_op jit(solution)/shard_map/ppermute | solution.py:301
  39.5 2.0 %collective-permute-start = (bf16[4,32,1152]{2,1,0:T(8,128)(2,1)S(1)}, bf16[4,32,1152]{2,1,0:T(8,128)(2,1)S(1)}, u32[]{:S(2)}, u32[]{:S(2)}) collective-permute-start(bf16[4,32,1152]{2,1,0:T(8,128)(2,1)S(1)} %bitcast.39), channel_id=1, source_target_pairs={{0,4},{4,8},{8,12},{12,16},{16,20},{20,24},{24,28},{28,32},{32,36}... | collective-permute-start | bytes 884744 | tf_op jit(solution)/shard_map/ppermute | solution.py:301
  41.5 4.3 %collective-permute-start.2 = (bf16[2,32,1152]{2,1,0:T(8,128)(2,1)S(1)}, bf16[2,32,1152]{2,1,0:T(8,128)(2,1)S(1)}, u32[]{:S(2)}, u32[]{:S(2)}) collective-permute-start(bf16[2,32,1152]{2,1,0:T(8,128)(2,1)S(1)} %bitcast.49), channel_id=1, source_target_pairs={{0,8},{4,12},{8,16},{12,20},{16,24},{20,28},{24,32},{28,36},{32,40... | collective-permute-start | bytes 442376 | tf_op jit(solution)/shard_map/ppermute | solution.py:301
  45.9 3.6 %collective-permute-start.3 = (bf16[2,32,1152]{2,1,0:T(8,128)(2,1)S(1)}, bf16[2,32,1152]{2,1,0:T(8,128)(2,1)S(1)}, u32[]{:S(2)}, u32[]{:S(2)}) collective-permute-start(bf16[2,32,1152]{2,1,0:T(8,128)(2,1)S(1)} %bitcast.48), channel_id=1, source_target_pairs={{0,56},{4,60},{8,0},{12,4},{16,8},{20,12},{24,16},{28,20},{32,24},... | collective-permute-start | bytes 442376 | tf_op jit(solution)/shard_map/ppermute | solution.py:301
  50.3 2.8 %collective-permute-done.2.refs_3_ = bf16[2,32,1152]{2,1,0:T(8,128)(2,1)S(1)} collective-permute-done((bf16[2,32,1152]{2,1,0:T(8,128)(2,1)S(1)}, bf16[2,32,1152]{2,1,0:T(8,128)(2,1)S(1)}, u32[]{:S(2)}, u32[]{:S(2)}) %collective-permute-start.2) | collective-permute-done | bytes 147488 | tf_op jit(solution)/shard_map/ppermute | solution.py:301
  53.4 1.9 %collective-permute-done.3.refs_4_ = bf16[2,32,1152]{2,1,0:T(8,128)(2,1)S(1)} collective-permute-done((bf16[2,32,1152]{2,1,0:T(8,128)(2,1)S(1)}, bf16[2,32,1152]{2,1,0:T(8,128)(2,1)S(1)}, u32[]{:S(2)}, u32[]{:S(2)}) %collective-permute-start.3) | collective-permute-done | bytes 147488 | tf_op jit(solution)/shard_map/ppermute | solution.py:301
  55.4 1.9 %collective-permute-start.4 = (bf16[512,1024]{1,0:T(8,128)(2,1)S(1)}, bf16[512,1024]{1,0:T(8,128)(2,1)S(1)}, u32[]{:S(2)}, u32[]{:S(2)}) collective-permute-start(bf16[512,1024]{1,0:T(8,128)(2,1)S(1)} %shard_map.38.ring_ref), channel_id=1, source_target_pairs={{0,64},{64,0},{1,65},{65,1},{2,66},{66,2},{3,67},{67,3},{4,68},{68... | collective-permute-start | bytes 3145736 | tf_op jit(solution)/shard_map/ppermute | solution.py:332
  57.3 2.6 %collective-permute-done.4.other_ref = bf16[512,1024]{1,0:T(8,128)(2,1)S(1)} collective-permute-done((bf16[512,1024]{1,0:T(8,128)(2,1)S(1)}, bf16[512,1024]{1,0:T(8,128)(2,1)S(1)}, u32[]{:S(2)}, u32[]{:S(2)}) %collective-permute-start.4) | collective-permute-done | bytes 1048608 | tf_op jit(solution)/shard_map/ppermute | solution.py:332
  60.0 4.0 %shard_map.40 = (bf16[256,1024]{1,0:T(8,128)(2,1)S(1)}, bf16[256,1024]{1,0:T(8,128)(2,1)S(1)}, bf16[256,1024]{1,0:T(8,128)(2,1)S(1)}, bf16[256,1024]{1,0:T(8,128)(2,1)S(1)}) custom-call(s32[1]{0:T(128)} %bitcast.1.x_ref, bf16[4,256,1024]{2,1,0:T(8,128)(2,1)} %all-to-all-done.pieces_ref, bf16[512,1024]{1,0:T(8,128)(2,1)S(1)} %shard_map.38.ring_ref, ...), custom_call_target="tpu_custom_call" | custom-call | tf_op jit(solution)/shard_map/pallas_call | solution.py:180
  66.1 1.3 collective-permute-start.9
  67.4 2.8 %collective-permute-start.8 = (bf16[256,1024]{1,0:T(8,128)(2,1)S(1)}, bf16[256,1024]{1,0:T(8,128)(2,1)S(1)}, u32[]{:S(2)}, u32[]{:S(2)}) collective-permute-start(bf16[256,1024]{1,0:T(8,128)(2,1)S(1)} %get-tuple-element.29), channel_id=1, source_target_pairs={{0,384},{128,0},{256,128},{384,256},{1,385},{129,1},{257,129},{385... | collective-permute-start | bytes 1572872 | tf_op jit(solution)/shard_map/ppermute | solution.py:192
  70.1 19.2 %collective-permute-done.9.refs_7_ = bf16[16,128]{1,0:T(8,128)(2,1)S(1)} collective-permute-done((bf16[16,128]{1,0:T(8,128)(2,1)S(1)}, bf16[16,128]{1,0:T(8,128)(2,1)S(1)}, u32[]{:S(2)}, u32[]{:S(2)}) %collective-permute-start.9) | collective-permute-done | bytes 4128 | tf_op jit(solution)/shard_map/ppermute | solution.py:197
  89.3 2.8 %collective-permute-start.10 = (bf16[256,1024]{1,0:T(8,128)(2,1)S(1)}, bf16[256,1024]{1,0:T(8,128)(2,1)S(1)}, u32[]{:S(2)}, u32[]{:S(2)}) collective-permute-start(bf16[256,1024]{1,0:T(8,128)(2,1)S(1)} %get-tuple-element.30), channel_id=1, source_target_pairs={{0,256},{128,384},{256,0},{384,128},{1,257},{129,385},{257,1},{385... | collective-permute-start | bytes 1572872 | tf_op jit(solution)/shard_map/ppermute | solution.py:192
  92.1 3.0 %collective-permute-start.11 = (bf16[256,1024]{1,0:T(8,128)(2,1)S(1)}, bf16[256,1024]{1,0:T(8,128)(2,1)S(1)}, u32[]{:S(2)}, u32[]{:S(2)}) collective-permute-start(bf16[256,1024]{1,0:T(8,128)(2,1)S(1)} %get-tuple-element.31), channel_id=1, source_target_pairs={{0,128},{128,256},{256,384},{384,0},{1,129},{129,257},{257,385},{3... | collective-permute-start | bytes 1572872 | tf_op jit(solution)/shard_map/ppermute | solution.py:192
  95.1 6.8 %collective-permute-done.10.refs_4_ = bf16[256,1024]{1,0:T(8,128)(2,1)S(1)} collective-permute-done((bf16[256,1024]{1,0:T(8,128)(2,1)S(1)}, bf16[256,1024]{1,0:T(8,128)(2,1)S(1)}, u32[]{:S(2)}, u32[]{:S(2)}) %collective-permute-start.10) | collective-permute-done | bytes 524320 | tf_op jit(solution)/shard_map/ppermute | solution.py:192
  101.9 2.9 %collective-permute-done.11.refs_5_ = bf16[256,1024]{1,0:T(8,128)(2,1)S(1)} collective-permute-done((bf16[256,1024]{1,0:T(8,128)(2,1)S(1)}, bf16[256,1024]{1,0:T(8,128)(2,1)S(1)}, u32[]{:S(2)}, u32[]{:S(2)}) %collective-permute-start.11) | collective-permute-done | bytes 524320 | tf_op jit(solution)/shard_map/ppermute | solution.py:192
  104.8 1.8 shard_map.41
  106.5 7.0 %all-to-all-start.1 = ((bf16[16,128,256]{2,1,0:T(8,128)(2,1)}), bf16[16,128,256]{2,1,0:T(8,128)(2,1)S(1)}, u32[]{:S(2)}, u32[]{:S(2)}) async-start(bf16[16,128,256]{2,1,0:T(8,128)(2,1)} %shard_map.41), calls=%async_computation.1 | async-start | bytes 2097152 | tf_op jit(solution)/shard_map/all_to_all | solution.py:339
  114.8 34.9 %all-to-all-done.1.block_ref = bf16[16,128,256]{2,1,0:T(8,128)(2,1)S(1)} async-done(((bf16[16,128,256]{2,1,0:T(8,128)(2,1)}), bf16[16,128,256]{2,1,0:T(8,128)(2,1)S(1)}, u32[]{:S(2)}, u32[]{:S(2)}) %all-to-all-start.1) | async-done | bytes 1048608 | tf_op jit(solution)/shard_map/all_to_all | solution.py:339
  149.7 3.1 %shard_map.43 = bf16[16,128,128]{2,1,0:T(8,128)(2,1)S(1)} custom-call(bf16[16,128,256]{2,1,0:T(8,128)(2,1)S(1)} %all-to-all-done.1.block_ref, bf16[4,16,512]{2,1,0:T(8,128)(2,1)S(1)} %shard_map.42.member_ref), custom_call_target="tpu_custom_call" | custom-call | tf_op jit(solution)/shard_map/pallas_call | solution.py:273
  152.8 29.9 %all_to_all.15.block_ref = bf16[16,128,128]{2,1,0:T(8,128)(2,1)S(1)} all-to-all(bf16[16,128,128]{2,1,0:T(8,128)(2,1)S(1)} %shard_map.43), channel_id=1, replica_groups=mesh['x'=4,'core'=2,'zq'=4,'zr'=4,'tp'=4] {'zq','zr'}, dimensions={0} | all-to-all | bytes 1048576 | tf_op jit(solution)/shard_map/all_to_all | solution.py:348
  (33 shorter events, 7.2 us)
Async XLA Ops:
  4.0 45.5 %copy-start = (s32[1,256,4]{1,2,0:T(4,128)S(1)}, s32[1,256,4]{1,2,0:T(4,128)}, u32[]{:S(2)}) copy-start(s32[1,256,4]{1,2,0:T(4,128)} %param.5) | copy-start | bytes 12292
  4.0 41.8 %all-to-all-start = ((bf16[4,256,1024]{2,1,0:T(8,128)(2,1)}), bf16[4,256,1024]{2,1,0:T(8,128)(2,1)}, u32[]{:S(2)}, u32[]{:S(2)}) async-start(bf16[4,256,1024]{2,1,0:T(8,128)(2,1)} %shard_map.37), calls=%async_computation | async-start | bytes 4194304 | tf_op jit(solution)/shard_map/all_to_all | solution.py:320
  35.4 17.7 %collective-permute-start.1 = (bf16[4,32,1152]{2,1,0:T(8,128)(2,1)S(1)}, bf16[4,32,1152]{2,1,0:T(8,128)(2,1)S(1)}, u32[]{:S(2)}, u32[]{:S(2)}) collective-permute-start(bf16[4,32,1152]{2,1,0:T(8,128)(2,1)S(1)} %bitcast.38), channel_id=1, source_target_pairs={{0,60},{4,0},{8,4},{12,8},{16,12},{20,16},{24,20},{28,24},{32,28},... | collective-permute-start | bytes 884744 | tf_op jit(solution)/shard_map/ppermute | solution.py:301
  39.5 13.9 %collective-permute-start = (bf16[4,32,1152]{2,1,0:T(8,128)(2,1)S(1)}, bf16[4,32,1152]{2,1,0:T(8,128)(2,1)S(1)}, u32[]{:S(2)}, u32[]{:S(2)}) collective-permute-start(bf16[4,32,1152]{2,1,0:T(8,128)(2,1)S(1)} %bitcast.39), channel_id=1, source_target_pairs={{0,4},{4,8},{8,12},{12,16},{16,20},{20,24},{24,28},{28,32},{32,36}... | collective-permute-start | bytes 884744 | tf_op jit(solution)/shard_map/ppermute | solution.py:301
  41.5 11.6 %collective-permute-start.2 = (bf16[2,32,1152]{2,1,0:T(8,128)(2,1)S(1)}, bf16[2,32,1152]{2,1,0:T(8,128)(2,1)S(1)}, u32[]{:S(2)}, u32[]{:S(2)}) collective-permute-start(bf16[2,32,1152]{2,1,0:T(8,128)(2,1)S(1)} %bitcast.49), channel_id=1, source_target_pairs={{0,8},{4,12},{8,16},{12,20},{16,24},{20,28},{24,32},{28,36},{32,40... | collective-permute-start | bytes 442376 | tf_op jit(solution)/shard_map/ppermute | solution.py:301
  45.9 9.5 %collective-permute-start.3 = (bf16[2,32,1152]{2,1,0:T(8,128)(2,1)S(1)}, bf16[2,32,1152]{2,1,0:T(8,128)(2,1)S(1)}, u32[]{:S(2)}, u32[]{:S(2)}) collective-permute-start(bf16[2,32,1152]{2,1,0:T(8,128)(2,1)S(1)} %bitcast.48), channel_id=1, source_target_pairs={{0,56},{4,60},{8,0},{12,4},{16,8},{20,12},{24,16},{28,20},{32,24},... | collective-permute-start | bytes 442376 | tf_op jit(solution)/shard_map/ppermute | solution.py:301
  55.4 4.6 %collective-permute-start.4 = (bf16[512,1024]{1,0:T(8,128)(2,1)S(1)}, bf16[512,1024]{1,0:T(8,128)(2,1)S(1)}, u32[]{:S(2)}, u32[]{:S(2)}) collective-permute-start(bf16[512,1024]{1,0:T(8,128)(2,1)S(1)} %shard_map.38.ring_ref), channel_id=1, source_target_pairs={{0,64},{64,0},{1,65},{65,1},{2,66},{66,2},{3,67},{67,3},{4,68},{68... | collective-permute-start | bytes 3145736 | tf_op jit(solution)/shard_map/ppermute | solution.py:332
  63.9 2.1 %collective-permute-start.5 = (bf16[256,1024]{1,0:T(8,128)(2,1)S(1)}, bf16[256,1024]{1,0:T(8,128)(2,1)S(1)}, u32[]{:S(2)}, u32[]{:S(2)}) collective-permute-start(bf16[256,1024]{1,0:T(8,128)(2,1)S(1)} %get-tuple-element.30), channel_id=1, source_target_pairs={{64,320},{192,448},{320,64},{448,192},{65,321},{193,449},{321,65},... | collective-permute-start | bytes 1572872 | tf_op jit(solution)/shard_map/ppermute | solution.py:192
  64.6 1.4 collective-permute-start.6
  65.3 0.7 collective-permute-start.7
  66.1 23.3 %collective-permute-start.9 = (bf16[16,128]{1,0:T(8,128)(2,1)S(1)}, bf16[16,128]{1,0:T(8,128)(2,1)S(1)}, u32[]{:S(2)}, u32[]{:S(2)}) collective-permute-start(bf16[16,128]{1,0:T(8,128)(2,1)S(1)} %slice_add_fusion), channel_id=1, source_target_pairs={{64,0},{65,1},{66,2},{67,3},{68,4},{69,5},{70,6},{71,7},{72,8},{73... | collective-permute-start | bytes 12296 | tf_op jit(solution)/shard_map/ppermute | solution.py:197
  67.4 27.7 %collective-permute-start.8 = (bf16[256,1024]{1,0:T(8,128)(2,1)S(1)}, bf16[256,1024]{1,0:T(8,128)(2,1)S(1)}, u32[]{:S(2)}, u32[]{:S(2)}) collective-permute-start(bf16[256,1024]{1,0:T(8,128)(2,1)S(1)} %get-tuple-element.29), channel_id=1, source_target_pairs={{0,384},{128,0},{256,128},{384,256},{1,385},{129,1},{257,129},{385... | collective-permute-start | bytes 1572872 | tf_op jit(solution)/shard_map/ppermute | solution.py:192
  89.3 12.6 %collective-permute-start.10 = (bf16[256,1024]{1,0:T(8,128)(2,1)S(1)}, bf16[256,1024]{1,0:T(8,128)(2,1)S(1)}, u32[]{:S(2)}, u32[]{:S(2)}) collective-permute-start(bf16[256,1024]{1,0:T(8,128)(2,1)S(1)} %get-tuple-element.30), channel_id=1, source_target_pairs={{0,256},{128,384},{256,0},{384,128},{1,257},{129,385},{257,1},{385... | collective-permute-start | bytes 1572872 | tf_op jit(solution)/shard_map/ppermute | solution.py:192
  92.1 12.7 %collective-permute-start.11 = (bf16[256,1024]{1,0:T(8,128)(2,1)S(1)}, bf16[256,1024]{1,0:T(8,128)(2,1)S(1)}, u32[]{:S(2)}, u32[]{:S(2)}) collective-permute-start(bf16[256,1024]{1,0:T(8,128)(2,1)S(1)} %get-tuple-element.31), channel_id=1, source_target_pairs={{0,128},{128,256},{256,384},{384,0},{1,129},{129,257},{257,385},{3... | collective-permute-start | bytes 1572872 | tf_op jit(solution)/shard_map/ppermute | solution.py:192
  106.5 43.2 %all-to-all-start.1 = ((bf16[16,128,256]{2,1,0:T(8,128)(2,1)}), bf16[16,128,256]{2,1,0:T(8,128)(2,1)S(1)}, u32[]{:S(2)}, u32[]{:S(2)}) async-start(bf16[16,128,256]{2,1,0:T(8,128)(2,1)} %shard_map.41), calls=%async_computation.1 | async-start | bytes 2097152 | tf_op jit(solution)/shard_map/all_to_all | solution.py:339

commit v19 on v14

--- a/solution.py
+++ b/solution.py
@@ -192,7 +192,8 @@
             pairs = [(2 * x + core, (x + step) % chips * 2 + core) for x in range(chips)]
             received.append(lax.ppermute(parts[i], ("x", "core"), pairs))
         if core == 1:
-            ready = lax.ppermute(received[0][:16, :128], "core", [(1, 0)])
+            ready = sum(part[:16, :128] for part in received)
+            ready = lax.ppermute(ready, "core", [(1, 0)])
             parts, ready = lax.optimization_barrier((parts, ready))
     return received, ready
 

time: 199 us -> 178 us (0.89)
  blocking collectives: 64 us -> 53.9 us
  waiting for transfers between devices: 71.9 us -> 62.8 us
    all_to_all x1, waiting for transfers between devices: 42.8 us -> 32.2 us  [body(): lax.all_to_all(outgoing, CLU, split_axis=0, concat_axis=0, tiled=True)]
    all_to_all x1, blocking collectives: 36.9 us -> 26.8 us  [body(): lax.all_to_all(replies, CLU, split_axis=0, concat_axis=0, tiled=True)]
    ppermute x1, waiting for transfers between devices: 10.1 us -> 16 us  [exchange_x(): ready = lax.ppermute(ready, 'core', [(1, 0)])]
    ppermute x6, waiting for transfers between devices: 11.8 us -> 7.37 us  [exchange_x(): received.append(lax.ppermute(parts[i], ('x', 'core'), pairs))]
where the time goes in v19:
time: 178 us; the launch traced here: 176 us
  waiting for transfers between devices  62.8 us (35%)
  blocking collectives  53.9 us (30%)
  starting transfers between devices  42.7 us (24%)
  Pallas kernels  14.2 us (8%)
    all_to_all x1, waiting for transfers between devices, body(): lax.all_to_all(outgoing, CLU, split_axis=0, concat_axis=0, tiled=True)  32.2 us
    all_gather x1, blocking collectives, body(): four = lax.all_gather(own, 'zq', axis=0)  27.1 us
    all_to_all x1, blocking collectives, body(): lax.all_to_all(replies, CLU, split_axis=0, concat_axis=0, tiled=True)  26.8 us
    ppermute x1, waiting for transfers between devices, exchange_x(): ready = lax.ppermute(ready, 'core', [(1, 0)])  16 us
    ppermute x4, starting transfers between devices, shifted(): lax.ppermute(block, axis, [(i, (i + step) % size) for i in range(size)])  14.2 us
    ppermute x6, starting transfers between devices, exchange_x(): received.append(lax.ppermute(parts[i], ('x', 'core'), pairs))  13.8 us
    ppermute x6, waiting for transfers between devices, exchange_x(): received.append(lax.ppermute(parts[i], ('x', 'core'), pairs))  7.37 us
    all_to_all x1, starting transfers between devices, body(): lax.all_to_all(outgoing, CLU, split_axis=0, concat_axis=0, tiled=True)  7.02 us
  transfers between devices with their start and end apart: 14, of which 9 were waited for; matrix products, arithmetic and copies ran while one was open for 0% of the time, Pallas kernels for 1%

profile of v19, /device:TPU:24, one launch (start us, length us, event | category | flops | bytes accessed | tf_op | source)
XLA Modules:
  0.0 175.8 jit_solution(6353803154181222349)
XLA Ops:
  1.6 2.4 %shard_map.37 = bf16[4,256,1024]{2,1,0:T(8,128)(2,1)} custom-call(s32[1]{0:T(128)} %bitcast.core_ref, bf16[256,4096]{1,0:T(8,128)(2,1)} %bitcast.46), custom_call_target="tpu_custom_call" | custom-call | tf_op jit(solution)/shard_map/pallas_call | solution.py:132
  4.0 4.5 %all-to-all-start = ((bf16[4,256,1024]{2,1,0:T(8,128)(2,1)}), bf16[4,256,1024]{2,1,0:T(8,128)(2,1)}, u32[]{:S(2)}, u32[]{:S(2)}) async-start(bf16[4,256,1024]{2,1,0:T(8,128)(2,1)} %shard_map.37), calls=%async_computation | async-start | bytes 4194304 | tf_op jit(solution)/shard_map/all_to_all | solution.py:318
  8.5 27.1 %all-gather = bf16[128,1152]{1,0:T(8,128)(2,1)S(1)} all-gather(bf16[32,1152]{1,0:T(8,128)(2,1)S(1)} %fusion.1), channel_id=2, replica_groups=mesh['x'=4,'core'=2,'zq'=4,'zr'=4,'tp'=4] {'zq'}, dimensions={0}, use_global_device_ids=true | all-gather | bytes 368640 | tf_op jit(solution)/shard_map/all_gather | solution.py:320
  35.6 4.2 %collective-permute-start.1 = (bf16[4,32,1152]{2,1,0:T(8,128)(2,1)S(1)}, bf16[4,32,1152]{2,1,0:T(8,128)(2,1)S(1)}, u32[]{:S(2)}, u32[]{:S(2)}) collective-permute-start(bf16[4,32,1152]{2,1,0:T(8,128)(2,1)S(1)} %bitcast.38), channel_id=1, source_target_pairs={{0,60},{4,0},{8,4},{12,8},{16,12},{20,16},{24,20},{28,24},{32,28},... | collective-permute-start | bytes 884744 | tf_op jit(solution)/shard_map/ppermute | solution.py:299
  39.8 2.0 %collective-permute-start = (bf16[4,32,1152]{2,1,0:T(8,128)(2,1)S(1)}, bf16[4,32,1152]{2,1,0:T(8,128)(2,1)S(1)}, u32[]{:S(2)}, u32[]{:S(2)}) collective-permute-start(bf16[4,32,1152]{2,1,0:T(8,128)(2,1)S(1)} %bitcast.39), channel_id=1, source_target_pairs={{0,4},{4,8},{8,12},{12,16},{16,20},{20,24},{24,28},{28,32},{32,36}... | collective-permute-start | bytes 884744 | tf_op jit(solution)/shard_map/ppermute | solution.py:299
  41.8 4.0 %collective-permute-start.2 = (bf16[2,32,1152]{2,1,0:T(8,128)(2,1)S(1)}, bf16[2,32,1152]{2,1,0:T(8,128)(2,1)S(1)}, u32[]{:S(2)}, u32[]{:S(2)}) collective-permute-start(bf16[2,32,1152]{2,1,0:T(8,128)(2,1)S(1)} %bitcast.49), channel_id=1, source_target_pairs={{0,8},{4,12},{8,16},{12,20},{16,24},{20,28},{24,32},{28,36},{32,40... | collective-permute-start | bytes 442376 | tf_op jit(solution)/shard_map/ppermute | solution.py:299
  45.9 3.9 %collective-permute-start.3 = (bf16[2,32,1152]{2,1,0:T(8,128)(2,1)S(1)}, bf16[2,32,1152]{2,1,0:T(8,128)(2,1)S(1)}, u32[]{:S(2)}, u32[]{:S(2)}) collective-permute-start(bf16[2,32,1152]{2,1,0:T(8,128)(2,1)S(1)} %bitcast.48), channel_id=1, source_target_pairs={{0,56},{4,60},{8,0},{12,4},{16,8},{20,12},{24,16},{28,20},{32,24},... | collective-permute-start | bytes 442376 | tf_op jit(solution)/shard_map/ppermute | solution.py:299
  50.6 2.7 %collective-permute-done.2.refs_3_ = bf16[2,32,1152]{2,1,0:T(8,128)(2,1)S(1)} collective-permute-done((bf16[2,32,1152]{2,1,0:T(8,128)(2,1)S(1)}, bf16[2,32,1152]{2,1,0:T(8,128)(2,1)S(1)}, u32[]{:S(2)}, u32[]{:S(2)}) %collective-permute-start.2) | collective-permute-done | bytes 147488 | tf_op jit(solution)/shard_map/ppermute | solution.py:299
  53.4 1.8 %collective-permute-done.3.refs_4_ = bf16[2,32,1152]{2,1,0:T(8,128)(2,1)S(1)} collective-permute-done((bf16[2,32,1152]{2,1,0:T(8,128)(2,1)S(1)}, bf16[2,32,1152]{2,1,0:T(8,128)(2,1)S(1)}, u32[]{:S(2)}, u32[]{:S(2)}) %collective-permute-start.3) | collective-permute-done | bytes 147488 | tf_op jit(solution)/shard_map/ppermute | solution.py:299
  55.3 1.9 %collective-permute-start.4 = (bf16[512,1024]{1,0:T(8,128)(2,1)S(1)}, bf16[512,1024]{1,0:T(8,128)(2,1)S(1)}, u32[]{:S(2)}, u32[]{:S(2)}) collective-permute-start(bf16[512,1024]{1,0:T(8,128)(2,1)S(1)} %shard_map.38.ring_ref), channel_id=1, source_target_pairs={{0,64},{64,0},{1,65},{65,1},{2,66},{66,2},{3,67},{67,3},{4,68},{68... | collective-permute-start | bytes 3145736 | tf_op jit(solution)/shard_map/ppermute | solution.py:330
  57.2 2.6 %collective-permute-done.4.other_ref = bf16[512,1024]{1,0:T(8,128)(2,1)S(1)} collective-permute-done((bf16[512,1024]{1,0:T(8,128)(2,1)S(1)}, bf16[512,1024]{1,0:T(8,128)(2,1)S(1)}, u32[]{:S(2)}, u32[]{:S(2)}) %collective-permute-start.4) | collective-permute-done | bytes 1048608 | tf_op jit(solution)/shard_map/ppermute | solution.py:330
  59.8 4.0 %shard_map.40 = (bf16[256,1024]{1,0:T(8,128)(2,1)S(1)}, bf16[256,1024]{1,0:T(8,128)(2,1)S(1)}, bf16[256,1024]{1,0:T(8,128)(2,1)S(1)}, bf16[256,1024]{1,0:T(8,128)(2,1)S(1)}) custom-call(s32[1]{0:T(128)} %bitcast.1.x_ref, bf16[4,256,1024]{2,1,0:T(8,128)(2,1)} %all-to-all-done.pieces_ref, bf16[512,1024]{1,0:T(8,128)(2,1)S(1)} %shard_map.38.ring_ref, ...), custom_call_target="tpu_custom_call" | custom-call | tf_op jit(solution)/shard_map/pallas_call | solution.py:180
  66.0 1.3 collective-permute-start.8
  67.3 16.0 %collective-permute-done.8.refs_7_ = bf16[16,128]{1,0:T(8,128)(2,1)S(1)} collective-permute-done((bf16[16,128]{1,0:T(8,128)(2,1)S(1)}, bf16[16,128]{1,0:T(8,128)(2,1)S(1)}, u32[]{:S(2)}, u32[]{:S(2)}) %collective-permute-start.8) | collective-permute-done | bytes 4128 | tf_op jit(solution)/shard_map/ppermute | solution.py:196
  83.3 4.7 %collective-permute-start.9 = (bf16[256,1024]{1,0:T(8,128)(2,1)S(1)}, bf16[256,1024]{1,0:T(8,128)(2,1)S(1)}, u32[]{:S(2)}, u32[]{:S(2)}) collective-permute-start(bf16[256,1024]{1,0:T(8,128)(2,1)S(1)} %get-tuple-element.31), channel_id=1, source_target_pairs={{0,256},{128,384},{256,0},{384,128},{1,257},{129,385},{257,1},{385... | collective-permute-start | bytes 1572872 | tf_op jit(solution)/shard_map/ppermute | solution.py:193
  88.0 3.3 %collective-permute-start.10 = (bf16[256,1024]{1,0:T(8,128)(2,1)S(1)}, bf16[256,1024]{1,0:T(8,128)(2,1)S(1)}, u32[]{:S(2)}, u32[]{:S(2)}) collective-permute-start(bf16[256,1024]{1,0:T(8,128)(2,1)S(1)} %get-tuple-element.32), channel_id=1, source_target_pairs={{0,128},{128,256},{256,384},{384,0},{1,129},{129,257},{257,385},{3... | collective-permute-start | bytes 1572872 | tf_op jit(solution)/shard_map/ppermute | solution.py:193
  91.4 3.7 %collective-permute-start.11 = (bf16[256,1024]{1,0:T(8,128)(2,1)S(1)}, bf16[256,1024]{1,0:T(8,128)(2,1)S(1)}, u32[]{:S(2)}, u32[]{:S(2)}) collective-permute-start(bf16[256,1024]{1,0:T(8,128)(2,1)S(1)} %get-tuple-element.33), channel_id=1, source_target_pairs={{0,384},{128,0},{256,128},{384,256},{1,385},{129,1},{257,129},{385... | collective-permute-start | bytes 1572872 | tf_op jit(solution)/shard_map/ppermute | solution.py:193
  96.0 5.5 %collective-permute-done.10.refs_4_ = bf16[256,1024]{1,0:T(8,128)(2,1)S(1)} collective-permute-done((bf16[256,1024]{1,0:T(8,128)(2,1)S(1)}, bf16[256,1024]{1,0:T(8,128)(2,1)S(1)}, u32[]{:S(2)}, u32[]{:S(2)}) %collective-permute-start.10) | collective-permute-done | bytes 524320 | tf_op jit(solution)/shard_map/ppermute | solution.py:193
  102.4 1.8 shard_map.41
  104.2 7.0 %all-to-all-start.1 = ((bf16[16,128,256]{2,1,0:T(8,128)(2,1)}), bf16[16,128,256]{2,1,0:T(8,128)(2,1)S(1)}, u32[]{:S(2)}, u32[]{:S(2)}) async-start(bf16[16,128,256]{2,1,0:T(8,128)(2,1)} %shard_map.41), calls=%async_computation.1 | async-start | bytes 2097152 | tf_op jit(solution)/shard_map/all_to_all | solution.py:337
  112.5 32.2 %all-to-all-done.1.block_ref = bf16[16,128,256]{2,1,0:T(8,128)(2,1)S(1)} async-done(((bf16[16,128,256]{2,1,0:T(8,128)(2,1)}), bf16[16,128,256]{2,1,0:T(8,128)(2,1)S(1)}, u32[]{:S(2)}, u32[]{:S(2)}) %all-to-all-start.1) | async-done | bytes 1048608 | tf_op jit(solution)/shard_map/all_to_all | solution.py:337
  144.7 3.1 %shard_map.43 = bf16[16,128,128]{2,1,0:T(8,128)(2,1)S(1)} custom-call(bf16[16,128,256]{2,1,0:T(8,128)(2,1)S(1)} %all-to-all-done.1.block_ref, bf16[4,16,512]{2,1,0:T(8,128)(2,1)S(1)} %shard_map.42.member_ref), custom_call_target="tpu_custom_call" | custom-call | tf_op jit(solution)/shard_map/pallas_call | solution.py:271
  147.8 26.8 %all_to_all.15.block_ref = bf16[16,128,128]{2,1,0:T(8,128)(2,1)S(1)} all-to-all(bf16[16,128,128]{2,1,0:T(8,128)(2,1)S(1)} %shard_map.43), channel_id=1, replica_groups=mesh['x'=4,'core'=2,'zq'=4,'zr'=4,'tp'=4] {'zq','zr'}, dimensions={0} | all-to-all | bytes 1048576 | tf_op jit(solution)/shard_map/all_to_all | solution.py:346
  174.6 1.2 shard_map.44
  (33 shorter events, 7.7 us)
Async XLA Ops:
  4.0 45.8 %copy-start = (s32[1,256,4]{1,2,0:T(4,128)S(1)}, s32[1,256,4]{1,2,0:T(4,128)}, u32[]{:S(2)}) copy-start(s32[1,256,4]{1,2,0:T(4,128)} %param.5) | copy-start | bytes 12292
  4.0 41.9 %all-to-all-start = ((bf16[4,256,1024]{2,1,0:T(8,128)(2,1)}), bf16[4,256,1024]{2,1,0:T(8,128)(2,1)}, u32[]{:S(2)}, u32[]{:S(2)}) async-start(bf16[4,256,1024]{2,1,0:T(8,128)(2,1)} %shard_map.37), calls=%async_computation | async-start | bytes 4194304 | tf_op jit(solution)/shard_map/all_to_all | solution.py:318
  35.6 17.8 %collective-permute-start.1 = (bf16[4,32,1152]{2,1,0:T(8,128)(2,1)S(1)}, bf16[4,32,1152]{2,1,0:T(8,128)(2,1)S(1)}, u32[]{:S(2)}, u32[]{:S(2)}) collective-permute-start(bf16[4,32,1152]{2,1,0:T(8,128)(2,1)S(1)} %bitcast.38), channel_id=1, source_target_pairs={{0,60},{4,0},{8,4},{12,8},{16,12},{20,16},{24,20},{28,24},{32,28},... | collective-permute-start | bytes 884744 | tf_op jit(solution)/shard_map/ppermute | solution.py:299
  39.8 13.7 %collective-permute-start = (bf16[4,32,1152]{2,1,0:T(8,128)(2,1)S(1)}, bf16[4,32,1152]{2,1,0:T(8,128)(2,1)S(1)}, u32[]{:S(2)}, u32[]{:S(2)}) collective-permute-start(bf16[4,32,1152]{2,1,0:T(8,128)(2,1)S(1)} %bitcast.39), channel_id=1, source_target_pairs={{0,4},{4,8},{8,12},{12,16},{16,20},{20,24},{24,28},{28,32},{32,36}... | collective-permute-start | bytes 884744 | tf_op jit(solution)/shard_map/ppermute | solution.py:299
  41.8 11.5 %collective-permute-start.2 = (bf16[2,32,1152]{2,1,0:T(8,128)(2,1)S(1)}, bf16[2,32,1152]{2,1,0:T(8,128)(2,1)S(1)}, u32[]{:S(2)}, u32[]{:S(2)}) collective-permute-start(bf16[2,32,1152]{2,1,0:T(8,128)(2,1)S(1)} %bitcast.49), channel_id=1, source_target_pairs={{0,8},{4,12},{8,16},{12,20},{16,24},{20,28},{24,32},{28,36},{32,40... | collective-permute-start | bytes 442376 | tf_op jit(solution)/shard_map/ppermute | solution.py:299
  45.9 9.3 %collective-permute-start.3 = (bf16[2,32,1152]{2,1,0:T(8,128)(2,1)S(1)}, bf16[2,32,1152]{2,1,0:T(8,128)(2,1)S(1)}, u32[]{:S(2)}, u32[]{:S(2)}) collective-permute-start(bf16[2,32,1152]{2,1,0:T(8,128)(2,1)S(1)} %bitcast.48), channel_id=1, source_target_pairs={{0,56},{4,60},{8,0},{12,4},{16,8},{20,12},{24,16},{28,20},{32,24},... | collective-permute-start | bytes 442376 | tf_op jit(solution)/shard_map/ppermute | solution.py:299
  55.3 4.6 %collective-permute-start.4 = (bf16[512,1024]{1,0:T(8,128)(2,1)S(1)}, bf16[512,1024]{1,0:T(8,128)(2,1)S(1)}, u32[]{:S(2)}, u32[]{:S(2)}) collective-permute-start(bf16[512,1024]{1,0:T(8,128)(2,1)S(1)} %shard_map.38.ring_ref), channel_id=1, source_target_pairs={{0,64},{64,0},{1,65},{65,1},{2,66},{66,2},{3,67},{67,3},{4,68},{68... | collective-permute-start | bytes 3145736 | tf_op jit(solution)/shard_map/ppermute | solution.py:330
  63.8 2.1 %collective-permute-start.5 = (bf16[256,1024]{1,0:T(8,128)(2,1)S(1)}, bf16[256,1024]{1,0:T(8,128)(2,1)S(1)}, u32[]{:S(2)}, u32[]{:S(2)}) collective-permute-start(bf16[256,1024]{1,0:T(8,128)(2,1)S(1)} %get-tuple-element.31), channel_id=1, source_target_pairs={{64,320},{192,448},{320,64},{448,192},{65,321},{193,449},{321,65},... | collective-permute-start | bytes 1572872 | tf_op jit(solution)/shard_map/ppermute | solution.py:193
  64.5 1.4 collective-permute-start.6
  65.2 0.7 collective-permute-start.7
  66.0 17.3 %collective-permute-start.8 = (bf16[16,128]{1,0:T(8,128)(2,1)S(1)}, bf16[16,128]{1,0:T(8,128)(2,1)S(1)}, u32[]{:S(2)}, u32[]{:S(2)}) collective-permute-start(bf16[16,128]{1,0:T(8,128)(2,1)S(1)} %slice_add_fusion), channel_id=1, source_target_pairs={{64,0},{65,1},{66,2},{67,3},{68,4},{69,5},{70,6},{71,7},{72,8},{73... | collective-permute-start | bytes 12296 | tf_op jit(solution)/shard_map/ppermute | solution.py:196
  83.3 12.7 %collective-permute-start.9 = (bf16[256,1024]{1,0:T(8,128)(2,1)S(1)}, bf16[256,1024]{1,0:T(8,128)(2,1)S(1)}, u32[]{:S(2)}, u32[]{:S(2)}) collective-permute-start(bf16[256,1024]{1,0:T(8,128)(2,1)S(1)} %get-tuple-element.31), channel_id=1, source_target_pairs={{0,256},{128,384},{256,0},{384,128},{1,257},{129,385},{257,1},{385... | collective-permute-start | bytes 1572872 | tf_op jit(solution)/shard_map/ppermute | solution.py:193
  88.0 13.5 %collective-permute-start.10 = (bf16[256,1024]{1,0:T(8,128)(2,1)S(1)}, bf16[256,1024]{1,0:T(8,128)(2,1)S(1)}, u32[]{:S(2)}, u32[]{:S(2)}) collective-permute-start(bf16[256,1024]{1,0:T(8,128)(2,1)S(1)} %get-tuple-element.32), channel_id=1, source_target_pairs={{0,128},{128,256},{256,384},{384,0},{1,129},{129,257},{257,385},{3... | collective-permute-start | bytes 1572872 | tf_op jit(solution)/shard_map/ppermute | solution.py:193
  91.4 11.1 %collective-permute-start.11 = (bf16[256,1024]{1,0:T(8,128)(2,1)S(1)}, bf16[256,1024]{1,0:T(8,128)(2,1)S(1)}, u32[]{:S(2)}, u32[]{:S(2)}) collective-permute-start(bf16[256,1024]{1,0:T(8,128)(2,1)S(1)} %get-tuple-element.33), channel_id=1, source_target_pairs={{0,384},{128,0},{256,128},{384,256},{1,385},{129,1},{257,129},{385... | collective-permute-start | bytes 1572872 | tf_op jit(solution)/shard_map/ppermute | solution.py:193
  104.2 40.5 %all-to-all-start.1 = ((bf16[16,128,256]{2,1,0:T(8,128)(2,1)}), bf16[16,128,256]{2,1,0:T(8,128)(2,1)S(1)}, u32[]{:S(2)}, u32[]{:S(2)}) async-start(bf16[16,128,256]{2,1,0:T(8,128)(2,1)} %shard_map.41), calls=%async_computation.1 | async-start | bytes 2097152 | tf_op jit(solution)/shard_map/all_to_all | solution.py:337

commit v20 on v15

--- a/solution.py
+++ b/solution.py
@@ -342,7 +342,7 @@
     slot_row, slot_col = routing(clusters[0], owners, capacity)
     ring, slot_row = lax.optimization_barrier((ring, slot_row))
     other = lax.ppermute(ring, "core", [(0, 1), (1, 0)])
-    steps = (2, 1, -1, 0)
+    steps = (2, -1, 1, 0)
     *sent, kept = project(pieces, ring, other, lax.axis_index("x"), steps)
     received, ready = exchange_x(sent, steps[:-1])
     outgoing = pack(

time: 178 us -> 178 us (level)
  waiting for transfers between devices: 62.8 us -> 66.6 us
  starting transfers between devices: 42.7 us -> 40.1 us
    ppermute x6, starting transfers between devices: 13.8 us -> 11.3 us  [exchange_x(): received.append(lax.ppermute(parts[i], ('x', 'core'), pairs))]
    ppermute x6, waiting for transfers between devices: 7.37 us -> 9.53 us  [exchange_x(): received.append(lax.ppermute(parts[i], ('x', 'core'), pairs))]
where the time goes in v20:
time: 178 us; the launch traced here: 177 us
  waiting for transfers between devices  66.6 us (37%)
  blocking collectives  53.4 us (30%)
  starting transfers between devices  40.1 us (23%)
  Pallas kernels  14.4 us (8%)
    all_to_all x1, waiting for transfers between devices, body(): lax.all_to_all(outgoing, CLU, split_axis=0, concat_axis=0, tiled=True)  32.5 us
    all_gather x1, blocking collectives, body(): four = lax.all_gather(own, 'zq', axis=0)  27.1 us
    all_to_all x1, blocking collectives, body(): lax.all_to_all(replies, CLU, split_axis=0, concat_axis=0, tiled=True)  26.3 us
    ppermute x1, waiting for transfers between devices, exchange_x(): ready = lax.ppermute(ready, 'core', [(1, 0)])  17.4 us
    ppermute x4, starting transfers between devices, shifted(): lax.ppermute(block, axis, [(i, (i + step) % size) for i in range(size)])  14.2 us
    ppermute x6, starting transfers between devices, exchange_x(): received.append(lax.ppermute(parts[i], ('x', 'core'), pairs))  11.3 us
    ppermute x6, waiting for transfers between devices, exchange_x(): received.append(lax.ppermute(parts[i], ('x', 'core'), pairs))  9.53 us
    all_to_all x1, starting transfers between devices, body(): lax.all_to_all(outgoing, CLU, split_axis=0, concat_axis=0, tiled=True)  7.03 us
  transfers between devices with their start and end apart: 14, of which 9 were waited for; matrix products, arithmetic and copies ran while one was open for 0% of the time, Pallas kernels for 1%

profile of v20, /device:TPU:24, one launch (start us, length us, event | category | flops | bytes accessed | tf_op | source)
XLA Modules:
  0.0 176.7 jit_solution(8293869868212119206)
XLA Ops:
  1.6 2.4 %shard_map.37 = bf16[4,256,1024]{2,1,0:T(8,128)(2,1)} custom-call(s32[1]{0:T(128)} %bitcast.core_ref, bf16[256,4096]{1,0:T(8,128)(2,1)} %bitcast.46), custom_call_target="tpu_custom_call" | custom-call | tf_op jit(solution)/shard_map/pallas_call | solution.py:132
  4.0 4.5 %all-to-all-start = ((bf16[4,256,1024]{2,1,0:T(8,128)(2,1)}), bf16[4,256,1024]{2,1,0:T(8,128)(2,1)}, u32[]{:S(2)}, u32[]{:S(2)}) async-start(bf16[4,256,1024]{2,1,0:T(8,128)(2,1)} %shard_map.37), calls=%async_computation | async-start | bytes 4194304 | tf_op jit(solution)/shard_map/all_to_all | solution.py:332
  8.5 27.1 %all-gather = bf16[128,1152]{1,0:T(8,128)(2,1)S(1)} all-gather(bf16[32,1152]{1,0:T(8,128)(2,1)S(1)} %fusion.1), channel_id=2, replica_groups=mesh['x'=4,'core'=2,'zq'=4,'zr'=4,'tp'=4] {'zq'}, dimensions={0}, use_global_device_ids=true | all-gather | bytes 368640 | tf_op jit(solution)/shard_map/all_gather | solution.py:334
  35.6 4.2 %collective-permute-start.1 = (bf16[4,32,1152]{2,1,0:T(8,128)(2,1)S(1)}, bf16[4,32,1152]{2,1,0:T(8,128)(2,1)S(1)}, u32[]{:S(2)}, u32[]{:S(2)}) collective-permute-start(bf16[4,32,1152]{2,1,0:T(8,128)(2,1)S(1)} %bitcast.38), channel_id=1, source_target_pairs={{0,60},{4,0},{8,4},{12,8},{16,12},{20,16},{24,20},{28,24},{32,28},... | collective-permute-start | bytes 884744 | tf_op jit(solution)/shard_map/ppermute | solution.py:313
  39.8 2.0 %collective-permute-start = (bf16[4,32,1152]{2,1,0:T(8,128)(2,1)S(1)}, bf16[4,32,1152]{2,1,0:T(8,128)(2,1)S(1)}, u32[]{:S(2)}, u32[]{:S(2)}) collective-permute-start(bf16[4,32,1152]{2,1,0:T(8,128)(2,1)S(1)} %bitcast.39), channel_id=1, source_target_pairs={{0,4},{4,8},{8,12},{12,16},{16,20},{20,24},{24,28},{28,32},{32,36}... | collective-permute-start | bytes 884744 | tf_op jit(solution)/shard_map/ppermute | solution.py:313
  41.8 4.0 %collective-permute-start.2 = (bf16[2,32,1152]{2,1,0:T(8,128)(2,1)S(1)}, bf16[2,32,1152]{2,1,0:T(8,128)(2,1)S(1)}, u32[]{:S(2)}, u32[]{:S(2)}) collective-permute-start(bf16[2,32,1152]{2,1,0:T(8,128)(2,1)S(1)} %bitcast.49), channel_id=1, source_target_pairs={{0,8},{4,12},{8,16},{12,20},{16,24},{20,28},{24,32},{28,36},{32,40... | collective-permute-start | bytes 442376 | tf_op jit(solution)/shard_map/ppermute | solution.py:313
  45.9 3.9 %collective-permute-start.3 = (bf16[2,32,1152]{2,1,0:T(8,128)(2,1)S(1)}, bf16[2,32,1152]{2,1,0:T(8,128)(2,1)S(1)}, u32[]{:S(2)}, u32[]{:S(2)}) collective-permute-start(bf16[2,32,1152]{2,1,0:T(8,128)(2,1)S(1)} %bitcast.48), channel_id=1, source_target_pairs={{0,56},{4,60},{8,0},{12,4},{16,8},{20,12},{24,16},{28,20},{32,24},... | collective-permute-start | bytes 442376 | tf_op jit(solution)/shard_map/ppermute | solution.py:313
  50.6 2.7 %collective-permute-done.2.refs_3_ = bf16[2,32,1152]{2,1,0:T(8,128)(2,1)S(1)} collective-permute-done((bf16[2,32,1152]{2,1,0:T(8,128)(2,1)S(1)}, bf16[2,32,1152]{2,1,0:T(8,128)(2,1)S(1)}, u32[]{:S(2)}, u32[]{:S(2)}) %collective-permute-start.2) | collective-permute-done | bytes 147488 | tf_op jit(solution)/shard_map/ppermute | solution.py:313
  53.4 1.8 collective-permute-done.3.refs_4_
  55.3 1.9 %collective-permute-start.4 = (bf16[512,1024]{1,0:T(8,128)(2,1)S(1)}, bf16[512,1024]{1,0:T(8,128)(2,1)S(1)}, u32[]{:S(2)}, u32[]{:S(2)}) collective-permute-start(bf16[512,1024]{1,0:T(8,128)(2,1)S(1)} %shard_map.38.ring_ref), channel_id=1, source_target_pairs={{0,64},{64,0},{1,65},{65,1},{2,66},{66,2},{3,67},{67,3},{4,68},{68... | collective-permute-start | bytes 3145736 | tf_op jit(solution)/shard_map/ppermute | solution.py:344
  57.2 2.6 %collective-permute-done.4.other_ref = bf16[512,1024]{1,0:T(8,128)(2,1)S(1)} collective-permute-done((bf16[512,1024]{1,0:T(8,128)(2,1)S(1)}, bf16[512,1024]{1,0:T(8,128)(2,1)S(1)}, u32[]{:S(2)}, u32[]{:S(2)}) %collective-permute-start.4) | collective-permute-done | bytes 1048608 | tf_op jit(solution)/shard_map/ppermute | solution.py:344
  59.8 4.0 %shard_map.40 = (bf16[256,1024]{1,0:T(8,128)(2,1)S(1)}, bf16[256,1024]{1,0:T(8,128)(2,1)S(1)}, bf16[256,1024]{1,0:T(8,128)(2,1)S(1)}, bf16[256,1024]{1,0:T(8,128)(2,1)S(1)}) custom-call(s32[1]{0:T(128)} %bitcast.9.x_ref, bf16[4,256,1024]{2,1,0:T(8,128)(2,1)} %all-to-all-done.pieces_ref, bf16[512,1024]{1,0:T(8,128)(2,1)S(1)} %shard_map.38.ring_ref, ...), custom_call_target="tpu_custom_call" | custom-call | tf_op jit(solution)/shard_map/pallas_call | solution.py:180
  67.3 17.4 %collective-permute-done.8.refs_6_ = bf16[16,128]{1,0:T(8,128)(2,1)S(1)} collective-permute-done((bf16[16,128]{1,0:T(8,128)(2,1)S(1)}, bf16[16,128]{1,0:T(8,128)(2,1)S(1)}, u32[]{:S(2)}, u32[]{:S(2)}) %collective-permute-start.8) | collective-permute-done | bytes 4128 | tf_op jit(solution)/shard_map/ppermute | solution.py:196
  84.6 3.4 %collective-permute-start.9 = (bf16[256,1024]{1,0:T(8,128)(2,1)S(1)}, bf16[256,1024]{1,0:T(8,128)(2,1)S(1)}, u32[]{:S(2)}, u32[]{:S(2)}) collective-permute-start(bf16[256,1024]{1,0:T(8,128)(2,1)S(1)} %get-tuple-element.32), channel_id=1, source_target_pairs={{0,256},{128,384},{256,0},{384,128},{1,257},{129,385},{257,1},{385... | collective-permute-start | bytes 1572872 | tf_op jit(solution)/shard_map/ppermute | solution.py:193
  88.0 3.1 %collective-permute-start.10 = (bf16[256,1024]{1,0:T(8,128)(2,1)S(1)}, bf16[256,1024]{1,0:T(8,128)(2,1)S(1)}, u32[]{:S(2)}, u32[]{:S(2)}) collective-permute-start(bf16[256,1024]{1,0:T(8,128)(2,1)S(1)} %get-tuple-element.33), channel_id=1, source_target_pairs={{0,384},{128,0},{256,128},{384,256},{1,385},{129,1},{257,129},{385... | collective-permute-start | bytes 1572872 | tf_op jit(solution)/shard_map/ppermute | solution.py:193
  91.1 2.8 %collective-permute-start.11 = (bf16[256,1024]{1,0:T(8,128)(2,1)S(1)}, bf16[256,1024]{1,0:T(8,128)(2,1)S(1)}, u32[]{:S(2)}, u32[]{:S(2)}) collective-permute-start(bf16[256,1024]{1,0:T(8,128)(2,1)S(1)} %get-tuple-element.34), channel_id=1, source_target_pairs={{0,128},{128,256},{256,384},{384,0},{1,129},{129,257},{257,385},{3... | collective-permute-start | bytes 1572872 | tf_op jit(solution)/shard_map/ppermute | solution.py:193
  93.8 3.3 %collective-permute-done.9.refs_3_ = bf16[256,1024]{1,0:T(8,128)(2,1)S(1)} collective-permute-done((bf16[256,1024]{1,0:T(8,128)(2,1)S(1)}, bf16[256,1024]{1,0:T(8,128)(2,1)S(1)}, u32[]{:S(2)}, u32[]{:S(2)}) %collective-permute-start.9) | collective-permute-done | bytes 524320 | tf_op jit(solution)/shard_map/ppermute | solution.py:193
  97.2 4.2 %collective-permute-done.10.refs_4_ = bf16[256,1024]{1,0:T(8,128)(2,1)S(1)} collective-permute-done((bf16[256,1024]{1,0:T(8,128)(2,1)S(1)}, bf16[256,1024]{1,0:T(8,128)(2,1)S(1)}, u32[]{:S(2)}, u32[]{:S(2)}) %collective-permute-start.10) | collective-permute-done | bytes 524320 | tf_op jit(solution)/shard_map/ppermute | solution.py:193
  101.4 2.0 %collective-permute-done.11.refs_5_ = bf16[256,1024]{1,0:T(8,128)(2,1)S(1)} collective-permute-done((bf16[256,1024]{1,0:T(8,128)(2,1)S(1)}, bf16[256,1024]{1,0:T(8,128)(2,1)S(1)}, u32[]{:S(2)}, u32[]{:S(2)}) %collective-permute-start.11) | collective-permute-done | bytes 524320 | tf_op jit(solution)/shard_map/ppermute | solution.py:193
  103.4 1.9 %shard_map.41 = bf16[16,128,256]{2,1,0:T(8,128)(2,1)} custom-call(s32[1]{0:T(128)} %bitcast.core_ref, s32[4,256]{1,0:T(4,128)S(1)} %get-tuple-element.25.slot_ref, bf16[256,1024]{1,0:T(8,128)(2,1)S(1)} %get-tuple-element.28.own_ref, bf16[256,1024]{1,0:T(8,128)(2,1)S(1)} %collective-permute-done.5.refs_0_, ...), custom_call_target="tpu_custom_call" | custom-call | tf_op jit(solution)/shard_map/pallas_call | solution.py:242
  105.3 7.0 %all-to-all-start.1 = ((bf16[16,128,256]{2,1,0:T(8,128)(2,1)}), bf16[16,128,256]{2,1,0:T(8,128)(2,1)S(1)}, u32[]{:S(2)}, u32[]{:S(2)}) async-start(bf16[16,128,256]{2,1,0:T(8,128)(2,1)} %shard_map.41), calls=%async_computation.1 | async-start | bytes 2097152 | tf_op jit(solution)/shard_map/all_to_all | solution.py:351
  113.6 32.5 %all-to-all-done.1.block_ref = bf16[16,128,256]{2,1,0:T(8,128)(2,1)S(1)} async-done(((bf16[16,128,256]{2,1,0:T(8,128)(2,1)}), bf16[16,128,256]{2,1,0:T(8,128)(2,1)S(1)}, u32[]{:S(2)}, u32[]{:S(2)}) %all-to-all-start.1) | async-done | bytes 1048608 | tf_op jit(solution)/shard_map/all_to_all | solution.py:351
  146.1 3.1 %shard_map.43 = bf16[16,128,128]{2,1,0:T(8,128)(2,1)S(1)} custom-call(bf16[16,128,256]{2,1,0:T(8,128)(2,1)S(1)} %all-to-all-done.1.block_ref, bf16[4,16,512]{2,1,0:T(8,128)(2,1)S(1)} %shard_map.42.member_ref), custom_call_target="tpu_custom_call" | custom-call | tf_op jit(solution)/shard_map/pallas_call | solution.py:285
  149.2 26.3 %all_to_all.15.block_ref = bf16[16,128,128]{2,1,0:T(8,128)(2,1)S(1)} all-to-all(bf16[16,128,128]{2,1,0:T(8,128)(2,1)S(1)} %shard_map.43), channel_id=1, replica_groups=mesh['x'=4,'core'=2,'zq'=4,'zr'=4,'tp'=4] {'zq','zr'}, dimensions={0} | all-to-all | bytes 1048576 | tf_op jit(solution)/shard_map/all_to_all | solution.py:360
  (33 shorter events, 8.3 us)
Async XLA Ops:
  4.0 45.8 %copy-start = (s32[1,256,4]{1,2,0:T(4,128)S(1)}, s32[1,256,4]{1,2,0:T(4,128)}, u32[]{:S(2)}) copy-start(s32[1,256,4]{1,2,0:T(4,128)} %param.5) | copy-start | bytes 12292
  4.0 41.9 %all-to-all-start = ((bf16[4,256,1024]{2,1,0:T(8,128)(2,1)}), bf16[4,256,1024]{2,1,0:T(8,128)(2,1)}, u32[]{:S(2)}, u32[]{:S(2)}) async-start(bf16[4,256,1024]{2,1,0:T(8,128)(2,1)} %shard_map.37), calls=%async_computation | async-start | bytes 4194304 | tf_op jit(solution)/shard_map/all_to_all | solution.py:332
  35.6 17.8 %collective-permute-start.1 = (bf16[4,32,1152]{2,1,0:T(8,128)(2,1)S(1)}, bf16[4,32,1152]{2,1,0:T(8,128)(2,1)S(1)}, u32[]{:S(2)}, u32[]{:S(2)}) collective-permute-start(bf16[4,32,1152]{2,1,0:T(8,128)(2,1)S(1)} %bitcast.38), channel_id=1, source_target_pairs={{0,60},{4,0},{8,4},{12,8},{16,12},{20,16},{24,20},{28,24},{32,28},... | collective-permute-start | bytes 884744 | tf_op jit(solution)/shard_map/ppermute | solution.py:313
  39.8 13.7 %collective-permute-start = (bf16[4,32,1152]{2,1,0:T(8,128)(2,1)S(1)}, bf16[4,32,1152]{2,1,0:T(8,128)(2,1)S(1)}, u32[]{:S(2)}, u32[]{:S(2)}) collective-permute-start(bf16[4,32,1152]{2,1,0:T(8,128)(2,1)S(1)} %bitcast.39), channel_id=1, source_target_pairs={{0,4},{4,8},{8,12},{12,16},{16,20},{20,24},{24,28},{28,32},{32,36}... | collective-permute-start | bytes 884744 | tf_op jit(solution)/shard_map/ppermute | solution.py:313
  41.8 11.5 %collective-permute-start.2 = (bf16[2,32,1152]{2,1,0:T(8,128)(2,1)S(1)}, bf16[2,32,1152]{2,1,0:T(8,128)(2,1)S(1)}, u32[]{:S(2)}, u32[]{:S(2)}) collective-permute-start(bf16[2,32,1152]{2,1,0:T(8,128)(2,1)S(1)} %bitcast.49), channel_id=1, source_target_pairs={{0,8},{4,12},{8,16},{12,20},{16,24},{20,28},{24,32},{28,36},{32,40... | collective-permute-start | bytes 442376 | tf_op jit(solution)/shard_map/ppermute | solution.py:313
  45.9 9.3 %collective-permute-start.3 = (bf16[2,32,1152]{2,1,0:T(8,128)(2,1)S(1)}, bf16[2,32,1152]{2,1,0:T(8,128)(2,1)S(1)}, u32[]{:S(2)}, u32[]{:S(2)}) collective-permute-start(bf16[2,32,1152]{2,1,0:T(8,128)(2,1)S(1)} %bitcast.48), channel_id=1, source_target_pairs={{0,56},{4,60},{8,0},{12,4},{16,8},{20,12},{24,16},{28,20},{32,24},... | collective-permute-start | bytes 442376 | tf_op jit(solution)/shard_map/ppermute | solution.py:313
  55.3 4.6 %collective-permute-start.4 = (bf16[512,1024]{1,0:T(8,128)(2,1)S(1)}, bf16[512,1024]{1,0:T(8,128)(2,1)S(1)}, u32[]{:S(2)}, u32[]{:S(2)}) collective-permute-start(bf16[512,1024]{1,0:T(8,128)(2,1)S(1)} %shard_map.38.ring_ref), channel_id=1, source_target_pairs={{0,64},{64,0},{1,65},{65,1},{2,66},{66,2},{3,67},{67,3},{4,68},{68... | collective-permute-start | bytes 3145736 | tf_op jit(solution)/shard_map/ppermute | solution.py:344
  63.8 2.1 %collective-permute-start.5 = (bf16[256,1024]{1,0:T(8,128)(2,1)S(1)}, bf16[256,1024]{1,0:T(8,128)(2,1)S(1)}, u32[]{:S(2)}, u32[]{:S(2)}) collective-permute-start(bf16[256,1024]{1,0:T(8,128)(2,1)S(1)} %get-tuple-element.32), channel_id=1, source_target_pairs={{64,320},{192,448},{320,64},{448,192},{65,321},{193,449},{321,65},... | collective-permute-start | bytes 1572872 | tf_op jit(solution)/shard_map/ppermute | solution.py:193
  64.5 1.4 collective-permute-start.6
  65.2 0.7 collective-permute-start.7
  66.0 18.7 %collective-permute-start.8 = (bf16[16,128]{1,0:T(8,128)(2,1)S(1)}, bf16[16,128]{1,0:T(8,128)(2,1)S(1)}, u32[]{:S(2)}, u32[]{:S(2)}) collective-permute-start(bf16[16,128]{1,0:T(8,128)(2,1)S(1)} %slice_add_fusion), channel_id=1, source_target_pairs={{64,0},{65,1},{66,2},{67,3},{68,4},{69,5},{70,6},{71,7},{72,8},{73... | collective-permute-start | bytes 12296 | tf_op jit(solution)/shard_map/ppermute | solution.py:196
  84.6 12.6 %collective-permute-start.9 = (bf16[256,1024]{1,0:T(8,128)(2,1)S(1)}, bf16[256,1024]{1,0:T(8,128)(2,1)S(1)}, u32[]{:S(2)}, u32[]{:S(2)}) collective-permute-start(bf16[256,1024]{1,0:T(8,128)(2,1)S(1)} %get-tuple-element.32), channel_id=1, source_target_pairs={{0,256},{128,384},{256,0},{384,128},{1,257},{129,385},{257,1},{385... | collective-permute-start | bytes 1572872 | tf_op jit(solution)/shard_map/ppermute | solution.py:193
  88.0 13.4 %collective-permute-start.10 = (bf16[256,1024]{1,0:T(8,128)(2,1)S(1)}, bf16[256,1024]{1,0:T(8,128)(2,1)S(1)}, u32[]{:S(2)}, u32[]{:S(2)}) collective-permute-start(bf16[256,1024]{1,0:T(8,128)(2,1)S(1)} %get-tuple-element.33), channel_id=1, source_target_pairs={{0,384},{128,0},{256,128},{384,256},{1,385},{129,1},{257,129},{385... | collective-permute-start | bytes 1572872 | tf_op jit(solution)/shard_map/ppermute | solution.py:193
  91.1 12.3 %collective-permute-start.11 = (bf16[256,1024]{1,0:T(8,128)(2,1)S(1)}, bf16[256,1024]{1,0:T(8,128)(2,1)S(1)}, u32[]{:S(2)}, u32[]{:S(2)}) collective-permute-start(bf16[256,1024]{1,0:T(8,128)(2,1)S(1)} %get-tuple-element.34), channel_id=1, source_target_pairs={{0,128},{128,256},{256,384},{384,0},{1,129},{129,257},{257,385},{3... | collective-permute-start | bytes 1572872 | tf_op jit(solution)/shard_map/ppermute | solution.py:193
  105.3 40.8 %all-to-all-start.1 = ((bf16[16,128,256]{2,1,0:T(8,128)(2,1)}), bf16[16,128,256]{2,1,0:T(8,128)(2,1)S(1)}, u32[]{:S(2)}, u32[]{:S(2)}) async-start(bf16[16,128,256]{2,1,0:T(8,128)(2,1)} %shard_map.41), calls=%async_computation.1 | async-start | bytes 2097152 | tf_op jit(solution)/shard_map/all_to_all | solution.py:351
